TPU v7x, 32 devices: a whole 2x2x4 slice. The times are simulated.
32 devices in a mesh: row: 4 (over y, x), col: 8 (over z, core).
Axes of the slice: x: 2, y: 2, z: 4, core: 2. Of those that a mesh axis runs over, the one named last changes fastest.
Arguments:
- tiles: bfloat16 [4, 8, 32, 256, 256], P('row', 'col'), may hold values from -6 to 6
- tile_ids: int32 [4, 8, 2, 32], P('row', 'col'), may hold values from 0 to 7, as said below
- tile_count: int32 [4, 8], P('row', 'col'), may hold values from 8 to 32
- query_degree: int32 [8192], P('row'), may hold values from 1 to 32
- product_degree: int32 [16384], P('col'), may hold values from 1 to 32
- panel: float32 [64, 16384], P(None, ('col', 'row')), may hold values from -6 to 6
Outputs:
- basis: float32 [64, 16384], P(None, ('col', 'row'))
Inputs may be any that keep to these rules, and one draw needn't show every extreme that they name: `tile_ids`: on each device the 32 (tile row, tile column) pairs are distinct; tile row is below 8 and tile column below 8.
All inputs are finite; a program needn't handle non-finite values.
Results may differ from a plain program's by a relative error of at most 0.0042.
Values may be sent and summed in bfloat16 or wider, within the bound.
No kernel may reach another device: no remote copies, remote signals or barrier semaphores. Data moves between devices by JAX's collectives and lax.ppermute only.
A program may use at most 64 MiB of HBM per device.

v0:
```python
import functools
import math

import jax
import jax.numpy as jnp
from jax import lax
from jax.experimental import pallas as pl
from jax.experimental.pallas import tpu as pltpu
from jax.sharding import PartitionSpec as P

ITERS = 2
GROUP = 16
LOADS = 8
PANEL_STEP = 8
HIGH = lax.Precision.HIGHEST
VMEM_BYTES = 12 * 1024 * 1024
NT = (((1,), (1,)), ((), ()))
NN = (((1,), (0,)), ((), ()))

def inverse_factor(gram):
    width = gram.shape[0]
    rows = lax.broadcasted_iota(jnp.int32, (width, width), 0)
    cols = lax.broadcasted_iota(jnp.int32, (width, width), 1)
    work = jnp.concatenate([gram, (rows == cols).astype(jnp.float32)], axis=1)
    done = []
    for first in range(0, width, PANEL_STEP):
        height = width - first
        columns = [
            jnp.broadcast_to(work[:, first + j : first + j + 1], (height, 2 * width))
            for j in range(PANEL_STEP)
        ]
        for j in range(PANEL_STEP):
            scale = lax.rsqrt(columns[j][j : j + 1, :])
            row = work[j : j + 1, :] * scale
            factor = columns[j] * scale
            done.append(row)
            for later in range(j + 1, PANEL_STEP):
                columns[later] = columns[later] - factor * (columns[later][j : j + 1, :] * scale)
            work = work - factor * row
        work = work[PANEL_STEP:, :]
    return jnp.concatenate(done, axis=0)[:, width:]


WHOLE = pl.BlockSpec(memory_space=pltpu.VMEM)
SCALARS = pl.BlockSpec(memory_space=pltpu.SMEM)
AWAY = pl.BlockSpec(memory_space=pltpu.MemorySpace.HBM)


def call(body, name, in_specs, out_shape, scratch=(), flops=0, moved=0):
    many = isinstance(out_shape, (tuple, list))
    return pl.pallas_call(
        body,
        out_shape=out_shape,
        in_specs=in_specs,
        out_specs=[WHOLE] * len(out_shape) if many else WHOLE,
        scratch_shapes=scratch,
        compiler_params=pltpu.CompilerParams(vmem_limit_bytes=VMEM_BYTES),
        cost_estimate=pl.CostEstimate(flops=flops, bytes_accessed=moved, transcendentals=0),
        name=name,
    )


def in_hbm(value):
    return pltpu.with_memory_space_constraint(value, pltpu.MemorySpace.HBM)


def f32(*shape):
    return jax.ShapeDtypeStruct(shape, jnp.float32)


def bf16(*shape):
    return jax.ShapeDtypeStruct(shape, jnp.bfloat16)


def put(held, owner, value, side):
    share = value.shape[1]
    if share >= side:
        per = share // side
        for piece in range(per):
            held[owner * per + piece] = value[:, piece * side : (piece + 1) * side]
    else:
        per = side // share
        for at in range(per):

            @pl.when(owner % per == at)
            def _():
                held[owner // per, :, at * share : (at + 1) * share] = value


def get(total, owner, out_ref, side):
    share = out_ref.shape[1]
    if share >= side:
        per = share // side
        for piece in range(per):
            out_ref[:, piece * side : (piece + 1) * side] = total[owner * per + piece].astype(out_ref.dtype)
    else:
        per = side // share
        for at in range(per):

            @pl.when(owner % per == at)
            def _():
                out_ref[...] = total[owner // per, :, at * share : (at + 1) * share].astype(out_ref.dtype)


def emit(total, out_refs, me, side):
    count = len(out_refs)
    for at, out_ref in enumerate(out_refs):
        get(total, me ^ ((count - at) % count), out_ref, side)


def emit_pairs(total, mine_ref, other_ref, me, side):
    for step in range(mine_ref.shape[0]):
        get(total, me ^ (2 * step), mine_ref.at[step], side)
        get(total, me ^ (2 * step + 1), other_ref.at[step], side)


def collect(held, piece_refs, me, side):
    for step, piece_ref in enumerate(piece_refs):
        put(held, me ^ step, piece_ref[...], side)


def collect_pairs(held, mine_ref, other_ref, me, side):
    for step in range(mine_ref.shape[0]):
        put(held, me ^ (2 * step), mine_ref[step], side)
        put(held, me ^ (2 * step + 1), other_ref[step], side)


def group_of(g, source, target, dims, count, ids, held, tile_ref, total):
    tiles, width, _ = total.shape
    for lane in range(GROUP):
        slot = g * GROUP + lane
        give = jnp.where(slot < count, ids[target, slot], tiles - 1)
        term = lax.dot_general(
            held[ids[source, slot]], tile_ref[slot], dims, preferred_element_type=jnp.float32
        )
        if term.shape[0] > width:
            term = term[:width] + term[width:]
        total[give] += term


def groups(source, target, dims, count, ids, held, tile_ref, total):
    def step(g, carry):
        group_of(g, source, target, dims, count, ids, held, tile_ref, total)
        return carry

    last = tile_ref.shape[0] // GROUP
    lax.fori_loop(0, jnp.minimum((count + GROUP - 1) // GROUP, last), step, 0)


def first_body(n_in, ids, live, place, *refs):
    pieces, (tile_ref, mine_ref, other_ref, held, total) = refs[:n_in], refs[n_in:]
    side = tile_ref.shape[1]
    collect(held, pieces, place[0], side)
    total[...] = jnp.zeros_like(total)
    groups(1, 0, NT, live[0], ids, held, tile_ref, total)
    emit_pairs(total, mine_ref, other_ref, place[1], side)


def back_body(ids, live, place, here_ref, there_ref, tile_ref, *refs):
    out_refs, (held, total) = refs[:-2], refs[-2:]
    side = tile_ref.shape[1]
    collect_pairs(held, here_ref, there_ref, place[1], side)
    total[...] = jnp.zeros_like(total)
    groups(0, 1, NN, live[0], ids, held, tile_ref, total)
    emit(total, out_refs, place[0], side)


def next_body(n_in, ids, live, place, *refs):
    pieces, (scale_ref, tile_ref, out_ref, spread, held, total) = refs[:n_in], refs[n_in:]
    tiles, width, side = out_ref.shape
    collect(spread, pieces, place[0], side)
    for tile in range(spread.shape[0]):
        value = spread[tile] * scale_ref[:, tile * side : (tile + 1) * side]
        high = value.astype(jnp.bfloat16)
        held[tile, :width] = high
        held[tile, width:] = (value - high.astype(jnp.float32)).astype(jnp.bfloat16)
    total[...] = jnp.zeros_like(total)
    groups(1, 0, NT, live[0], ids, held, tile_ref, total)
    out_ref[...] = total[:tiles]


def add(refs):
    total = refs[0][...].astype(jnp.float32)
    for ref in refs[1:]:
        total = total + ref[...].astype(jnp.float32)
    return total


def start_body(place, panel_ref, degree_ref, out_ref, held, degrees, sems):
    share = panel_ref.shape[1]
    at = pl.multiple_of(place[0] * share, 128)
    loads = [
        pltpu.make_async_copy(degree_ref, degrees, sems.at[0]),
        pltpu.make_async_copy(panel_ref, held, sems.at[1]),
    ]
    for load in loads:
        load.start()
    for load in loads:
        load.wait()
    scale = 1.0 / jnp.sqrt(degrees[:, pl.ds(at, share)].astype(jnp.float32))
    out_ref[...] = (held[...] * scale).astype(out_ref.dtype)


def load_body(place, after_ref, tile_ref, product_ref, query_ref, *refs):
    keep, my_product_ref, product_out, my_query_ref, degrees, counts, sems = refs
    loads = [
        pltpu.make_async_copy(product_ref, degrees, sems.at[0]),
        pltpu.make_async_copy(query_ref, counts, sems.at[1]),
    ]
    part = tile_ref.shape[0] // LOADS
    for step in range(LOADS):
        span = pl.ds(step * part, part)
        loads.append(pltpu.make_async_copy(tile_ref.at[span], keep.at[span], sems.at[2 + step]))
    for load in loads:
        load.start()
    loads[0].wait()
    product_out[...] = 1.0 / jnp.sqrt(degrees[...].astype(jnp.float32))
    share = my_product_ref.shape[1]
    at = pl.multiple_of(place[0] * share, 128)
    my_product_ref[...] = product_out[:, pl.ds(at, share)]
    loads[1].wait()
    columns = my_query_ref.shape[1]
    if columns % 128 == 0:
        at = pl.multiple_of(place[1] * columns, 128)
        my_query_ref[...] = 1.0 / jnp.sqrt(counts[:, pl.ds(at, columns)].astype(jnp.float32))
    else:
        for step in range(counts.shape[1] // columns):

            @pl.when(place[1] == step)
            def _():
                degree = counts[:, step * columns : (step + 1) * columns]
                my_query_ref[...] = 1.0 / jnp.sqrt(degree.astype(jnp.float32))
    for load in loads[2:]:
        load.wait()


def pair_body(mine_ref, got_ref, *outs):
    count = len(outs)
    for at, out_ref in enumerate(outs):
        step = (count - at) % count
        out_ref[...] = (mine_ref[step] + got_ref[step]).astype(out_ref.dtype)


def join_body(*refs):
    for step, ref in enumerate(refs[:-1]):
        refs[-1][step] = ref[...]


def query_body(*refs):
    part_refs, scale_ref, out_ref = refs[:-2], refs[-2], refs[-1]
    out_ref[...] = (add(part_refs) * scale_ref[...]).astype(out_ref.dtype)


def lift_body(*refs):
    part_refs, scale_ref, lifted_ref, gram_ref = refs[:-3], refs[-3], refs[-2], refs[-1]
    lifted = add(part_refs) * scale_ref[...]
    lifted_ref[...] = lifted
    gram_ref[...] = lax.dot_general(lifted, lifted, NT, precision=HIGH, preferred_element_type=jnp.float32)


def gram_body(*refs):
    total = jnp.zeros(refs[-1].shape, jnp.float32)
    for ref in refs[:-1]:
        total = total + lax.dot_general(
            ref[...], ref[...], NT, precision=HIGH, preferred_element_type=jnp.float32
        )
    refs[-1][...] = total


def sum_body(*refs):
    refs[-1][...] = add(refs[:-1])


def apply_body(n_in, place, *refs):
    grams, (total_ref, mine_ref, other_ref, done) = refs[:n_in], refs[n_in:]
    tiles, _, side = total_ref.shape
    inverse = inverse_factor(add(grams))
    for tile in range(tiles):
        done[tile] = lax.dot_general(
            inverse, total_ref[tile], NN, precision=HIGH, preferred_element_type=jnp.float32
        )
    emit_pairs(done, mine_ref, other_ref, place[1], side)


def finish_body(after, *refs):
    grams, lifted_ref, out_ref = refs[:-2], refs[-2], refs[-1]
    out_ref[...] = (
        lax.dot_general(
            inverse_factor(add(grams)), lifted_ref[...], NN, precision=HIGH, preferred_element_type=jnp.float32
        )
        * after
    )


def swap(value, axis, step):
    return lax.ppermute(value, axis, [(i, i ^ step) for i in range(lax.axis_size(axis))])


def spread_to(value, axis, stride=1):
    return [value] + [swap(value, axis, step) for step in range(stride, lax.axis_size(axis), stride)]


def deal(values, axis, stride=1):
    count = len(values)
    return [values[0]] + [swap(value, axis, (count - at) * stride) for at, value in enumerate(values[1:], 1)]


def add_up(*values):
    return call(sum_body, "sum", [WHOLE] * len(values), f32(*values[0].shape))(*values)


def terms_over_col(gram):
    return spread_to(add_up(gram, swap(gram, "col", 1)), "col", 2)


def shards(tiles, tile_ids, tile_count, query_degree, product_degree, panel):
    tile_set = tiles[0, 0]
    ids = tile_ids[0, 0]
    live = tile_count[0]
    slots, side, _ = tile_set.shape
    width, share = panel.shape
    queries, products = query_degree.shape[0], product_degree.shape[0]
    query_tiles, product_tiles = queries // side, products // side
    n_row, n_col = lax.axis_size("row"), lax.axis_size("col")
    chips = n_col // 2
    place = jnp.stack([lax.axis_index("row"), lax.axis_index("col")]).astype(jnp.int32)
    columns = queries // n_col
    work = dict(flops=2 * slots * width * side * side, moved=2 * slots * side * side)
    scaled = call(
        start_body,
        "start",
        [SCALARS, AWAY, AWAY],
        bf16(width, share),
        [
            pltpu.VMEM((width, share), jnp.float32),
            pltpu.VMEM((1, products), jnp.int32),
            pltpu.SemaphoreType.DMA((2,)),
        ],
    )(place, in_hbm(panel), in_hbm(product_degree[None, :]))
    pieces = spread_to(scaled, "row")
    tile_set, my_pscale, pscale, my_qscale = call(
        load_body,
        "load",
        [SCALARS, WHOLE, AWAY, AWAY, AWAY],
        [pltpu.VMEM((slots, side, side), jnp.bfloat16), f32(1, share), f32(1, products), f32(1, columns)],
        [
            pltpu.VMEM((1, products), jnp.int32),
            pltpu.VMEM((1, queries), jnp.int32),
            pltpu.SemaphoreType.DMA((2 + LOADS,)),
        ],
        moved=4 * slots * side * side,
    )(place, scaled, in_hbm(tile_set), in_hbm(product_degree[None, :]), in_hbm(query_degree[None, :]))
    tile_set = pltpu.with_memory_space_constraint(tile_set, pltpu.VMEM)
    root_count = math.sqrt(products * n_col)
    half_shapes = [f32(chips, width, columns)] * 2
    query_scratch = pltpu.VMEM((query_tiles + 1, width, side), jnp.float32)
    product_scratch = pltpu.VMEM((product_tiles + 1, width, side), jnp.float32)
    for iteration in range(ITERS):
        if iteration == 0:
            mine, other = call(
                functools.partial(first_body, n_row),
                "forward",
                [SCALARS] * 3 + [WHOLE] * (n_row + 1),
                half_shapes,
                [pltpu.VMEM((product_tiles, width, side), jnp.bfloat16), query_scratch],
                **work,
            )(ids, live, place, *pieces, tile_set)
        else:
            pieces = spread_to(lifted, "row")
            gram = call(gram_body, "gram", [WHOLE] * n_row, f32(width, width))(*pieces)
            grams = terms_over_col(gram)
            total = call(
                functools.partial(next_body, n_row),
                "forward",
                [SCALARS] * 3 + [WHOLE] * (n_row + 2),
                f32(query_tiles, width, side),
                [
                    pltpu.VMEM((product_tiles, width, side), jnp.float32),
                    pltpu.VMEM((product_tiles, 2 * width, side), jnp.bfloat16),
                    query_scratch,
                ],
                **work,
            )(ids, live, place, *pieces, pscale, tile_set)
            mine, other = call(
                functools.partial(apply_body, chips),
                "apply",
                [SCALARS] + [WHOLE] * (chips + 1),
                half_shapes,
                [pltpu.VMEM((query_tiles, width, side), jnp.float32)],
            )(place, *grams, total)
        sums = call(
            pair_body, "pair", [WHOLE] * 2, [f32(width, columns)] + [bf16(width, columns)] * (chips - 1)
        )(mine, swap(other, "col", 1))
        parts = deal(sums, "col", 2)
        rounded = call(query_body, "query", [WHOLE] * (chips + 1), bf16(width, columns))(*parts, my_qscale)
        here = call(join_body, "join", [WHOLE] * chips, bf16(chips, width, columns))(
            *spread_to(rounded, "col", 2)
        )
        sums = call(
            back_body,
            "backward",
            [SCALARS] * 3 + [WHOLE] * 3,
            [f32(width, share)] * n_row,
            [pltpu.VMEM((query_tiles, width, side), jnp.bfloat16), product_scratch],
            **work,
        )(ids, live, place, here, swap(here, "col", 1), tile_set)
        lifted, gram = call(
            lift_body, "lift", [WHOLE] * (n_row + 1), [f32(width, share), f32(width, width)]
        )(*deal(sums, "row"), my_pscale)
    return call(
        functools.partial(finish_body, root_count), "finish", [WHOLE] * (chips + 1), f32(width, share)
    )(*terms_over_col(add_up(*spread_to(gram, "row"))), lifted)


def solution(mesh):
    in_specs = (
        P("row", "col", None, None, None),
        P("row", "col", None, None),
        P("row", "col"),
        P("row"),
        P("col"),
        P(None, ("col", "row")),
    )
    out_specs = P(None, ("col", "row"))
    return jax.shard_map(shards, mesh=mesh, in_specs=in_specs, out_specs=out_specs, check_vma=False)
```

profile of v0, /device:TPU:0, one launch (start us, length us, event | category | flops | bytes accessed | tf_op | source)
XLA Modules:
  0.0 109.7 jit_solution(9454682370878684919)
XLA Ops:
  0.1 1.5 %start.1.after_ref.refs_0_ = bf16[64,512]{1,0:T(8,128)(2,1)S(1)} custom-call(s32[2]{0:T(128)S(1)} %pad_add_fusion.place, f32[64,512]{1,0:T(8,128)} %panel_ref.1, s32[1,2048]{1,0:T(1,128)} %bitcast.16), custom_call_target="tpu_custom_call" | custom-call | tf_op jit(solution)/shard_map/start/pallas_call | solution.py:329
  1.6 4.0 %collective-permute-start.2 = (bf16[64,512]{1,0:T(8,128)(2,1)S(1)}, bf16[64,512]{1,0:T(8,128)(2,1)S(1)}, u32[]{:S(2)}, u32[]{:S(2)}) collective-permute-start(bf16[64,512]{1,0:T(8,128)(2,1)S(1)} %start.1.after_ref.refs_0_), channel_id=1, source_target_pairs={{0,24},{8,16},{16,8},{24,0},{1,25},{9,17},{17,9},{25,1},{2,26},{10... | collective-permute-start | bytes 196616 | tf_op jit(solution)/shard_map/ppermute | solution.py:296
  6.8 2.8 %load.1 = (bf16[32,256,256]{2,1,0:T(8,128)(2,1)S(1)}, f32[1,512]{1,0:T(1,128)S(1)}, f32[1,2048]{1,0:T(1,128)S(1)}, f32[1,256]{1,0:T(1,128)S(1)}) custom-call(s32[2]{0:T(128)S(1)} %pad_add_fusion.place, bf16[64,512]{1,0:T(8,128)(2,1)S(1)} %start.1.after_ref.refs_0_, bf16[32,256,256]{2,1,0:T(8,128)(2,1)} %bitcast.15, s32[1,2048]{1,0:T(1,128)} %bitcast.17, ...), custom_call_target="tpu_custom_call" | custom-call | bytes 8388608 | tf_op jit(solution)/shard_map/load/pallas_call | solution.py:341
  10.3 2.2 %forward.2 = (f32[4,64,256]{2,1,0:T(8,128)S(1)}, f32[4,64,256]{2,1,0:T(8,128)S(1)}) custom-call(s32[2,32]{1,0:T(2,128)S(1)} %bitcast.11, s32[1]{0:T(128)} %bitcast.7.live, s32[2]{0:T(128)S(1)} %pad_add_fusion.place, bf16[64,512]{1,0:T(8,128)(2,1)S(1)} %start.1.after_ref.refs_0_, bf16[64,512]{1,0:T(8,128)(2,1)S(1)} %collective-permute-done.refs_1_, ...), custom_call_target="tpu_custom_call" | custom-call | flops 268435456 | bytes 4194304 | tf_op jit(solution)/shard_map/forward/pallas_call | solution.py:360
  12.6 1.5 %collective-permute-done.3.got_ref = f32[4,64,256]{2,1,0:T(8,128)S(1)} collective-permute-done((f32[4,64,256]{2,1,0:T(8,128)S(1)}, f32[4,64,256]{2,1,0:T(8,128)S(1)}, u32[]{:S(2)}, u32[]{:S(2)}) %collective-permute-start.3) | collective-permute-done | bytes 262176 | tf_op jit(solution)/shard_map/ppermute | solution.py:296
  14.1 2.9 %collective-permute-start.4 = (bf16[64,256]{1,0:T(8,128)(2,1)S(1)}, bf16[64,256]{1,0:T(8,128)(2,1)S(1)}, u32[]{:S(2)}, u32[]{:S(2)}) collective-permute-start(bf16[64,256]{1,0:T(8,128)(2,1)S(1)} %get-tuple-element.36), channel_id=1, source_target_pairs={{0,6},{1,7},{2,4},{3,5},{4,2},{5,3},{6,0},{7,1},{8,14},{9,15},{10,... | collective-permute-start | bytes 98312 | tf_op jit(solution)/shard_map/ppermute | solution.py:296
  18.6 1.4 %collective-permute-done.4.refs_1_ = bf16[64,256]{1,0:T(8,128)(2,1)S(1)} collective-permute-done((bf16[64,256]{1,0:T(8,128)(2,1)S(1)}, bf16[64,256]{1,0:T(8,128)(2,1)S(1)}, u32[]{:S(2)}, u32[]{:S(2)}) %collective-permute-start.4) | collective-permute-done | bytes 32800 | tf_op jit(solution)/shard_map/ppermute | solution.py:296
  20.0 1.9 %collective-permute-done.5.refs_2_ = bf16[64,256]{1,0:T(8,128)(2,1)S(1)} collective-permute-done((bf16[64,256]{1,0:T(8,128)(2,1)S(1)}, bf16[64,256]{1,0:T(8,128)(2,1)S(1)}, u32[]{:S(2)}, u32[]{:S(2)}) %collective-permute-start.5) | collective-permute-done | bytes 32800 | tf_op jit(solution)/shard_map/ppermute | solution.py:296
  22.0 2.0 %collective-permute-start.9 = (bf16[64,256]{1,0:T(8,128)(2,1)S(1)}, bf16[64,256]{1,0:T(8,128)(2,1)S(1)}, u32[]{:S(2)}, u32[]{:S(2)}) collective-permute-start(bf16[64,256]{1,0:T(8,128)(2,1)S(1)} %query.2.refs_0_), channel_id=1, source_target_pairs={{0,6},{1,7},{2,4},{3,5},{4,2},{5,3},{6,0},{7,1},{8,14},{9,15},{10,... | collective-permute-start | bytes 98312 | tf_op jit(solution)/shard_map/ppermute | solution.py:296
  24.1 2.4 %collective-permute-start.7 = (bf16[64,256]{1,0:T(8,128)(2,1)S(1)}, bf16[64,256]{1,0:T(8,128)(2,1)S(1)}, u32[]{:S(2)}, u32[]{:S(2)}) collective-permute-start(bf16[64,256]{1,0:T(8,128)(2,1)S(1)} %query.2.refs_0_), channel_id=1, source_target_pairs={{0,2},{1,3},{2,0},{3,1},{4,6},{5,7},{6,4},{7,5},{8,10},{9,11},{10,... | collective-permute-start | bytes 98312 | tf_op jit(solution)/shard_map/ppermute | solution.py:296
  30.6 1.6 %backward.2 = (f32[64,512]{1,0:T(8,128)S(1)}, f32[64,512]{1,0:T(8,128)S(1)}, f32[64,512]{1,0:T(8,128)S(1)}, f32[64,512]{1,0:T(8,128)S(1)}) custom-call(s32[2,32]{1,0:T(2,128)S(1)} %bitcast.12, s32[1]{0:T(128)} %bitcast.8.live, s32[2]{0:T(128)S(1)} %pad_add_fusion.place, bf16[4,64,256]{2,1,0:T(8,128)(2,1)S(1)} %join.2.here_ref, ...), custom_call_target="tpu_custom_call" | custom-call | flops 268435456 | bytes 4194304 | tf_op jit(solution)/shard_map/backward/pallas_call | solution.py:399
  32.2 2.3 %collective-permute-start.11 = (f32[64,512]{1,0:T(8,128)S(1)}, f32[64,512]{1,0:T(8,128)S(1)}, u32[]{:S(2)}, u32[]{:S(2)}) collective-permute-start(f32[64,512]{1,0:T(8,128)S(1)} %get-tuple-element.41), channel_id=1, source_target_pairs={{0,24},{8,16},{16,8},{24,0},{1,25},{9,17},{17,9},{25,1},{2,26},{10... | collective-permute-start | bytes 393224 | tf_op jit(solution)/shard_map/ppermute | solution.py:296
  35.8 2.7 %collective-permute-done.11.refs_1_ = f32[64,512]{1,0:T(8,128)S(1)} collective-permute-done((f32[64,512]{1,0:T(8,128)S(1)}, f32[64,512]{1,0:T(8,128)S(1)}, u32[]{:S(2)}, u32[]{:S(2)}) %collective-permute-start.11) | collective-permute-done | bytes 131104 | tf_op jit(solution)/shard_map/ppermute | solution.py:296
  38.4 2.7 %collective-permute-done.12.refs_2_ = f32[64,512]{1,0:T(8,128)S(1)} collective-permute-done((f32[64,512]{1,0:T(8,128)S(1)}, f32[64,512]{1,0:T(8,128)S(1)}, u32[]{:S(2)}, u32[]{:S(2)}) %collective-permute-start.12) | collective-permute-done | bytes 131104 | tf_op jit(solution)/shard_map/ppermute | solution.py:296
  46.2 3.8 %collective-permute-done.16.refs_3_ = f32[64,512]{1,0:T(8,128)S(1)} collective-permute-done((f32[64,512]{1,0:T(8,128)S(1)}, f32[64,512]{1,0:T(8,128)S(1)}, u32[]{:S(2)}, u32[]{:S(2)}) %collective-permute-start.16) | collective-permute-done | bytes 131104 | tf_op jit(solution)/shard_map/ppermute | solution.py:296
  50.0 1.6 %collective-permute-done.15.refs_2_ = f32[64,512]{1,0:T(8,128)S(1)} collective-permute-done((f32[64,512]{1,0:T(8,128)S(1)}, f32[64,512]{1,0:T(8,128)S(1)}, u32[]{:S(2)}, u32[]{:S(2)}) %collective-permute-start.15) | collective-permute-done | bytes 131104 | tf_op jit(solution)/shard_map/ppermute | solution.py:296
  53.7 2.3 %collective-permute-start.20 = (f32[64,64]{1,0:T(8,128)S(1)}, f32[64,64]{1,0:T(8,128)S(1)}, u32[]{:S(2)}, u32[]{:S(2)}) collective-permute-start(f32[64,64]{1,0:T(8,128)S(1)} %sum.3.refs_0_), channel_id=1, source_target_pairs={{0,6},{1,7},{2,4},{3,5},{4,2},{5,3},{6,0},{7,1},{8,14},{9,15},{10,... | collective-permute-start | bytes 49160 | tf_op jit(solution)/shard_map/ppermute | solution.py:296
  58.1 2.4 %forward.3.refs_4_ = f32[8,64,256]{2,1,0:T(8,128)S(1)} custom-call(s32[2,32]{1,0:T(2,128)S(1)} %bitcast.13, s32[1]{0:T(128)} %bitcast.9.live, s32[2]{0:T(128)S(1)} %pad_add_fusion.place, f32[64,512]{1,0:T(8,128)S(1)} %get-tuple-element.45.refs_0_, f32[64,512]{1,0:T(8,128)S(1)} %collective-permute-done.14.refs_1_, ...), custom_call_target="tpu_custom_call" | custom-call | flops 268435456 | bytes 4194304 | tf_op jit(solution)/shard_map/forward/pallas_call | solution.py:372
  61.1 2.7 %apply.1 = (f32[4,64,256]{2,1,0:T(8,128)S(1)}, f32[4,64,256]{2,1,0:T(8,128)S(1)}) custom-call(s32[2]{0:T(128)S(1)} %pad_add_fusion.place, f32[64,64]{1,0:T(8,128)S(1)} %sum.3.refs_0_, f32[64,64]{1,0:T(8,128)S(1)} %collective-permute-done.18.refs_1_, f32[64,64]{1,0:T(8,128)S(1)} %collective-permute-done.19.refs_2_, ...), custom_call_target="tpu_custom_call" | custom-call | tf_op jit(solution)/shard_map/apply/pallas_call | solution.py:384
  63.9 1.5 %collective-permute-done.21.got_ref = f32[4,64,256]{2,1,0:T(8,128)S(1)} collective-permute-done((f32[4,64,256]{2,1,0:T(8,128)S(1)}, f32[4,64,256]{2,1,0:T(8,128)S(1)}, u32[]{:S(2)}, u32[]{:S(2)}) %collective-permute-start.21) | collective-permute-done | bytes 262176 | tf_op jit(solution)/shard_map/ppermute | solution.py:296
  65.5 1.7 %collective-permute-start.22 = (bf16[64,256]{1,0:T(8,128)(2,1)S(1)}, bf16[64,256]{1,0:T(8,128)(2,1)S(1)}, u32[]{:S(2)}, u32[]{:S(2)}) collective-permute-start(bf16[64,256]{1,0:T(8,128)(2,1)S(1)} %get-tuple-element.50), channel_id=1, source_target_pairs={{0,6},{1,7},{2,4},{3,5},{4,2},{5,3},{6,0},{7,1},{8,14},{9,15},{10,... | collective-permute-start | bytes 98312 | tf_op jit(solution)/shard_map/ppermute | solution.py:296
  68.0 2.0 %collective-permute-start.24 = (bf16[64,256]{1,0:T(8,128)(2,1)S(1)}, bf16[64,256]{1,0:T(8,128)(2,1)S(1)}, u32[]{:S(2)}, u32[]{:S(2)}) collective-permute-start(bf16[64,256]{1,0:T(8,128)(2,1)S(1)} %get-tuple-element.52), channel_id=1, source_target_pairs={{0,2},{1,3},{2,0},{3,1},{4,6},{5,7},{6,4},{7,5},{8,10},{9,11},{10,... | collective-permute-start | bytes 98312 | tf_op jit(solution)/shard_map/ppermute | solution.py:296
  69.9 1.6 %collective-permute-done.22.refs_1_ = bf16[64,256]{1,0:T(8,128)(2,1)S(1)} collective-permute-done((bf16[64,256]{1,0:T(8,128)(2,1)S(1)}, bf16[64,256]{1,0:T(8,128)(2,1)S(1)}, u32[]{:S(2)}, u32[]{:S(2)}) %collective-permute-start.22) | collective-permute-done | bytes 32800 | tf_op jit(solution)/shard_map/ppermute | solution.py:296
  72.3 2.3 %collective-permute-start.27 = (bf16[64,256]{1,0:T(8,128)(2,1)S(1)}, bf16[64,256]{1,0:T(8,128)(2,1)S(1)}, u32[]{:S(2)}, u32[]{:S(2)}) collective-permute-start(bf16[64,256]{1,0:T(8,128)(2,1)S(1)} %query.3.refs_0_), channel_id=1, source_target_pairs={{0,6},{1,7},{2,4},{3,5},{4,2},{5,3},{6,0},{7,1},{8,14},{9,15},{10,... | collective-permute-start | bytes 98312 | tf_op jit(solution)/shard_map/ppermute | solution.py:296
  78.1 1.5 %collective-permute-done.26.refs_2_ = bf16[64,256]{1,0:T(8,128)(2,1)S(1)} collective-permute-done((bf16[64,256]{1,0:T(8,128)(2,1)S(1)}, bf16[64,256]{1,0:T(8,128)(2,1)S(1)}, u32[]{:S(2)}, u32[]{:S(2)}) %collective-permute-start.26) | collective-permute-done | bytes 32800 | tf_op jit(solution)/shard_map/ppermute | solution.py:296
  81.1 1.6 %backward.3 = (f32[64,512]{1,0:T(8,128)S(1)}, f32[64,512]{1,0:T(8,128)S(1)}, f32[64,512]{1,0:T(8,128)S(1)}, f32[64,512]{1,0:T(8,128)S(1)}) custom-call(s32[2,32]{1,0:T(2,128)S(1)} %bitcast.14, s32[1]{0:T(128)} %bitcast.10.live, s32[2]{0:T(128)S(1)} %pad_add_fusion.place, bf16[4,64,256]{2,1,0:T(8,128)(2,1)S(1)} %join.3.here_ref, ...), custom_call_target="tpu_custom_call" | custom-call | flops 268435456 | bytes 4194304 | tf_op jit(solution)/shard_map/backward/pallas_call | solution.py:399
  86.3 3.6 %collective-permute-done.29.refs_1_ = f32[64,512]{1,0:T(8,128)S(1)} collective-permute-done((f32[64,512]{1,0:T(8,128)S(1)}, f32[64,512]{1,0:T(8,128)S(1)}, u32[]{:S(2)}, u32[]{:S(2)}) %collective-permute-start.29) | collective-permute-done | bytes 131104 | tf_op jit(solution)/shard_map/ppermute | solution.py:296
  89.8 1.7 %collective-permute-done.30.refs_2_ = f32[64,512]{1,0:T(8,128)S(1)} collective-permute-done((f32[64,512]{1,0:T(8,128)S(1)}, f32[64,512]{1,0:T(8,128)S(1)}, u32[]{:S(2)}, u32[]{:S(2)}) %collective-permute-start.30) | collective-permute-done | bytes 131104 | tf_op jit(solution)/shard_map/ppermute | solution.py:296
  100.3 1.8 %collective-permute-start.38 = (f32[64,64]{1,0:T(8,128)S(1)}, f32[64,64]{1,0:T(8,128)S(1)}, u32[]{:S(2)}, u32[]{:S(2)}) collective-permute-start(f32[64,64]{1,0:T(8,128)S(1)} %sum.5.refs_0_), channel_id=1, source_target_pairs={{0,6},{1,7},{2,4},{3,5},{4,2},{5,3},{6,0},{7,1},{8,14},{9,15},{10,... | collective-permute-start | bytes 49160 | tf_op jit(solution)/shard_map/ppermute | solution.py:296
  102.9 1.7 %collective-permute-start.36 = (f32[64,64]{1,0:T(8,128)S(1)}, f32[64,64]{1,0:T(8,128)S(1)}, u32[]{:S(2)}, u32[]{:S(2)}) collective-permute-start(f32[64,64]{1,0:T(8,128)S(1)} %sum.5.refs_0_), channel_id=1, source_target_pairs={{0,2},{1,3},{2,0},{3,1},{4,6},{5,7},{6,4},{7,5},{8,10},{9,11},{10,... | collective-permute-start | bytes 49160 | tf_op jit(solution)/shard_map/ppermute | solution.py:296
  104.6 1.7 %collective-permute-done.38.refs_3_ = f32[64,64]{1,0:T(8,128)S(1)} collective-permute-done((f32[64,64]{1,0:T(8,128)S(1)}, f32[64,64]{1,0:T(8,128)S(1)}, u32[]{:S(2)}, u32[]{:S(2)}) %collective-permute-start.38) | collective-permute-done | bytes 16416 | tf_op jit(solution)/shard_map/ppermute | solution.py:296
  107.2 2.5 %finish.1 = f32[64,512]{1,0:T(8,128)} custom-call(f32[64,64]{1,0:T(8,128)S(1)} %sum.5.refs_0_, f32[64,64]{1,0:T(8,128)S(1)} %collective-permute-done.36.refs_1_, f32[64,64]{1,0:T(8,128)S(1)} %collective-permute-done.37.refs_2_, f32[64,64]{1,0:T(8,128)S(1)} %collective-permute-done.38.refs_3_, f32[64,512]{1,0:T(8,128)S(1)} %get-tuple-element.58.refs_4_), custom_call_target="tpu_custom_call" | custom-call | tf_op jit(solution)/shard_map/finish/pallas_call | solution.py:410
  (69 shorter events, 39.1 us)
Async XLA Ops:
  1.6 8.1 %collective-permute-start.2 = (bf16[64,512]{1,0:T(8,128)(2,1)S(1)}, bf16[64,512]{1,0:T(8,128)(2,1)S(1)}, u32[]{:S(2)}, u32[]{:S(2)}) collective-permute-start(bf16[64,512]{1,0:T(8,128)(2,1)S(1)} %start.1.after_ref.refs_0_), channel_id=1, source_target_pairs={{0,24},{8,16},{16,8},{24,0},{1,25},{9,17},{17,9},{25,1},{2,26},{10... | collective-permute-start | bytes 196616 | tf_op jit(solution)/shard_map/ppermute | solution.py:296
  5.5 4.3 %collective-permute-start.1 = (bf16[64,512]{1,0:T(8,128)(2,1)S(1)}, bf16[64,512]{1,0:T(8,128)(2,1)S(1)}, u32[]{:S(2)}, u32[]{:S(2)}) collective-permute-start(bf16[64,512]{1,0:T(8,128)(2,1)S(1)} %start.1.after_ref.refs_0_), channel_id=1, source_target_pairs={{0,16},{8,24},{16,0},{24,8},{1,17},{9,25},{17,1},{25,9},{2,18},{10... | collective-permute-start | bytes 196616 | tf_op jit(solution)/shard_map/ppermute | solution.py:296
  6.1 4.3 %collective-permute-start = (bf16[64,512]{1,0:T(8,128)(2,1)S(1)}, bf16[64,512]{1,0:T(8,128)(2,1)S(1)}, u32[]{:S(2)}, u32[]{:S(2)}) collective-permute-start(bf16[64,512]{1,0:T(8,128)(2,1)S(1)} %start.1.after_ref.refs_0_), channel_id=1, source_target_pairs={{0,8},{8,0},{16,24},{24,16},{1,9},{9,1},{17,25},{25,17},{2,10},{10... | collective-permute-start | bytes 196616 | tf_op jit(solution)/shard_map/ppermute | solution.py:296
  14.1 5.9 %collective-permute-start.4 = (bf16[64,256]{1,0:T(8,128)(2,1)S(1)}, bf16[64,256]{1,0:T(8,128)(2,1)S(1)}, u32[]{:S(2)}, u32[]{:S(2)}) collective-permute-start(bf16[64,256]{1,0:T(8,128)(2,1)S(1)} %get-tuple-element.36), channel_id=1, source_target_pairs={{0,6},{1,7},{2,4},{3,5},{4,2},{5,3},{6,0},{7,1},{8,14},{9,15},{10,... | collective-permute-start | bytes 98312 | tf_op jit(solution)/shard_map/ppermute | solution.py:296
  17.0 4.9 %collective-permute-start.5 = (bf16[64,256]{1,0:T(8,128)(2,1)S(1)}, bf16[64,256]{1,0:T(8,128)(2,1)S(1)}, u32[]{:S(2)}, u32[]{:S(2)}) collective-permute-start(bf16[64,256]{1,0:T(8,128)(2,1)S(1)} %get-tuple-element.37), channel_id=1, source_target_pairs={{0,4},{1,5},{2,6},{3,7},{4,0},{5,1},{6,2},{7,3},{8,12},{9,13},{10,... | collective-permute-start | bytes 98312 | tf_op jit(solution)/shard_map/ppermute | solution.py:296
  17.2 4.7 %collective-permute-start.6 = (bf16[64,256]{1,0:T(8,128)(2,1)S(1)}, bf16[64,256]{1,0:T(8,128)(2,1)S(1)}, u32[]{:S(2)}, u32[]{:S(2)}) collective-permute-start(bf16[64,256]{1,0:T(8,128)(2,1)S(1)} %get-tuple-element.38), channel_id=1, source_target_pairs={{0,2},{1,3},{2,0},{3,1},{4,6},{5,7},{6,4},{7,5},{8,10},{9,11},{10,... | collective-permute-start | bytes 98312 | tf_op jit(solution)/shard_map/ppermute | solution.py:296
  22.0 5.8 %collective-permute-start.9 = (bf16[64,256]{1,0:T(8,128)(2,1)S(1)}, bf16[64,256]{1,0:T(8,128)(2,1)S(1)}, u32[]{:S(2)}, u32[]{:S(2)}) collective-permute-start(bf16[64,256]{1,0:T(8,128)(2,1)S(1)} %query.2.refs_0_), channel_id=1, source_target_pairs={{0,6},{1,7},{2,4},{3,5},{4,2},{5,3},{6,0},{7,1},{8,14},{9,15},{10,... | collective-permute-start | bytes 98312 | tf_op jit(solution)/shard_map/ppermute | solution.py:296
  24.0 5.2 %collective-permute-start.8 = (bf16[64,256]{1,0:T(8,128)(2,1)S(1)}, bf16[64,256]{1,0:T(8,128)(2,1)S(1)}, u32[]{:S(2)}, u32[]{:S(2)}) collective-permute-start(bf16[64,256]{1,0:T(8,128)(2,1)S(1)} %query.2.refs_0_), channel_id=1, source_target_pairs={{0,4},{1,5},{2,6},{3,7},{4,0},{5,1},{6,2},{7,3},{8,12},{9,13},{10,... | collective-permute-start | bytes 98312 | tf_op jit(solution)/shard_map/ppermute | solution.py:296
  24.1 5.1 %collective-permute-start.7 = (bf16[64,256]{1,0:T(8,128)(2,1)S(1)}, bf16[64,256]{1,0:T(8,128)(2,1)S(1)}, u32[]{:S(2)}, u32[]{:S(2)}) collective-permute-start(bf16[64,256]{1,0:T(8,128)(2,1)S(1)} %query.2.refs_0_), channel_id=1, source_target_pairs={{0,2},{1,3},{2,0},{3,1},{4,6},{5,7},{6,4},{7,5},{8,10},{9,11},{10,... | collective-permute-start | bytes 98312 | tf_op jit(solution)/shard_map/ppermute | solution.py:296
  32.2 6.2 %collective-permute-start.11 = (f32[64,512]{1,0:T(8,128)S(1)}, f32[64,512]{1,0:T(8,128)S(1)}, u32[]{:S(2)}, u32[]{:S(2)}) collective-permute-start(f32[64,512]{1,0:T(8,128)S(1)} %get-tuple-element.41), channel_id=1, source_target_pairs={{0,24},{8,16},{16,8},{24,0},{1,25},{9,17},{17,9},{25,1},{2,26},{10... | collective-permute-start | bytes 393224 | tf_op jit(solution)/shard_map/ppermute | solution.py:296
  34.5 6.6 %collective-permute-start.12 = (f32[64,512]{1,0:T(8,128)S(1)}, f32[64,512]{1,0:T(8,128)S(1)}, u32[]{:S(2)}, u32[]{:S(2)}) collective-permute-start(f32[64,512]{1,0:T(8,128)S(1)} %get-tuple-element.42), channel_id=1, source_target_pairs={{0,16},{8,24},{16,0},{24,8},{1,17},{9,25},{17,1},{25,9},{2,18},{10... | collective-permute-start | bytes 393224 | tf_op jit(solution)/shard_map/ppermute | solution.py:296
  34.7 7.1 %collective-permute-start.13 = (f32[64,512]{1,0:T(8,128)S(1)}, f32[64,512]{1,0:T(8,128)S(1)}, u32[]{:S(2)}, u32[]{:S(2)}) collective-permute-start(f32[64,512]{1,0:T(8,128)S(1)} %get-tuple-element.43), channel_id=1, source_target_pairs={{0,8},{8,0},{16,24},{24,16},{1,9},{9,1},{17,25},{25,17},{2,10},{10... | collective-permute-start | bytes 393224 | tf_op jit(solution)/shard_map/ppermute | solution.py:296
  42.7 7.3 %collective-permute-start.16 = (f32[64,512]{1,0:T(8,128)S(1)}, f32[64,512]{1,0:T(8,128)S(1)}, u32[]{:S(2)}, u32[]{:S(2)}) collective-permute-start(f32[64,512]{1,0:T(8,128)S(1)} %get-tuple-element.45.refs_0_), channel_id=1, source_target_pairs={{0,24},{8,16},{16,8},{24,0},{1,25},{9,17},{17,9},{25,1},{2,26},{10... | collective-permute-start | bytes 393224 | tf_op jit(solution)/shard_map/ppermute | solution.py:296
  44.1 7.5 %collective-permute-start.15 = (f32[64,512]{1,0:T(8,128)S(1)}, f32[64,512]{1,0:T(8,128)S(1)}, u32[]{:S(2)}, u32[]{:S(2)}) collective-permute-start(f32[64,512]{1,0:T(8,128)S(1)} %get-tuple-element.45.refs_0_), channel_id=1, source_target_pairs={{0,16},{8,24},{16,0},{24,8},{1,17},{9,25},{17,1},{25,9},{2,18},{10... | collective-permute-start | bytes 393224 | tf_op jit(solution)/shard_map/ppermute | solution.py:296
  45.4 6.5 %collective-permute-start.14 = (f32[64,512]{1,0:T(8,128)S(1)}, f32[64,512]{1,0:T(8,128)S(1)}, u32[]{:S(2)}, u32[]{:S(2)}) collective-permute-start(f32[64,512]{1,0:T(8,128)S(1)} %get-tuple-element.45.refs_0_), channel_id=1, source_target_pairs={{0,8},{8,0},{16,24},{24,16},{1,9},{9,1},{17,25},{25,17},{2,10},{10... | collective-permute-start | bytes 393224 | tf_op jit(solution)/shard_map/ppermute | solution.py:296
  53.7 6.8 %collective-permute-start.20 = (f32[64,64]{1,0:T(8,128)S(1)}, f32[64,64]{1,0:T(8,128)S(1)}, u32[]{:S(2)}, u32[]{:S(2)}) collective-permute-start(f32[64,64]{1,0:T(8,128)S(1)} %sum.3.refs_0_), channel_id=1, source_target_pairs={{0,6},{1,7},{2,4},{3,5},{4,2},{5,3},{6,0},{7,1},{8,14},{9,15},{10,... | collective-permute-start | bytes 49160 | tf_op jit(solution)/shard_map/ppermute | solution.py:296
  56.1 4.9 %collective-permute-start.19 = (f32[64,64]{1,0:T(8,128)S(1)}, f32[64,64]{1,0:T(8,128)S(1)}, u32[]{:S(2)}, u32[]{:S(2)}) collective-permute-start(f32[64,64]{1,0:T(8,128)S(1)} %sum.3.refs_0_), channel_id=1, source_target_pairs={{0,4},{1,5},{2,6},{3,7},{4,0},{5,1},{6,2},{7,3},{8,12},{9,13},{10,... | collective-permute-start | bytes 49160 | tf_op jit(solution)/shard_map/ppermute | solution.py:296
  56.8 4.3 %collective-permute-start.18 = (f32[64,64]{1,0:T(8,128)S(1)}, f32[64,64]{1,0:T(8,128)S(1)}, u32[]{:S(2)}, u32[]{:S(2)}) collective-permute-start(f32[64,64]{1,0:T(8,128)S(1)} %sum.3.refs_0_), channel_id=1, source_target_pairs={{0,2},{1,3},{2,0},{3,1},{4,6},{5,7},{6,4},{7,5},{8,10},{9,11},{10,... | collective-permute-start | bytes 49160 | tf_op jit(solution)/shard_map/ppermute | solution.py:296
  65.5 6.0 %collective-permute-start.22 = (bf16[64,256]{1,0:T(8,128)(2,1)S(1)}, bf16[64,256]{1,0:T(8,128)(2,1)S(1)}, u32[]{:S(2)}, u32[]{:S(2)}) collective-permute-start(bf16[64,256]{1,0:T(8,128)(2,1)S(1)} %get-tuple-element.50), channel_id=1, source_target_pairs={{0,6},{1,7},{2,4},{3,5},{4,2},{5,3},{6,0},{7,1},{8,14},{9,15},{10,... | collective-permute-start | bytes 98312 | tf_op jit(solution)/shard_map/ppermute | solution.py:296
  67.2 5.0 %collective-permute-start.23 = (bf16[64,256]{1,0:T(8,128)(2,1)S(1)}, bf16[64,256]{1,0:T(8,128)(2,1)S(1)}, u32[]{:S(2)}, u32[]{:S(2)}) collective-permute-start(bf16[64,256]{1,0:T(8,128)(2,1)S(1)} %get-tuple-element.51), channel_id=1, source_target_pairs={{0,4},{1,5},{2,6},{3,7},{4,0},{5,1},{6,2},{7,3},{8,12},{9,13},{10,... | collective-permute-start | bytes 98312 | tf_op jit(solution)/shard_map/ppermute | solution.py:296
  68.0 4.3 %collective-permute-start.24 = (bf16[64,256]{1,0:T(8,128)(2,1)S(1)}, bf16[64,256]{1,0:T(8,128)(2,1)S(1)}, u32[]{:S(2)}, u32[]{:S(2)}) collective-permute-start(bf16[64,256]{1,0:T(8,128)(2,1)S(1)} %get-tuple-element.52), channel_id=1, source_target_pairs={{0,2},{1,3},{2,0},{3,1},{4,6},{5,7},{6,4},{7,5},{8,10},{9,11},{10,... | collective-permute-start | bytes 98312 | tf_op jit(solution)/shard_map/ppermute | solution.py:296
  72.3 5.8 %collective-permute-start.27 = (bf16[64,256]{1,0:T(8,128)(2,1)S(1)}, bf16[64,256]{1,0:T(8,128)(2,1)S(1)}, u32[]{:S(2)}, u32[]{:S(2)}) collective-permute-start(bf16[64,256]{1,0:T(8,128)(2,1)S(1)} %query.3.refs_0_), channel_id=1, source_target_pairs={{0,6},{1,7},{2,4},{3,5},{4,2},{5,3},{6,0},{7,1},{8,14},{9,15},{10,... | collective-permute-start | bytes 98312 | tf_op jit(solution)/shard_map/ppermute | solution.py:296
  74.6 4.9 %collective-permute-start.26 = (bf16[64,256]{1,0:T(8,128)(2,1)S(1)}, bf16[64,256]{1,0:T(8,128)(2,1)S(1)}, u32[]{:S(2)}, u32[]{:S(2)}) collective-permute-start(bf16[64,256]{1,0:T(8,128)(2,1)S(1)} %query.3.refs_0_), channel_id=1, source_target_pairs={{0,4},{1,5},{2,6},{3,7},{4,0},{5,1},{6,2},{7,3},{8,12},{9,13},{10,... | collective-permute-start | bytes 98312 | tf_op jit(solution)/shard_map/ppermute | solution.py:296
  75.4 4.3 %collective-permute-start.25 = (bf16[64,256]{1,0:T(8,128)(2,1)S(1)}, bf16[64,256]{1,0:T(8,128)(2,1)S(1)}, u32[]{:S(2)}, u32[]{:S(2)}) collective-permute-start(bf16[64,256]{1,0:T(8,128)(2,1)S(1)} %query.3.refs_0_), channel_id=1, source_target_pairs={{0,2},{1,3},{2,0},{3,1},{4,6},{5,7},{6,4},{7,5},{8,10},{9,11},{10,... | collective-permute-start | bytes 98312 | tf_op jit(solution)/shard_map/ppermute | solution.py:296
  82.7 7.1 %collective-permute-start.29 = (f32[64,512]{1,0:T(8,128)S(1)}, f32[64,512]{1,0:T(8,128)S(1)}, u32[]{:S(2)}, u32[]{:S(2)}) collective-permute-start(f32[64,512]{1,0:T(8,128)S(1)} %get-tuple-element.54), channel_id=1, source_target_pairs={{0,24},{8,16},{16,8},{24,0},{1,25},{9,17},{17,9},{25,1},{2,26},{10... | collective-permute-start | bytes 393224 | tf_op jit(solution)/shard_map/ppermute | solution.py:296
  84.1 7.5 %collective-permute-start.30 = (f32[64,512]{1,0:T(8,128)S(1)}, f32[64,512]{1,0:T(8,128)S(1)}, u32[]{:S(2)}, u32[]{:S(2)}) collective-permute-start(f32[64,512]{1,0:T(8,128)S(1)} %get-tuple-element.55), channel_id=1, source_target_pairs={{0,16},{8,24},{16,0},{24,8},{1,17},{9,25},{17,1},{25,9},{2,18},{10... | collective-permute-start | bytes 393224 | tf_op jit(solution)/shard_map/ppermute | solution.py:296
  84.9 7.1 %collective-permute-start.31 = (f32[64,512]{1,0:T(8,128)S(1)}, f32[64,512]{1,0:T(8,128)S(1)}, u32[]{:S(2)}, u32[]{:S(2)}) collective-permute-start(f32[64,512]{1,0:T(8,128)S(1)} %get-tuple-element.56), channel_id=1, source_target_pairs={{0,8},{8,0},{16,24},{24,16},{1,9},{9,1},{17,25},{25,17},{2,10},{10... | collective-permute-start | bytes 393224 | tf_op jit(solution)/shard_map/ppermute | solution.py:296
  92.3 4.9 %collective-permute-start.34 = (f32[64,64]{1,0:T(8,128)S(1)}, f32[64,64]{1,0:T(8,128)S(1)}, u32[]{:S(2)}, u32[]{:S(2)}) collective-permute-start(f32[64,64]{1,0:T(8,128)S(1)} %get-tuple-element.57.refs_0_), channel_id=1, source_target_pairs={{0,24},{8,16},{16,8},{24,0},{1,25},{9,17},{17,9},{25,1},{2,26},{10... | collective-permute-start | bytes 49160 | tf_op jit(solution)/shard_map/ppermute | solution.py:296
  93.7 3.9 %collective-permute-start.33 = (f32[64,64]{1,0:T(8,128)S(1)}, f32[64,64]{1,0:T(8,128)S(1)}, u32[]{:S(2)}, u32[]{:S(2)}) collective-permute-start(f32[64,64]{1,0:T(8,128)S(1)} %get-tuple-element.57.refs_0_), channel_id=1, source_target_pairs={{0,16},{8,24},{16,0},{24,8},{1,17},{9,25},{17,1},{25,9},{2,18},{10... | collective-permute-start | bytes 49160 | tf_op jit(solution)/shard_map/ppermute | solution.py:296
  100.3 6.1 %collective-permute-start.38 = (f32[64,64]{1,0:T(8,128)S(1)}, f32[64,64]{1,0:T(8,128)S(1)}, u32[]{:S(2)}, u32[]{:S(2)}) collective-permute-start(f32[64,64]{1,0:T(8,128)S(1)} %sum.5.refs_0_), channel_id=1, source_target_pairs={{0,6},{1,7},{2,4},{3,5},{4,2},{5,3},{6,0},{7,1},{8,14},{9,15},{10,... | collective-permute-start | bytes 49160 | tf_op jit(solution)/shard_map/ppermute | solution.py:296
  102.0 5.1 %collective-permute-start.37 = (f32[64,64]{1,0:T(8,128)S(1)}, f32[64,64]{1,0:T(8,128)S(1)}, u32[]{:S(2)}, u32[]{:S(2)}) collective-permute-start(f32[64,64]{1,0:T(8,128)S(1)} %sum.5.refs_0_), channel_id=1, source_target_pairs={{0,4},{1,5},{2,6},{3,7},{4,0},{5,1},{6,2},{7,3},{8,12},{9,13},{10,... | collective-permute-start | bytes 49160 | tf_op jit(solution)/shard_map/ppermute | solution.py:296
  102.9 4.3 %collective-permute-start.36 = (f32[64,64]{1,0:T(8,128)S(1)}, f32[64,64]{1,0:T(8,128)S(1)}, u32[]{:S(2)}, u32[]{:S(2)}) collective-permute-start(f32[64,64]{1,0:T(8,128)S(1)} %sum.5.refs_0_), channel_id=1, source_target_pairs={{0,2},{1,3},{2,0},{3,1},{4,6},{5,7},{6,4},{7,5},{8,10},{9,11},{10,... | collective-permute-start | bytes 49160 | tf_op jit(solution)/shard_map/ppermute | solution.py:296
  (8 other events, 22.8 us)
where the time goes:
time: 110 us
  starting transfers between devices  45.8 us (42%)
  waiting for transfers between devices  43.8 us (40%)
  Pallas kernels  19.2 us (17%)
    ppermute x39, starting transfers between devices, swap(): lax.ppermute(value, axis, [(i, i ^ step) for i in range(lax.axis_size(axi...  45.8 us
    ppermute x39, waiting for transfers between devices, swap(): lax.ppermute(value, axis, [(i, i ^ step) for i in range(lax.axis_size(axi...  43.8 us
    pallas_call x2, Pallas kernels, shards(): call(back_body, 'backward', [SCALARS] * 3 + [WHOLE] * 3, [f32(width, shar...  3.22 us
    pallas_call x1, Pallas kernels, shards(): call(load_body, 'load', [SCALARS, WHOLE, AWAY, AWAY, AWAY], [pltpu.VMEM((...  2.81 us
    pallas_call x1, Pallas kernels, shards(): call(functools.partial(apply_body, chips), 'apply', [SCALARS] + [WHOLE] *...  2.73 us
    pallas_call x1, Pallas kernels, shards(): call(functools.partial(finish_body, root_count), 'finish', [WHOLE] * (chi...  2.52 us
    pallas_call x1, Pallas kernels, shards(): call(functools.partial(next_body, n_row), 'forward', [SCALARS] * 3 + [WHO...  2.37 us
  transfers between devices with their start and end apart: 39, of which 34 were waited for; matrix products, arithmetic and copies ran while one was open for 0% of the time, Pallas kernels for 5%

commit v1 on v0

--- a/solution.py
+++ b/solution.py
@@ -10,6 +10,7 @@
 
 ITERS = 2
 GROUP = 16
+HALF_GROUP = 8
 LOADS = 8
 PANEL_STEP = 8
 HIGH = lax.Precision.HIGHEST
@@ -46,13 +47,13 @@
 AWAY = pl.BlockSpec(memory_space=pltpu.MemorySpace.HBM)
 
 
-def call(body, name, in_specs, out_shape, scratch=(), flops=0, moved=0):
+def call(body, name, in_specs, out_shape, scratch=(), flops=0, moved=0, out_specs=None):
     many = isinstance(out_shape, (tuple, list))
     return pl.pallas_call(
         body,
         out_shape=out_shape,
         in_specs=in_specs,
-        out_specs=[WHOLE] * len(out_shape) if many else WHOLE,
+        out_specs=out_specs or ([WHOLE] * len(out_shape) if many else WHOLE),
         scratch_shapes=scratch,
         compiler_params=pltpu.CompilerParams(vmem_limit_bytes=VMEM_BYTES),
         cost_estimate=pl.CostEstimate(flops=flops, bytes_accessed=moved, transcendentals=0),
@@ -162,6 +163,66 @@
     collect_pairs(held, here_ref, there_ref, place[1], side)
     total[...] = jnp.zeros_like(total)
     groups(0, 1, NN, live[0], ids, held, tile_ref, total)
+    emit(total, out_refs, place[0], side)
+
+
+def listed(source, target, dims, side_of, ids, order, held, tile_ref, total):
+    tiles = total.shape[0]
+    slots = tile_ref.shape[0]
+    count = order[2, side_of]
+
+    def step(g, carry):
+        for lane in range(HALF_GROUP):
+            at = g * HALF_GROUP + lane
+            slot = order[side_of, at]
+            give = jnp.where(at < count, ids[target, slot], tiles - 1)
+            total[give] += lax.dot_general(
+                held[ids[source, slot]], tile_ref[slot], dims, preferred_element_type=jnp.float32
+            )
+        return carry
+
+    lax.fori_loop(0, jnp.minimum((count + HALF_GROUP - 1) // HALF_GROUP, slots // HALF_GROUP), step, 0)
+
+
+def emit_half(total, out_ref, me, side, flip):
+    for step in range(out_ref.shape[0]):
+        get(total, me ^ (2 * step + flip), out_ref.at[step], side)
+
+
+def collect_half(held, piece_refs, me, side, flip):
+    for step, piece_ref in enumerate(piece_refs):
+        put(held, me ^ (2 * step + flip), piece_ref[...], side)
+
+
+def forward_other_body(n_in, ids, order, place, *refs):
+    pieces, (tile_ref, held, other_ref, total) = refs[:n_in], refs[n_in:]
+    side = tile_ref.shape[1]
+    collect(held, pieces, place[0], side)
+    total[...] = jnp.zeros_like(total)
+    listed(1, 0, NT, 1 - place[1] % 2, ids, order, held, tile_ref, total)
+    emit_half(total, other_ref, place[1], side, 1)
+
+
+def forward_mine_body(ids, order, place, held, tile_ref, mine_ref, total):
+    side = tile_ref.shape[1]
+    total[...] = jnp.zeros_like(total)
+    listed(1, 0, NT, place[1] % 2, ids, order, held, tile_ref, total)
+    emit_half(total, mine_ref, place[1], side, 0)
+
+
+def back_mine_body(n_in, ids, order, place, *refs):
+    pieces, (tile_ref, total, held) = refs[:n_in], refs[n_in:]
+    collect_half(held, pieces, place[1], tile_ref.shape[1], 0)
+    total[...] = jnp.zeros_like(total)
+    listed(0, 1, NN, place[1] % 2, ids, order, held, tile_ref, total)
+
+
+def back_other_body(ids, order, place, there_ref, begun_ref, tile_ref, *refs):
+    out_refs, (held, total) = refs[:-2], refs[-2:]
+    side = tile_ref.shape[1]
+    collect_half(held, [there_ref.at[step] for step in range(there_ref.shape[0])], place[1], side, 1)
+    total[...] = begun_ref[...]
+    listed(0, 1, NN, 1 - place[1] % 2, ids, order, held, tile_ref, total)
     emit(total, out_refs, place[0], side)
 
 
@@ -201,8 +262,8 @@
     out_ref[...] = (held[...] * scale).astype(out_ref.dtype)
 
 
-def load_body(place, after_ref, tile_ref, product_ref, query_ref, *refs):
-    keep, my_product_ref, product_out, my_query_ref, degrees, counts, sems = refs
+def load_body(per, ids, live, place, after_ref, tile_ref, product_ref, query_ref, *refs):
+    keep, my_product_ref, product_out, my_query_ref, order, degrees, counts, sems = refs
     loads = [
         pltpu.make_async_copy(product_ref, degrees, sems.at[0]),
         pltpu.make_async_copy(query_ref, counts, sems.at[1]),
@@ -213,6 +274,20 @@
         loads.append(pltpu.make_async_copy(tile_ref.at[span], keep.at[span], sems.at[2 + step]))
     for load in loads:
         load.start()
+    order[2, 0] = 0
+    order[2, 1] = 0
+    for slot in range(tile_ref.shape[0]):
+        order[0, slot] = 0
+        order[1, slot] = 0
+    for slot in range(tile_ref.shape[0]):
+
+        @pl.when(slot < live[0])
+        def _():
+            core = ids[0, slot] // per % 2
+            at = order[2, core]
+            order[core, at] = slot
+            order[2, core] = at + 1
+
     loads[0].wait()
     product_out[...] = 1.0 / jnp.sqrt(degrees[...].astype(jnp.float32))
     share = my_product_ref.shape[1]
@@ -251,6 +326,11 @@
     out_ref[...] = (add(part_refs) * scale_ref[...]).astype(out_ref.dtype)
 
 
+def lift_only_body(*refs):
+    part_refs, scale_ref, lifted_ref = refs[:-2], refs[-2], refs[-1]
+    lifted_ref[...] = add(part_refs) * scale_ref[...]
+
+
 def lift_body(*refs):
     part_refs, scale_ref, lifted_ref, gram_ref = refs[:-3], refs[-3], refs[-2], refs[-1]
     lifted = add(part_refs) * scale_ref[...]
@@ -271,15 +351,44 @@
     refs[-1][...] = add(refs[:-1])
 
 
-def apply_body(n_in, place, *refs):
-    grams, (total_ref, mine_ref, other_ref, done) = refs[:n_in], refs[n_in:]
-    tiles, _, side = total_ref.shape
+def apply_tile(inverse, total_ref, owner, out_ref):
+    width, share = out_ref.shape
+    side = total_ref.shape[2]
+    if share >= side:
+        for piece in range(share // side):
+            out_ref[:, piece * side : (piece + 1) * side] = lax.dot_general(
+                inverse,
+                total_ref[owner * (share // side) + piece],
+                NN,
+                precision=HIGH,
+                preferred_element_type=jnp.float32,
+            )
+    else:
+        per = side // share
+        for at in range(per):
+
+            @pl.when(owner % per == at)
+            def _():
+                out_ref[...] = lax.dot_general(
+                    inverse,
+                    total_ref[owner // per],
+                    NN,
+                    precision=HIGH,
+                    preferred_element_type=jnp.float32,
+                )[:, at * share : (at + 1) * share]
+
+
+def apply_other_body(n_in, place, *refs):
+    grams, (total_ref, inverse_ref, other_ref) = refs[:n_in], refs[n_in:]
     inverse = inverse_factor(add(grams))
-    for tile in range(tiles):
-        done[tile] = lax.dot_general(
-            inverse, total_ref[tile], NN, precision=HIGH, preferred_element_type=jnp.float32
-        )
-    emit_pairs(done, mine_ref, other_ref, place[1], side)
+    inverse_ref[...] = inverse
+    for step in range(other_ref.shape[0]):
+        apply_tile(inverse, total_ref, place[1] ^ (2 * step + 1), other_ref.at[step])
+
+
+def apply_mine_body(place, inverse_ref, total_ref, mine_ref):
+    for step in range(mine_ref.shape[0]):
+        apply_tile(inverse_ref[...], total_ref, place[1] ^ (2 * step), mine_ref.at[step])
 
 
 def finish_body(after, *refs):
@@ -338,34 +447,35 @@
         ],
     )(place, in_hbm(panel), in_hbm(product_degree[None, :]))
     pieces = spread_to(scaled, "row")
-    tile_set, my_pscale, pscale, my_qscale = call(
-        load_body,
+    split = columns % side == 0
+    tile_set, my_pscale, pscale, my_qscale, order = call(
+        functools.partial(load_body, max(columns // side, 1)),
         "load",
-        [SCALARS, WHOLE, AWAY, AWAY, AWAY],
-        [pltpu.VMEM((slots, side, side), jnp.bfloat16), f32(1, share), f32(1, products), f32(1, columns)],
+        [SCALARS] * 3 + [WHOLE, AWAY, AWAY, AWAY],
+        [
+            pltpu.VMEM((slots, side, side), jnp.bfloat16),
+            f32(1, share),
+            f32(1, products),
+            f32(1, columns),
+            jax.ShapeDtypeStruct((3, slots), jnp.int32),
+        ],
         [
             pltpu.VMEM((1, products), jnp.int32),
             pltpu.VMEM((1, queries), jnp.int32),
             pltpu.SemaphoreType.DMA((2 + LOADS,)),
         ],
         moved=4 * slots * side * side,
-    )(place, scaled, in_hbm(tile_set), in_hbm(product_degree[None, :]), in_hbm(query_degree[None, :]))
+        out_specs=[WHOLE] * 4 + [SCALARS],
+    )(ids, live, place, scaled, in_hbm(tile_set), in_hbm(product_degree[None, :]), in_hbm(query_degree[None, :]))
     tile_set = pltpu.with_memory_space_constraint(tile_set, pltpu.VMEM)
     root_count = math.sqrt(products * n_col)
-    half_shapes = [f32(chips, width, columns)] * 2
+    half = f32(chips, width, columns)
+    half_work = dict(flops=slots * width * side * side, moved=slots * side * side)
     query_scratch = pltpu.VMEM((query_tiles + 1, width, side), jnp.float32)
     product_scratch = pltpu.VMEM((product_tiles + 1, width, side), jnp.float32)
+    query_held = pltpu.VMEM((query_tiles, width, side), jnp.bfloat16)
     for iteration in range(ITERS):
-        if iteration == 0:
-            mine, other = call(
-                functools.partial(first_body, n_row),
-                "forward",
-                [SCALARS] * 3 + [WHOLE] * (n_row + 1),
-                half_shapes,
-                [pltpu.VMEM((product_tiles, width, side), jnp.bfloat16), query_scratch],
-                **work,
-            )(ids, live, place, *pieces, tile_set)
-        else:
+        if iteration > 0:
             pieces = spread_to(lifted, "row")
             gram = call(gram_body, "gram", [WHOLE] * n_row, f32(width, width))(*pieces)
             grams = terms_over_col(gram)
@@ -381,32 +491,84 @@
                 ],
                 **work,
             )(ids, live, place, *pieces, pscale, tile_set)
-            mine, other = call(
-                functools.partial(apply_body, chips),
+            inverse, other = call(
+                functools.partial(apply_other_body, chips),
                 "apply",
                 [SCALARS] + [WHOLE] * (chips + 1),
-                half_shapes,
-                [pltpu.VMEM((query_tiles, width, side), jnp.float32)],
+                [f32(width, width), half],
             )(place, *grams, total)
+            got = swap(other, "col", 1)
+            mine = call(apply_mine_body, "apply_rest", [SCALARS] + [WHOLE] * 2, half, **half_work)(
+                place, inverse, total
+            )
+        elif split:
+            held, other = call(
+                functools.partial(forward_other_body, n_row),
+                "forward",
+                [SCALARS] * 3 + [WHOLE] * (n_row + 1),
+                [bf16(product_tiles, width, side), half],
+                [query_scratch],
+                **half_work,
+            )(ids, order, place, *pieces, tile_set)
+            got = swap(other, "col", 1)
+            mine = call(
+                forward_mine_body,
+                "forward_rest",
+                [SCALARS] * 3 + [WHOLE] * 2,
+                half,
+                [query_scratch],
+                **half_work,
+            )(ids, order, place, held, tile_set)
+        else:
+            mine, other = call(
+                functools.partial(first_body, n_row),
+                "forward",
+                [SCALARS] * 3 + [WHOLE] * (n_row + 1),
+                [half] * 2,
+                [pltpu.VMEM((product_tiles, width, side), jnp.bfloat16), query_scratch],
+                **work,
+            )(ids, live, place, *pieces, tile_set)
+            got = swap(other, "col", 1)
         sums = call(
             pair_body, "pair", [WHOLE] * 2, [f32(width, columns)] + [bf16(width, columns)] * (chips - 1)
-        )(mine, swap(other, "col", 1))
+        )(mine, got)
         parts = deal(sums, "col", 2)
         rounded = call(query_body, "query", [WHOLE] * (chips + 1), bf16(width, columns))(*parts, my_qscale)
-        here = call(join_body, "join", [WHOLE] * chips, bf16(chips, width, columns))(
-            *spread_to(rounded, "col", 2)
-        )
-        sums = call(
-            back_body,
-            "backward",
-            [SCALARS] * 3 + [WHOLE] * 3,
-            [f32(width, share)] * n_row,
-            [pltpu.VMEM((query_tiles, width, side), jnp.bfloat16), product_scratch],
-            **work,
-        )(ids, live, place, here, swap(here, "col", 1), tile_set)
-        lifted, gram = call(
-            lift_body, "lift", [WHOLE] * (n_row + 1), [f32(width, share), f32(width, width)]
-        )(*deal(sums, "row"), my_pscale)
+        pieces = spread_to(rounded, "col", 2)
+        here = call(join_body, "join", [WHOLE] * chips, bf16(chips, width, columns))(*pieces)
+        there = swap(here, "col", 1)
+        if split:
+            begun = call(
+                functools.partial(back_mine_body, chips),
+                "backward",
+                [SCALARS] * 3 + [WHOLE] * (chips + 1),
+                f32(product_tiles + 1, width, side),
+                [query_held],
+                **half_work,
+            )(ids, order, place, *pieces, tile_set)
+            sums = call(
+                back_other_body,
+                "backward_rest",
+                [SCALARS] * 3 + [WHOLE] * 3,
+                [f32(width, share)] * n_row,
+                [query_held, product_scratch],
+                **half_work,
+            )(ids, order, place, there, begun, tile_set)
+        else:
+            sums = call(
+                back_body,
+                "backward",
+                [SCALARS] * 3 + [WHOLE] * 3,
+                [f32(width, share)] * n_row,
+                [query_held, product_scratch],
+                **work,
+            )(ids, live, place, here, there, tile_set)
+        parts = deal(sums, "row")
+        if iteration < ITERS - 1:
+            lifted = call(lift_only_body, "lift", [WHOLE] * (n_row + 1), f32(width, share))(*parts, my_pscale)
+    lifted, gram = call(
+        lift_body, "lift", [WHOLE] * (n_row + 1), [f32(width, share), f32(width, width)]
+    )(*parts, my_pscale)
     return call(
         functools.partial(finish_body, root_count), "finish", [WHOLE] * (chips + 1), f32(width, share)
     )(*terms_over_col(add_up(*spread_to(gram, "row"))), lifted)

time: 110 us -> 109 us (level)
  waiting for transfers between devices: 43.8 us -> 38.2 us
  Pallas kernels: 19.2 us -> 23.6 us
    ppermute x39, waiting for transfers between devices: 43.8 us -> 38.2 us  [swap(): lax.ppermute(value, axis, [(i, i ^ step) for i in range(lax.axis_size(axi...]
    pallas_call x5 -> x10, Pallas kernels: 10.9 us -> 16.2 us  [the longest x1 3.43 us: shards(): call(functools.partial(load_body, max(columns // side, 1)), 'load', [SCAL...]
  transfers between devices with their start and end apart: 39 -> 39, of which waited for: 34 -> 31; matrix products, arithmetic and copies ran while one was open for 0% -> 0% of each run, Pallas kernels for 5% -> 10%
where the time goes in v1:
time: 109 us
  starting transfers between devices  45.8 us (42%)
  waiting for transfers between devices  38.2 us (35%)
  Pallas kernels  23.6 us (22%)
    ppermute x39, starting transfers between devices, swap(): lax.ppermute(value, axis, [(i, i ^ step) for i in range(lax.axis_size(axi...  45.8 us
    ppermute x39, waiting for transfers between devices, swap(): lax.ppermute(value, axis, [(i, i ^ step) for i in range(lax.axis_size(axi...  38.2 us
    pallas_call x1, Pallas kernels, shards(): call(functools.partial(load_body, max(columns // side, 1)), 'load', [SCAL...  3.43 us
    pallas_call x2, Pallas kernels, shards(): call(back_other_body, 'backward_rest', [SCALARS] * 3 + [WHOLE] * 3, [f32(...  3.22 us
    pallas_call x1, Pallas kernels, shards(): call(functools.partial(finish_body, root_count), 'finish', [WHOLE] * (chi...  2.52 us
    pallas_call x2, Pallas kernels, shards(): call(functools.partial(back_mine_body, chips), 'backward', [SCALARS] * 3...  2.52 us
    pallas_call x1, Pallas kernels, shards(): call(functools.partial(apply_other_body, chips), 'apply', [SCALARS] + [WH...  2.5 us
    pallas_call x1, Pallas kernels, shards(): call(functools.partial(next_body, n_row), 'forward', [SCALARS] * 3 + [WHO...  2.38 us
  transfers between devices with their start and end apart: 39, of which 31 were waited for; matrix products, arithmetic and copies ran while one was open for 0% of the time, Pallas kernels for 10%

profile of v1, /device:TPU:0, one launch (start us, length us, event | category | flops | bytes accessed | tf_op | source)
XLA Modules:
  0.0 109.2 jit_solution(5955774309797685898)
XLA Ops:
  0.1 1.5 %start.1.after_ref.refs_0_ = bf16[64,512]{1,0:T(8,128)(2,1)S(1)} custom-call(s32[2]{0:T(128)S(1)} %pad_add_fusion.place, f32[64,512]{1,0:T(8,128)} %panel_ref.1, s32[1,2048]{1,0:T(1,128)} %bitcast.18), custom_call_target="tpu_custom_call" | custom-call | tf_op jit(solution)/shard_map/start/pallas_call | solution.py:438
  1.6 4.0 %collective-permute-start.2 = (bf16[64,512]{1,0:T(8,128)(2,1)S(1)}, bf16[64,512]{1,0:T(8,128)(2,1)S(1)}, u32[]{:S(2)}, u32[]{:S(2)}) collective-permute-start(bf16[64,512]{1,0:T(8,128)(2,1)S(1)} %start.1.after_ref.refs_0_), channel_id=1, source_target_pairs={{0,24},{8,16},{16,8},{24,0},{1,25},{9,17},{17,9},{25,1},{2,26},{10... | collective-permute-start | bytes 196616 | tf_op jit(solution)/shard_map/ppermute | solution.py:405
  7.5 3.4 %load.1 = (bf16[32,256,256]{2,1,0:T(8,128)(2,1)S(1)}, f32[1,512]{1,0:T(1,128)S(1)}, f32[1,2048]{1,0:T(1,128)S(1)}, f32[1,256]{1,0:T(1,128)S(1)}, s32[3,32]{1,0:T(4,128)S(1)}) custom-call(s32[2,32]{1,0:T(2,128)S(1)} %bitcast.9, s32[1]{0:T(128)} %bitcast.7.live, s32[2]{0:T(128)S(1)} %pad_add_fusion.place, bf16[64,512]{1,0:T(8,128)(2,1)S(1)} %start.1.after_ref.refs_0_, ...), custom_call_target="tpu_custom_call" | custom-call | bytes 8388608 | tf_op jit(solution)/shard_map/load/pallas_call | solution.py:451
  11.0 2.0 %forward.2 = (bf16[8,64,256]{2,1,0:T(8,128)(2,1)S(1)}, f32[4,64,256]{2,1,0:T(8,128)S(1)}) custom-call(s32[2,32]{1,0:T(2,128)S(1)} %bitcast.10, s32[3,32]{1,0:T(4,128)S(1)} %get-tuple-element.32.order, s32[2]{0:T(128)S(1)} %pad_add_fusion.place, bf16[64,512]{1,0:T(8,128)(2,1)S(1)} %start.1.after_ref.refs_0_, ...), custom_call_target="tpu_custom_call" | custom-call | flops 134217728 | bytes 2097152 | tf_op jit(solution)/shard_map/forward/pallas_call | solution.py:505
  13.1 1.5 %forward_rest.1.mine_ref = f32[4,64,256]{2,1,0:T(8,128)S(1)} custom-call(s32[2,32]{1,0:T(2,128)S(1)} %bitcast.11, s32[3,32]{1,0:T(4,128)S(1)} %get-tuple-element.32.order, s32[2]{0:T(128)S(1)} %pad_add_fusion.place, bf16[8,64,256]{2,1,0:T(8,128)(2,1)S(1)} %get-tuple-element.34.held, bf16[32,256,256]{2,1,0:T(8,128)(2,1)S(1)} %get-tuple-element.33.refs_4_.tile_ref.refs_5_), custom_call_target="tpu_custom_call" | custom-call | flops 134217728 | bytes 2097152 | tf_op jit(solution)/shard_map/forward_rest/pallas_call | solution.py:514
  14.7 3.6 %collective-permute-start.4 = (bf16[64,256]{1,0:T(8,128)(2,1)S(1)}, bf16[64,256]{1,0:T(8,128)(2,1)S(1)}, u32[]{:S(2)}, u32[]{:S(2)}) collective-permute-start(bf16[64,256]{1,0:T(8,128)(2,1)S(1)} %get-tuple-element.37), channel_id=1, source_target_pairs={{0,6},{1,7},{2,4},{3,5},{4,2},{5,3},{6,0},{7,1},{8,14},{9,15},{10,... | collective-permute-start | bytes 98312 | tf_op jit(solution)/shard_map/ppermute | solution.py:405
  20.5 2.7 %collective-permute-done.5.refs_2_ = bf16[64,256]{1,0:T(8,128)(2,1)S(1)} collective-permute-done((bf16[64,256]{1,0:T(8,128)(2,1)S(1)}, bf16[64,256]{1,0:T(8,128)(2,1)S(1)}, u32[]{:S(2)}, u32[]{:S(2)}) %collective-permute-start.5) | collective-permute-done | bytes 32800 | tf_op jit(solution)/shard_map/ppermute | solution.py:405
  23.2 1.7 %collective-permute-start.9 = (bf16[64,256]{1,0:T(8,128)(2,1)S(1)}, bf16[64,256]{1,0:T(8,128)(2,1)S(1)}, u32[]{:S(2)}, u32[]{:S(2)}) collective-permute-start(bf16[64,256]{1,0:T(8,128)(2,1)S(1)} %query.2.refs_0_), channel_id=1, source_target_pairs={{0,6},{1,7},{2,4},{3,5},{4,2},{5,3},{6,0},{7,1},{8,14},{9,15},{10,... | collective-permute-start | bytes 98312 | tf_op jit(solution)/shard_map/ppermute | solution.py:405
  25.4 2.3 %collective-permute-start.7 = (bf16[64,256]{1,0:T(8,128)(2,1)S(1)}, bf16[64,256]{1,0:T(8,128)(2,1)S(1)}, u32[]{:S(2)}, u32[]{:S(2)}) collective-permute-start(bf16[64,256]{1,0:T(8,128)(2,1)S(1)} %query.2.refs_0_), channel_id=1, source_target_pairs={{0,2},{1,3},{2,0},{3,1},{4,6},{5,7},{6,4},{7,5},{8,10},{9,11},{10,... | collective-permute-start | bytes 98312 | tf_op jit(solution)/shard_map/ppermute | solution.py:405
  31.3 1.6 %backward_rest.2 = (f32[64,512]{1,0:T(8,128)S(1)}, f32[64,512]{1,0:T(8,128)S(1)}, f32[64,512]{1,0:T(8,128)S(1)}, f32[64,512]{1,0:T(8,128)S(1)}) custom-call(s32[2,32]{1,0:T(2,128)S(1)} %bitcast.13, s32[3,32]{1,0:T(4,128)S(1)} %get-tuple-element.32.order, s32[2]{0:T(128)S(1)} %pad_add_fusion.place, bf16[4,64,256]{2,1,0:T(8,128)(2,1)S(1)} %collective-permute-done.10.there_ref, ...), custom_call_target="tpu_custom_call" | custom-call | flops 134217728 | bytes 2097152 | tf_op jit(solution)/shard_map/backward_rest/pallas_call | solution.py:549
  32.9 1.9 %collective-permute-start.11 = (f32[64,512]{1,0:T(8,128)S(1)}, f32[64,512]{1,0:T(8,128)S(1)}, u32[]{:S(2)}, u32[]{:S(2)}) collective-permute-start(f32[64,512]{1,0:T(8,128)S(1)} %get-tuple-element.42), channel_id=1, source_target_pairs={{0,24},{8,16},{16,8},{24,0},{1,25},{9,17},{17,9},{25,1},{2,26},{10... | collective-permute-start | bytes 393224 | tf_op jit(solution)/shard_map/ppermute | solution.py:405
  36.5 2.8 %collective-permute-done.11.refs_1_ = f32[64,512]{1,0:T(8,128)S(1)} collective-permute-done((f32[64,512]{1,0:T(8,128)S(1)}, f32[64,512]{1,0:T(8,128)S(1)}, u32[]{:S(2)}, u32[]{:S(2)}) %collective-permute-start.11) | collective-permute-done | bytes 131104 | tf_op jit(solution)/shard_map/ppermute | solution.py:405
  39.3 2.3 %collective-permute-done.12.refs_2_ = f32[64,512]{1,0:T(8,128)S(1)} collective-permute-done((f32[64,512]{1,0:T(8,128)S(1)}, f32[64,512]{1,0:T(8,128)S(1)}, u32[]{:S(2)}, u32[]{:S(2)}) %collective-permute-start.12) | collective-permute-done | bytes 131104 | tf_op jit(solution)/shard_map/ppermute | solution.py:405
  42.4 1.6 %collective-permute-start.16 = (f32[64,512]{1,0:T(8,128)S(1)}, f32[64,512]{1,0:T(8,128)S(1)}, u32[]{:S(2)}, u32[]{:S(2)}) collective-permute-start(f32[64,512]{1,0:T(8,128)S(1)} %lift.2.refs_0_), channel_id=1, source_target_pairs={{0,24},{8,16},{16,8},{24,0},{1,25},{9,17},{17,9},{25,1},{2,26},{10... | collective-permute-start | bytes 393224 | tf_op jit(solution)/shard_map/ppermute | solution.py:405
  44.0 1.4 %collective-permute-start.15 = (f32[64,512]{1,0:T(8,128)S(1)}, f32[64,512]{1,0:T(8,128)S(1)}, u32[]{:S(2)}, u32[]{:S(2)}) collective-permute-start(f32[64,512]{1,0:T(8,128)S(1)} %lift.2.refs_0_), channel_id=1, source_target_pairs={{0,16},{8,24},{16,0},{24,8},{1,17},{9,25},{17,1},{25,9},{2,18},{10... | collective-permute-start | bytes 393224 | tf_op jit(solution)/shard_map/ppermute | solution.py:405
  45.9 3.8 %collective-permute-done.16.refs_3_ = f32[64,512]{1,0:T(8,128)S(1)} collective-permute-done((f32[64,512]{1,0:T(8,128)S(1)}, f32[64,512]{1,0:T(8,128)S(1)}, u32[]{:S(2)}, u32[]{:S(2)}) %collective-permute-start.16) | collective-permute-done | bytes 131104 | tf_op jit(solution)/shard_map/ppermute | solution.py:405
  49.7 1.7 %collective-permute-done.15.refs_2_ = f32[64,512]{1,0:T(8,128)S(1)} collective-permute-done((f32[64,512]{1,0:T(8,128)S(1)}, f32[64,512]{1,0:T(8,128)S(1)}, u32[]{:S(2)}, u32[]{:S(2)}) %collective-permute-start.15) | collective-permute-done | bytes 131104 | tf_op jit(solution)/shard_map/ppermute | solution.py:405
  53.4 2.1 %collective-permute-start.20 = (f32[64,64]{1,0:T(8,128)S(1)}, f32[64,64]{1,0:T(8,128)S(1)}, u32[]{:S(2)}, u32[]{:S(2)}) collective-permute-start(f32[64,64]{1,0:T(8,128)S(1)} %sum.3.refs_0_), channel_id=1, source_target_pairs={{0,6},{1,7},{2,4},{3,5},{4,2},{5,3},{6,0},{7,1},{8,14},{9,15},{10,... | collective-permute-start | bytes 49160 | tf_op jit(solution)/shard_map/ppermute | solution.py:405
  57.8 2.4 %forward.3.refs_4_.total_ref = f32[8,64,256]{2,1,0:T(8,128)S(1)} custom-call(s32[2,32]{1,0:T(2,128)S(1)} %bitcast.14, s32[1]{0:T(128)} %bitcast.8.live, s32[2]{0:T(128)S(1)} %pad_add_fusion.place, f32[64,512]{1,0:T(8,128)S(1)} %lift.2.refs_0_, f32[64,512]{1,0:T(8,128)S(1)} %collective-permute-done.14.refs_1_, f32[64,512]{1,0:T(8,128)S(1)} %collective-permute-done.15.refs_2_, ...), custom_call_target="tpu_custom_call" | custom-call | flops 268435456 | bytes 4194304 | tf_op jit(solution)/shard_map/forward/pallas_call | solution.py:482
  60.8 2.5 %apply.1 = (f32[64,64]{1,0:T(8,128)S(1)}, f32[4,64,256]{2,1,0:T(8,128)S(1)}) custom-call(s32[2]{0:T(128)S(1)} %pad_add_fusion.place, f32[64,64]{1,0:T(8,128)S(1)} %sum.3.refs_0_, f32[64,64]{1,0:T(8,128)S(1)} %collective-permute-done.18.refs_1_, f32[64,64]{1,0:T(8,128)S(1)} %collective-permute-done.19.refs_2_, f32[64,64]{1,0:T(8,128)S(1)} %collective-permute-done.20.refs_3_, ...), custom_call_target="tpu_custom_call" | custom-call | tf_op jit(solution)/shard_map/apply/pallas_call | solution.py:494
  64.9 1.7 %collective-permute-start.22 = (bf16[64,256]{1,0:T(8,128)(2,1)S(1)}, bf16[64,256]{1,0:T(8,128)(2,1)S(1)}, u32[]{:S(2)}, u32[]{:S(2)}) collective-permute-start(bf16[64,256]{1,0:T(8,128)(2,1)S(1)} %get-tuple-element.50), channel_id=1, source_target_pairs={{0,6},{1,7},{2,4},{3,5},{4,2},{5,3},{6,0},{7,1},{8,14},{9,15},{10,... | collective-permute-start | bytes 98312 | tf_op jit(solution)/shard_map/ppermute | solution.py:405
  67.4 2.0 %collective-permute-start.24 = (bf16[64,256]{1,0:T(8,128)(2,1)S(1)}, bf16[64,256]{1,0:T(8,128)(2,1)S(1)}, u32[]{:S(2)}, u32[]{:S(2)}) collective-permute-start(bf16[64,256]{1,0:T(8,128)(2,1)S(1)} %get-tuple-element.52), channel_id=1, source_target_pairs={{0,2},{1,3},{2,0},{3,1},{4,6},{5,7},{6,4},{7,5},{8,10},{9,11},{10,... | collective-permute-start | bytes 98312 | tf_op jit(solution)/shard_map/ppermute | solution.py:405
  71.8 2.1 %collective-permute-start.27 = (bf16[64,256]{1,0:T(8,128)(2,1)S(1)}, bf16[64,256]{1,0:T(8,128)(2,1)S(1)}, u32[]{:S(2)}, u32[]{:S(2)}) collective-permute-start(bf16[64,256]{1,0:T(8,128)(2,1)S(1)} %query.3.refs_0_), channel_id=1, source_target_pairs={{0,6},{1,7},{2,4},{3,5},{4,2},{5,3},{6,0},{7,1},{8,14},{9,15},{10,... | collective-permute-start | bytes 98312 | tf_op jit(solution)/shard_map/ppermute | solution.py:405
  80.5 1.6 %backward_rest.3 = (f32[64,512]{1,0:T(8,128)S(1)}, f32[64,512]{1,0:T(8,128)S(1)}, f32[64,512]{1,0:T(8,128)S(1)}, f32[64,512]{1,0:T(8,128)S(1)}) custom-call(s32[2,32]{1,0:T(2,128)S(1)} %bitcast.16, s32[3,32]{1,0:T(4,128)S(1)} %get-tuple-element.32.order, s32[2]{0:T(128)S(1)} %pad_add_fusion.place, bf16[4,64,256]{2,1,0:T(8,128)(2,1)S(1)} %collective-permute-done.28.there_ref, ...), custom_call_target="tpu_custom_call" | custom-call | flops 134217728 | bytes 2097152 | tf_op jit(solution)/shard_map/backward_rest/pallas_call | solution.py:549
  83.1 1.7 %collective-permute-start.30 = (f32[64,512]{1,0:T(8,128)S(1)}, f32[64,512]{1,0:T(8,128)S(1)}, u32[]{:S(2)}, u32[]{:S(2)}) collective-permute-start(f32[64,512]{1,0:T(8,128)S(1)} %get-tuple-element.55), channel_id=1, source_target_pairs={{0,16},{8,24},{16,0},{24,8},{1,17},{9,25},{17,1},{25,9},{2,18},{10... | collective-permute-start | bytes 393224 | tf_op jit(solution)/shard_map/ppermute | solution.py:405
  85.7 3.5 %collective-permute-done.29.refs_1_ = f32[64,512]{1,0:T(8,128)S(1)} collective-permute-done((f32[64,512]{1,0:T(8,128)S(1)}, f32[64,512]{1,0:T(8,128)S(1)}, u32[]{:S(2)}, u32[]{:S(2)}) %collective-permute-start.29) | collective-permute-done | bytes 131104 | tf_op jit(solution)/shard_map/ppermute | solution.py:405
  89.2 1.6 %collective-permute-done.30.refs_2_ = f32[64,512]{1,0:T(8,128)S(1)} collective-permute-done((f32[64,512]{1,0:T(8,128)S(1)}, f32[64,512]{1,0:T(8,128)S(1)}, u32[]{:S(2)}, u32[]{:S(2)}) %collective-permute-start.30) | collective-permute-done | bytes 131104 | tf_op jit(solution)/shard_map/ppermute | solution.py:405
  91.6 1.8 %collective-permute-start.34 = (f32[64,64]{1,0:T(8,128)S(1)}, f32[64,64]{1,0:T(8,128)S(1)}, u32[]{:S(2)}, u32[]{:S(2)}) collective-permute-start(f32[64,64]{1,0:T(8,128)S(1)} %get-tuple-element.57.refs_0_), channel_id=1, source_target_pairs={{0,24},{8,16},{16,8},{24,0},{1,25},{9,17},{17,9},{25,1},{2,26},{10... | collective-permute-start | bytes 49160 | tf_op jit(solution)/shard_map/ppermute | solution.py:405
  93.3 1.4 %collective-permute-start.33 = (f32[64,64]{1,0:T(8,128)S(1)}, f32[64,64]{1,0:T(8,128)S(1)}, u32[]{:S(2)}, u32[]{:S(2)}) collective-permute-start(f32[64,64]{1,0:T(8,128)S(1)} %get-tuple-element.57.refs_0_), channel_id=1, source_target_pairs={{0,16},{8,24},{16,0},{24,8},{1,17},{9,25},{17,1},{25,9},{2,18},{10... | collective-permute-start | bytes 49160 | tf_op jit(solution)/shard_map/ppermute | solution.py:405
  99.9 1.6 %collective-permute-start.38 = (f32[64,64]{1,0:T(8,128)S(1)}, f32[64,64]{1,0:T(8,128)S(1)}, u32[]{:S(2)}, u32[]{:S(2)}) collective-permute-start(f32[64,64]{1,0:T(8,128)S(1)} %sum.5.refs_0_), channel_id=1, source_target_pairs={{0,6},{1,7},{2,4},{3,5},{4,2},{5,3},{6,0},{7,1},{8,14},{9,15},{10,... | collective-permute-start | bytes 49160 | tf_op jit(solution)/shard_map/ppermute | solution.py:405
  102.0 2.3 %collective-permute-start.36 = (f32[64,64]{1,0:T(8,128)S(1)}, f32[64,64]{1,0:T(8,128)S(1)}, u32[]{:S(2)}, u32[]{:S(2)}) collective-permute-start(f32[64,64]{1,0:T(8,128)S(1)} %sum.5.refs_0_), channel_id=1, source_target_pairs={{0,2},{1,3},{2,0},{3,1},{4,6},{5,7},{6,4},{7,5},{8,10},{9,11},{10,... | collective-permute-start | bytes 49160 | tf_op jit(solution)/shard_map/ppermute | solution.py:405
  106.7 2.5 %finish.1 = f32[64,512]{1,0:T(8,128)} custom-call(f32[64,64]{1,0:T(8,128)S(1)} %sum.5.refs_0_, f32[64,64]{1,0:T(8,128)S(1)} %collective-permute-done.36.refs_1_, f32[64,64]{1,0:T(8,128)S(1)} %collective-permute-done.37.refs_2_, f32[64,64]{1,0:T(8,128)S(1)} %collective-permute-done.38.refs_3_, f32[64,512]{1,0:T(8,128)S(1)} %get-tuple-element.58.refs_4_), custom_call_target="tpu_custom_call" | custom-call | tf_op jit(solution)/shard_map/finish/pallas_call | solution.py:572
  (75 shorter events, 37.6 us)
Async XLA Ops:
  1.6 9.4 %collective-permute-start.2 = (bf16[64,512]{1,0:T(8,128)(2,1)S(1)}, bf16[64,512]{1,0:T(8,128)(2,1)S(1)}, u32[]{:S(2)}, u32[]{:S(2)}) collective-permute-start(bf16[64,512]{1,0:T(8,128)(2,1)S(1)} %start.1.after_ref.refs_0_), channel_id=1, source_target_pairs={{0,24},{8,16},{16,8},{24,0},{1,25},{9,17},{17,9},{25,1},{2,26},{10... | collective-permute-start | bytes 196616 | tf_op jit(solution)/shard_map/ppermute | solution.py:405
  5.5 5.4 %collective-permute-start.1 = (bf16[64,512]{1,0:T(8,128)(2,1)S(1)}, bf16[64,512]{1,0:T(8,128)(2,1)S(1)}, u32[]{:S(2)}, u32[]{:S(2)}) collective-permute-start(bf16[64,512]{1,0:T(8,128)(2,1)S(1)} %start.1.after_ref.refs_0_), channel_id=1, source_target_pairs={{0,16},{8,24},{16,0},{24,8},{1,17},{9,25},{17,1},{25,9},{2,18},{10... | collective-permute-start | bytes 196616 | tf_op jit(solution)/shard_map/ppermute | solution.py:405
  6.1 4.9 %collective-permute-start = (bf16[64,512]{1,0:T(8,128)(2,1)S(1)}, bf16[64,512]{1,0:T(8,128)(2,1)S(1)}, u32[]{:S(2)}, u32[]{:S(2)}) collective-permute-start(bf16[64,512]{1,0:T(8,128)(2,1)S(1)} %start.1.after_ref.refs_0_), channel_id=1, source_target_pairs={{0,8},{8,0},{16,24},{24,16},{1,9},{9,1},{17,25},{25,17},{2,10},{10... | collective-permute-start | bytes 196616 | tf_op jit(solution)/shard_map/ppermute | solution.py:405
  14.7 5.8 %collective-permute-start.4 = (bf16[64,256]{1,0:T(8,128)(2,1)S(1)}, bf16[64,256]{1,0:T(8,128)(2,1)S(1)}, u32[]{:S(2)}, u32[]{:S(2)}) collective-permute-start(bf16[64,256]{1,0:T(8,128)(2,1)S(1)} %get-tuple-element.37), channel_id=1, source_target_pairs={{0,6},{1,7},{2,4},{3,5},{4,2},{5,3},{6,0},{7,1},{8,14},{9,15},{10,... | collective-permute-start | bytes 98312 | tf_op jit(solution)/shard_map/ppermute | solution.py:405
  18.3 4.8 %collective-permute-start.5 = (bf16[64,256]{1,0:T(8,128)(2,1)S(1)}, bf16[64,256]{1,0:T(8,128)(2,1)S(1)}, u32[]{:S(2)}, u32[]{:S(2)}) collective-permute-start(bf16[64,256]{1,0:T(8,128)(2,1)S(1)} %get-tuple-element.38), channel_id=1, source_target_pairs={{0,4},{1,5},{2,6},{3,7},{4,0},{5,1},{6,2},{7,3},{8,12},{9,13},{10,... | collective-permute-start | bytes 98312 | tf_op jit(solution)/shard_map/ppermute | solution.py:405
  18.4 4.8 %collective-permute-start.6 = (bf16[64,256]{1,0:T(8,128)(2,1)S(1)}, bf16[64,256]{1,0:T(8,128)(2,1)S(1)}, u32[]{:S(2)}, u32[]{:S(2)}) collective-permute-start(bf16[64,256]{1,0:T(8,128)(2,1)S(1)} %get-tuple-element.39), channel_id=1, source_target_pairs={{0,2},{1,3},{2,0},{3,1},{4,6},{5,7},{6,4},{7,5},{8,10},{9,11},{10,... | collective-permute-start | bytes 98312 | tf_op jit(solution)/shard_map/ppermute | solution.py:405
  23.2 5.8 %collective-permute-start.9 = (bf16[64,256]{1,0:T(8,128)(2,1)S(1)}, bf16[64,256]{1,0:T(8,128)(2,1)S(1)}, u32[]{:S(2)}, u32[]{:S(2)}) collective-permute-start(bf16[64,256]{1,0:T(8,128)(2,1)S(1)} %query.2.refs_0_), channel_id=1, source_target_pairs={{0,6},{1,7},{2,4},{3,5},{4,2},{5,3},{6,0},{7,1},{8,14},{9,15},{10,... | collective-permute-start | bytes 98312 | tf_op jit(solution)/shard_map/ppermute | solution.py:405
  24.9 4.9 %collective-permute-start.8 = (bf16[64,256]{1,0:T(8,128)(2,1)S(1)}, bf16[64,256]{1,0:T(8,128)(2,1)S(1)}, u32[]{:S(2)}, u32[]{:S(2)}) collective-permute-start(bf16[64,256]{1,0:T(8,128)(2,1)S(1)} %query.2.refs_0_), channel_id=1, source_target_pairs={{0,4},{1,5},{2,6},{3,7},{4,0},{5,1},{6,2},{7,3},{8,12},{9,13},{10,... | collective-permute-start | bytes 98312 | tf_op jit(solution)/shard_map/ppermute | solution.py:405
  25.4 4.5 %collective-permute-start.7 = (bf16[64,256]{1,0:T(8,128)(2,1)S(1)}, bf16[64,256]{1,0:T(8,128)(2,1)S(1)}, u32[]{:S(2)}, u32[]{:S(2)}) collective-permute-start(bf16[64,256]{1,0:T(8,128)(2,1)S(1)} %query.2.refs_0_), channel_id=1, source_target_pairs={{0,2},{1,3},{2,0},{3,1},{4,6},{5,7},{6,4},{7,5},{8,10},{9,11},{10,... | collective-permute-start | bytes 98312 | tf_op jit(solution)/shard_map/ppermute | solution.py:405
  32.9 6.4 %collective-permute-start.11 = (f32[64,512]{1,0:T(8,128)S(1)}, f32[64,512]{1,0:T(8,128)S(1)}, u32[]{:S(2)}, u32[]{:S(2)}) collective-permute-start(f32[64,512]{1,0:T(8,128)S(1)} %get-tuple-element.42), channel_id=1, source_target_pairs={{0,24},{8,16},{16,8},{24,0},{1,25},{9,17},{17,9},{25,1},{2,26},{10... | collective-permute-start | bytes 393224 | tf_op jit(solution)/shard_map/ppermute | solution.py:405
  34.8 6.8 %collective-permute-start.12 = (f32[64,512]{1,0:T(8,128)S(1)}, f32[64,512]{1,0:T(8,128)S(1)}, u32[]{:S(2)}, u32[]{:S(2)}) collective-permute-start(f32[64,512]{1,0:T(8,128)S(1)} %get-tuple-element.43), channel_id=1, source_target_pairs={{0,16},{8,24},{16,0},{24,8},{1,17},{9,25},{17,1},{25,9},{2,18},{10... | collective-permute-start | bytes 393224 | tf_op jit(solution)/shard_map/ppermute | solution.py:405
  35.7 6.6 %collective-permute-start.13 = (f32[64,512]{1,0:T(8,128)S(1)}, f32[64,512]{1,0:T(8,128)S(1)}, u32[]{:S(2)}, u32[]{:S(2)}) collective-permute-start(f32[64,512]{1,0:T(8,128)S(1)} %get-tuple-element.44), channel_id=1, source_target_pairs={{0,8},{8,0},{16,24},{24,16},{1,9},{9,1},{17,25},{25,17},{2,10},{10... | collective-permute-start | bytes 393224 | tf_op jit(solution)/shard_map/ppermute | solution.py:405
  42.4 7.3 %collective-permute-start.16 = (f32[64,512]{1,0:T(8,128)S(1)}, f32[64,512]{1,0:T(8,128)S(1)}, u32[]{:S(2)}, u32[]{:S(2)}) collective-permute-start(f32[64,512]{1,0:T(8,128)S(1)} %lift.2.refs_0_), channel_id=1, source_target_pairs={{0,24},{8,16},{16,8},{24,0},{1,25},{9,17},{17,9},{25,1},{2,26},{10... | collective-permute-start | bytes 393224 | tf_op jit(solution)/shard_map/ppermute | solution.py:405
  44.0 7.5 %collective-permute-start.15 = (f32[64,512]{1,0:T(8,128)S(1)}, f32[64,512]{1,0:T(8,128)S(1)}, u32[]{:S(2)}, u32[]{:S(2)}) collective-permute-start(f32[64,512]{1,0:T(8,128)S(1)} %lift.2.refs_0_), channel_id=1, source_target_pairs={{0,16},{8,24},{16,0},{24,8},{1,17},{9,25},{17,1},{25,9},{2,18},{10... | collective-permute-start | bytes 393224 | tf_op jit(solution)/shard_map/ppermute | solution.py:405
  45.4 6.2 %collective-permute-start.14 = (f32[64,512]{1,0:T(8,128)S(1)}, f32[64,512]{1,0:T(8,128)S(1)}, u32[]{:S(2)}, u32[]{:S(2)}) collective-permute-start(f32[64,512]{1,0:T(8,128)S(1)} %lift.2.refs_0_), channel_id=1, source_target_pairs={{0,8},{8,0},{16,24},{24,16},{1,9},{9,1},{17,25},{25,17},{2,10},{10... | collective-permute-start | bytes 393224 | tf_op jit(solution)/shard_map/ppermute | solution.py:405
  53.4 6.8 %collective-permute-start.20 = (f32[64,64]{1,0:T(8,128)S(1)}, f32[64,64]{1,0:T(8,128)S(1)}, u32[]{:S(2)}, u32[]{:S(2)}) collective-permute-start(f32[64,64]{1,0:T(8,128)S(1)} %sum.3.refs_0_), channel_id=1, source_target_pairs={{0,6},{1,7},{2,4},{3,5},{4,2},{5,3},{6,0},{7,1},{8,14},{9,15},{10,... | collective-permute-start | bytes 49160 | tf_op jit(solution)/shard_map/ppermute | solution.py:405
  55.5 4.9 %collective-permute-start.19 = (f32[64,64]{1,0:T(8,128)S(1)}, f32[64,64]{1,0:T(8,128)S(1)}, u32[]{:S(2)}, u32[]{:S(2)}) collective-permute-start(f32[64,64]{1,0:T(8,128)S(1)} %sum.3.refs_0_), channel_id=1, source_target_pairs={{0,4},{1,5},{2,6},{3,7},{4,0},{5,1},{6,2},{7,3},{8,12},{9,13},{10,... | collective-permute-start | bytes 49160 | tf_op jit(solution)/shard_map/ppermute | solution.py:405
  56.5 4.3 %collective-permute-start.18 = (f32[64,64]{1,0:T(8,128)S(1)}, f32[64,64]{1,0:T(8,128)S(1)}, u32[]{:S(2)}, u32[]{:S(2)}) collective-permute-start(f32[64,64]{1,0:T(8,128)S(1)} %sum.3.refs_0_), channel_id=1, source_target_pairs={{0,2},{1,3},{2,0},{3,1},{4,6},{5,7},{6,4},{7,5},{8,10},{9,11},{10,... | collective-permute-start | bytes 49160 | tf_op jit(solution)/shard_map/ppermute | solution.py:405
  64.9 5.8 %collective-permute-start.22 = (bf16[64,256]{1,0:T(8,128)(2,1)S(1)}, bf16[64,256]{1,0:T(8,128)(2,1)S(1)}, u32[]{:S(2)}, u32[]{:S(2)}) collective-permute-start(bf16[64,256]{1,0:T(8,128)(2,1)S(1)} %get-tuple-element.50), channel_id=1, source_target_pairs={{0,6},{1,7},{2,4},{3,5},{4,2},{5,3},{6,0},{7,1},{8,14},{9,15},{10,... | collective-permute-start | bytes 98312 | tf_op jit(solution)/shard_map/ppermute | solution.py:405
  66.6 5.2 %collective-permute-start.23 = (bf16[64,256]{1,0:T(8,128)(2,1)S(1)}, bf16[64,256]{1,0:T(8,128)(2,1)S(1)}, u32[]{:S(2)}, u32[]{:S(2)}) collective-permute-start(bf16[64,256]{1,0:T(8,128)(2,1)S(1)} %get-tuple-element.51), channel_id=1, source_target_pairs={{0,4},{1,5},{2,6},{3,7},{4,0},{5,1},{6,2},{7,3},{8,12},{9,13},{10,... | collective-permute-start | bytes 98312 | tf_op jit(solution)/shard_map/ppermute | solution.py:405
  67.4 4.4 %collective-permute-start.24 = (bf16[64,256]{1,0:T(8,128)(2,1)S(1)}, bf16[64,256]{1,0:T(8,128)(2,1)S(1)}, u32[]{:S(2)}, u32[]{:S(2)}) collective-permute-start(bf16[64,256]{1,0:T(8,128)(2,1)S(1)} %get-tuple-element.52), channel_id=1, source_target_pairs={{0,2},{1,3},{2,0},{3,1},{4,6},{5,7},{6,4},{7,5},{8,10},{9,11},{10,... | collective-permute-start | bytes 98312 | tf_op jit(solution)/shard_map/ppermute | solution.py:405
  71.8 5.8 %collective-permute-start.27 = (bf16[64,256]{1,0:T(8,128)(2,1)S(1)}, bf16[64,256]{1,0:T(8,128)(2,1)S(1)}, u32[]{:S(2)}, u32[]{:S(2)}) collective-permute-start(bf16[64,256]{1,0:T(8,128)(2,1)S(1)} %query.3.refs_0_), channel_id=1, source_target_pairs={{0,6},{1,7},{2,4},{3,5},{4,2},{5,3},{6,0},{7,1},{8,14},{9,15},{10,... | collective-permute-start | bytes 98312 | tf_op jit(solution)/shard_map/ppermute | solution.py:405
  73.9 4.8 %collective-permute-start.26 = (bf16[64,256]{1,0:T(8,128)(2,1)S(1)}, bf16[64,256]{1,0:T(8,128)(2,1)S(1)}, u32[]{:S(2)}, u32[]{:S(2)}) collective-permute-start(bf16[64,256]{1,0:T(8,128)(2,1)S(1)} %query.3.refs_0_), channel_id=1, source_target_pairs={{0,4},{1,5},{2,6},{3,7},{4,0},{5,1},{6,2},{7,3},{8,12},{9,13},{10,... | collective-permute-start | bytes 98312 | tf_op jit(solution)/shard_map/ppermute | solution.py:405
  74.8 4.2 %collective-permute-start.25 = (bf16[64,256]{1,0:T(8,128)(2,1)S(1)}, bf16[64,256]{1,0:T(8,128)(2,1)S(1)}, u32[]{:S(2)}, u32[]{:S(2)}) collective-permute-start(bf16[64,256]{1,0:T(8,128)(2,1)S(1)} %query.3.refs_0_), channel_id=1, source_target_pairs={{0,2},{1,3},{2,0},{3,1},{4,6},{5,7},{6,4},{7,5},{8,10},{9,11},{10,... | collective-permute-start | bytes 98312 | tf_op jit(solution)/shard_map/ppermute | solution.py:405
  82.1 7.1 %collective-permute-start.29 = (f32[64,512]{1,0:T(8,128)S(1)}, f32[64,512]{1,0:T(8,128)S(1)}, u32[]{:S(2)}, u32[]{:S(2)}) collective-permute-start(f32[64,512]{1,0:T(8,128)S(1)} %get-tuple-element.54), channel_id=1, source_target_pairs={{0,24},{8,16},{16,8},{24,0},{1,25},{9,17},{17,9},{25,1},{2,26},{10... | collective-permute-start | bytes 393224 | tf_op jit(solution)/shard_map/ppermute | solution.py:405
  83.1 7.7 %collective-permute-start.30 = (f32[64,512]{1,0:T(8,128)S(1)}, f32[64,512]{1,0:T(8,128)S(1)}, u32[]{:S(2)}, u32[]{:S(2)}) collective-permute-start(f32[64,512]{1,0:T(8,128)S(1)} %get-tuple-element.55), channel_id=1, source_target_pairs={{0,16},{8,24},{16,0},{24,8},{1,17},{9,25},{17,1},{25,9},{2,18},{10... | collective-permute-start | bytes 393224 | tf_op jit(solution)/shard_map/ppermute | solution.py:405
  84.8 6.4 %collective-permute-start.31 = (f32[64,512]{1,0:T(8,128)S(1)}, f32[64,512]{1,0:T(8,128)S(1)}, u32[]{:S(2)}, u32[]{:S(2)}) collective-permute-start(f32[64,512]{1,0:T(8,128)S(1)} %get-tuple-element.56), channel_id=1, source_target_pairs={{0,8},{8,0},{16,24},{24,16},{1,9},{9,1},{17,25},{25,17},{2,10},{10... | collective-permute-start | bytes 393224 | tf_op jit(solution)/shard_map/ppermute | solution.py:405
  91.6 4.9 %collective-permute-start.34 = (f32[64,64]{1,0:T(8,128)S(1)}, f32[64,64]{1,0:T(8,128)S(1)}, u32[]{:S(2)}, u32[]{:S(2)}) collective-permute-start(f32[64,64]{1,0:T(8,128)S(1)} %get-tuple-element.57.refs_0_), channel_id=1, source_target_pairs={{0,24},{8,16},{16,8},{24,0},{1,25},{9,17},{17,9},{25,1},{2,26},{10... | collective-permute-start | bytes 49160 | tf_op jit(solution)/shard_map/ppermute | solution.py:405
  93.3 3.9 %collective-permute-start.33 = (f32[64,64]{1,0:T(8,128)S(1)}, f32[64,64]{1,0:T(8,128)S(1)}, u32[]{:S(2)}, u32[]{:S(2)}) collective-permute-start(f32[64,64]{1,0:T(8,128)S(1)} %get-tuple-element.57.refs_0_), channel_id=1, source_target_pairs={{0,16},{8,24},{16,0},{24,8},{1,17},{9,25},{17,1},{25,9},{2,18},{10... | collective-permute-start | bytes 49160 | tf_op jit(solution)/shard_map/ppermute | solution.py:405
  99.9 5.7 %collective-permute-start.38 = (f32[64,64]{1,0:T(8,128)S(1)}, f32[64,64]{1,0:T(8,128)S(1)}, u32[]{:S(2)}, u32[]{:S(2)}) collective-permute-start(f32[64,64]{1,0:T(8,128)S(1)} %sum.5.refs_0_), channel_id=1, source_target_pairs={{0,6},{1,7},{2,4},{3,5},{4,2},{5,3},{6,0},{7,1},{8,14},{9,15},{10,... | collective-permute-start | bytes 49160 | tf_op jit(solution)/shard_map/ppermute | solution.py:405
  101.5 5.1 %collective-permute-start.37 = (f32[64,64]{1,0:T(8,128)S(1)}, f32[64,64]{1,0:T(8,128)S(1)}, u32[]{:S(2)}, u32[]{:S(2)}) collective-permute-start(f32[64,64]{1,0:T(8,128)S(1)} %sum.5.refs_0_), channel_id=1, source_target_pairs={{0,4},{1,5},{2,6},{3,7},{4,0},{5,1},{6,2},{7,3},{8,12},{9,13},{10,... | collective-permute-start | bytes 49160 | tf_op jit(solution)/shard_map/ppermute | solution.py:405
  102.0 4.7 %collective-permute-start.36 = (f32[64,64]{1,0:T(8,128)S(1)}, f32[64,64]{1,0:T(8,128)S(1)}, u32[]{:S(2)}, u32[]{:S(2)}) collective-permute-start(f32[64,64]{1,0:T(8,128)S(1)} %sum.5.refs_0_), channel_id=1, source_target_pairs={{0,2},{1,3},{2,0},{3,1},{4,6},{5,7},{6,4},{7,5},{8,10},{9,11},{10,... | collective-permute-start | bytes 49160 | tf_op jit(solution)/shard_map/ppermute | solution.py:405
  (9 other events, 24.2 us)

commit v2 on v1

--- a/solution.py
+++ b/solution.py
@@ -9,8 +9,7 @@
 from jax.sharding import PartitionSpec as P
 
 ITERS = 2
-GROUP = 16
-HALF_GROUP = 8
+GROUP = 8
 LOADS = 8
 PANEL_STEP = 8
 HIGH = lax.Precision.HIGHEST
@@ -42,6 +41,10 @@
     return jnp.concatenate(done, axis=0)[:, width:]
 
 
+SLOT, QUERY_GIVE, PRODUCT_TAKE, QUERY_TAKE, PRODUCT_GIVE = range(5)
+FIELDS, LISTS, ALL = 5, 3, 2
+SINGLES = FIELDS * LISTS
+ROW_AT, COL_AT = 3, 4
 WHOLE = pl.BlockSpec(memory_space=pltpu.VMEM)
 SCALARS = pl.BlockSpec(memory_space=pltpu.SMEM)
 AWAY = pl.BlockSpec(memory_space=pltpu.MemorySpace.HBM)
@@ -109,79 +112,35 @@
         get(total, me ^ ((count - at) % count), out_ref, side)
 
 
-def emit_pairs(total, mine_ref, other_ref, me, side):
-    for step in range(mine_ref.shape[0]):
-        get(total, me ^ (2 * step), mine_ref.at[step], side)
-        get(total, me ^ (2 * step + 1), other_ref.at[step], side)
-
-
 def collect(held, piece_refs, me, side):
     for step, piece_ref in enumerate(piece_refs):
         put(held, me ^ step, piece_ref[...], side)
 
 
-def collect_pairs(held, mine_ref, other_ref, me, side):
-    for step in range(mine_ref.shape[0]):
-        put(held, me ^ (2 * step), mine_ref[step], side)
-        put(held, me ^ (2 * step + 1), other_ref[step], side)
-
-
-def group_of(g, source, target, dims, count, ids, held, tile_ref, total):
-    tiles, width, _ = total.shape
-    for lane in range(GROUP):
-        slot = g * GROUP + lane
-        give = jnp.where(slot < count, ids[target, slot], tiles - 1)
-        term = lax.dot_general(
-            held[ids[source, slot]], tile_ref[slot], dims, preferred_element_type=jnp.float32
-        )
-        if term.shape[0] > width:
-            term = term[:width] + term[width:]
-        total[give] += term
-
-
-def groups(source, target, dims, count, ids, held, tile_ref, total):
+def products(which, take, give, dims, table, held, tile_ref, total):
+    width = total.shape[1]
+    count = table[SINGLES, which]
+
     def step(g, carry):
-        group_of(g, source, target, dims, count, ids, held, tile_ref, total)
+        for lane in range(GROUP):
+            at = g * GROUP + lane
+            term = lax.dot_general(
+                held[table[which * FIELDS + take, at]],
+                tile_ref[table[which * FIELDS + SLOT, at]],
+                dims,
+                preferred_element_type=jnp.float32,
+            )
+            if term.shape[0] > width:
+                term = term[:width] + term[width:]
+            total[table[which * FIELDS + give, at]] += term
         return carry
 
     last = tile_ref.shape[0] // GROUP
     lax.fori_loop(0, jnp.minimum((count + GROUP - 1) // GROUP, last), step, 0)
 
 
-def first_body(n_in, ids, live, place, *refs):
-    pieces, (tile_ref, mine_ref, other_ref, held, total) = refs[:n_in], refs[n_in:]
-    side = tile_ref.shape[1]
-    collect(held, pieces, place[0], side)
-    total[...] = jnp.zeros_like(total)
-    groups(1, 0, NT, live[0], ids, held, tile_ref, total)
-    emit_pairs(total, mine_ref, other_ref, place[1], side)
-
-
-def back_body(ids, live, place, here_ref, there_ref, tile_ref, *refs):
-    out_refs, (held, total) = refs[:-2], refs[-2:]
-    side = tile_ref.shape[1]
-    collect_pairs(held, here_ref, there_ref, place[1], side)
-    total[...] = jnp.zeros_like(total)
-    groups(0, 1, NN, live[0], ids, held, tile_ref, total)
-    emit(total, out_refs, place[0], side)
-
-
-def listed(source, target, dims, side_of, ids, order, held, tile_ref, total):
-    tiles = total.shape[0]
-    slots = tile_ref.shape[0]
-    count = order[2, side_of]
-
-    def step(g, carry):
-        for lane in range(HALF_GROUP):
-            at = g * HALF_GROUP + lane
-            slot = order[side_of, at]
-            give = jnp.where(at < count, ids[target, slot], tiles - 1)
-            total[give] += lax.dot_general(
-                held[ids[source, slot]], tile_ref[slot], dims, preferred_element_type=jnp.float32
-            )
-        return carry
-
-    lax.fori_loop(0, jnp.minimum((count + HALF_GROUP - 1) // HALF_GROUP, slots // HALF_GROUP), step, 0)
+forward = functools.partial(products, take=PRODUCT_TAKE, give=QUERY_GIVE, dims=NT)
+backward = functools.partial(products, take=QUERY_TAKE, give=PRODUCT_GIVE, dims=NN)
 
 
 def emit_half(total, out_ref, me, side, flip):
@@ -194,49 +153,70 @@
         put(held, me ^ (2 * step + flip), piece_ref[...], side)
 
 
-def forward_other_body(n_in, ids, order, place, *refs):
+def forward_body(n_in, table, *refs):
+    pieces, (tile_ref, mine_ref, other_ref, held, total) = refs[:n_in], refs[n_in:]
+    side = tile_ref.shape[1]
+    collect(held, pieces, table[SINGLES, ROW_AT], side)
+    total[...] = jnp.zeros_like(total)
+    forward(ALL, table=table, held=held, tile_ref=tile_ref, total=total)
+    emit_half(total, mine_ref, table[SINGLES, COL_AT], side, 0)
+    emit_half(total, other_ref, table[SINGLES, COL_AT], side, 1)
+
+
+def forward_other_body(n_in, table, *refs):
     pieces, (tile_ref, held, other_ref, total) = refs[:n_in], refs[n_in:]
-    side = tile_ref.shape[1]
-    collect(held, pieces, place[0], side)
+    side, me = tile_ref.shape[1], table[SINGLES, COL_AT]
+    collect(held, pieces, table[SINGLES, ROW_AT], side)
     total[...] = jnp.zeros_like(total)
-    listed(1, 0, NT, 1 - place[1] % 2, ids, order, held, tile_ref, total)
-    emit_half(total, other_ref, place[1], side, 1)
-
-
-def forward_mine_body(ids, order, place, held, tile_ref, mine_ref, total):
-    side = tile_ref.shape[1]
+    forward(1 - me % 2, table=table, held=held, tile_ref=tile_ref, total=total)
+    emit_half(total, other_ref, me, side, 1)
+
+
+def forward_mine_body(table, held, tile_ref, mine_ref, total):
+    side, me = tile_ref.shape[1], table[SINGLES, COL_AT]
     total[...] = jnp.zeros_like(total)
-    listed(1, 0, NT, place[1] % 2, ids, order, held, tile_ref, total)
-    emit_half(total, mine_ref, place[1], side, 0)
-
-
-def back_mine_body(n_in, ids, order, place, *refs):
-    pieces, (tile_ref, total, held) = refs[:n_in], refs[n_in:]
-    collect_half(held, pieces, place[1], tile_ref.shape[1], 0)
-    total[...] = jnp.zeros_like(total)
-    listed(0, 1, NN, place[1] % 2, ids, order, held, tile_ref, total)
-
-
-def back_other_body(ids, order, place, there_ref, begun_ref, tile_ref, *refs):
+    forward(me % 2, table=table, held=held, tile_ref=tile_ref, total=total)
+    emit_half(total, mine_ref, me, side, 0)
+
+
+def back_body(table, here_ref, there_ref, tile_ref, *refs):
     out_refs, (held, total) = refs[:-2], refs[-2:]
     side = tile_ref.shape[1]
-    collect_half(held, [there_ref.at[step] for step in range(there_ref.shape[0])], place[1], side, 1)
+    for flip, ref in enumerate((here_ref, there_ref)):
+        collect_half(held, [ref.at[step] for step in range(ref.shape[0])], table[SINGLES, COL_AT], side, flip)
+    total[...] = jnp.zeros_like(total)
+    backward(ALL, table=table, held=held, tile_ref=tile_ref, total=total)
+    emit(total, out_refs, table[SINGLES, ROW_AT], side)
+
+
+def back_mine_body(n_in, table, *refs):
+    pieces, (tile_ref, total, held) = refs[:n_in], refs[n_in:]
+    me = table[SINGLES, COL_AT]
+    collect_half(held, pieces, me, tile_ref.shape[1], 0)
+    total[...] = jnp.zeros_like(total)
+    backward(me % 2, table=table, held=held, tile_ref=tile_ref, total=total)
+
+
+def back_other_body(table, there_ref, begun_ref, tile_ref, *refs):
+    out_refs, (held, total) = refs[:-2], refs[-2:]
+    side, me = tile_ref.shape[1], table[SINGLES, COL_AT]
+    collect_half(held, [there_ref.at[step] for step in range(there_ref.shape[0])], me, side, 1)
     total[...] = begun_ref[...]
-    listed(0, 1, NN, 1 - place[1] % 2, ids, order, held, tile_ref, total)
-    emit(total, out_refs, place[0], side)
-
-
-def next_body(n_in, ids, live, place, *refs):
+    backward(1 - me % 2, table=table, held=held, tile_ref=tile_ref, total=total)
+    emit(total, out_refs, table[SINGLES, ROW_AT], side)
+
+
+def next_body(n_in, table, *refs):
     pieces, (scale_ref, tile_ref, out_ref, spread, held, total) = refs[:n_in], refs[n_in:]
     tiles, width, side = out_ref.shape
-    collect(spread, pieces, place[0], side)
+    collect(spread, pieces, table[SINGLES, ROW_AT], side)
     for tile in range(spread.shape[0]):
         value = spread[tile] * scale_ref[:, tile * side : (tile + 1) * side]
         high = value.astype(jnp.bfloat16)
         held[tile, :width] = high
         held[tile, width:] = (value - high.astype(jnp.float32)).astype(jnp.bfloat16)
     total[...] = jnp.zeros_like(total)
-    groups(1, 0, NT, live[0], ids, held, tile_ref, total)
+    forward(ALL, table=table, held=held, tile_ref=tile_ref, total=total)
     out_ref[...] = total[:tiles]
 
 
@@ -262,38 +242,56 @@
     out_ref[...] = (held[...] * scale).astype(out_ref.dtype)
 
 
-def load_body(per, ids, live, place, after_ref, tile_ref, product_ref, query_ref, *refs):
-    keep, my_product_ref, product_out, my_query_ref, order, degrees, counts, sems = refs
+def write_table(table, ids, place, per, query_tiles, product_tiles):
+    slots = ids.shape[1]
+    for which in range(LISTS):
+        table[SINGLES, which] = 0
+        for at in range(slots):
+            table[which * FIELDS + SLOT, at] = 0
+            table[which * FIELDS + QUERY_GIVE, at] = query_tiles
+            table[which * FIELDS + PRODUCT_TAKE, at] = 0
+            table[which * FIELDS + QUERY_TAKE, at] = 0
+            table[which * FIELDS + PRODUCT_GIVE, at] = product_tiles
+    table[SINGLES, ROW_AT] = place[0]
+    table[SINGLES, COL_AT] = place[1]
+
+    def step(slot, carry):
+        query, product = ids[0, slot], ids[1, slot]
+        for which in (query // per % 2, ALL):
+            at = table[SINGLES, which]
+            table[which * FIELDS + SLOT, at] = slot
+            table[which * FIELDS + QUERY_GIVE, at] = query
+            table[which * FIELDS + PRODUCT_TAKE, at] = product
+            table[which * FIELDS + QUERY_TAKE, at] = query
+            table[which * FIELDS + PRODUCT_GIVE, at] = product
+            table[SINGLES, which] = at + 1
+        return carry
+
+    lax.fori_loop(0, jnp.minimum(place[2], slots), step, 0)
+
+
+def load_body(per, place, after_ref, tile_ref, id_ref, product_ref, query_ref, *refs):
+    keep, my_product_ref, product_out, my_query_ref, table, ids, degrees, counts, sems = refs
     loads = [
-        pltpu.make_async_copy(product_ref, degrees, sems.at[0]),
-        pltpu.make_async_copy(query_ref, counts, sems.at[1]),
+        pltpu.make_async_copy(id_ref, ids, sems.at[0]),
+        pltpu.make_async_copy(product_ref, degrees, sems.at[1]),
+        pltpu.make_async_copy(query_ref, counts, sems.at[2]),
     ]
     part = tile_ref.shape[0] // LOADS
     for step in range(LOADS):
         span = pl.ds(step * part, part)
-        loads.append(pltpu.make_async_copy(tile_ref.at[span], keep.at[span], sems.at[2 + step]))
+        loads.append(pltpu.make_async_copy(tile_ref.at[span], keep.at[span], sems.at[3 + step]))
     for load in loads:
         load.start()
-    order[2, 0] = 0
-    order[2, 1] = 0
-    for slot in range(tile_ref.shape[0]):
-        order[0, slot] = 0
-        order[1, slot] = 0
-    for slot in range(tile_ref.shape[0]):
-
-        @pl.when(slot < live[0])
-        def _():
-            core = ids[0, slot] // per % 2
-            at = order[2, core]
-            order[core, at] = slot
-            order[2, core] = at + 1
-
     loads[0].wait()
+    side = tile_ref.shape[1]
+    write_table(table, ids, place, per, query_ref.shape[1] // side, product_ref.shape[1] // side)
+    loads[1].wait()
     product_out[...] = 1.0 / jnp.sqrt(degrees[...].astype(jnp.float32))
     share = my_product_ref.shape[1]
     at = pl.multiple_of(place[0] * share, 128)
     my_product_ref[...] = product_out[:, pl.ds(at, share)]
-    loads[1].wait()
+    loads[2].wait()
     columns = my_query_ref.shape[1]
     if columns % 128 == 0:
         at = pl.multiple_of(place[1] * columns, 128)
@@ -305,7 +303,7 @@
             def _():
                 degree = counts[:, step * columns : (step + 1) * columns]
                 my_query_ref[...] = 1.0 / jnp.sqrt(degree.astype(jnp.float32))
-    for load in loads[2:]:
+    for load in loads[3:]:
         load.wait()
 
 
@@ -378,17 +376,17 @@
                 )[:, at * share : (at + 1) * share]
 
 
-def apply_other_body(n_in, place, *refs):
+def apply_other_body(n_in, table, *refs):
     grams, (total_ref, inverse_ref, other_ref) = refs[:n_in], refs[n_in:]
     inverse = inverse_factor(add(grams))
     inverse_ref[...] = inverse
     for step in range(other_ref.shape[0]):
-        apply_tile(inverse, total_ref, place[1] ^ (2 * step + 1), other_ref.at[step])
-
-
-def apply_mine_body(place, inverse_ref, total_ref, mine_ref):
+        apply_tile(inverse, total_ref, table[SINGLES, COL_AT] ^ (2 * step + 1), other_ref.at[step])
+
+
+def apply_mine_body(table, inverse_ref, total_ref, mine_ref):
     for step in range(mine_ref.shape[0]):
-        apply_tile(inverse_ref[...], total_ref, place[1] ^ (2 * step), mine_ref.at[step])
+        apply_tile(inverse_ref[...], total_ref, table[SINGLES, COL_AT] ^ (2 * step), mine_ref.at[step])
 
 
 def finish_body(after, *refs):
@@ -425,14 +423,13 @@
 def shards(tiles, tile_ids, tile_count, query_degree, product_degree, panel):
     tile_set = tiles[0, 0]
     ids = tile_ids[0, 0]
-    live = tile_count[0]
     slots, side, _ = tile_set.shape
     width, share = panel.shape
     queries, products = query_degree.shape[0], product_degree.shape[0]
     query_tiles, product_tiles = queries // side, products // side
     n_row, n_col = lax.axis_size("row"), lax.axis_size("col")
     chips = n_col // 2
-    place = jnp.stack([lax.axis_index("row"), lax.axis_index("col")]).astype(jnp.int32)
+    row_at, col_at = lax.axis_index("row").astype(jnp.int32), lax.axis_index("col").astype(jnp.int32)
     columns = queries // n_col
     work = dict(flops=2 * slots * width * side * side, moved=2 * slots * side * side)
     scaled = call(
@@ -445,28 +442,36 @@
             pltpu.VMEM((1, products), jnp.int32),
             pltpu.SemaphoreType.DMA((2,)),
         ],
-    )(place, in_hbm(panel), in_hbm(product_degree[None, :]))
+    )(row_at[None], in_hbm(panel), in_hbm(product_degree[None, :]))
     pieces = spread_to(scaled, "row")
     split = columns % side == 0
-    tile_set, my_pscale, pscale, my_qscale, order = call(
+    tile_set, my_pscale, pscale, my_qscale, table = call(
         functools.partial(load_body, max(columns // side, 1)),
         "load",
-        [SCALARS] * 3 + [WHOLE, AWAY, AWAY, AWAY],
+        [SCALARS, WHOLE] + [AWAY] * 4,
         [
             pltpu.VMEM((slots, side, side), jnp.bfloat16),
             f32(1, share),
             f32(1, products),
             f32(1, columns),
-            jax.ShapeDtypeStruct((3, slots), jnp.int32),
+            jax.ShapeDtypeStruct((SINGLES + 1, slots), jnp.int32),
         ],
         [
+            pltpu.SMEM(ids.shape, jnp.int32),
             pltpu.VMEM((1, products), jnp.int32),
             pltpu.VMEM((1, queries), jnp.int32),
-            pltpu.SemaphoreType.DMA((2 + LOADS,)),
+            pltpu.SemaphoreType.DMA((3 + LOADS,)),
         ],
         moved=4 * slots * side * side,
         out_specs=[WHOLE] * 4 + [SCALARS],
-    )(ids, live, place, scaled, in_hbm(tile_set), in_hbm(product_degree[None, :]), in_hbm(query_degree[None, :]))
+    )(
+        jnp.stack([row_at, col_at, tile_count[0, 0]]),
+        scaled,
+        in_hbm(tile_set),
+        in_hbm(ids),
+        in_hbm(product_degree[None, :]),
+        in_hbm(query_degree[None, :]),
+    )
     tile_set = pltpu.with_memory_space_constraint(tile_set, pltpu.VMEM)
     root_count = math.sqrt(products * n_col)
     half = f32(chips, width, columns)
@@ -482,7 +487,7 @@
             total = call(
                 functools.partial(next_body, n_row),
                 "forward",
-                [SCALARS] * 3 + [WHOLE] * (n_row + 2),
+                [SCALARS] + [WHOLE] * (n_row + 2),
                 f32(query_tiles, width, side),
                 [
                     pltpu.VMEM((product_tiles, width, side), jnp.float32),
@@ -490,44 +495,44 @@
                     query_scratch,
                 ],
                 **work,
-            )(ids, live, place, *pieces, pscale, tile_set)
+            )(table, *pieces, pscale, tile_set)
             inverse, other = call(
                 functools.partial(apply_other_body, chips),
                 "apply",
                 [SCALARS] + [WHOLE] * (chips + 1),
                 [f32(width, width), half],
-            )(place, *grams, total)
+            )(table, *grams, total)
             got = swap(other, "col", 1)
             mine = call(apply_mine_body, "apply_rest", [SCALARS] + [WHOLE] * 2, half, **half_work)(
-                place, inverse, total
+                table, inverse, total
             )
         elif split:
             held, other = call(
                 functools.partial(forward_other_body, n_row),
                 "forward",
-                [SCALARS] * 3 + [WHOLE] * (n_row + 1),
+                [SCALARS] + [WHOLE] * (n_row + 1),
                 [bf16(product_tiles, width, side), half],
                 [query_scratch],
                 **half_work,
-            )(ids, order, place, *pieces, tile_set)
+            )(table, *pieces, tile_set)
             got = swap(other, "col", 1)
             mine = call(
                 forward_mine_body,
                 "forward_rest",
-                [SCALARS] * 3 + [WHOLE] * 2,
+                [SCALARS] + [WHOLE] * 2,
                 half,
                 [query_scratch],
                 **half_work,
-            )(ids, order, place, held, tile_set)
+            )(table, held, tile_set)
         else:
             mine, other = call(
-                functools.partial(first_body, n_row),
+                functools.partial(forward_body, n_row),
                 "forward",
-                [SCALARS] * 3 + [WHOLE] * (n_row + 1),
+                [SCALARS] + [WHOLE] * (n_row + 1),
                 [half] * 2,
                 [pltpu.VMEM((product_tiles, width, side), jnp.bfloat16), query_scratch],
                 **work,
-            )(ids, live, place, *pieces, tile_set)
+            )(table, *pieces, tile_set)
             got = swap(other, "col", 1)
         sums = call(
             pair_body, "pair", [WHOLE] * 2, [f32(width, columns)] + [bf16(width, columns)] * (chips - 1)
@@ -541,28 +546,28 @@
             begun = call(
                 functools.partial(back_mine_body, chips),
                 "backward",
-                [SCALARS] * 3 + [WHOLE] * (chips + 1),
+                [SCALARS] + [WHOLE] * (chips + 1),
                 f32(product_tiles + 1, width, side),
                 [query_held],
                 **half_work,
-            )(ids, order, place, *pieces, tile_set)
+            )(table, *pieces, tile_set)
             sums = call(
                 back_other_body,
                 "backward_rest",
-                [SCALARS] * 3 + [WHOLE] * 3,
+                [SCALARS] + [WHOLE] * 3,
                 [f32(width, share)] * n_row,
                 [query_held, product_scratch],
                 **half_work,
-            )(ids, order, place, there, begun, tile_set)
+            )(table, there, begun, tile_set)
         else:
             sums = call(
                 back_body,
                 "backward",
-                [SCALARS] * 3 + [WHOLE] * 3,
+                [SCALARS] + [WHOLE] * 3,
                 [f32(width, share)] * n_row,
                 [query_held, product_scratch],
                 **work,
-            )(ids, live, place, here, there, tile_set)
+            )(table, here, there, tile_set)
         parts = deal(sums, "row")
         if iteration < ITERS - 1:
             lifted = call(lift_only_body, "lift", [WHOLE] * (n_row + 1), f32(width, share))(*parts, my_pscale)

time: 109 us -> 109 us (level); the launches traced: 109 us -> 108 us
  waiting for transfers between devices: 38.2 us -> 36.8 us
    ppermute x39, waiting for transfers between devices: 38.2 us -> 36.8 us  [swap(): lax.ppermute(value, axis, [(i, i ^ step) for i in range(lax.axis_size(axi...]
  transfers between devices with their start and end apart: 39 -> 39, of which waited for: 31 -> 27; matrix products, arithmetic and copies ran while one was open for 0% -> 0% of each run, Pallas kernels for 10% -> 12%
where the time goes in v2:
time: 109 us; the launch traced here: 108 us
  starting transfers between devices  45.8 us (42%)
  waiting for transfers between devices  36.8 us (34%)
  Pallas kernels  24.4 us (22%)
    ppermute x39, starting transfers between devices, swap(): lax.ppermute(value, axis, [(i, i ^ step) for i in range(lax.axis_size(axi...  45.8 us
    ppermute x39, waiting for transfers between devices, swap(): lax.ppermute(value, axis, [(i, i ^ step) for i in range(lax.axis_size(axi...  36.8 us
    pallas_call x1, Pallas kernels, shards(): call(functools.partial(load_body, max(columns // side, 1)), 'load', [SCAL...  3.53 us
    pallas_call x2, Pallas kernels, shards(): call(functools.partial(back_mine_body, chips), 'backward', [SCALARS] + [W...  3.33 us
    pallas_call x1, Pallas kernels, shards(): call(functools.partial(next_body, n_row), 'forward', [SCALARS] + [WHOLE]...  2.83 us
    pallas_call x2, Pallas kernels, shards(): call(back_other_body, 'backward_rest', [SCALARS] + [WHOLE] * 3, [f32(widt...  2.78 us
    pallas_call x1, Pallas kernels, shards(): call(functools.partial(apply_other_body, chips), 'apply', [SCALARS] + [WH...  2.64 us
    pallas_call x1, Pallas kernels, shards(): call(functools.partial(finish_body, root_count), 'finish', [WHOLE] * (chi...  2.52 us
  transfers between devices with their start and end apart: 39, of which 27 were waited for; matrix products, arithmetic and copies ran while one was open for 0% of the time, Pallas kernels for 12%

profile of v2, /device:TPU:0, one launch (start us, length us, event | category | flops | bytes accessed | tf_op | source)
XLA Modules:
  0.0 108.1 jit_solution(11009242443841893506)
XLA Ops:
  1.0 4.0 %collective-permute-start.2 = (bf16[64,512]{1,0:T(8,128)(2,1)S(1)}, bf16[64,512]{1,0:T(8,128)(2,1)S(1)}, u32[]{:S(2)}, u32[]{:S(2)}) collective-permute-start(bf16[64,512]{1,0:T(8,128)(2,1)S(1)} %start.1.after_ref.refs_0_), channel_id=1, source_target_pairs={{0,24},{8,16},{16,8},{24,0},{1,25},{9,17},{17,9},{25,1},{2,26},{10... | collective-permute-start | bytes 196616 | tf_op jit(solution)/shard_map/ppermute | solution.py:403
  6.3 3.5 %load.1 = (bf16[32,256,256]{2,1,0:T(8,128)(2,1)S(1)}, f32[1,512]{1,0:T(1,128)S(1)}, f32[1,2048]{1,0:T(1,128)S(1)}, f32[1,256]{1,0:T(1,128)S(1)}, s32[16,32]{1,0:T(8,128)S(1)}) custom-call(s32[3]{0:T(128)S(1)} %pad_add_fusion.place, bf16[64,512]{1,0:T(8,128)(2,1)S(1)} %start.1.after_ref.refs_0_, bf16[32,256,256]{2,1,0:T(8,128)(2,1)} %bitcast.8, ...), custom_call_target="tpu_custom_call" | custom-call | bytes 8388608 | tf_op jit(solution)/shard_map/load/pallas_call | solution.py:448
  9.9 1.7 %forward.2 = (bf16[8,64,256]{2,1,0:T(8,128)(2,1)S(1)}, f32[4,64,256]{2,1,0:T(8,128)S(1)}) custom-call(s32[16,32]{1,0:T(8,128)S(1)} %get-tuple-element.32.table, bf16[64,512]{1,0:T(8,128)(2,1)S(1)} %start.1.after_ref.refs_0_, bf16[64,512]{1,0:T(8,128)(2,1)S(1)} %collective-permute-done.refs_1_, bf16[64,512]{1,0:T(8,128)(2,1)S(1)} %collective-permute-done.1.refs_2_, ...), custom_call_target="tpu_custom_call" | custom-call | flops 134217728 | bytes 2097152 | tf_op jit(solution)/shard_map/forward/pallas_call | solution.py:510
  11.6 2.1 %forward_rest.1.mine_ref = f32[4,64,256]{2,1,0:T(8,128)S(1)} custom-call(s32[16,32]{1,0:T(8,128)S(1)} %get-tuple-element.32.table, bf16[8,64,256]{2,1,0:T(8,128)(2,1)S(1)} %get-tuple-element.34.held, bf16[32,256,256]{2,1,0:T(8,128)(2,1)S(1)} %get-tuple-element.33.refs_4_.tile_ref.refs_5_), custom_call_target="tpu_custom_call" | custom-call | flops 134217728 | bytes 2097152 | tf_op jit(solution)/shard_map/forward_rest/pallas_call | solution.py:519
  13.8 3.0 %collective-permute-start.4 = (bf16[64,256]{1,0:T(8,128)(2,1)S(1)}, bf16[64,256]{1,0:T(8,128)(2,1)S(1)}, u32[]{:S(2)}, u32[]{:S(2)}) collective-permute-start(bf16[64,256]{1,0:T(8,128)(2,1)S(1)} %get-tuple-element.37), channel_id=1, source_target_pairs={{0,6},{1,7},{2,4},{3,5},{4,2},{5,3},{6,0},{7,1},{8,14},{9,15},{10,... | collective-permute-start | bytes 98312 | tf_op jit(solution)/shard_map/ppermute | solution.py:403
  16.8 1.4 %collective-permute-start.6 = (bf16[64,256]{1,0:T(8,128)(2,1)S(1)}, bf16[64,256]{1,0:T(8,128)(2,1)S(1)}, u32[]{:S(2)}, u32[]{:S(2)}) collective-permute-start(bf16[64,256]{1,0:T(8,128)(2,1)S(1)} %get-tuple-element.39), channel_id=1, source_target_pairs={{0,2},{1,3},{2,0},{3,1},{4,6},{5,7},{6,4},{7,5},{8,10},{9,11},{10,... | collective-permute-start | bytes 98312 | tf_op jit(solution)/shard_map/ppermute | solution.py:403
  19.6 2.1 %collective-permute-done.5.refs_2_ = bf16[64,256]{1,0:T(8,128)(2,1)S(1)} collective-permute-done((bf16[64,256]{1,0:T(8,128)(2,1)S(1)}, bf16[64,256]{1,0:T(8,128)(2,1)S(1)}, u32[]{:S(2)}, u32[]{:S(2)}) %collective-permute-start.5) | collective-permute-done | bytes 32800 | tf_op jit(solution)/shard_map/ppermute | solution.py:403
  21.7 1.9 %collective-permute-start.9 = (bf16[64,256]{1,0:T(8,128)(2,1)S(1)}, bf16[64,256]{1,0:T(8,128)(2,1)S(1)}, u32[]{:S(2)}, u32[]{:S(2)}) collective-permute-start(bf16[64,256]{1,0:T(8,128)(2,1)S(1)} %query.2.refs_0_), channel_id=1, source_target_pairs={{0,6},{1,7},{2,4},{3,5},{4,2},{5,3},{6,0},{7,1},{8,14},{9,15},{10,... | collective-permute-start | bytes 98312 | tf_op jit(solution)/shard_map/ppermute | solution.py:403
  23.8 2.4 %collective-permute-start.7 = (bf16[64,256]{1,0:T(8,128)(2,1)S(1)}, bf16[64,256]{1,0:T(8,128)(2,1)S(1)}, u32[]{:S(2)}, u32[]{:S(2)}) collective-permute-start(bf16[64,256]{1,0:T(8,128)(2,1)S(1)} %query.2.refs_0_), channel_id=1, source_target_pairs={{0,2},{1,3},{2,0},{3,1},{4,6},{5,7},{6,4},{7,5},{8,10},{9,11},{10,... | collective-permute-start | bytes 98312 | tf_op jit(solution)/shard_map/ppermute | solution.py:403
  28.9 1.7 %backward.2.begun_ref = f32[9,64,256]{2,1,0:T(8,128)S(1)} custom-call(s32[16,32]{1,0:T(8,128)S(1)} %get-tuple-element.32.table, bf16[64,256]{1,0:T(8,128)(2,1)S(1)} %query.2.refs_0_, bf16[64,256]{1,0:T(8,128)(2,1)S(1)} %collective-permute-done.7.refs_1_, bf16[64,256]{1,0:T(8,128)(2,1)S(1)} %collective-permute-done.8.refs_2_, ...), custom_call_target="tpu_custom_call" | custom-call | flops 134217728 | bytes 2097152 | tf_op jit(solution)/shard_map/backward/pallas_call | solution.py:546
  32.0 1.4 %collective-permute-start.11 = (f32[64,512]{1,0:T(8,128)S(1)}, f32[64,512]{1,0:T(8,128)S(1)}, u32[]{:S(2)}, u32[]{:S(2)}) collective-permute-start(f32[64,512]{1,0:T(8,128)S(1)} %get-tuple-element.42), channel_id=1, source_target_pairs={{0,24},{8,16},{16,8},{24,0},{1,25},{9,17},{17,9},{25,1},{2,26},{10... | collective-permute-start | bytes 393224 | tf_op jit(solution)/shard_map/ppermute | solution.py:403
  35.6 2.5 %collective-permute-done.11.refs_1_ = f32[64,512]{1,0:T(8,128)S(1)} collective-permute-done((f32[64,512]{1,0:T(8,128)S(1)}, f32[64,512]{1,0:T(8,128)S(1)}, u32[]{:S(2)}, u32[]{:S(2)}) %collective-permute-start.11) | collective-permute-done | bytes 131104 | tf_op jit(solution)/shard_map/ppermute | solution.py:403
  38.1 2.7 %collective-permute-done.12.refs_2_ = f32[64,512]{1,0:T(8,128)S(1)} collective-permute-done((f32[64,512]{1,0:T(8,128)S(1)}, f32[64,512]{1,0:T(8,128)S(1)}, u32[]{:S(2)}, u32[]{:S(2)}) %collective-permute-start.12) | collective-permute-done | bytes 131104 | tf_op jit(solution)/shard_map/ppermute | solution.py:403
  41.6 1.5 %collective-permute-start.16 = (f32[64,512]{1,0:T(8,128)S(1)}, f32[64,512]{1,0:T(8,128)S(1)}, u32[]{:S(2)}, u32[]{:S(2)}) collective-permute-start(f32[64,512]{1,0:T(8,128)S(1)} %lift.2.refs_0_), channel_id=1, source_target_pairs={{0,24},{8,16},{16,8},{24,0},{1,25},{9,17},{17,9},{25,1},{2,26},{10... | collective-permute-start | bytes 393224 | tf_op jit(solution)/shard_map/ppermute | solution.py:403
  45.1 3.8 %collective-permute-done.16.refs_3_ = f32[64,512]{1,0:T(8,128)S(1)} collective-permute-done((f32[64,512]{1,0:T(8,128)S(1)}, f32[64,512]{1,0:T(8,128)S(1)}, u32[]{:S(2)}, u32[]{:S(2)}) %collective-permute-start.16) | collective-permute-done | bytes 131104 | tf_op jit(solution)/shard_map/ppermute | solution.py:403
  48.9 1.7 %collective-permute-done.15.refs_2_ = f32[64,512]{1,0:T(8,128)S(1)} collective-permute-done((f32[64,512]{1,0:T(8,128)S(1)}, f32[64,512]{1,0:T(8,128)S(1)}, u32[]{:S(2)}, u32[]{:S(2)}) %collective-permute-start.15) | collective-permute-done | bytes 131104 | tf_op jit(solution)/shard_map/ppermute | solution.py:403
  52.6 2.0 %collective-permute-start.20 = (f32[64,64]{1,0:T(8,128)S(1)}, f32[64,64]{1,0:T(8,128)S(1)}, u32[]{:S(2)}, u32[]{:S(2)}) collective-permute-start(f32[64,64]{1,0:T(8,128)S(1)} %sum.3.refs_0_), channel_id=1, source_target_pairs={{0,6},{1,7},{2,4},{3,5},{4,2},{5,3},{6,0},{7,1},{8,14},{9,15},{10,... | collective-permute-start | bytes 49160 | tf_op jit(solution)/shard_map/ppermute | solution.py:403
  55.5 1.6 %collective-permute-start.18 = (f32[64,64]{1,0:T(8,128)S(1)}, f32[64,64]{1,0:T(8,128)S(1)}, u32[]{:S(2)}, u32[]{:S(2)}) collective-permute-start(f32[64,64]{1,0:T(8,128)S(1)} %sum.3.refs_0_), channel_id=1, source_target_pairs={{0,2},{1,3},{2,0},{3,1},{4,6},{5,7},{6,4},{7,5},{8,10},{9,11},{10,... | collective-permute-start | bytes 49160 | tf_op jit(solution)/shard_map/ppermute | solution.py:403
  57.0 2.8 %forward.3.refs_4_.total_ref = f32[8,64,256]{2,1,0:T(8,128)S(1)} custom-call(s32[16,32]{1,0:T(8,128)S(1)} %get-tuple-element.32.table, f32[64,512]{1,0:T(8,128)S(1)} %lift.2.refs_0_, f32[64,512]{1,0:T(8,128)S(1)} %collective-permute-done.14.refs_1_, f32[64,512]{1,0:T(8,128)S(1)} %collective-permute-done.15.refs_2_, ...), custom_call_target="tpu_custom_call" | custom-call | flops 268435456 | bytes 4194304 | tf_op jit(solution)/shard_map/forward/pallas_call | solution.py:487
  59.9 2.6 %apply.1 = (f32[64,64]{1,0:T(8,128)S(1)}, f32[4,64,256]{2,1,0:T(8,128)S(1)}) custom-call(s32[16,32]{1,0:T(8,128)S(1)} %get-tuple-element.32.table, f32[64,64]{1,0:T(8,128)S(1)} %sum.3.refs_0_, f32[64,64]{1,0:T(8,128)S(1)} %collective-permute-done.18.refs_1_, f32[64,64]{1,0:T(8,128)S(1)} %collective-permute-done.19.refs_2_, ...), custom_call_target="tpu_custom_call" | custom-call | tf_op jit(solution)/shard_map/apply/pallas_call | solution.py:499
  64.2 1.9 %collective-permute-start.22 = (bf16[64,256]{1,0:T(8,128)(2,1)S(1)}, bf16[64,256]{1,0:T(8,128)(2,1)S(1)}, u32[]{:S(2)}, u32[]{:S(2)}) collective-permute-start(bf16[64,256]{1,0:T(8,128)(2,1)S(1)} %get-tuple-element.50), channel_id=1, source_target_pairs={{0,6},{1,7},{2,4},{3,5},{4,2},{5,3},{6,0},{7,1},{8,14},{9,15},{10,... | collective-permute-start | bytes 98312 | tf_op jit(solution)/shard_map/ppermute | solution.py:403
  66.7 1.9 %collective-permute-start.24 = (bf16[64,256]{1,0:T(8,128)(2,1)S(1)}, bf16[64,256]{1,0:T(8,128)(2,1)S(1)}, u32[]{:S(2)}, u32[]{:S(2)}) collective-permute-start(bf16[64,256]{1,0:T(8,128)(2,1)S(1)} %get-tuple-element.52), channel_id=1, source_target_pairs={{0,2},{1,3},{2,0},{3,1},{4,6},{5,7},{6,4},{7,5},{8,10},{9,11},{10,... | collective-permute-start | bytes 98312 | tf_op jit(solution)/shard_map/ppermute | solution.py:403
  71.1 2.1 %collective-permute-start.27 = (bf16[64,256]{1,0:T(8,128)(2,1)S(1)}, bf16[64,256]{1,0:T(8,128)(2,1)S(1)}, u32[]{:S(2)}, u32[]{:S(2)}) collective-permute-start(bf16[64,256]{1,0:T(8,128)(2,1)S(1)} %query.3.refs_0_), channel_id=1, source_target_pairs={{0,6},{1,7},{2,4},{3,5},{4,2},{5,3},{6,0},{7,1},{8,14},{9,15},{10,... | collective-permute-start | bytes 98312 | tf_op jit(solution)/shard_map/ppermute | solution.py:403
  74.1 1.4 %collective-permute-start.25 = (bf16[64,256]{1,0:T(8,128)(2,1)S(1)}, bf16[64,256]{1,0:T(8,128)(2,1)S(1)}, u32[]{:S(2)}, u32[]{:S(2)}) collective-permute-start(bf16[64,256]{1,0:T(8,128)(2,1)S(1)} %query.3.refs_0_), channel_id=1, source_target_pairs={{0,2},{1,3},{2,0},{3,1},{4,6},{5,7},{6,4},{7,5},{8,10},{9,11},{10,... | collective-permute-start | bytes 98312 | tf_op jit(solution)/shard_map/ppermute | solution.py:403
  78.5 1.7 %backward.3.begun_ref = f32[9,64,256]{2,1,0:T(8,128)S(1)} custom-call(s32[16,32]{1,0:T(8,128)S(1)} %get-tuple-element.32.table, bf16[64,256]{1,0:T(8,128)(2,1)S(1)} %query.3.refs_0_, bf16[64,256]{1,0:T(8,128)(2,1)S(1)} %collective-permute-done.25.refs_1_, bf16[64,256]{1,0:T(8,128)(2,1)S(1)} %collective-permute-done.26.refs_2_, ...), custom_call_target="tpu_custom_call" | custom-call | flops 134217728 | bytes 2097152 | tf_op jit(solution)/shard_map/backward/pallas_call | solution.py:546
  83.6 1.5 %collective-permute-start.31 = (f32[64,512]{1,0:T(8,128)S(1)}, f32[64,512]{1,0:T(8,128)S(1)}, u32[]{:S(2)}, u32[]{:S(2)}) collective-permute-start(f32[64,512]{1,0:T(8,128)S(1)} %get-tuple-element.56), channel_id=1, source_target_pairs={{0,8},{8,0},{16,24},{24,16},{1,9},{9,1},{17,25},{25,17},{2,10},{10... | collective-permute-start | bytes 393224 | tf_op jit(solution)/shard_map/ppermute | solution.py:403
  85.1 3.3 %collective-permute-done.29.refs_1_ = f32[64,512]{1,0:T(8,128)S(1)} collective-permute-done((f32[64,512]{1,0:T(8,128)S(1)}, f32[64,512]{1,0:T(8,128)S(1)}, u32[]{:S(2)}, u32[]{:S(2)}) %collective-permute-start.29) | collective-permute-done | bytes 131104 | tf_op jit(solution)/shard_map/ppermute | solution.py:403
  88.4 1.9 %collective-permute-done.30.refs_2_ = f32[64,512]{1,0:T(8,128)S(1)} collective-permute-done((f32[64,512]{1,0:T(8,128)S(1)}, f32[64,512]{1,0:T(8,128)S(1)}, u32[]{:S(2)}, u32[]{:S(2)}) %collective-permute-start.30) | collective-permute-done | bytes 131104 | tf_op jit(solution)/shard_map/ppermute | solution.py:403
  90.7 1.7 %collective-permute-start.34 = (f32[64,64]{1,0:T(8,128)S(1)}, f32[64,64]{1,0:T(8,128)S(1)}, u32[]{:S(2)}, u32[]{:S(2)}) collective-permute-start(f32[64,64]{1,0:T(8,128)S(1)} %get-tuple-element.57.refs_0_), channel_id=1, source_target_pairs={{0,24},{8,16},{16,8},{24,0},{1,25},{9,17},{17,9},{25,1},{2,26},{10... | collective-permute-start | bytes 49160 | tf_op jit(solution)/shard_map/ppermute | solution.py:403
  98.8 1.4 %collective-permute-start.38 = (f32[64,64]{1,0:T(8,128)S(1)}, f32[64,64]{1,0:T(8,128)S(1)}, u32[]{:S(2)}, u32[]{:S(2)}) collective-permute-start(f32[64,64]{1,0:T(8,128)S(1)} %sum.5.refs_0_), channel_id=1, source_target_pairs={{0,6},{1,7},{2,4},{3,5},{4,2},{5,3},{6,0},{7,1},{8,14},{9,15},{10,... | collective-permute-start | bytes 49160 | tf_op jit(solution)/shard_map/ppermute | solution.py:403
  101.5 1.7 %collective-permute-start.36 = (f32[64,64]{1,0:T(8,128)S(1)}, f32[64,64]{1,0:T(8,128)S(1)}, u32[]{:S(2)}, u32[]{:S(2)}) collective-permute-start(f32[64,64]{1,0:T(8,128)S(1)} %sum.5.refs_0_), channel_id=1, source_target_pairs={{0,2},{1,3},{2,0},{3,1},{4,6},{5,7},{6,4},{7,5},{8,10},{9,11},{10,... | collective-permute-start | bytes 49160 | tf_op jit(solution)/shard_map/ppermute | solution.py:403
  105.5 2.5 %finish.1 = f32[64,512]{1,0:T(8,128)} custom-call(f32[64,64]{1,0:T(8,128)S(1)} %sum.5.refs_0_, f32[64,64]{1,0:T(8,128)S(1)} %collective-permute-done.36.refs_1_, f32[64,64]{1,0:T(8,128)S(1)} %collective-permute-done.37.refs_2_, f32[64,64]{1,0:T(8,128)S(1)} %collective-permute-done.38.refs_3_, f32[64,512]{1,0:T(8,128)S(1)} %get-tuple-element.58.refs_4_), custom_call_target="tpu_custom_call" | custom-call | tf_op jit(solution)/shard_map/finish/pallas_call | solution.py:577
  (71 shorter events, 37.7 us)
Async XLA Ops:
  1.0 8.9 %collective-permute-start.2 = (bf16[64,512]{1,0:T(8,128)(2,1)S(1)}, bf16[64,512]{1,0:T(8,128)(2,1)S(1)}, u32[]{:S(2)}, u32[]{:S(2)}) collective-permute-start(bf16[64,512]{1,0:T(8,128)(2,1)S(1)} %start.1.after_ref.refs_0_), channel_id=1, source_target_pairs={{0,24},{8,16},{16,8},{24,0},{1,25},{9,17},{17,9},{25,1},{2,26},{10... | collective-permute-start | bytes 196616 | tf_op jit(solution)/shard_map/ppermute | solution.py:403
  4.9 4.9 %collective-permute-start.1 = (bf16[64,512]{1,0:T(8,128)(2,1)S(1)}, bf16[64,512]{1,0:T(8,128)(2,1)S(1)}, u32[]{:S(2)}, u32[]{:S(2)}) collective-permute-start(bf16[64,512]{1,0:T(8,128)(2,1)S(1)} %start.1.after_ref.refs_0_), channel_id=1, source_target_pairs={{0,16},{8,24},{16,0},{24,8},{1,17},{9,25},{17,1},{25,9},{2,18},{10... | collective-permute-start | bytes 196616 | tf_op jit(solution)/shard_map/ppermute | solution.py:403
  5.4 4.4 %collective-permute-start = (bf16[64,512]{1,0:T(8,128)(2,1)S(1)}, bf16[64,512]{1,0:T(8,128)(2,1)S(1)}, u32[]{:S(2)}, u32[]{:S(2)}) collective-permute-start(bf16[64,512]{1,0:T(8,128)(2,1)S(1)} %start.1.after_ref.refs_0_), channel_id=1, source_target_pairs={{0,8},{8,0},{16,24},{24,16},{1,9},{9,1},{17,25},{25,17},{2,10},{10... | collective-permute-start | bytes 196616 | tf_op jit(solution)/shard_map/ppermute | solution.py:403
  13.8 5.8 %collective-permute-start.4 = (bf16[64,256]{1,0:T(8,128)(2,1)S(1)}, bf16[64,256]{1,0:T(8,128)(2,1)S(1)}, u32[]{:S(2)}, u32[]{:S(2)}) collective-permute-start(bf16[64,256]{1,0:T(8,128)(2,1)S(1)} %get-tuple-element.37), channel_id=1, source_target_pairs={{0,6},{1,7},{2,4},{3,5},{4,2},{5,3},{6,0},{7,1},{8,14},{9,15},{10,... | collective-permute-start | bytes 98312 | tf_op jit(solution)/shard_map/ppermute | solution.py:403
  16.8 4.9 %collective-permute-start.5 = (bf16[64,256]{1,0:T(8,128)(2,1)S(1)}, bf16[64,256]{1,0:T(8,128)(2,1)S(1)}, u32[]{:S(2)}, u32[]{:S(2)}) collective-permute-start(bf16[64,256]{1,0:T(8,128)(2,1)S(1)} %get-tuple-element.38), channel_id=1, source_target_pairs={{0,4},{1,5},{2,6},{3,7},{4,0},{5,1},{6,2},{7,3},{8,12},{9,13},{10,... | collective-permute-start | bytes 98312 | tf_op jit(solution)/shard_map/ppermute | solution.py:403
  16.8 4.9 %collective-permute-start.6 = (bf16[64,256]{1,0:T(8,128)(2,1)S(1)}, bf16[64,256]{1,0:T(8,128)(2,1)S(1)}, u32[]{:S(2)}, u32[]{:S(2)}) collective-permute-start(bf16[64,256]{1,0:T(8,128)(2,1)S(1)} %get-tuple-element.39), channel_id=1, source_target_pairs={{0,2},{1,3},{2,0},{3,1},{4,6},{5,7},{6,4},{7,5},{8,10},{9,11},{10,... | collective-permute-start | bytes 98312 | tf_op jit(solution)/shard_map/ppermute | solution.py:403
  21.7 5.8 %collective-permute-start.9 = (bf16[64,256]{1,0:T(8,128)(2,1)S(1)}, bf16[64,256]{1,0:T(8,128)(2,1)S(1)}, u32[]{:S(2)}, u32[]{:S(2)}) collective-permute-start(bf16[64,256]{1,0:T(8,128)(2,1)S(1)} %query.2.refs_0_), channel_id=1, source_target_pairs={{0,6},{1,7},{2,4},{3,5},{4,2},{5,3},{6,0},{7,1},{8,14},{9,15},{10,... | collective-permute-start | bytes 98312 | tf_op jit(solution)/shard_map/ppermute | solution.py:403
  23.7 5.2 %collective-permute-start.8 = (bf16[64,256]{1,0:T(8,128)(2,1)S(1)}, bf16[64,256]{1,0:T(8,128)(2,1)S(1)}, u32[]{:S(2)}, u32[]{:S(2)}) collective-permute-start(bf16[64,256]{1,0:T(8,128)(2,1)S(1)} %query.2.refs_0_), channel_id=1, source_target_pairs={{0,4},{1,5},{2,6},{3,7},{4,0},{5,1},{6,2},{7,3},{8,12},{9,13},{10,... | collective-permute-start | bytes 98312 | tf_op jit(solution)/shard_map/ppermute | solution.py:403
  23.8 5.0 %collective-permute-start.7 = (bf16[64,256]{1,0:T(8,128)(2,1)S(1)}, bf16[64,256]{1,0:T(8,128)(2,1)S(1)}, u32[]{:S(2)}, u32[]{:S(2)}) collective-permute-start(bf16[64,256]{1,0:T(8,128)(2,1)S(1)} %query.2.refs_0_), channel_id=1, source_target_pairs={{0,2},{1,3},{2,0},{3,1},{4,6},{5,7},{6,4},{7,5},{8,10},{9,11},{10,... | collective-permute-start | bytes 98312 | tf_op jit(solution)/shard_map/ppermute | solution.py:403
  32.0 6.1 %collective-permute-start.11 = (f32[64,512]{1,0:T(8,128)S(1)}, f32[64,512]{1,0:T(8,128)S(1)}, u32[]{:S(2)}, u32[]{:S(2)}) collective-permute-start(f32[64,512]{1,0:T(8,128)S(1)} %get-tuple-element.42), channel_id=1, source_target_pairs={{0,24},{8,16},{16,8},{24,0},{1,25},{9,17},{17,9},{25,1},{2,26},{10... | collective-permute-start | bytes 393224 | tf_op jit(solution)/shard_map/ppermute | solution.py:403
  33.4 7.3 %collective-permute-start.12 = (f32[64,512]{1,0:T(8,128)S(1)}, f32[64,512]{1,0:T(8,128)S(1)}, u32[]{:S(2)}, u32[]{:S(2)}) collective-permute-start(f32[64,512]{1,0:T(8,128)S(1)} %get-tuple-element.43), channel_id=1, source_target_pairs={{0,16},{8,24},{16,0},{24,8},{1,17},{9,25},{17,1},{25,9},{2,18},{10... | collective-permute-start | bytes 393224 | tf_op jit(solution)/shard_map/ppermute | solution.py:403
  34.7 6.9 %collective-permute-start.13 = (f32[64,512]{1,0:T(8,128)S(1)}, f32[64,512]{1,0:T(8,128)S(1)}, u32[]{:S(2)}, u32[]{:S(2)}) collective-permute-start(f32[64,512]{1,0:T(8,128)S(1)} %get-tuple-element.44), channel_id=1, source_target_pairs={{0,8},{8,0},{16,24},{24,16},{1,9},{9,1},{17,25},{25,17},{2,10},{10... | collective-permute-start | bytes 393224 | tf_op jit(solution)/shard_map/ppermute | solution.py:403
  41.6 7.3 %collective-permute-start.16 = (f32[64,512]{1,0:T(8,128)S(1)}, f32[64,512]{1,0:T(8,128)S(1)}, u32[]{:S(2)}, u32[]{:S(2)}) collective-permute-start(f32[64,512]{1,0:T(8,128)S(1)} %lift.2.refs_0_), channel_id=1, source_target_pairs={{0,24},{8,16},{16,8},{24,0},{1,25},{9,17},{17,9},{25,1},{2,26},{10... | collective-permute-start | bytes 393224 | tf_op jit(solution)/shard_map/ppermute | solution.py:403
  43.1 7.6 %collective-permute-start.15 = (f32[64,512]{1,0:T(8,128)S(1)}, f32[64,512]{1,0:T(8,128)S(1)}, u32[]{:S(2)}, u32[]{:S(2)}) collective-permute-start(f32[64,512]{1,0:T(8,128)S(1)} %lift.2.refs_0_), channel_id=1, source_target_pairs={{0,16},{8,24},{16,0},{24,8},{1,17},{9,25},{17,1},{25,9},{2,18},{10... | collective-permute-start | bytes 393224 | tf_op jit(solution)/shard_map/ppermute | solution.py:403
  44.4 6.4 %collective-permute-start.14 = (f32[64,512]{1,0:T(8,128)S(1)}, f32[64,512]{1,0:T(8,128)S(1)}, u32[]{:S(2)}, u32[]{:S(2)}) collective-permute-start(f32[64,512]{1,0:T(8,128)S(1)} %lift.2.refs_0_), channel_id=1, source_target_pairs={{0,8},{8,0},{16,24},{24,16},{1,9},{9,1},{17,25},{25,17},{2,10},{10... | collective-permute-start | bytes 393224 | tf_op jit(solution)/shard_map/ppermute | solution.py:403
  52.6 7.2 %collective-permute-start.20 = (f32[64,64]{1,0:T(8,128)S(1)}, f32[64,64]{1,0:T(8,128)S(1)}, u32[]{:S(2)}, u32[]{:S(2)}) collective-permute-start(f32[64,64]{1,0:T(8,128)S(1)} %sum.3.refs_0_), channel_id=1, source_target_pairs={{0,6},{1,7},{2,4},{3,5},{4,2},{5,3},{6,0},{7,1},{8,14},{9,15},{10,... | collective-permute-start | bytes 49160 | tf_op jit(solution)/shard_map/ppermute | solution.py:403
  54.7 5.2 %collective-permute-start.19 = (f32[64,64]{1,0:T(8,128)S(1)}, f32[64,64]{1,0:T(8,128)S(1)}, u32[]{:S(2)}, u32[]{:S(2)}) collective-permute-start(f32[64,64]{1,0:T(8,128)S(1)} %sum.3.refs_0_), channel_id=1, source_target_pairs={{0,4},{1,5},{2,6},{3,7},{4,0},{5,1},{6,2},{7,3},{8,12},{9,13},{10,... | collective-permute-start | bytes 49160 | tf_op jit(solution)/shard_map/ppermute | solution.py:403
  55.5 4.4 %collective-permute-start.18 = (f32[64,64]{1,0:T(8,128)S(1)}, f32[64,64]{1,0:T(8,128)S(1)}, u32[]{:S(2)}, u32[]{:S(2)}) collective-permute-start(f32[64,64]{1,0:T(8,128)S(1)} %sum.3.refs_0_), channel_id=1, source_target_pairs={{0,2},{1,3},{2,0},{3,1},{4,6},{5,7},{6,4},{7,5},{8,10},{9,11},{10,... | collective-permute-start | bytes 49160 | tf_op jit(solution)/shard_map/ppermute | solution.py:403
  64.2 5.8 %collective-permute-start.22 = (bf16[64,256]{1,0:T(8,128)(2,1)S(1)}, bf16[64,256]{1,0:T(8,128)(2,1)S(1)}, u32[]{:S(2)}, u32[]{:S(2)}) collective-permute-start(bf16[64,256]{1,0:T(8,128)(2,1)S(1)} %get-tuple-element.50), channel_id=1, source_target_pairs={{0,6},{1,7},{2,4},{3,5},{4,2},{5,3},{6,0},{7,1},{8,14},{9,15},{10,... | collective-permute-start | bytes 98312 | tf_op jit(solution)/shard_map/ppermute | solution.py:403
  66.1 5.0 %collective-permute-start.23 = (bf16[64,256]{1,0:T(8,128)(2,1)S(1)}, bf16[64,256]{1,0:T(8,128)(2,1)S(1)}, u32[]{:S(2)}, u32[]{:S(2)}) collective-permute-start(bf16[64,256]{1,0:T(8,128)(2,1)S(1)} %get-tuple-element.51), channel_id=1, source_target_pairs={{0,4},{1,5},{2,6},{3,7},{4,0},{5,1},{6,2},{7,3},{8,12},{9,13},{10,... | collective-permute-start | bytes 98312 | tf_op jit(solution)/shard_map/ppermute | solution.py:403
  66.7 4.3 %collective-permute-start.24 = (bf16[64,256]{1,0:T(8,128)(2,1)S(1)}, bf16[64,256]{1,0:T(8,128)(2,1)S(1)}, u32[]{:S(2)}, u32[]{:S(2)}) collective-permute-start(bf16[64,256]{1,0:T(8,128)(2,1)S(1)} %get-tuple-element.52), channel_id=1, source_target_pairs={{0,2},{1,3},{2,0},{3,1},{4,6},{5,7},{6,4},{7,5},{8,10},{9,11},{10,... | collective-permute-start | bytes 98312 | tf_op jit(solution)/shard_map/ppermute | solution.py:403
  71.1 5.8 %collective-permute-start.27 = (bf16[64,256]{1,0:T(8,128)(2,1)S(1)}, bf16[64,256]{1,0:T(8,128)(2,1)S(1)}, u32[]{:S(2)}, u32[]{:S(2)}) collective-permute-start(bf16[64,256]{1,0:T(8,128)(2,1)S(1)} %query.3.refs_0_), channel_id=1, source_target_pairs={{0,6},{1,7},{2,4},{3,5},{4,2},{5,3},{6,0},{7,1},{8,14},{9,15},{10,... | collective-permute-start | bytes 98312 | tf_op jit(solution)/shard_map/ppermute | solution.py:403
  73.2 5.1 %collective-permute-start.26 = (bf16[64,256]{1,0:T(8,128)(2,1)S(1)}, bf16[64,256]{1,0:T(8,128)(2,1)S(1)}, u32[]{:S(2)}, u32[]{:S(2)}) collective-permute-start(bf16[64,256]{1,0:T(8,128)(2,1)S(1)} %query.3.refs_0_), channel_id=1, source_target_pairs={{0,4},{1,5},{2,6},{3,7},{4,0},{5,1},{6,2},{7,3},{8,12},{9,13},{10,... | collective-permute-start | bytes 98312 | tf_op jit(solution)/shard_map/ppermute | solution.py:403
  74.1 4.3 %collective-permute-start.25 = (bf16[64,256]{1,0:T(8,128)(2,1)S(1)}, bf16[64,256]{1,0:T(8,128)(2,1)S(1)}, u32[]{:S(2)}, u32[]{:S(2)}) collective-permute-start(bf16[64,256]{1,0:T(8,128)(2,1)S(1)} %query.3.refs_0_), channel_id=1, source_target_pairs={{0,2},{1,3},{2,0},{3,1},{4,6},{5,7},{6,4},{7,5},{8,10},{9,11},{10,... | collective-permute-start | bytes 98312 | tf_op jit(solution)/shard_map/ppermute | solution.py:403
  81.5 6.9 %collective-permute-start.29 = (f32[64,512]{1,0:T(8,128)S(1)}, f32[64,512]{1,0:T(8,128)S(1)}, u32[]{:S(2)}, u32[]{:S(2)}) collective-permute-start(f32[64,512]{1,0:T(8,128)S(1)} %get-tuple-element.54), channel_id=1, source_target_pairs={{0,24},{8,16},{16,8},{24,0},{1,25},{9,17},{17,9},{25,1},{2,26},{10... | collective-permute-start | bytes 393224 | tf_op jit(solution)/shard_map/ppermute | solution.py:403
  82.3 8.0 %collective-permute-start.30 = (f32[64,512]{1,0:T(8,128)S(1)}, f32[64,512]{1,0:T(8,128)S(1)}, u32[]{:S(2)}, u32[]{:S(2)}) collective-permute-start(f32[64,512]{1,0:T(8,128)S(1)} %get-tuple-element.55), channel_id=1, source_target_pairs={{0,16},{8,24},{16,0},{24,8},{1,17},{9,25},{17,1},{25,9},{2,18},{10... | collective-permute-start | bytes 393224 | tf_op jit(solution)/shard_map/ppermute | solution.py:403
  83.6 6.7 %collective-permute-start.31 = (f32[64,512]{1,0:T(8,128)S(1)}, f32[64,512]{1,0:T(8,128)S(1)}, u32[]{:S(2)}, u32[]{:S(2)}) collective-permute-start(f32[64,512]{1,0:T(8,128)S(1)} %get-tuple-element.56), channel_id=1, source_target_pairs={{0,8},{8,0},{16,24},{24,16},{1,9},{9,1},{17,25},{25,17},{2,10},{10... | collective-permute-start | bytes 393224 | tf_op jit(solution)/shard_map/ppermute | solution.py:403
  90.7 4.9 %collective-permute-start.34 = (f32[64,64]{1,0:T(8,128)S(1)}, f32[64,64]{1,0:T(8,128)S(1)}, u32[]{:S(2)}, u32[]{:S(2)}) collective-permute-start(f32[64,64]{1,0:T(8,128)S(1)} %get-tuple-element.57.refs_0_), channel_id=1, source_target_pairs={{0,24},{8,16},{16,8},{24,0},{1,25},{9,17},{17,9},{25,1},{2,26},{10... | collective-permute-start | bytes 49160 | tf_op jit(solution)/shard_map/ppermute | solution.py:403
  92.4 3.9 %collective-permute-start.33 = (f32[64,64]{1,0:T(8,128)S(1)}, f32[64,64]{1,0:T(8,128)S(1)}, u32[]{:S(2)}, u32[]{:S(2)}) collective-permute-start(f32[64,64]{1,0:T(8,128)S(1)} %get-tuple-element.57.refs_0_), channel_id=1, source_target_pairs={{0,16},{8,24},{16,0},{24,8},{1,17},{9,25},{17,1},{25,9},{2,18},{10... | collective-permute-start | bytes 49160 | tf_op jit(solution)/shard_map/ppermute | solution.py:403
  98.8 5.8 %collective-permute-start.38 = (f32[64,64]{1,0:T(8,128)S(1)}, f32[64,64]{1,0:T(8,128)S(1)}, u32[]{:S(2)}, u32[]{:S(2)}) collective-permute-start(f32[64,64]{1,0:T(8,128)S(1)} %sum.5.refs_0_), channel_id=1, source_target_pairs={{0,6},{1,7},{2,4},{3,5},{4,2},{5,3},{6,0},{7,1},{8,14},{9,15},{10,... | collective-permute-start | bytes 49160 | tf_op jit(solution)/shard_map/ppermute | solution.py:403
  100.2 5.1 %collective-permute-start.37 = (f32[64,64]{1,0:T(8,128)S(1)}, f32[64,64]{1,0:T(8,128)S(1)}, u32[]{:S(2)}, u32[]{:S(2)}) collective-permute-start(f32[64,64]{1,0:T(8,128)S(1)} %sum.5.refs_0_), channel_id=1, source_target_pairs={{0,4},{1,5},{2,6},{3,7},{4,0},{5,1},{6,2},{7,3},{8,12},{9,13},{10,... | collective-permute-start | bytes 49160 | tf_op jit(solution)/shard_map/ppermute | solution.py:403
  101.5 4.0 %collective-permute-start.36 = (f32[64,64]{1,0:T(8,128)S(1)}, f32[64,64]{1,0:T(8,128)S(1)}, u32[]{:S(2)}, u32[]{:S(2)}) collective-permute-start(f32[64,64]{1,0:T(8,128)S(1)} %sum.5.refs_0_), channel_id=1, source_target_pairs={{0,2},{1,3},{2,0},{3,1},{4,6},{5,7},{6,4},{7,5},{8,10},{9,11},{10,... | collective-permute-start | bytes 49160 | tf_op jit(solution)/shard_map/ppermute | solution.py:403
  (7 other events, 13.7 us)

commit v3 on v2

--- a/solution.py
+++ b/solution.py
@@ -119,11 +119,11 @@
 
 def products(which, take, give, dims, table, held, tile_ref, total):
     width = total.shape[1]
-    count = table[SINGLES, which]
-
-    def step(g, carry):
-        for lane in range(GROUP):
-            at = g * GROUP + lane
+    slots = tile_ref.shape[0]
+
+    def run(first, length):
+        for lane in range(length):
+            at = first + lane
             term = lax.dot_general(
                 held[table[which * FIELDS + take, at]],
                 tile_ref[table[which * FIELDS + SLOT, at]],
@@ -133,10 +133,18 @@
             if term.shape[0] > width:
                 term = term[:width] + term[width:]
             total[table[which * FIELDS + give, at]] += term
+
+    if isinstance(which, int):
+        run(0, slots)
+        return
+
+    def step(g, carry):
+        run(slots // 2 + g * GROUP, GROUP)
         return carry
 
-    last = tile_ref.shape[0] // GROUP
-    lax.fori_loop(0, jnp.minimum((count + GROUP - 1) // GROUP, last), step, 0)
+    run(0, slots // 2)
+    rest = jnp.maximum(table[SINGLES, which] - slots // 2, 0)
+    lax.fori_loop(0, jnp.minimum((rest + GROUP - 1) // GROUP, slots // 2 // GROUP), step, 0)
 
 
 forward = functools.partial(products, take=PRODUCT_TAKE, give=QUERY_GIVE, dims=NT)

time: 109 us -> 108 us (level)
  Pallas kernels: 24.4 us -> 22.7 us
  waiting for transfers between devices: 36.8 us -> 38.4 us
    ppermute x39, waiting for transfers between devices: 36.8 us -> 38.4 us  [swap(): lax.ppermute(value, axis, [(i, i ^ step) for i in range(lax.axis_size(axi...]
  transfers between devices with their start and end apart: 39 -> 39, of which waited for: 27 -> 27; matrix products, arithmetic and copies ran while one was open for 0% -> 0% of each run, Pallas kernels for 12% -> 11%
where the time goes in v3:
time: 108 us
  starting transfers between devices  45.8 us (42%)
  waiting for transfers between devices  38.4 us (36%)
  Pallas kernels  22.7 us (21%)
    ppermute x39, starting transfers between devices, swap(): lax.ppermute(value, axis, [(i, i ^ step) for i in range(lax.axis_size(axi...  45.8 us
    ppermute x39, waiting for transfers between devices, swap(): lax.ppermute(value, axis, [(i, i ^ step) for i in range(lax.axis_size(axi...  38.4 us
    pallas_call x1, Pallas kernels, shards(): call(functools.partial(load_body, max(columns // side, 1)), 'load', [SCAL...  3.53 us
    pallas_call x2, Pallas kernels, shards(): call(functools.partial(back_mine_body, chips), 'backward', [SCALARS] + [W...  2.97 us
    pallas_call x1, Pallas kernels, shards(): call(functools.partial(apply_other_body, chips), 'apply', [SCALARS] + [WH...  2.63 us
    pallas_call x1, Pallas kernels, shards(): call(functools.partial(finish_body, root_count), 'finish', [WHOLE] * (chi...  2.53 us
    pallas_call x2, Pallas kernels, shards(): call(back_other_body, 'backward_rest', [SCALARS] + [WHOLE] * 3, [f32(widt...  2.47 us
    pallas_call x1, Pallas kernels, shards(): call(functools.partial(next_body, n_row), 'forward', [SCALARS] + [WHOLE]...  2.26 us
  transfers between devices with their start and end apart: 39, of which 27 were waited for; matrix products, arithmetic and copies ran while one was open for 0% of the time, Pallas kernels for 11%

profile of v3, /device:TPU:0, one launch (start us, length us, event | category | flops | bytes accessed | tf_op | source)
XLA Modules:
  0.0 107.9 jit_solution(26335450227686034)
XLA Ops:
  1.0 4.0 %collective-permute-start.2 = (bf16[64,512]{1,0:T(8,128)(2,1)S(1)}, bf16[64,512]{1,0:T(8,128)(2,1)S(1)}, u32[]{:S(2)}, u32[]{:S(2)}) collective-permute-start(bf16[64,512]{1,0:T(8,128)(2,1)S(1)} %start.1.after_ref.refs_0_), channel_id=1, source_target_pairs={{0,24},{8,16},{16,8},{24,0},{1,25},{9,17},{17,9},{25,1},{2,26},{10... | collective-permute-start | bytes 196616 | tf_op jit(solution)/shard_map/ppermute | solution.py:411
  6.3 3.5 %load.1 = (bf16[32,256,256]{2,1,0:T(8,128)(2,1)S(1)}, f32[1,512]{1,0:T(1,128)S(1)}, f32[1,2048]{1,0:T(1,128)S(1)}, f32[1,256]{1,0:T(1,128)S(1)}, s32[16,32]{1,0:T(8,128)S(1)}) custom-call(s32[3]{0:T(128)S(1)} %pad_add_fusion.place, bf16[64,512]{1,0:T(8,128)(2,1)S(1)} %start.1.after_ref.refs_0_, bf16[32,256,256]{2,1,0:T(8,128)(2,1)} %bitcast.8, ...), custom_call_target="tpu_custom_call" | custom-call | bytes 8388608 | tf_op jit(solution)/shard_map/load/pallas_call | solution.py:456
  11.4 1.9 %forward_rest.1.mine_ref = f32[4,64,256]{2,1,0:T(8,128)S(1)} custom-call(s32[16,32]{1,0:T(8,128)S(1)} %get-tuple-element.32.table, bf16[8,64,256]{2,1,0:T(8,128)(2,1)S(1)} %get-tuple-element.34.held, bf16[32,256,256]{2,1,0:T(8,128)(2,1)S(1)} %get-tuple-element.33.refs_4_.tile_ref.refs_5_), custom_call_target="tpu_custom_call" | custom-call | flops 134217728 | bytes 2097152 | tf_op jit(solution)/shard_map/forward_rest/pallas_call | solution.py:527
  13.3 3.7 %collective-permute-start.4 = (bf16[64,256]{1,0:T(8,128)(2,1)S(1)}, bf16[64,256]{1,0:T(8,128)(2,1)S(1)}, u32[]{:S(2)}, u32[]{:S(2)}) collective-permute-start(bf16[64,256]{1,0:T(8,128)(2,1)S(1)} %get-tuple-element.37), channel_id=1, source_target_pairs={{0,6},{1,7},{2,4},{3,5},{4,2},{5,3},{6,0},{7,1},{8,14},{9,15},{10,... | collective-permute-start | bytes 98312 | tf_op jit(solution)/shard_map/ppermute | solution.py:411
  19.2 2.7 %collective-permute-done.5.refs_2_ = bf16[64,256]{1,0:T(8,128)(2,1)S(1)} collective-permute-done((bf16[64,256]{1,0:T(8,128)(2,1)S(1)}, bf16[64,256]{1,0:T(8,128)(2,1)S(1)}, u32[]{:S(2)}, u32[]{:S(2)}) %collective-permute-start.5) | collective-permute-done | bytes 32800 | tf_op jit(solution)/shard_map/ppermute | solution.py:411
  21.8 1.7 %collective-permute-start.9 = (bf16[64,256]{1,0:T(8,128)(2,1)S(1)}, bf16[64,256]{1,0:T(8,128)(2,1)S(1)}, u32[]{:S(2)}, u32[]{:S(2)}) collective-permute-start(bf16[64,256]{1,0:T(8,128)(2,1)S(1)} %query.2.refs_0_), channel_id=1, source_target_pairs={{0,6},{1,7},{2,4},{3,5},{4,2},{5,3},{6,0},{7,1},{8,14},{9,15},{10,... | collective-permute-start | bytes 98312 | tf_op jit(solution)/shard_map/ppermute | solution.py:411
  24.0 2.3 %collective-permute-start.7 = (bf16[64,256]{1,0:T(8,128)(2,1)S(1)}, bf16[64,256]{1,0:T(8,128)(2,1)S(1)}, u32[]{:S(2)}, u32[]{:S(2)}) collective-permute-start(bf16[64,256]{1,0:T(8,128)(2,1)S(1)} %query.2.refs_0_), channel_id=1, source_target_pairs={{0,2},{1,3},{2,0},{3,1},{4,6},{5,7},{6,4},{7,5},{8,10},{9,11},{10,... | collective-permute-start | bytes 98312 | tf_op jit(solution)/shard_map/ppermute | solution.py:411
  26.3 1.4 %collective-permute-done.9.refs_3_ = bf16[64,256]{1,0:T(8,128)(2,1)S(1)} collective-permute-done((bf16[64,256]{1,0:T(8,128)(2,1)S(1)}, bf16[64,256]{1,0:T(8,128)(2,1)S(1)}, u32[]{:S(2)}, u32[]{:S(2)}) %collective-permute-start.9) | collective-permute-done | bytes 32800 | tf_op jit(solution)/shard_map/ppermute | solution.py:411
  28.6 1.5 %backward.2.begun_ref = f32[9,64,256]{2,1,0:T(8,128)S(1)} custom-call(s32[16,32]{1,0:T(8,128)S(1)} %get-tuple-element.32.table, bf16[64,256]{1,0:T(8,128)(2,1)S(1)} %query.2.refs_0_, bf16[64,256]{1,0:T(8,128)(2,1)S(1)} %collective-permute-done.7.refs_1_, bf16[64,256]{1,0:T(8,128)(2,1)S(1)} %collective-permute-done.8.refs_2_, ...), custom_call_target="tpu_custom_call" | custom-call | flops 134217728 | bytes 2097152 | tf_op jit(solution)/shard_map/backward/pallas_call | solution.py:554
  31.4 2.8 %collective-permute-start.11 = (f32[64,512]{1,0:T(8,128)S(1)}, f32[64,512]{1,0:T(8,128)S(1)}, u32[]{:S(2)}, u32[]{:S(2)}) collective-permute-start(f32[64,512]{1,0:T(8,128)S(1)} %get-tuple-element.42), channel_id=1, source_target_pairs={{0,24},{8,16},{16,8},{24,0},{1,25},{9,17},{17,9},{25,1},{2,26},{10... | collective-permute-start | bytes 393224 | tf_op jit(solution)/shard_map/ppermute | solution.py:411
  34.9 3.7 %collective-permute-done.11.refs_1_ = f32[64,512]{1,0:T(8,128)S(1)} collective-permute-done((f32[64,512]{1,0:T(8,128)S(1)}, f32[64,512]{1,0:T(8,128)S(1)}, u32[]{:S(2)}, u32[]{:S(2)}) %collective-permute-start.11) | collective-permute-done | bytes 131104 | tf_op jit(solution)/shard_map/ppermute | solution.py:411
  38.6 2.7 %collective-permute-done.12.refs_2_ = f32[64,512]{1,0:T(8,128)S(1)} collective-permute-done((f32[64,512]{1,0:T(8,128)S(1)}, f32[64,512]{1,0:T(8,128)S(1)}, u32[]{:S(2)}, u32[]{:S(2)}) %collective-permute-start.12) | collective-permute-done | bytes 131104 | tf_op jit(solution)/shard_map/ppermute | solution.py:411
  41.4 1.9 %collective-permute-start.16 = (f32[64,512]{1,0:T(8,128)S(1)}, f32[64,512]{1,0:T(8,128)S(1)}, u32[]{:S(2)}, u32[]{:S(2)}) collective-permute-start(f32[64,512]{1,0:T(8,128)S(1)} %lift.2.refs_0_), channel_id=1, source_target_pairs={{0,24},{8,16},{16,8},{24,0},{1,25},{9,17},{17,9},{25,1},{2,26},{10... | collective-permute-start | bytes 393224 | tf_op jit(solution)/shard_map/ppermute | solution.py:411
  43.2 1.4 %collective-permute-start.15 = (f32[64,512]{1,0:T(8,128)S(1)}, f32[64,512]{1,0:T(8,128)S(1)}, u32[]{:S(2)}, u32[]{:S(2)}) collective-permute-start(f32[64,512]{1,0:T(8,128)S(1)} %lift.2.refs_0_), channel_id=1, source_target_pairs={{0,16},{8,24},{16,0},{24,8},{1,17},{9,25},{17,1},{25,9},{2,18},{10... | collective-permute-start | bytes 393224 | tf_op jit(solution)/shard_map/ppermute | solution.py:411
  44.9 3.8 %collective-permute-done.16.refs_3_ = f32[64,512]{1,0:T(8,128)S(1)} collective-permute-done((f32[64,512]{1,0:T(8,128)S(1)}, f32[64,512]{1,0:T(8,128)S(1)}, u32[]{:S(2)}, u32[]{:S(2)}) %collective-permute-start.16) | collective-permute-done | bytes 131104 | tf_op jit(solution)/shard_map/ppermute | solution.py:411
  48.7 1.9 %collective-permute-done.15.refs_2_ = f32[64,512]{1,0:T(8,128)S(1)} collective-permute-done((f32[64,512]{1,0:T(8,128)S(1)}, f32[64,512]{1,0:T(8,128)S(1)}, u32[]{:S(2)}, u32[]{:S(2)}) %collective-permute-start.15) | collective-permute-done | bytes 131104 | tf_op jit(solution)/shard_map/ppermute | solution.py:411
  52.4 1.8 %collective-permute-start.20 = (f32[64,64]{1,0:T(8,128)S(1)}, f32[64,64]{1,0:T(8,128)S(1)}, u32[]{:S(2)}, u32[]{:S(2)}) collective-permute-start(f32[64,64]{1,0:T(8,128)S(1)} %sum.3.refs_0_), channel_id=1, source_target_pairs={{0,6},{1,7},{2,4},{3,5},{4,2},{5,3},{6,0},{7,1},{8,14},{9,15},{10,... | collective-permute-start | bytes 49160 | tf_op jit(solution)/shard_map/ppermute | solution.py:411
  55.2 1.6 %collective-permute-start.18 = (f32[64,64]{1,0:T(8,128)S(1)}, f32[64,64]{1,0:T(8,128)S(1)}, u32[]{:S(2)}, u32[]{:S(2)}) collective-permute-start(f32[64,64]{1,0:T(8,128)S(1)} %sum.3.refs_0_), channel_id=1, source_target_pairs={{0,2},{1,3},{2,0},{3,1},{4,6},{5,7},{6,4},{7,5},{8,10},{9,11},{10,... | collective-permute-start | bytes 49160 | tf_op jit(solution)/shard_map/ppermute | solution.py:411
  56.8 2.3 %forward.3.refs_4_.total_ref = f32[8,64,256]{2,1,0:T(8,128)S(1)} custom-call(s32[16,32]{1,0:T(8,128)S(1)} %get-tuple-element.32.table, f32[64,512]{1,0:T(8,128)S(1)} %lift.2.refs_0_, f32[64,512]{1,0:T(8,128)S(1)} %collective-permute-done.14.refs_1_, f32[64,512]{1,0:T(8,128)S(1)} %collective-permute-done.15.refs_2_, ...), custom_call_target="tpu_custom_call" | custom-call | flops 268435456 | bytes 4194304 | tf_op jit(solution)/shard_map/forward/pallas_call | solution.py:495
  59.6 2.6 %apply.1 = (f32[64,64]{1,0:T(8,128)S(1)}, f32[4,64,256]{2,1,0:T(8,128)S(1)}) custom-call(s32[16,32]{1,0:T(8,128)S(1)} %get-tuple-element.32.table, f32[64,64]{1,0:T(8,128)S(1)} %sum.3.refs_0_, f32[64,64]{1,0:T(8,128)S(1)} %collective-permute-done.18.refs_1_, f32[64,64]{1,0:T(8,128)S(1)} %collective-permute-done.19.refs_2_, ...), custom_call_target="tpu_custom_call" | custom-call | tf_op jit(solution)/shard_map/apply/pallas_call | solution.py:507
  63.8 1.8 %collective-permute-start.22 = (bf16[64,256]{1,0:T(8,128)(2,1)S(1)}, bf16[64,256]{1,0:T(8,128)(2,1)S(1)}, u32[]{:S(2)}, u32[]{:S(2)}) collective-permute-start(bf16[64,256]{1,0:T(8,128)(2,1)S(1)} %get-tuple-element.50), channel_id=1, source_target_pairs={{0,6},{1,7},{2,4},{3,5},{4,2},{5,3},{6,0},{7,1},{8,14},{9,15},{10,... | collective-permute-start | bytes 98312 | tf_op jit(solution)/shard_map/ppermute | solution.py:411
  66.5 1.8 %collective-permute-start.24 = (bf16[64,256]{1,0:T(8,128)(2,1)S(1)}, bf16[64,256]{1,0:T(8,128)(2,1)S(1)}, u32[]{:S(2)}, u32[]{:S(2)}) collective-permute-start(bf16[64,256]{1,0:T(8,128)(2,1)S(1)} %get-tuple-element.52), channel_id=1, source_target_pairs={{0,2},{1,3},{2,0},{3,1},{4,6},{5,7},{6,4},{7,5},{8,10},{9,11},{10,... | collective-permute-start | bytes 98312 | tf_op jit(solution)/shard_map/ppermute | solution.py:411
  70.8 1.9 %collective-permute-start.27 = (bf16[64,256]{1,0:T(8,128)(2,1)S(1)}, bf16[64,256]{1,0:T(8,128)(2,1)S(1)}, u32[]{:S(2)}, u32[]{:S(2)}) collective-permute-start(bf16[64,256]{1,0:T(8,128)(2,1)S(1)} %query.3.refs_0_), channel_id=1, source_target_pairs={{0,6},{1,7},{2,4},{3,5},{4,2},{5,3},{6,0},{7,1},{8,14},{9,15},{10,... | collective-permute-start | bytes 98312 | tf_op jit(solution)/shard_map/ppermute | solution.py:411
  73.8 1.5 %collective-permute-start.25 = (bf16[64,256]{1,0:T(8,128)(2,1)S(1)}, bf16[64,256]{1,0:T(8,128)(2,1)S(1)}, u32[]{:S(2)}, u32[]{:S(2)}) collective-permute-start(bf16[64,256]{1,0:T(8,128)(2,1)S(1)} %query.3.refs_0_), channel_id=1, source_target_pairs={{0,2},{1,3},{2,0},{3,1},{4,6},{5,7},{6,4},{7,5},{8,10},{9,11},{10,... | collective-permute-start | bytes 98312 | tf_op jit(solution)/shard_map/ppermute | solution.py:411
  75.3 1.6 %collective-permute-done.27.refs_3_ = bf16[64,256]{1,0:T(8,128)(2,1)S(1)} collective-permute-done((bf16[64,256]{1,0:T(8,128)(2,1)S(1)}, bf16[64,256]{1,0:T(8,128)(2,1)S(1)}, u32[]{:S(2)}, u32[]{:S(2)}) %collective-permute-start.27) | collective-permute-done | bytes 32800 | tf_op jit(solution)/shard_map/ppermute | solution.py:411
  78.1 1.5 %backward.3.begun_ref = f32[9,64,256]{2,1,0:T(8,128)S(1)} custom-call(s32[16,32]{1,0:T(8,128)S(1)} %get-tuple-element.32.table, bf16[64,256]{1,0:T(8,128)(2,1)S(1)} %query.3.refs_0_, bf16[64,256]{1,0:T(8,128)(2,1)S(1)} %collective-permute-done.25.refs_1_, bf16[64,256]{1,0:T(8,128)(2,1)S(1)} %collective-permute-done.26.refs_2_, ...), custom_call_target="tpu_custom_call" | custom-call | flops 134217728 | bytes 2097152 | tf_op jit(solution)/shard_map/backward/pallas_call | solution.py:554
  84.4 3.7 %collective-permute-done.29.refs_1_ = f32[64,512]{1,0:T(8,128)S(1)} collective-permute-done((f32[64,512]{1,0:T(8,128)S(1)}, f32[64,512]{1,0:T(8,128)S(1)}, u32[]{:S(2)}, u32[]{:S(2)}) %collective-permute-start.29) | collective-permute-done | bytes 131104 | tf_op jit(solution)/shard_map/ppermute | solution.py:411
  88.2 2.1 %collective-permute-done.30.refs_2_ = f32[64,512]{1,0:T(8,128)S(1)} collective-permute-done((f32[64,512]{1,0:T(8,128)S(1)}, f32[64,512]{1,0:T(8,128)S(1)}, u32[]{:S(2)}, u32[]{:S(2)}) %collective-permute-start.30) | collective-permute-done | bytes 131104 | tf_op jit(solution)/shard_map/ppermute | solution.py:411
  90.5 1.8 %collective-permute-start.34 = (f32[64,64]{1,0:T(8,128)S(1)}, f32[64,64]{1,0:T(8,128)S(1)}, u32[]{:S(2)}, u32[]{:S(2)}) collective-permute-start(f32[64,64]{1,0:T(8,128)S(1)} %get-tuple-element.57.refs_0_), channel_id=1, source_target_pairs={{0,24},{8,16},{16,8},{24,0},{1,25},{9,17},{17,9},{25,1},{2,26},{10... | collective-permute-start | bytes 49160 | tf_op jit(solution)/shard_map/ppermute | solution.py:411
  98.6 1.8 %collective-permute-start.38 = (f32[64,64]{1,0:T(8,128)S(1)}, f32[64,64]{1,0:T(8,128)S(1)}, u32[]{:S(2)}, u32[]{:S(2)}) collective-permute-start(f32[64,64]{1,0:T(8,128)S(1)} %sum.5.refs_0_), channel_id=1, source_target_pairs={{0,6},{1,7},{2,4},{3,5},{4,2},{5,3},{6,0},{7,1},{8,14},{9,15},{10,... | collective-permute-start | bytes 49160 | tf_op jit(solution)/shard_map/ppermute | solution.py:411
  101.1 1.8 %collective-permute-start.36 = (f32[64,64]{1,0:T(8,128)S(1)}, f32[64,64]{1,0:T(8,128)S(1)}, u32[]{:S(2)}, u32[]{:S(2)}) collective-permute-start(f32[64,64]{1,0:T(8,128)S(1)} %sum.5.refs_0_), channel_id=1, source_target_pairs={{0,2},{1,3},{2,0},{3,1},{4,6},{5,7},{6,4},{7,5},{8,10},{9,11},{10,... | collective-permute-start | bytes 49160 | tf_op jit(solution)/shard_map/ppermute | solution.py:411
  105.4 2.5 %finish.1 = f32[64,512]{1,0:T(8,128)} custom-call(f32[64,64]{1,0:T(8,128)S(1)} %sum.5.refs_0_, f32[64,64]{1,0:T(8,128)S(1)} %collective-permute-done.36.refs_1_, f32[64,64]{1,0:T(8,128)S(1)} %collective-permute-done.37.refs_2_, f32[64,64]{1,0:T(8,128)S(1)} %collective-permute-done.38.refs_3_, f32[64,512]{1,0:T(8,128)S(1)} %get-tuple-element.58.refs_4_), custom_call_target="tpu_custom_call" | custom-call | tf_op jit(solution)/shard_map/finish/pallas_call | solution.py:585
  (71 shorter events, 34.1 us)
Async XLA Ops:
  1.0 8.9 %collective-permute-start.2 = (bf16[64,512]{1,0:T(8,128)(2,1)S(1)}, bf16[64,512]{1,0:T(8,128)(2,1)S(1)}, u32[]{:S(2)}, u32[]{:S(2)}) collective-permute-start(bf16[64,512]{1,0:T(8,128)(2,1)S(1)} %start.1.after_ref.refs_0_), channel_id=1, source_target_pairs={{0,24},{8,16},{16,8},{24,0},{1,25},{9,17},{17,9},{25,1},{2,26},{10... | collective-permute-start | bytes 196616 | tf_op jit(solution)/shard_map/ppermute | solution.py:411
  4.9 4.9 %collective-permute-start.1 = (bf16[64,512]{1,0:T(8,128)(2,1)S(1)}, bf16[64,512]{1,0:T(8,128)(2,1)S(1)}, u32[]{:S(2)}, u32[]{:S(2)}) collective-permute-start(bf16[64,512]{1,0:T(8,128)(2,1)S(1)} %start.1.after_ref.refs_0_), channel_id=1, source_target_pairs={{0,16},{8,24},{16,0},{24,8},{1,17},{9,25},{17,1},{25,9},{2,18},{10... | collective-permute-start | bytes 196616 | tf_op jit(solution)/shard_map/ppermute | solution.py:411
  5.4 4.4 %collective-permute-start = (bf16[64,512]{1,0:T(8,128)(2,1)S(1)}, bf16[64,512]{1,0:T(8,128)(2,1)S(1)}, u32[]{:S(2)}, u32[]{:S(2)}) collective-permute-start(bf16[64,512]{1,0:T(8,128)(2,1)S(1)} %start.1.after_ref.refs_0_), channel_id=1, source_target_pairs={{0,8},{8,0},{16,24},{24,16},{1,9},{9,1},{17,25},{25,17},{2,10},{10... | collective-permute-start | bytes 196616 | tf_op jit(solution)/shard_map/ppermute | solution.py:411
  13.3 5.8 %collective-permute-start.4 = (bf16[64,256]{1,0:T(8,128)(2,1)S(1)}, bf16[64,256]{1,0:T(8,128)(2,1)S(1)}, u32[]{:S(2)}, u32[]{:S(2)}) collective-permute-start(bf16[64,256]{1,0:T(8,128)(2,1)S(1)} %get-tuple-element.37), channel_id=1, source_target_pairs={{0,6},{1,7},{2,4},{3,5},{4,2},{5,3},{6,0},{7,1},{8,14},{9,15},{10,... | collective-permute-start | bytes 98312 | tf_op jit(solution)/shard_map/ppermute | solution.py:411
  17.0 4.8 %collective-permute-start.5 = (bf16[64,256]{1,0:T(8,128)(2,1)S(1)}, bf16[64,256]{1,0:T(8,128)(2,1)S(1)}, u32[]{:S(2)}, u32[]{:S(2)}) collective-permute-start(bf16[64,256]{1,0:T(8,128)(2,1)S(1)} %get-tuple-element.38), channel_id=1, source_target_pairs={{0,4},{1,5},{2,6},{3,7},{4,0},{5,1},{6,2},{7,3},{8,12},{9,13},{10,... | collective-permute-start | bytes 98312 | tf_op jit(solution)/shard_map/ppermute | solution.py:411
  17.0 4.8 %collective-permute-start.6 = (bf16[64,256]{1,0:T(8,128)(2,1)S(1)}, bf16[64,256]{1,0:T(8,128)(2,1)S(1)}, u32[]{:S(2)}, u32[]{:S(2)}) collective-permute-start(bf16[64,256]{1,0:T(8,128)(2,1)S(1)} %get-tuple-element.39), channel_id=1, source_target_pairs={{0,2},{1,3},{2,0},{3,1},{4,6},{5,7},{6,4},{7,5},{8,10},{9,11},{10,... | collective-permute-start | bytes 98312 | tf_op jit(solution)/shard_map/ppermute | solution.py:411
  21.8 5.9 %collective-permute-start.9 = (bf16[64,256]{1,0:T(8,128)(2,1)S(1)}, bf16[64,256]{1,0:T(8,128)(2,1)S(1)}, u32[]{:S(2)}, u32[]{:S(2)}) collective-permute-start(bf16[64,256]{1,0:T(8,128)(2,1)S(1)} %query.2.refs_0_), channel_id=1, source_target_pairs={{0,6},{1,7},{2,4},{3,5},{4,2},{5,3},{6,0},{7,1},{8,14},{9,15},{10,... | collective-permute-start | bytes 98312 | tf_op jit(solution)/shard_map/ppermute | solution.py:411
  23.5 4.9 %collective-permute-start.8 = (bf16[64,256]{1,0:T(8,128)(2,1)S(1)}, bf16[64,256]{1,0:T(8,128)(2,1)S(1)}, u32[]{:S(2)}, u32[]{:S(2)}) collective-permute-start(bf16[64,256]{1,0:T(8,128)(2,1)S(1)} %query.2.refs_0_), channel_id=1, source_target_pairs={{0,4},{1,5},{2,6},{3,7},{4,0},{5,1},{6,2},{7,3},{8,12},{9,13},{10,... | collective-permute-start | bytes 98312 | tf_op jit(solution)/shard_map/ppermute | solution.py:411
  24.0 4.5 %collective-permute-start.7 = (bf16[64,256]{1,0:T(8,128)(2,1)S(1)}, bf16[64,256]{1,0:T(8,128)(2,1)S(1)}, u32[]{:S(2)}, u32[]{:S(2)}) collective-permute-start(bf16[64,256]{1,0:T(8,128)(2,1)S(1)} %query.2.refs_0_), channel_id=1, source_target_pairs={{0,2},{1,3},{2,0},{3,1},{4,6},{5,7},{6,4},{7,5},{8,10},{9,11},{10,... | collective-permute-start | bytes 98312 | tf_op jit(solution)/shard_map/ppermute | solution.py:411
  31.4 7.2 %collective-permute-start.11 = (f32[64,512]{1,0:T(8,128)S(1)}, f32[64,512]{1,0:T(8,128)S(1)}, u32[]{:S(2)}, u32[]{:S(2)}) collective-permute-start(f32[64,512]{1,0:T(8,128)S(1)} %get-tuple-element.42), channel_id=1, source_target_pairs={{0,24},{8,16},{16,8},{24,0},{1,25},{9,17},{17,9},{25,1},{2,26},{10... | collective-permute-start | bytes 393224 | tf_op jit(solution)/shard_map/ppermute | solution.py:411
  34.2 7.1 %collective-permute-start.12 = (f32[64,512]{1,0:T(8,128)S(1)}, f32[64,512]{1,0:T(8,128)S(1)}, u32[]{:S(2)}, u32[]{:S(2)}) collective-permute-start(f32[64,512]{1,0:T(8,128)S(1)} %get-tuple-element.43), channel_id=1, source_target_pairs={{0,16},{8,24},{16,0},{24,8},{1,17},{9,25},{17,1},{25,9},{2,18},{10... | collective-permute-start | bytes 393224 | tf_op jit(solution)/shard_map/ppermute | solution.py:411
  34.2 7.1 %collective-permute-start.13 = (f32[64,512]{1,0:T(8,128)S(1)}, f32[64,512]{1,0:T(8,128)S(1)}, u32[]{:S(2)}, u32[]{:S(2)}) collective-permute-start(f32[64,512]{1,0:T(8,128)S(1)} %get-tuple-element.44), channel_id=1, source_target_pairs={{0,8},{8,0},{16,24},{24,16},{1,9},{9,1},{17,25},{25,17},{2,10},{10... | collective-permute-start | bytes 393224 | tf_op jit(solution)/shard_map/ppermute | solution.py:411
  41.4 7.3 %collective-permute-start.16 = (f32[64,512]{1,0:T(8,128)S(1)}, f32[64,512]{1,0:T(8,128)S(1)}, u32[]{:S(2)}, u32[]{:S(2)}) collective-permute-start(f32[64,512]{1,0:T(8,128)S(1)} %lift.2.refs_0_), channel_id=1, source_target_pairs={{0,24},{8,16},{16,8},{24,0},{1,25},{9,17},{17,9},{25,1},{2,26},{10... | collective-permute-start | bytes 393224 | tf_op jit(solution)/shard_map/ppermute | solution.py:411
  43.2 7.3 %collective-permute-start.15 = (f32[64,512]{1,0:T(8,128)S(1)}, f32[64,512]{1,0:T(8,128)S(1)}, u32[]{:S(2)}, u32[]{:S(2)}) collective-permute-start(f32[64,512]{1,0:T(8,128)S(1)} %lift.2.refs_0_), channel_id=1, source_target_pairs={{0,16},{8,24},{16,0},{24,8},{1,17},{9,25},{17,1},{25,9},{2,18},{10... | collective-permute-start | bytes 393224 | tf_op jit(solution)/shard_map/ppermute | solution.py:411
  44.7 5.9 %collective-permute-start.14 = (f32[64,512]{1,0:T(8,128)S(1)}, f32[64,512]{1,0:T(8,128)S(1)}, u32[]{:S(2)}, u32[]{:S(2)}) collective-permute-start(f32[64,512]{1,0:T(8,128)S(1)} %lift.2.refs_0_), channel_id=1, source_target_pairs={{0,8},{8,0},{16,24},{24,16},{1,9},{9,1},{17,25},{25,17},{2,10},{10... | collective-permute-start | bytes 393224 | tf_op jit(solution)/shard_map/ppermute | solution.py:411
  52.4 6.7 %collective-permute-start.20 = (f32[64,64]{1,0:T(8,128)S(1)}, f32[64,64]{1,0:T(8,128)S(1)}, u32[]{:S(2)}, u32[]{:S(2)}) collective-permute-start(f32[64,64]{1,0:T(8,128)S(1)} %sum.3.refs_0_), channel_id=1, source_target_pairs={{0,6},{1,7},{2,4},{3,5},{4,2},{5,3},{6,0},{7,1},{8,14},{9,15},{10,... | collective-permute-start | bytes 49160 | tf_op jit(solution)/shard_map/ppermute | solution.py:411
  54.3 5.0 %collective-permute-start.19 = (f32[64,64]{1,0:T(8,128)S(1)}, f32[64,64]{1,0:T(8,128)S(1)}, u32[]{:S(2)}, u32[]{:S(2)}) collective-permute-start(f32[64,64]{1,0:T(8,128)S(1)} %sum.3.refs_0_), channel_id=1, source_target_pairs={{0,4},{1,5},{2,6},{3,7},{4,0},{5,1},{6,2},{7,3},{8,12},{9,13},{10,... | collective-permute-start | bytes 49160 | tf_op jit(solution)/shard_map/ppermute | solution.py:411
  55.2 4.3 %collective-permute-start.18 = (f32[64,64]{1,0:T(8,128)S(1)}, f32[64,64]{1,0:T(8,128)S(1)}, u32[]{:S(2)}, u32[]{:S(2)}) collective-permute-start(f32[64,64]{1,0:T(8,128)S(1)} %sum.3.refs_0_), channel_id=1, source_target_pairs={{0,2},{1,3},{2,0},{3,1},{4,6},{5,7},{6,4},{7,5},{8,10},{9,11},{10,... | collective-permute-start | bytes 49160 | tf_op jit(solution)/shard_map/ppermute | solution.py:411
  63.8 5.8 %collective-permute-start.22 = (bf16[64,256]{1,0:T(8,128)(2,1)S(1)}, bf16[64,256]{1,0:T(8,128)(2,1)S(1)}, u32[]{:S(2)}, u32[]{:S(2)}) collective-permute-start(bf16[64,256]{1,0:T(8,128)(2,1)S(1)} %get-tuple-element.50), channel_id=1, source_target_pairs={{0,6},{1,7},{2,4},{3,5},{4,2},{5,3},{6,0},{7,1},{8,14},{9,15},{10,... | collective-permute-start | bytes 98312 | tf_op jit(solution)/shard_map/ppermute | solution.py:411
  65.6 5.0 %collective-permute-start.23 = (bf16[64,256]{1,0:T(8,128)(2,1)S(1)}, bf16[64,256]{1,0:T(8,128)(2,1)S(1)}, u32[]{:S(2)}, u32[]{:S(2)}) collective-permute-start(bf16[64,256]{1,0:T(8,128)(2,1)S(1)} %get-tuple-element.51), channel_id=1, source_target_pairs={{0,4},{1,5},{2,6},{3,7},{4,0},{5,1},{6,2},{7,3},{8,12},{9,13},{10,... | collective-permute-start | bytes 98312 | tf_op jit(solution)/shard_map/ppermute | solution.py:411
  66.5 4.3 %collective-permute-start.24 = (bf16[64,256]{1,0:T(8,128)(2,1)S(1)}, bf16[64,256]{1,0:T(8,128)(2,1)S(1)}, u32[]{:S(2)}, u32[]{:S(2)}) collective-permute-start(bf16[64,256]{1,0:T(8,128)(2,1)S(1)} %get-tuple-element.52), channel_id=1, source_target_pairs={{0,2},{1,3},{2,0},{3,1},{4,6},{5,7},{6,4},{7,5},{8,10},{9,11},{10,... | collective-permute-start | bytes 98312 | tf_op jit(solution)/shard_map/ppermute | solution.py:411
  70.8 6.0 %collective-permute-start.27 = (bf16[64,256]{1,0:T(8,128)(2,1)S(1)}, bf16[64,256]{1,0:T(8,128)(2,1)S(1)}, u32[]{:S(2)}, u32[]{:S(2)}) collective-permute-start(bf16[64,256]{1,0:T(8,128)(2,1)S(1)} %query.3.refs_0_), channel_id=1, source_target_pairs={{0,6},{1,7},{2,4},{3,5},{4,2},{5,3},{6,0},{7,1},{8,14},{9,15},{10,... | collective-permute-start | bytes 98312 | tf_op jit(solution)/shard_map/ppermute | solution.py:411
  72.7 5.1 %collective-permute-start.26 = (bf16[64,256]{1,0:T(8,128)(2,1)S(1)}, bf16[64,256]{1,0:T(8,128)(2,1)S(1)}, u32[]{:S(2)}, u32[]{:S(2)}) collective-permute-start(bf16[64,256]{1,0:T(8,128)(2,1)S(1)} %query.3.refs_0_), channel_id=1, source_target_pairs={{0,4},{1,5},{2,6},{3,7},{4,0},{5,1},{6,2},{7,3},{8,12},{9,13},{10,... | collective-permute-start | bytes 98312 | tf_op jit(solution)/shard_map/ppermute | solution.py:411
  73.8 4.3 %collective-permute-start.25 = (bf16[64,256]{1,0:T(8,128)(2,1)S(1)}, bf16[64,256]{1,0:T(8,128)(2,1)S(1)}, u32[]{:S(2)}, u32[]{:S(2)}) collective-permute-start(bf16[64,256]{1,0:T(8,128)(2,1)S(1)} %query.3.refs_0_), channel_id=1, source_target_pairs={{0,2},{1,3},{2,0},{3,1},{4,6},{5,7},{6,4},{7,5},{8,10},{9,11},{10,... | collective-permute-start | bytes 98312 | tf_op jit(solution)/shard_map/ppermute | solution.py:411
  80.9 7.3 %collective-permute-start.29 = (f32[64,512]{1,0:T(8,128)S(1)}, f32[64,512]{1,0:T(8,128)S(1)}, u32[]{:S(2)}, u32[]{:S(2)}) collective-permute-start(f32[64,512]{1,0:T(8,128)S(1)} %get-tuple-element.54), channel_id=1, source_target_pairs={{0,24},{8,16},{16,8},{24,0},{1,25},{9,17},{17,9},{25,1},{2,26},{10... | collective-permute-start | bytes 393224 | tf_op jit(solution)/shard_map/ppermute | solution.py:411
  82.2 8.0 %collective-permute-start.30 = (f32[64,512]{1,0:T(8,128)S(1)}, f32[64,512]{1,0:T(8,128)S(1)}, u32[]{:S(2)}, u32[]{:S(2)}) collective-permute-start(f32[64,512]{1,0:T(8,128)S(1)} %get-tuple-element.55), channel_id=1, source_target_pairs={{0,16},{8,24},{16,0},{24,8},{1,17},{9,25},{17,1},{25,9},{2,18},{10... | collective-permute-start | bytes 393224 | tf_op jit(solution)/shard_map/ppermute | solution.py:411
  83.5 6.7 %collective-permute-start.31 = (f32[64,512]{1,0:T(8,128)S(1)}, f32[64,512]{1,0:T(8,128)S(1)}, u32[]{:S(2)}, u32[]{:S(2)}) collective-permute-start(f32[64,512]{1,0:T(8,128)S(1)} %get-tuple-element.56), channel_id=1, source_target_pairs={{0,8},{8,0},{16,24},{24,16},{1,9},{9,1},{17,25},{25,17},{2,10},{10... | collective-permute-start | bytes 393224 | tf_op jit(solution)/shard_map/ppermute | solution.py:411
  90.5 4.9 %collective-permute-start.34 = (f32[64,64]{1,0:T(8,128)S(1)}, f32[64,64]{1,0:T(8,128)S(1)}, u32[]{:S(2)}, u32[]{:S(2)}) collective-permute-start(f32[64,64]{1,0:T(8,128)S(1)} %get-tuple-element.57.refs_0_), channel_id=1, source_target_pairs={{0,24},{8,16},{16,8},{24,0},{1,25},{9,17},{17,9},{25,1},{2,26},{10... | collective-permute-start | bytes 49160 | tf_op jit(solution)/shard_map/ppermute | solution.py:411
  92.3 3.9 %collective-permute-start.33 = (f32[64,64]{1,0:T(8,128)S(1)}, f32[64,64]{1,0:T(8,128)S(1)}, u32[]{:S(2)}, u32[]{:S(2)}) collective-permute-start(f32[64,64]{1,0:T(8,128)S(1)} %get-tuple-element.57.refs_0_), channel_id=1, source_target_pairs={{0,16},{8,24},{16,0},{24,8},{1,17},{9,25},{17,1},{25,9},{2,18},{10... | collective-permute-start | bytes 49160 | tf_op jit(solution)/shard_map/ppermute | solution.py:411
  98.6 5.8 %collective-permute-start.38 = (f32[64,64]{1,0:T(8,128)S(1)}, f32[64,64]{1,0:T(8,128)S(1)}, u32[]{:S(2)}, u32[]{:S(2)}) collective-permute-start(f32[64,64]{1,0:T(8,128)S(1)} %sum.5.refs_0_), channel_id=1, source_target_pairs={{0,6},{1,7},{2,4},{3,5},{4,2},{5,3},{6,0},{7,1},{8,14},{9,15},{10,... | collective-permute-start | bytes 49160 | tf_op jit(solution)/shard_map/ppermute | solution.py:411
  100.4 5.0 %collective-permute-start.37 = (f32[64,64]{1,0:T(8,128)S(1)}, f32[64,64]{1,0:T(8,128)S(1)}, u32[]{:S(2)}, u32[]{:S(2)}) collective-permute-start(f32[64,64]{1,0:T(8,128)S(1)} %sum.5.refs_0_), channel_id=1, source_target_pairs={{0,4},{1,5},{2,6},{3,7},{4,0},{5,1},{6,2},{7,3},{8,12},{9,13},{10,... | collective-permute-start | bytes 49160 | tf_op jit(solution)/shard_map/ppermute | solution.py:411
  101.1 4.3 %collective-permute-start.36 = (f32[64,64]{1,0:T(8,128)S(1)}, f32[64,64]{1,0:T(8,128)S(1)}, u32[]{:S(2)}, u32[]{:S(2)}) collective-permute-start(f32[64,64]{1,0:T(8,128)S(1)} %sum.5.refs_0_), channel_id=1, source_target_pairs={{0,2},{1,3},{2,0},{3,1},{4,6},{5,7},{6,4},{7,5},{8,10},{9,11},{10,... | collective-permute-start | bytes 49160 | tf_op jit(solution)/shard_map/ppermute | solution.py:411
  (7 other events, 13.2 us)

commit v4 on v3

--- a/solution.py
+++ b/solution.py
@@ -214,18 +214,85 @@
     emit(total, out_refs, table[SINGLES, ROW_AT], side)
 
 
-def next_body(n_in, table, *refs):
-    pieces, (scale_ref, tile_ref, out_ref, spread, held, total) = refs[:n_in], refs[n_in:]
-    tiles, width, side = out_ref.shape
-    collect(spread, pieces, table[SINGLES, ROW_AT], side)
+def pack_gram(gram, columns):
+    per = columns // gram.shape[0]
+    rows = gram.shape[0] // per
+    return jnp.concatenate([gram[at * rows : (at + 1) * rows] for at in range(per)], axis=1)
+
+
+def unpack_gram(rows, width):
+    return jnp.concatenate([rows[:, at : at + width] for at in range(0, rows.shape[1], width)], axis=0)
+
+
+def split_panel(pieces, scale_ref, spread, held, me):
+    width, side = spread.shape[1:]
+    collect(spread, pieces, me, side)
     for tile in range(spread.shape[0]):
         value = spread[tile] * scale_ref[:, tile * side : (tile + 1) * side]
         high = value.astype(jnp.bfloat16)
         held[tile, :width] = high
         held[tile, width:] = (value - high.astype(jnp.float32)).astype(jnp.bfloat16)
+    gram = jnp.zeros((width, width), jnp.float32)
+    for piece in pieces:
+        gram = gram + lax.dot_general(
+            piece[...], piece[...], NT, precision=HIGH, preferred_element_type=jnp.float32
+        )
+    return gram
+
+
+def emit_rows(total, out_ref, chips, me, side, flip):
+    width = total.shape[1]
+    for step in range(chips):
+        get(total, me ^ (2 * step + flip), out_ref.at[step * width : (step + 1) * width], side)
+
+
+def next_body(n_in, chips, table, *refs):
+    pieces, (scale_ref, tile_ref, mine_ref, other_ref, gram_ref, spread, held, total) = refs[:n_in], refs[n_in:]
+    side, me, width = tile_ref.shape[1], table[SINGLES, COL_AT], total.shape[1]
+    rows = pack_gram(split_panel(pieces, scale_ref, spread, held, table[SINGLES, ROW_AT]), gram_ref.shape[1])
+    gram_ref[...] = rows
+    other_ref[chips * width :] = rows
     total[...] = jnp.zeros_like(total)
     forward(ALL, table=table, held=held, tile_ref=tile_ref, total=total)
-    out_ref[...] = total[:tiles]
+    emit_rows(total, mine_ref, chips, me, side, 0)
+    emit_rows(total, other_ref, chips, me, side, 1)
+
+
+def next_other_body(n_in, chips, table, *refs):
+    pieces, (scale_ref, tile_ref, held, other_ref, gram_ref, spread, total) = refs[:n_in], refs[n_in:]
+    side, me, width = tile_ref.shape[1], table[SINGLES, COL_AT], total.shape[1]
+    rows = pack_gram(split_panel(pieces, scale_ref, spread, held, table[SINGLES, ROW_AT]), gram_ref.shape[1])
+    gram_ref[...] = rows
+    other_ref[chips * width :] = rows
+    total[...] = jnp.zeros_like(total)
+    forward(1 - me % 2, table=table, held=held, tile_ref=tile_ref, total=total)
+    emit_rows(total, other_ref, chips, me, side, 1)
+
+
+def next_mine_body(chips, table, held, tile_ref, mine_ref, total):
+    side, me = tile_ref.shape[1], table[SINGLES, COL_AT]
+    total[...] = jnp.zeros_like(total)
+    forward(me % 2, table=table, held=held, tile_ref=tile_ref, total=total)
+    emit_rows(total, mine_ref, chips, me, side, 0)
+
+
+def next_pair_body(width, mine_ref, got_ref, gram_ref, *outs):
+    count = len(outs)
+    gram = gram_ref[...] + got_ref[count * width :]
+    for at, out_ref in enumerate(outs):
+        step = (count - at) % count
+        span = slice(step * width, (step + 1) * width)
+        out_ref[:width] = mine_ref[span] + got_ref[span]
+        out_ref[width:] = gram
+
+
+def next_query_body(*refs):
+    part_refs, scale_ref, out_ref = refs[:-2], refs[-2], refs[-1]
+    width = out_ref.shape[0]
+    total = add(part_refs)
+    inverse = inverse_factor(unpack_gram(total[width:], width))
+    current = lax.dot_general(inverse, total[:width], NN, precision=HIGH, preferred_element_type=jnp.float32)
+    out_ref[...] = (current * scale_ref[...]).astype(out_ref.dtype)
 
 
 def add(refs):
@@ -344,57 +411,8 @@
     gram_ref[...] = lax.dot_general(lifted, lifted, NT, precision=HIGH, preferred_element_type=jnp.float32)
 
 
-def gram_body(*refs):
-    total = jnp.zeros(refs[-1].shape, jnp.float32)
-    for ref in refs[:-1]:
-        total = total + lax.dot_general(
-            ref[...], ref[...], NT, precision=HIGH, preferred_element_type=jnp.float32
-        )
-    refs[-1][...] = total
-
-
 def sum_body(*refs):
     refs[-1][...] = add(refs[:-1])
-
-
-def apply_tile(inverse, total_ref, owner, out_ref):
-    width, share = out_ref.shape
-    side = total_ref.shape[2]
-    if share >= side:
-        for piece in range(share // side):
-            out_ref[:, piece * side : (piece + 1) * side] = lax.dot_general(
-                inverse,
-                total_ref[owner * (share // side) + piece],
-                NN,
-                precision=HIGH,
-                preferred_element_type=jnp.float32,
-            )
-    else:
-        per = side // share
-        for at in range(per):
-
-            @pl.when(owner % per == at)
-            def _():
-                out_ref[...] = lax.dot_general(
-                    inverse,
-                    total_ref[owner // per],
-                    NN,
-                    precision=HIGH,
-                    preferred_element_type=jnp.float32,
-                )[:, at * share : (at + 1) * share]
-
-
-def apply_other_body(n_in, table, *refs):
-    grams, (total_ref, inverse_ref, other_ref) = refs[:n_in], refs[n_in:]
-    inverse = inverse_factor(add(grams))
-    inverse_ref[...] = inverse
-    for step in range(other_ref.shape[0]):
-        apply_tile(inverse, total_ref, table[SINGLES, COL_AT] ^ (2 * step + 1), other_ref.at[step])
-
-
-def apply_mine_body(table, inverse_ref, total_ref, mine_ref):
-    for step in range(mine_ref.shape[0]):
-        apply_tile(inverse_ref[...], total_ref, table[SINGLES, COL_AT] ^ (2 * step), mine_ref.at[step])
 
 
 def finish_body(after, *refs):
@@ -483,6 +501,7 @@
     tile_set = pltpu.with_memory_space_constraint(tile_set, pltpu.VMEM)
     root_count = math.sqrt(products * n_col)
     half = f32(chips, width, columns)
+    gram_rows = width * width // columns
     half_work = dict(flops=slots * width * side * side, moved=slots * side * side)
     query_scratch = pltpu.VMEM((query_tiles + 1, width, side), jnp.float32)
     product_scratch = pltpu.VMEM((product_tiles + 1, width, side), jnp.float32)
@@ -490,30 +509,43 @@
     for iteration in range(ITERS):
         if iteration > 0:
             pieces = spread_to(lifted, "row")
-            gram = call(gram_body, "gram", [WHOLE] * n_row, f32(width, width))(*pieces)
-            grams = terms_over_col(gram)
-            total = call(
-                functools.partial(next_body, n_row),
-                "forward",
-                [SCALARS] + [WHOLE] * (n_row + 2),
-                f32(query_tiles, width, side),
-                [
-                    pltpu.VMEM((product_tiles, width, side), jnp.float32),
-                    pltpu.VMEM((product_tiles, 2 * width, side), jnp.bfloat16),
-                    query_scratch,
-                ],
-                **work,
-            )(table, *pieces, pscale, tile_set)
-            inverse, other = call(
-                functools.partial(apply_other_body, chips),
-                "apply",
-                [SCALARS] + [WHOLE] * (chips + 1),
-                [f32(width, width), half],
-            )(table, *grams, total)
-            got = swap(other, "col", 1)
-            mine = call(apply_mine_body, "apply_rest", [SCALARS] + [WHOLE] * 2, half, **half_work)(
-                table, inverse, total
-            )
+            arrays = [WHOLE] * (n_row + 2)
+            message = f32(chips * width + gram_rows, columns)
+            spread = pltpu.VMEM((product_tiles, width, side), jnp.float32)
+            if split:
+                held, other, gram = call(
+                    functools.partial(next_other_body, n_row, chips),
+                    "forward",
+                    [SCALARS] + arrays,
+                    [bf16(product_tiles, 2 * width, side), message, f32(gram_rows, columns)],
+                    [spread, query_scratch],
+                    **half_work,
+                )(table, *pieces, pscale, tile_set)
+                got = swap(other, "col", 1)
+                mine = call(
+                    functools.partial(next_mine_body, chips),
+                    "forward_rest",
+                    [SCALARS] + [WHOLE] * 2,
+                    f32(chips * width, columns),
+                    [query_scratch],
+                    **half_work,
+                )(table, held, tile_set)
+            else:
+                mine, other, gram = call(
+                    functools.partial(next_body, n_row, chips),
+                    "forward",
+                    [SCALARS] + arrays,
+                    [f32(chips * width, columns), message, f32(gram_rows, columns)],
+                    [spread, pltpu.VMEM((product_tiles, 2 * width, side), jnp.bfloat16), query_scratch],
+                    **work,
+                )(table, *pieces, pscale, tile_set)
+                got = swap(other, "col", 1)
+            sums = call(
+                functools.partial(next_pair_body, width),
+                "pair",
+                [WHOLE] * 3,
+                [f32(width + gram_rows, columns)] * chips,
+            )(mine, got, gram)
         elif split:
             held, other = call(
                 functools.partial(forward_other_body, n_row),
@@ -542,11 +574,12 @@
                 **work,
             )(table, *pieces, tile_set)
             got = swap(other, "col", 1)
-        sums = call(
-            pair_body, "pair", [WHOLE] * 2, [f32(width, columns)] + [bf16(width, columns)] * (chips - 1)
-        )(mine, got)
+        if iteration == 0:
+            sums = call(
+                pair_body, "pair", [WHOLE] * 2, [f32(width, columns)] + [bf16(width, columns)] * (chips - 1)
+            )(mine, got)
         parts = deal(sums, "col", 2)
-        rounded = call(query_body, "query", [WHOLE] * (chips + 1), bf16(width, columns))(*parts, my_qscale)
+        rounded = call(next_query_body if iteration else query_body, "query", [WHOLE] * (chips + 1), bf16(width, columns))(*parts, my_qscale)
         pieces = spread_to(rounded, "col", 2)
         here = call(join_body, "join", [WHOLE] * chips, bf16(chips, width, columns))(*pieces)
         there = swap(here, "col", 1)

time: 108 us -> 104 us (0.963)
  starting transfers between devices: 45.8 us -> 41.4 us
  waiting for transfers between devices: 38.4 us -> 39.7 us
    ppermute x39 -> x35, starting transfers between devices: 45.8 us -> 41.4 us  [swap(): lax.ppermute(value, axis, [(i, i ^ step) for i in range(lax.axis_size(axi...]
    ppermute x39 -> x35, waiting for transfers between devices: 38.4 us -> 39.7 us  [swap(): lax.ppermute(value, axis, [(i, i ^ step) for i in range(lax.axis_size(axi...]
    pallas_call x6 -> x5, Pallas kernels: 6.54 us -> 5.8 us  [the longest x1 2.01 us: shards(): call(functools.partial(next_mine_body, chips), 'forward_rest', [SCALARS]...]
  transfers between devices with their start and end apart: 39 -> 35, of which waited for: 27 -> 25; matrix products, arithmetic and copies ran while one was open for 0% -> 0% of each run, Pallas kernels for 11% -> 10%
where the time goes in v4:
time: 104 us
  starting transfers between devices  41.4 us (40%)
  waiting for transfers between devices  39.7 us (38%)
  Pallas kernels  21.9 us (21%)
    ppermute x35, starting transfers between devices, swap(): lax.ppermute(value, axis, [(i, i ^ step) for i in range(lax.axis_size(axi...  41.4 us
    ppermute x35, waiting for transfers between devices, swap(): lax.ppermute(value, axis, [(i, i ^ step) for i in range(lax.axis_size(axi...  39.7 us
    pallas_call x1, Pallas kernels, shards(): call(functools.partial(load_body, max(columns // side, 1)), 'load', [SCAL...  3.53 us
    pallas_call x2, Pallas kernels, shards(): call(functools.partial(back_mine_body, chips), 'backward', [SCALARS] + [W...  2.94 us
    pallas_call x1, Pallas kernels, shards(): call(functools.partial(finish_body, root_count), 'finish', [WHOLE] * (chi...  2.53 us
    pallas_call x2, Pallas kernels, shards(): call(back_other_body, 'backward_rest', [SCALARS] + [WHOLE] * 3, [f32(widt...  2.41 us
  transfers between devices with their start and end apart: 35, of which 25 were waited for; matrix products, arithmetic and copies ran while one was open for 0% of the time, Pallas kernels for 10%

profile of v4, /device:TPU:0, one launch (start us, length us, event | category | flops | bytes accessed | tf_op | source)
XLA Modules:
  0.0 103.9 jit_solution(9214478442606757254)
XLA Ops:
  1.0 4.0 %collective-permute-start.2 = (bf16[64,512]{1,0:T(8,128)(2,1)S(1)}, bf16[64,512]{1,0:T(8,128)(2,1)S(1)}, u32[]{:S(2)}, u32[]{:S(2)}) collective-permute-start(bf16[64,512]{1,0:T(8,128)(2,1)S(1)} %start.1.after_ref.refs_0_), channel_id=1, source_target_pairs={{0,24},{8,16},{16,8},{24,0},{1,25},{9,17},{17,9},{25,1},{2,26},{10... | collective-permute-start | bytes 196616 | tf_op jit(solution)/shard_map/ppermute | solution.py:429
  6.3 3.5 %load.1 = (bf16[32,256,256]{2,1,0:T(8,128)(2,1)S(1)}, f32[1,512]{1,0:T(1,128)S(1)}, f32[1,2048]{1,0:T(1,128)S(1)}, f32[1,256]{1,0:T(1,128)S(1)}, s32[16,32]{1,0:T(8,128)S(1)}) custom-call(s32[3]{0:T(128)S(1)} %pad_add_fusion.place, bf16[64,512]{1,0:T(8,128)(2,1)S(1)} %start.1.after_ref.refs_0_, bf16[32,256,256]{2,1,0:T(8,128)(2,1)} %bitcast.8, ...), custom_call_target="tpu_custom_call" | custom-call | bytes 8388608 | tf_op jit(solution)/shard_map/load/pallas_call | solution.py:474
  11.4 1.9 %forward_rest.2.mine_ref = f32[4,64,256]{2,1,0:T(8,128)S(1)} custom-call(s32[16,32]{1,0:T(8,128)S(1)} %get-tuple-element.33.table, bf16[8,64,256]{2,1,0:T(8,128)(2,1)S(1)} %get-tuple-element.35.held, bf16[32,256,256]{2,1,0:T(8,128)(2,1)S(1)} %get-tuple-element.34.refs_4_.tile_ref.refs_5_), custom_call_target="tpu_custom_call" | custom-call | flops 134217728 | bytes 2097152 | tf_op jit(solution)/shard_map/forward_rest/pallas_call | solution.py:559
  13.4 3.7 %collective-permute-start.4 = (bf16[64,256]{1,0:T(8,128)(2,1)S(1)}, bf16[64,256]{1,0:T(8,128)(2,1)S(1)}, u32[]{:S(2)}, u32[]{:S(2)}) collective-permute-start(bf16[64,256]{1,0:T(8,128)(2,1)S(1)} %get-tuple-element.38), channel_id=1, source_target_pairs={{0,6},{1,7},{2,4},{3,5},{4,2},{5,3},{6,0},{7,1},{8,14},{9,15},{10,... | collective-permute-start | bytes 98312 | tf_op jit(solution)/shard_map/ppermute | solution.py:429
  19.1 2.7 %collective-permute-done.5.refs_2_ = bf16[64,256]{1,0:T(8,128)(2,1)S(1)} collective-permute-done((bf16[64,256]{1,0:T(8,128)(2,1)S(1)}, bf16[64,256]{1,0:T(8,128)(2,1)S(1)}, u32[]{:S(2)}, u32[]{:S(2)}) %collective-permute-start.5) | collective-permute-done | bytes 32800 | tf_op jit(solution)/shard_map/ppermute | solution.py:429
  21.9 1.7 %collective-permute-start.9 = (bf16[64,256]{1,0:T(8,128)(2,1)S(1)}, bf16[64,256]{1,0:T(8,128)(2,1)S(1)}, u32[]{:S(2)}, u32[]{:S(2)}) collective-permute-start(bf16[64,256]{1,0:T(8,128)(2,1)S(1)} %query.2.refs_0_), channel_id=1, source_target_pairs={{0,6},{1,7},{2,4},{3,5},{4,2},{5,3},{6,0},{7,1},{8,14},{9,15},{10,... | collective-permute-start | bytes 98312 | tf_op jit(solution)/shard_map/ppermute | solution.py:429
  24.0 2.3 %collective-permute-start.7 = (bf16[64,256]{1,0:T(8,128)(2,1)S(1)}, bf16[64,256]{1,0:T(8,128)(2,1)S(1)}, u32[]{:S(2)}, u32[]{:S(2)}) collective-permute-start(bf16[64,256]{1,0:T(8,128)(2,1)S(1)} %query.2.refs_0_), channel_id=1, source_target_pairs={{0,2},{1,3},{2,0},{3,1},{4,6},{5,7},{6,4},{7,5},{8,10},{9,11},{10,... | collective-permute-start | bytes 98312 | tf_op jit(solution)/shard_map/ppermute | solution.py:429
  26.3 1.4 %collective-permute-done.9.refs_3_ = bf16[64,256]{1,0:T(8,128)(2,1)S(1)} collective-permute-done((bf16[64,256]{1,0:T(8,128)(2,1)S(1)}, bf16[64,256]{1,0:T(8,128)(2,1)S(1)}, u32[]{:S(2)}, u32[]{:S(2)}) %collective-permute-start.9) | collective-permute-done | bytes 32800 | tf_op jit(solution)/shard_map/ppermute | solution.py:429
  28.6 1.5 %backward.2.begun_ref = f32[9,64,256]{2,1,0:T(8,128)S(1)} custom-call(s32[16,32]{1,0:T(8,128)S(1)} %get-tuple-element.33.table, bf16[64,256]{1,0:T(8,128)(2,1)S(1)} %query.2.refs_0_, bf16[64,256]{1,0:T(8,128)(2,1)S(1)} %collective-permute-done.7.refs_1_, bf16[64,256]{1,0:T(8,128)(2,1)S(1)} %collective-permute-done.8.refs_2_, ...), custom_call_target="tpu_custom_call" | custom-call | flops 134217728 | bytes 2097152 | tf_op jit(solution)/shard_map/backward/pallas_call | solution.py:587
  31.3 2.4 %collective-permute-start.11 = (f32[64,512]{1,0:T(8,128)S(1)}, f32[64,512]{1,0:T(8,128)S(1)}, u32[]{:S(2)}, u32[]{:S(2)}) collective-permute-start(f32[64,512]{1,0:T(8,128)S(1)} %get-tuple-element.43), channel_id=1, source_target_pairs={{0,24},{8,16},{16,8},{24,0},{1,25},{9,17},{17,9},{25,1},{2,26},{10... | collective-permute-start | bytes 393224 | tf_op jit(solution)/shard_map/ppermute | solution.py:429
  34.9 3.3 %collective-permute-done.11.refs_1_ = f32[64,512]{1,0:T(8,128)S(1)} collective-permute-done((f32[64,512]{1,0:T(8,128)S(1)}, f32[64,512]{1,0:T(8,128)S(1)}, u32[]{:S(2)}, u32[]{:S(2)}) %collective-permute-start.11) | collective-permute-done | bytes 131104 | tf_op jit(solution)/shard_map/ppermute | solution.py:429
  38.2 2.5 %collective-permute-done.12.refs_2_ = f32[64,512]{1,0:T(8,128)S(1)} collective-permute-done((f32[64,512]{1,0:T(8,128)S(1)}, f32[64,512]{1,0:T(8,128)S(1)}, u32[]{:S(2)}, u32[]{:S(2)}) %collective-permute-start.12) | collective-permute-done | bytes 131104 | tf_op jit(solution)/shard_map/ppermute | solution.py:429
  40.8 1.8 %collective-permute-start.16 = (f32[64,512]{1,0:T(8,128)S(1)}, f32[64,512]{1,0:T(8,128)S(1)}, u32[]{:S(2)}, u32[]{:S(2)}) collective-permute-start(f32[64,512]{1,0:T(8,128)S(1)} %lift.2.refs_0_), channel_id=1, source_target_pairs={{0,24},{8,16},{16,8},{24,0},{1,25},{9,17},{17,9},{25,1},{2,26},{10... | collective-permute-start | bytes 393224 | tf_op jit(solution)/shard_map/ppermute | solution.py:429
  44.4 3.8 %collective-permute-done.16.refs_3_ = f32[64,512]{1,0:T(8,128)S(1)} collective-permute-done((f32[64,512]{1,0:T(8,128)S(1)}, f32[64,512]{1,0:T(8,128)S(1)}, u32[]{:S(2)}, u32[]{:S(2)}) %collective-permute-start.16) | collective-permute-done | bytes 131104 | tf_op jit(solution)/shard_map/ppermute | solution.py:429
  48.2 1.8 %collective-permute-done.15.refs_2_ = f32[64,512]{1,0:T(8,128)S(1)} collective-permute-done((f32[64,512]{1,0:T(8,128)S(1)}, f32[64,512]{1,0:T(8,128)S(1)}, u32[]{:S(2)}, u32[]{:S(2)}) %collective-permute-start.15) | collective-permute-done | bytes 131104 | tf_op jit(solution)/shard_map/ppermute | solution.py:429
  50.0 1.9 %forward.3 = (bf16[8,128,256]{2,1,0:T(8,128)(2,1)S(1)}, f32[272,256]{1,0:T(8,128)S(1)}, f32[16,256]{1,0:T(8,128)S(1)}) custom-call(s32[16,32]{1,0:T(8,128)S(1)} %get-tuple-element.33.table, f32[64,512]{1,0:T(8,128)S(1)} %lift.2.refs_0_, f32[64,512]{1,0:T(8,128)S(1)} %collective-permute-done.14.refs_1_, f32[64,512]{1,0:T(8,128)S(1)} %collective-permute-done.15.refs_2_, ...), custom_call_target="tpu_custom_call" | custom-call | flops 134217728 | bytes 2097152 | tf_op jit(solution)/shard_map/forward/pallas_call | solution.py:516
  52.0 2.0 %forward_rest.3.mine_ref = f32[256,256]{1,0:T(8,128)S(1)} custom-call(s32[16,32]{1,0:T(8,128)S(1)} %get-tuple-element.33.table, bf16[8,128,256]{2,1,0:T(8,128)(2,1)S(1)} %get-tuple-element.48.held, bf16[32,256,256]{2,1,0:T(8,128)(2,1)S(1)} %get-tuple-element.34.refs_4_.tile_ref.refs_5_), custom_call_target="tpu_custom_call" | custom-call | flops 134217728 | bytes 2097152 | tf_op jit(solution)/shard_map/forward_rest/pallas_call | solution.py:525
  54.1 2.0 %collective-permute-start.18 = (f32[80,256]{1,0:T(8,128)S(1)}, f32[80,256]{1,0:T(8,128)S(1)}, u32[]{:S(2)}, u32[]{:S(2)}) collective-permute-start(f32[80,256]{1,0:T(8,128)S(1)} %get-tuple-element.52), channel_id=1, source_target_pairs={{0,6},{1,7},{2,4},{3,5},{4,2},{5,3},{6,0},{7,1},{8,14},{9,15},{10,... | collective-permute-start | bytes 245768 | tf_op jit(solution)/shard_map/ppermute | solution.py:429
  56.8 1.7 %collective-permute-start.20 = (f32[80,256]{1,0:T(8,128)S(1)}, f32[80,256]{1,0:T(8,128)S(1)}, u32[]{:S(2)}, u32[]{:S(2)}) collective-permute-start(f32[80,256]{1,0:T(8,128)S(1)} %get-tuple-element.54), channel_id=1, source_target_pairs={{0,2},{1,3},{2,0},{3,1},{4,6},{5,7},{6,4},{7,5},{8,10},{9,11},{10,... | collective-permute-start | bytes 245768 | tf_op jit(solution)/shard_map/ppermute | solution.py:429
  58.5 2.7 %collective-permute-done.18.refs_1_ = f32[80,256]{1,0:T(8,128)S(1)} collective-permute-done((f32[80,256]{1,0:T(8,128)S(1)}, f32[80,256]{1,0:T(8,128)S(1)}, u32[]{:S(2)}, u32[]{:S(2)}) %collective-permute-start.18) | collective-permute-done | bytes 81952 | tf_op jit(solution)/shard_map/ppermute | solution.py:429
  61.3 3.6 %collective-permute-done.19.refs_2_ = f32[80,256]{1,0:T(8,128)S(1)} collective-permute-done((f32[80,256]{1,0:T(8,128)S(1)}, f32[80,256]{1,0:T(8,128)S(1)}, u32[]{:S(2)}, u32[]{:S(2)}) %collective-permute-start.19) | collective-permute-done | bytes 81952 | tf_op jit(solution)/shard_map/ppermute | solution.py:429
  64.9 1.8 %query.3.refs_0_ = bf16[64,256]{1,0:T(8,128)(2,1)S(1)} custom-call(f32[80,256]{1,0:T(8,128)S(1)} %get-tuple-element.51.refs_0_, f32[80,256]{1,0:T(8,128)S(1)} %collective-permute-done.18.refs_1_, f32[80,256]{1,0:T(8,128)S(1)} %collective-permute-done.19.refs_2_, f32[80,256]{1,0:T(8,128)S(1)} %collective-permute-done.20.refs_3_, ...), custom_call_target="tpu_custom_call" | custom-call | tf_op jit(solution)/shard_map/query/pallas_call | solution.py:582
  66.7 2.0 %collective-permute-start.23 = (bf16[64,256]{1,0:T(8,128)(2,1)S(1)}, bf16[64,256]{1,0:T(8,128)(2,1)S(1)}, u32[]{:S(2)}, u32[]{:S(2)}) collective-permute-start(bf16[64,256]{1,0:T(8,128)(2,1)S(1)} %query.3.refs_0_), channel_id=1, source_target_pairs={{0,6},{1,7},{2,4},{3,5},{4,2},{5,3},{6,0},{7,1},{8,14},{9,15},{10,... | collective-permute-start | bytes 98312 | tf_op jit(solution)/shard_map/ppermute | solution.py:429
  68.7 2.4 %collective-permute-start.21 = (bf16[64,256]{1,0:T(8,128)(2,1)S(1)}, bf16[64,256]{1,0:T(8,128)(2,1)S(1)}, u32[]{:S(2)}, u32[]{:S(2)}) collective-permute-start(bf16[64,256]{1,0:T(8,128)(2,1)S(1)} %query.3.refs_0_), channel_id=1, source_target_pairs={{0,2},{1,3},{2,0},{3,1},{4,6},{5,7},{6,4},{7,5},{8,10},{9,11},{10,... | collective-permute-start | bytes 98312 | tf_op jit(solution)/shard_map/ppermute | solution.py:429
  73.6 1.5 %backward.3.begun_ref = f32[9,64,256]{2,1,0:T(8,128)S(1)} custom-call(s32[16,32]{1,0:T(8,128)S(1)} %get-tuple-element.33.table, bf16[64,256]{1,0:T(8,128)(2,1)S(1)} %query.3.refs_0_, bf16[64,256]{1,0:T(8,128)(2,1)S(1)} %collective-permute-done.21.refs_1_, bf16[64,256]{1,0:T(8,128)(2,1)S(1)} %collective-permute-done.22.refs_2_, ...), custom_call_target="tpu_custom_call" | custom-call | flops 134217728 | bytes 2097152 | tf_op jit(solution)/shard_map/backward/pallas_call | solution.py:587
  76.3 1.7 %collective-permute-start.25 = (f32[64,512]{1,0:T(8,128)S(1)}, f32[64,512]{1,0:T(8,128)S(1)}, u32[]{:S(2)}, u32[]{:S(2)}) collective-permute-start(f32[64,512]{1,0:T(8,128)S(1)} %get-tuple-element.56), channel_id=1, source_target_pairs={{0,24},{8,16},{16,8},{24,0},{1,25},{9,17},{17,9},{25,1},{2,26},{10... | collective-permute-start | bytes 393224 | tf_op jit(solution)/shard_map/ppermute | solution.py:429
  79.9 3.7 %collective-permute-done.25.refs_1_ = f32[64,512]{1,0:T(8,128)S(1)} collective-permute-done((f32[64,512]{1,0:T(8,128)S(1)}, f32[64,512]{1,0:T(8,128)S(1)}, u32[]{:S(2)}, u32[]{:S(2)}) %collective-permute-start.25) | collective-permute-done | bytes 131104 | tf_op jit(solution)/shard_map/ppermute | solution.py:429
  83.6 2.1 %collective-permute-done.26.refs_2_ = f32[64,512]{1,0:T(8,128)S(1)} collective-permute-done((f32[64,512]{1,0:T(8,128)S(1)}, f32[64,512]{1,0:T(8,128)S(1)}, u32[]{:S(2)}, u32[]{:S(2)}) %collective-permute-start.26) | collective-permute-done | bytes 131104 | tf_op jit(solution)/shard_map/ppermute | solution.py:429
  86.2 1.6 %collective-permute-start.30 = (f32[64,64]{1,0:T(8,128)S(1)}, f32[64,64]{1,0:T(8,128)S(1)}, u32[]{:S(2)}, u32[]{:S(2)}) collective-permute-start(f32[64,64]{1,0:T(8,128)S(1)} %get-tuple-element.59.refs_0_), channel_id=1, source_target_pairs={{0,24},{8,16},{16,8},{24,0},{1,25},{9,17},{17,9},{25,1},{2,26},{10... | collective-permute-start | bytes 49160 | tf_op jit(solution)/shard_map/ppermute | solution.py:429
  94.1 2.2 %collective-permute-start.34 = (f32[64,64]{1,0:T(8,128)S(1)}, f32[64,64]{1,0:T(8,128)S(1)}, u32[]{:S(2)}, u32[]{:S(2)}) collective-permute-start(f32[64,64]{1,0:T(8,128)S(1)} %sum.3.refs_0_), channel_id=1, source_target_pairs={{0,6},{1,7},{2,4},{3,5},{4,2},{5,3},{6,0},{7,1},{8,14},{9,15},{10,... | collective-permute-start | bytes 49160 | tf_op jit(solution)/shard_map/ppermute | solution.py:429
  98.5 1.6 %collective-permute-done.34.refs_3_ = f32[64,64]{1,0:T(8,128)S(1)} collective-permute-done((f32[64,64]{1,0:T(8,128)S(1)}, f32[64,64]{1,0:T(8,128)S(1)}, u32[]{:S(2)}, u32[]{:S(2)}) %collective-permute-start.34) | collective-permute-done | bytes 16416 | tf_op jit(solution)/shard_map/ppermute | solution.py:429
  101.4 2.5 %finish.1 = f32[64,512]{1,0:T(8,128)} custom-call(f32[64,64]{1,0:T(8,128)S(1)} %sum.3.refs_0_, f32[64,64]{1,0:T(8,128)S(1)} %collective-permute-done.32.refs_1_, f32[64,64]{1,0:T(8,128)S(1)} %collective-permute-done.33.refs_2_, f32[64,64]{1,0:T(8,128)S(1)} %collective-permute-done.34.refs_3_, f32[64,512]{1,0:T(8,128)S(1)} %get-tuple-element.60.refs_4_), custom_call_target="tpu_custom_call" | custom-call | tf_op jit(solution)/shard_map/finish/pallas_call | solution.py:618
  (60 shorter events, 27.6 us)
Async XLA Ops:
  1.0 8.9 %collective-permute-start.2 = (bf16[64,512]{1,0:T(8,128)(2,1)S(1)}, bf16[64,512]{1,0:T(8,128)(2,1)S(1)}, u32[]{:S(2)}, u32[]{:S(2)}) collective-permute-start(bf16[64,512]{1,0:T(8,128)(2,1)S(1)} %start.1.after_ref.refs_0_), channel_id=1, source_target_pairs={{0,24},{8,16},{16,8},{24,0},{1,25},{9,17},{17,9},{25,1},{2,26},{10... | collective-permute-start | bytes 196616 | tf_op jit(solution)/shard_map/ppermute | solution.py:429
  4.9 4.9 %collective-permute-start.1 = (bf16[64,512]{1,0:T(8,128)(2,1)S(1)}, bf16[64,512]{1,0:T(8,128)(2,1)S(1)}, u32[]{:S(2)}, u32[]{:S(2)}) collective-permute-start(bf16[64,512]{1,0:T(8,128)(2,1)S(1)} %start.1.after_ref.refs_0_), channel_id=1, source_target_pairs={{0,16},{8,24},{16,0},{24,8},{1,17},{9,25},{17,1},{25,9},{2,18},{10... | collective-permute-start | bytes 196616 | tf_op jit(solution)/shard_map/ppermute | solution.py:429
  5.4 4.4 %collective-permute-start = (bf16[64,512]{1,0:T(8,128)(2,1)S(1)}, bf16[64,512]{1,0:T(8,128)(2,1)S(1)}, u32[]{:S(2)}, u32[]{:S(2)}) collective-permute-start(bf16[64,512]{1,0:T(8,128)(2,1)S(1)} %start.1.after_ref.refs_0_), channel_id=1, source_target_pairs={{0,8},{8,0},{16,24},{24,16},{1,9},{9,1},{17,25},{25,17},{2,10},{10... | collective-permute-start | bytes 196616 | tf_op jit(solution)/shard_map/ppermute | solution.py:429
  11.3 2.0 %collective-permute-start.3 = (f32[4,64,256]{2,1,0:T(8,128)S(1)}, f32[4,64,256]{2,1,0:T(8,128)S(1)}, u32[]{:S(2)}, u32[]{:S(2)}) collective-permute-start(f32[4,64,256]{2,1,0:T(8,128)S(1)} %get-tuple-element.36), channel_id=1, source_target_pairs={{0,1},{1,0},{2,3},{3,2},{4,5},{5,4},{6,7},{7,6},{8,9},{9,8},{10,11... | collective-permute-start | bytes 786440 | tf_op jit(solution)/shard_map/ppermute | solution.py:429
  13.4 5.8 %collective-permute-start.4 = (bf16[64,256]{1,0:T(8,128)(2,1)S(1)}, bf16[64,256]{1,0:T(8,128)(2,1)S(1)}, u32[]{:S(2)}, u32[]{:S(2)}) collective-permute-start(bf16[64,256]{1,0:T(8,128)(2,1)S(1)} %get-tuple-element.38), channel_id=1, source_target_pairs={{0,6},{1,7},{2,4},{3,5},{4,2},{5,3},{6,0},{7,1},{8,14},{9,15},{10,... | collective-permute-start | bytes 98312 | tf_op jit(solution)/shard_map/ppermute | solution.py:429
  17.0 4.8 %collective-permute-start.5 = (bf16[64,256]{1,0:T(8,128)(2,1)S(1)}, bf16[64,256]{1,0:T(8,128)(2,1)S(1)}, u32[]{:S(2)}, u32[]{:S(2)}) collective-permute-start(bf16[64,256]{1,0:T(8,128)(2,1)S(1)} %get-tuple-element.39), channel_id=1, source_target_pairs={{0,4},{1,5},{2,6},{3,7},{4,0},{5,1},{6,2},{7,3},{8,12},{9,13},{10,... | collective-permute-start | bytes 98312 | tf_op jit(solution)/shard_map/ppermute | solution.py:429
  17.0 4.8 %collective-permute-start.6 = (bf16[64,256]{1,0:T(8,128)(2,1)S(1)}, bf16[64,256]{1,0:T(8,128)(2,1)S(1)}, u32[]{:S(2)}, u32[]{:S(2)}) collective-permute-start(bf16[64,256]{1,0:T(8,128)(2,1)S(1)} %get-tuple-element.40), channel_id=1, source_target_pairs={{0,2},{1,3},{2,0},{3,1},{4,6},{5,7},{6,4},{7,5},{8,10},{9,11},{10,... | collective-permute-start | bytes 98312 | tf_op jit(solution)/shard_map/ppermute | solution.py:429
  21.9 5.9 %collective-permute-start.9 = (bf16[64,256]{1,0:T(8,128)(2,1)S(1)}, bf16[64,256]{1,0:T(8,128)(2,1)S(1)}, u32[]{:S(2)}, u32[]{:S(2)}) collective-permute-start(bf16[64,256]{1,0:T(8,128)(2,1)S(1)} %query.2.refs_0_), channel_id=1, source_target_pairs={{0,6},{1,7},{2,4},{3,5},{4,2},{5,3},{6,0},{7,1},{8,14},{9,15},{10,... | collective-permute-start | bytes 98312 | tf_op jit(solution)/shard_map/ppermute | solution.py:429
  23.6 4.9 %collective-permute-start.8 = (bf16[64,256]{1,0:T(8,128)(2,1)S(1)}, bf16[64,256]{1,0:T(8,128)(2,1)S(1)}, u32[]{:S(2)}, u32[]{:S(2)}) collective-permute-start(bf16[64,256]{1,0:T(8,128)(2,1)S(1)} %query.2.refs_0_), channel_id=1, source_target_pairs={{0,4},{1,5},{2,6},{3,7},{4,0},{5,1},{6,2},{7,3},{8,12},{9,13},{10,... | collective-permute-start | bytes 98312 | tf_op jit(solution)/shard_map/ppermute | solution.py:429
  24.0 4.5 %collective-permute-start.7 = (bf16[64,256]{1,0:T(8,128)(2,1)S(1)}, bf16[64,256]{1,0:T(8,128)(2,1)S(1)}, u32[]{:S(2)}, u32[]{:S(2)}) collective-permute-start(bf16[64,256]{1,0:T(8,128)(2,1)S(1)} %query.2.refs_0_), channel_id=1, source_target_pairs={{0,2},{1,3},{2,0},{3,1},{4,6},{5,7},{6,4},{7,5},{8,10},{9,11},{10,... | collective-permute-start | bytes 98312 | tf_op jit(solution)/shard_map/ppermute | solution.py:429
  31.3 6.8 %collective-permute-start.11 = (f32[64,512]{1,0:T(8,128)S(1)}, f32[64,512]{1,0:T(8,128)S(1)}, u32[]{:S(2)}, u32[]{:S(2)}) collective-permute-start(f32[64,512]{1,0:T(8,128)S(1)} %get-tuple-element.43), channel_id=1, source_target_pairs={{0,24},{8,16},{16,8},{24,0},{1,25},{9,17},{17,9},{25,1},{2,26},{10... | collective-permute-start | bytes 393224 | tf_op jit(solution)/shard_map/ppermute | solution.py:429
  33.7 7.0 %collective-permute-start.12 = (f32[64,512]{1,0:T(8,128)S(1)}, f32[64,512]{1,0:T(8,128)S(1)}, u32[]{:S(2)}, u32[]{:S(2)}) collective-permute-start(f32[64,512]{1,0:T(8,128)S(1)} %get-tuple-element.44), channel_id=1, source_target_pairs={{0,16},{8,24},{16,0},{24,8},{1,17},{9,25},{17,1},{25,9},{2,18},{10... | collective-permute-start | bytes 393224 | tf_op jit(solution)/shard_map/ppermute | solution.py:429
  34.5 6.3 %collective-permute-start.13 = (f32[64,512]{1,0:T(8,128)S(1)}, f32[64,512]{1,0:T(8,128)S(1)}, u32[]{:S(2)}, u32[]{:S(2)}) collective-permute-start(f32[64,512]{1,0:T(8,128)S(1)} %get-tuple-element.45), channel_id=1, source_target_pairs={{0,8},{8,0},{16,24},{24,16},{1,9},{9,1},{17,25},{25,17},{2,10},{10... | collective-permute-start | bytes 393224 | tf_op jit(solution)/shard_map/ppermute | solution.py:429
  40.8 7.3 %collective-permute-start.16 = (f32[64,512]{1,0:T(8,128)S(1)}, f32[64,512]{1,0:T(8,128)S(1)}, u32[]{:S(2)}, u32[]{:S(2)}) collective-permute-start(f32[64,512]{1,0:T(8,128)S(1)} %lift.2.refs_0_), channel_id=1, source_target_pairs={{0,24},{8,16},{16,8},{24,0},{1,25},{9,17},{17,9},{25,1},{2,26},{10... | collective-permute-start | bytes 393224 | tf_op jit(solution)/shard_map/ppermute | solution.py:429
  42.6 7.3 %collective-permute-start.15 = (f32[64,512]{1,0:T(8,128)S(1)}, f32[64,512]{1,0:T(8,128)S(1)}, u32[]{:S(2)}, u32[]{:S(2)}) collective-permute-start(f32[64,512]{1,0:T(8,128)S(1)} %lift.2.refs_0_), channel_id=1, source_target_pairs={{0,16},{8,24},{16,0},{24,8},{1,17},{9,25},{17,1},{25,9},{2,18},{10... | collective-permute-start | bytes 393224 | tf_op jit(solution)/shard_map/ppermute | solution.py:429
  44.0 6.0 %collective-permute-start.14 = (f32[64,512]{1,0:T(8,128)S(1)}, f32[64,512]{1,0:T(8,128)S(1)}, u32[]{:S(2)}, u32[]{:S(2)}) collective-permute-start(f32[64,512]{1,0:T(8,128)S(1)} %lift.2.refs_0_), channel_id=1, source_target_pairs={{0,8},{8,0},{16,24},{24,16},{1,9},{9,1},{17,25},{25,17},{2,10},{10... | collective-permute-start | bytes 393224 | tf_op jit(solution)/shard_map/ppermute | solution.py:429
  51.9 2.1 %collective-permute-start.17 = (f32[272,256]{1,0:T(8,128)S(1)}, f32[272,256]{1,0:T(8,128)S(1)}, u32[]{:S(2)}, u32[]{:S(2)}) collective-permute-start(f32[272,256]{1,0:T(8,128)S(1)} %get-tuple-element.49), channel_id=1, source_target_pairs={{0,1},{1,0},{2,3},{3,2},{4,5},{5,4},{6,7},{7,6},{8,9},{9,8},{10,11... | collective-permute-start | bytes 835592 | tf_op jit(solution)/shard_map/ppermute | solution.py:429
  54.1 7.2 %collective-permute-start.18 = (f32[80,256]{1,0:T(8,128)S(1)}, f32[80,256]{1,0:T(8,128)S(1)}, u32[]{:S(2)}, u32[]{:S(2)}) collective-permute-start(f32[80,256]{1,0:T(8,128)S(1)} %get-tuple-element.52), channel_id=1, source_target_pairs={{0,6},{1,7},{2,4},{3,5},{4,2},{5,3},{6,0},{7,1},{8,14},{9,15},{10,... | collective-permute-start | bytes 245768 | tf_op jit(solution)/shard_map/ppermute | solution.py:429
  56.0 8.8 %collective-permute-start.19 = (f32[80,256]{1,0:T(8,128)S(1)}, f32[80,256]{1,0:T(8,128)S(1)}, u32[]{:S(2)}, u32[]{:S(2)}) collective-permute-start(f32[80,256]{1,0:T(8,128)S(1)} %get-tuple-element.53), channel_id=1, source_target_pairs={{0,4},{1,5},{2,6},{3,7},{4,0},{5,1},{6,2},{7,3},{8,12},{9,13},{10,... | collective-permute-start | bytes 245768 | tf_op jit(solution)/shard_map/ppermute | solution.py:429
  56.8 8.1 %collective-permute-start.20 = (f32[80,256]{1,0:T(8,128)S(1)}, f32[80,256]{1,0:T(8,128)S(1)}, u32[]{:S(2)}, u32[]{:S(2)}) collective-permute-start(f32[80,256]{1,0:T(8,128)S(1)} %get-tuple-element.54), channel_id=1, source_target_pairs={{0,2},{1,3},{2,0},{3,1},{4,6},{5,7},{6,4},{7,5},{8,10},{9,11},{10,... | collective-permute-start | bytes 245768 | tf_op jit(solution)/shard_map/ppermute | solution.py:429
  66.7 5.8 %collective-permute-start.23 = (bf16[64,256]{1,0:T(8,128)(2,1)S(1)}, bf16[64,256]{1,0:T(8,128)(2,1)S(1)}, u32[]{:S(2)}, u32[]{:S(2)}) collective-permute-start(bf16[64,256]{1,0:T(8,128)(2,1)S(1)} %query.3.refs_0_), channel_id=1, source_target_pairs={{0,6},{1,7},{2,4},{3,5},{4,2},{5,3},{6,0},{7,1},{8,14},{9,15},{10,... | collective-permute-start | bytes 98312 | tf_op jit(solution)/shard_map/ppermute | solution.py:429
  68.7 4.8 %collective-permute-start.22 = (bf16[64,256]{1,0:T(8,128)(2,1)S(1)}, bf16[64,256]{1,0:T(8,128)(2,1)S(1)}, u32[]{:S(2)}, u32[]{:S(2)}) collective-permute-start(bf16[64,256]{1,0:T(8,128)(2,1)S(1)} %query.3.refs_0_), channel_id=1, source_target_pairs={{0,4},{1,5},{2,6},{3,7},{4,0},{5,1},{6,2},{7,3},{8,12},{9,13},{10,... | collective-permute-start | bytes 98312 | tf_op jit(solution)/shard_map/ppermute | solution.py:429
  68.7 4.8 %collective-permute-start.21 = (bf16[64,256]{1,0:T(8,128)(2,1)S(1)}, bf16[64,256]{1,0:T(8,128)(2,1)S(1)}, u32[]{:S(2)}, u32[]{:S(2)}) collective-permute-start(bf16[64,256]{1,0:T(8,128)(2,1)S(1)} %query.3.refs_0_), channel_id=1, source_target_pairs={{0,2},{1,3},{2,0},{3,1},{4,6},{5,7},{6,4},{7,5},{8,10},{9,11},{10,... | collective-permute-start | bytes 98312 | tf_op jit(solution)/shard_map/ppermute | solution.py:429
  76.3 7.3 %collective-permute-start.25 = (f32[64,512]{1,0:T(8,128)S(1)}, f32[64,512]{1,0:T(8,128)S(1)}, u32[]{:S(2)}, u32[]{:S(2)}) collective-permute-start(f32[64,512]{1,0:T(8,128)S(1)} %get-tuple-element.56), channel_id=1, source_target_pairs={{0,24},{8,16},{16,8},{24,0},{1,25},{9,17},{17,9},{25,1},{2,26},{10... | collective-permute-start | bytes 393224 | tf_op jit(solution)/shard_map/ppermute | solution.py:429
  78.1 7.6 %collective-permute-start.26 = (f32[64,512]{1,0:T(8,128)S(1)}, f32[64,512]{1,0:T(8,128)S(1)}, u32[]{:S(2)}, u32[]{:S(2)}) collective-permute-start(f32[64,512]{1,0:T(8,128)S(1)} %get-tuple-element.57), channel_id=1, source_target_pairs={{0,16},{8,24},{16,0},{24,8},{1,17},{9,25},{17,1},{25,9},{2,18},{10... | collective-permute-start | bytes 393224 | tf_op jit(solution)/shard_map/ppermute | solution.py:429
  79.1 6.9 %collective-permute-start.27 = (f32[64,512]{1,0:T(8,128)S(1)}, f32[64,512]{1,0:T(8,128)S(1)}, u32[]{:S(2)}, u32[]{:S(2)}) collective-permute-start(f32[64,512]{1,0:T(8,128)S(1)} %get-tuple-element.58), channel_id=1, source_target_pairs={{0,8},{8,0},{16,24},{24,16},{1,9},{9,1},{17,25},{25,17},{2,10},{10... | collective-permute-start | bytes 393224 | tf_op jit(solution)/shard_map/ppermute | solution.py:429
  86.2 4.9 %collective-permute-start.30 = (f32[64,64]{1,0:T(8,128)S(1)}, f32[64,64]{1,0:T(8,128)S(1)}, u32[]{:S(2)}, u32[]{:S(2)}) collective-permute-start(f32[64,64]{1,0:T(8,128)S(1)} %get-tuple-element.59.refs_0_), channel_id=1, source_target_pairs={{0,24},{8,16},{16,8},{24,0},{1,25},{9,17},{17,9},{25,1},{2,26},{10... | collective-permute-start | bytes 49160 | tf_op jit(solution)/shard_map/ppermute | solution.py:429
  87.8 3.9 %collective-permute-start.29 = (f32[64,64]{1,0:T(8,128)S(1)}, f32[64,64]{1,0:T(8,128)S(1)}, u32[]{:S(2)}, u32[]{:S(2)}) collective-permute-start(f32[64,64]{1,0:T(8,128)S(1)} %get-tuple-element.59.refs_0_), channel_id=1, source_target_pairs={{0,16},{8,24},{16,0},{24,8},{1,17},{9,25},{17,1},{25,9},{2,18},{10... | collective-permute-start | bytes 49160 | tf_op jit(solution)/shard_map/ppermute | solution.py:429
  88.9 3.9 %collective-permute-start.28 = (f32[64,64]{1,0:T(8,128)S(1)}, f32[64,64]{1,0:T(8,128)S(1)}, u32[]{:S(2)}, u32[]{:S(2)}) collective-permute-start(f32[64,64]{1,0:T(8,128)S(1)} %get-tuple-element.59.refs_0_), channel_id=1, source_target_pairs={{0,8},{8,0},{16,24},{24,16},{1,9},{9,1},{17,25},{25,17},{2,10},{10... | collective-permute-start | bytes 49160 | tf_op jit(solution)/shard_map/ppermute | solution.py:429
  94.1 6.0 %collective-permute-start.34 = (f32[64,64]{1,0:T(8,128)S(1)}, f32[64,64]{1,0:T(8,128)S(1)}, u32[]{:S(2)}, u32[]{:S(2)}) collective-permute-start(f32[64,64]{1,0:T(8,128)S(1)} %sum.3.refs_0_), channel_id=1, source_target_pairs={{0,6},{1,7},{2,4},{3,5},{4,2},{5,3},{6,0},{7,1},{8,14},{9,15},{10,... | collective-permute-start | bytes 49160 | tf_op jit(solution)/shard_map/ppermute | solution.py:429
  96.3 5.0 %collective-permute-start.33 = (f32[64,64]{1,0:T(8,128)S(1)}, f32[64,64]{1,0:T(8,128)S(1)}, u32[]{:S(2)}, u32[]{:S(2)}) collective-permute-start(f32[64,64]{1,0:T(8,128)S(1)} %sum.3.refs_0_), channel_id=1, source_target_pairs={{0,4},{1,5},{2,6},{3,7},{4,0},{5,1},{6,2},{7,3},{8,12},{9,13},{10,... | collective-permute-start | bytes 49160 | tf_op jit(solution)/shard_map/ppermute | solution.py:429
  97.1 4.3 %collective-permute-start.32 = (f32[64,64]{1,0:T(8,128)S(1)}, f32[64,64]{1,0:T(8,128)S(1)}, u32[]{:S(2)}, u32[]{:S(2)}) collective-permute-start(f32[64,64]{1,0:T(8,128)S(1)} %sum.3.refs_0_), channel_id=1, source_target_pairs={{0,2},{1,3},{2,0},{3,1},{4,6},{5,7},{6,4},{7,5},{8,10},{9,11},{10,... | collective-permute-start | bytes 49160 | tf_op jit(solution)/shard_map/ppermute | solution.py:429
  (3 other events, 4.4 us)

commit v5 on v4

--- a/solution.py
+++ b/solution.py
@@ -11,6 +11,7 @@
 ITERS = 2
 GROUP = 8
 LOADS = 8
+SETS = 2
 PANEL_STEP = 8
 HIGH = lax.Precision.HIGHEST
 VMEM_BYTES = 12 * 1024 * 1024
@@ -76,45 +77,50 @@
     return jax.ShapeDtypeStruct(shape, jnp.bfloat16)
 
 
-def put(held, owner, value, side):
-    share = value.shape[1]
+def put(held, owner, value, side, row=0):
+    span, share = slice(row, row + value.shape[0]), value.shape[1]
     if share >= side:
         per = share // side
         for piece in range(per):
-            held[owner * per + piece] = value[:, piece * side : (piece + 1) * side]
+            held[owner * per + piece, span] = value[:, piece * side : (piece + 1) * side]
     else:
         per = side // share
         for at in range(per):
 
             @pl.when(owner % per == at)
             def _():
-                held[owner // per, :, at * share : (at + 1) * share] = value
-
-
-def get(total, owner, out_ref, side):
-    share = out_ref.shape[1]
+                held[owner // per, span, at * share : (at + 1) * share] = value
+
+
+def get(total, owner, out_ref, side, row=0):
+    span, share = slice(row, row + out_ref.shape[0]), out_ref.shape[1]
     if share >= side:
         per = share // side
         for piece in range(per):
-            out_ref[:, piece * side : (piece + 1) * side] = total[owner * per + piece].astype(out_ref.dtype)
+            out_ref[:, piece * side : (piece + 1) * side] = total[owner * per + piece, span].astype(out_ref.dtype)
     else:
         per = side // share
         for at in range(per):
 
             @pl.when(owner % per == at)
             def _():
-                out_ref[...] = total[owner // per, :, at * share : (at + 1) * share].astype(out_ref.dtype)
+                out_ref[...] = total[owner // per, span, at * share : (at + 1) * share].astype(out_ref.dtype)
 
 
 def emit(total, out_refs, me, side):
-    count = len(out_refs)
+    sets = total.shape[1] // out_refs[0].shape[0]
+    count = len(out_refs) // sets
     for at, out_ref in enumerate(out_refs):
-        get(total, me ^ ((count - at) % count), out_ref, side)
+        part, at = divmod(at, count)
+        get(total, me ^ ((count - at) % count), out_ref, side, part * out_ref.shape[0])
 
 
 def collect(held, piece_refs, me, side):
-    for step, piece_ref in enumerate(piece_refs):
-        put(held, me ^ step, piece_ref[...], side)
+    sets = held.shape[1] // piece_refs[0].shape[0]
+    count = len(piece_refs) // sets
+    for at, piece_ref in enumerate(piece_refs):
+        part, step = divmod(at, count)
+        put(held, me ^ step, piece_ref[...], side, part * piece_ref.shape[0])
 
 
 def products(which, take, give, dims, table, held, tile_ref, total):
@@ -233,9 +239,9 @@
         held[tile, :width] = high
         held[tile, width:] = (value - high.astype(jnp.float32)).astype(jnp.bfloat16)
     gram = jnp.zeros((width, width), jnp.float32)
-    for piece in pieces:
+    for tile in range(spread.shape[0]):
         gram = gram + lax.dot_general(
-            piece[...], piece[...], NT, precision=HIGH, preferred_element_type=jnp.float32
+            spread[tile], spread[tile], NT, precision=HIGH, preferred_element_type=jnp.float32
         )
     return gram
 
@@ -507,14 +513,15 @@
     product_scratch = pltpu.VMEM((product_tiles + 1, width, side), jnp.float32)
     query_held = pltpu.VMEM((query_tiles, width, side), jnp.bfloat16)
     for iteration in range(ITERS):
+        sets = SETS if iteration < ITERS - 1 else 1
         if iteration > 0:
-            pieces = spread_to(lifted, "row")
-            arrays = [WHOLE] * (n_row + 2)
+            pieces = [piece for part in lifted for piece in spread_to(part, "row")]
+            arrays = [WHOLE] * (len(pieces) + 2)
             message = f32(chips * width + gram_rows, columns)
             spread = pltpu.VMEM((product_tiles, width, side), jnp.float32)
             if split:
                 held, other, gram = call(
-                    functools.partial(next_other_body, n_row, chips),
+                    functools.partial(next_other_body, len(pieces), chips),
                     "forward",
                     [SCALARS] + arrays,
                     [bf16(product_tiles, 2 * width, side), message, f32(gram_rows, columns)],
@@ -532,7 +539,7 @@
                 )(table, held, tile_set)
             else:
                 mine, other, gram = call(
-                    functools.partial(next_body, n_row, chips),
+                    functools.partial(next_body, len(pieces), chips),
                     "forward",
                     [SCALARS] + arrays,
                     [f32(chips * width, columns), message, f32(gram_rows, columns)],
@@ -596,7 +603,7 @@
                 back_other_body,
                 "backward_rest",
                 [SCALARS] + [WHOLE] * 3,
-                [f32(width, share)] * n_row,
+                [f32(width // sets, share)] * (sets * n_row),
                 [query_held, product_scratch],
                 **half_work,
             )(table, there, begun, tile_set)
@@ -605,16 +612,19 @@
                 back_body,
                 "backward",
                 [SCALARS] + [WHOLE] * 3,
-                [f32(width, share)] * n_row,
+                [f32(width // sets, share)] * (sets * n_row),
                 [query_held, product_scratch],
                 **work,
             )(table, here, there, tile_set)
-        parts = deal(sums, "row")
+        parts = [deal(sums[n_row * part : n_row * (part + 1)], "row") for part in range(sets)]
         if iteration < ITERS - 1:
-            lifted = call(lift_only_body, "lift", [WHOLE] * (n_row + 1), f32(width, share))(*parts, my_pscale)
+            lifted = [
+                call(lift_only_body, "lift", [WHOLE] * (n_row + 1), f32(width // sets, share))(*part, my_pscale)
+                for part in parts
+            ]
     lifted, gram = call(
         lift_body, "lift", [WHOLE] * (n_row + 1), [f32(width, share), f32(width, width)]
-    )(*parts, my_pscale)
+    )(*parts[0], my_pscale)
     return call(
         functools.partial(finish_body, root_count), "finish", [WHOLE] * (chips + 1), f32(width, share)
     )(*terms_over_col(add_up(*spread_to(gram, "row"))), lifted)

time: 104 us -> 103 us (level)
  waiting for transfers between devices: 39.7 us -> 31.6 us
  starting transfers between devices: 41.4 us -> 48.8 us
    ppermute x35 -> x41, waiting for transfers between devices: 39.7 us -> 31.6 us  [swap(): lax.ppermute(value, axis, [(i, i ^ step) for i in range(lax.axis_size(axi...]
    ppermute x35 -> x41, starting transfers between devices: 41.4 us -> 48.8 us  [swap(): lax.ppermute(value, axis, [(i, i ^ step) for i in range(lax.axis_size(axi...]
    pallas_call x2 -> x3, Pallas kernels: 1.94 us -> 2.44 us  [the longest x1 2.41 us: shards(): call(functools.partial(next_other_body, len(pieces), chips), 'forward', [...]
  transfers between devices with their start and end apart: 35 -> 41, of which waited for: 25 -> 26; matrix products, arithmetic and copies ran while one was open for 0% -> 0% of each run, Pallas kernels for 10% -> 9%
where the time goes in v5:
time: 103 us
  starting transfers between devices  48.8 us (47%)
  waiting for transfers between devices  31.6 us (31%)
  Pallas kernels  21.9 us (21%)
    ppermute x41, starting transfers between devices, swap(): lax.ppermute(value, axis, [(i, i ^ step) for i in range(lax.axis_size(axi...  48.8 us
    ppermute x41, waiting for transfers between devices, swap(): lax.ppermute(value, axis, [(i, i ^ step) for i in range(lax.axis_size(axi...  31.6 us
    pallas_call x1, Pallas kernels, shards(): call(functools.partial(load_body, max(columns // side, 1)), 'load', [SCAL...  3.53 us
    pallas_call x2, Pallas kernels, shards(): call(back_other_body, 'backward_rest', [SCALARS] + [WHOLE] * 3, [f32(widt...  3.02 us
    pallas_call x1, Pallas kernels, shards(): call(functools.partial(finish_body, root_count), 'finish', [WHOLE] * (chi...  2.52 us
    pallas_call x1, Pallas kernels, shards(): call(functools.partial(next_other_body, len(pieces), chips), 'forward', [...  2.41 us
    pallas_call x2, Pallas kernels, shards(): call(functools.partial(back_mine_body, chips), 'backward', [SCALARS] + [W...  2.33 us
  transfers between devices with their start and end apart: 41, of which 26 were waited for; matrix products, arithmetic and copies ran while one was open for 0% of the time, Pallas kernels for 9%

profile of v5, /device:TPU:0, one launch (start us, length us, event | category | flops | bytes accessed | tf_op | source)
XLA Modules:
  0.0 103.2 jit_solution(17383115841316236410)
XLA Ops:
  1.0 4.0 %collective-permute-start.2 = (bf16[64,512]{1,0:T(8,128)(2,1)S(1)}, bf16[64,512]{1,0:T(8,128)(2,1)S(1)}, u32[]{:S(2)}, u32[]{:S(2)}) collective-permute-start(bf16[64,512]{1,0:T(8,128)(2,1)S(1)} %start.1.after_ref.refs_0_), channel_id=1, source_target_pairs={{0,24},{8,16},{16,8},{24,0},{1,25},{9,17},{17,9},{25,1},{2,26},{10... | collective-permute-start | bytes 196616 | tf_op jit(solution)/shard_map/ppermute | solution.py:435
  6.3 3.5 %load.1 = (bf16[32,256,256]{2,1,0:T(8,128)(2,1)S(1)}, f32[1,512]{1,0:T(1,128)S(1)}, f32[1,2048]{1,0:T(1,128)S(1)}, f32[1,256]{1,0:T(1,128)S(1)}, s32[16,32]{1,0:T(8,128)S(1)}) custom-call(s32[3]{0:T(128)S(1)} %pad_add_fusion.place, bf16[64,512]{1,0:T(8,128)(2,1)S(1)} %start.1.after_ref.refs_0_, bf16[32,256,256]{2,1,0:T(8,128)(2,1)} %bitcast.8, ...), custom_call_target="tpu_custom_call" | custom-call | bytes 8388608 | tf_op jit(solution)/shard_map/load/pallas_call | solution.py:480
  9.9 1.9 %forward.2 = (bf16[8,64,256]{2,1,0:T(8,128)(2,1)S(1)}, f32[4,64,256]{2,1,0:T(8,128)S(1)}) custom-call(s32[16,32]{1,0:T(8,128)S(1)} %get-tuple-element.37.table, bf16[64,512]{1,0:T(8,128)(2,1)S(1)} %start.1.after_ref.refs_0_, bf16[64,512]{1,0:T(8,128)(2,1)S(1)} %collective-permute-done.refs_1_, bf16[64,512]{1,0:T(8,128)(2,1)S(1)} %collective-permute-done.1.refs_2_, ...), custom_call_target="tpu_custom_call" | custom-call | flops 134217728 | bytes 2097152 | tf_op jit(solution)/shard_map/forward/pallas_call | solution.py:557
  11.8 1.5 %forward_rest.2.mine_ref = f32[4,64,256]{2,1,0:T(8,128)S(1)} custom-call(s32[16,32]{1,0:T(8,128)S(1)} %get-tuple-element.37.table, bf16[8,64,256]{2,1,0:T(8,128)(2,1)S(1)} %get-tuple-element.39.held, bf16[32,256,256]{2,1,0:T(8,128)(2,1)S(1)} %get-tuple-element.38.refs_4_.tile_ref.refs_9_), custom_call_target="tpu_custom_call" | custom-call | flops 134217728 | bytes 2097152 | tf_op jit(solution)/shard_map/forward_rest/pallas_call | solution.py:566
  13.4 3.6 %collective-permute-start.4 = (bf16[64,256]{1,0:T(8,128)(2,1)S(1)}, bf16[64,256]{1,0:T(8,128)(2,1)S(1)}, u32[]{:S(2)}, u32[]{:S(2)}) collective-permute-start(bf16[64,256]{1,0:T(8,128)(2,1)S(1)} %get-tuple-element.42), channel_id=1, source_target_pairs={{0,6},{1,7},{2,4},{3,5},{4,2},{5,3},{6,0},{7,1},{8,14},{9,15},{10,... | collective-permute-start | bytes 98312 | tf_op jit(solution)/shard_map/ppermute | solution.py:435
  19.2 2.6 %collective-permute-done.5.refs_2_ = bf16[64,256]{1,0:T(8,128)(2,1)S(1)} collective-permute-done((bf16[64,256]{1,0:T(8,128)(2,1)S(1)}, bf16[64,256]{1,0:T(8,128)(2,1)S(1)}, u32[]{:S(2)}, u32[]{:S(2)}) %collective-permute-start.5) | collective-permute-done | bytes 32800 | tf_op jit(solution)/shard_map/ppermute | solution.py:435
  21.9 1.7 %collective-permute-start.9 = (bf16[64,256]{1,0:T(8,128)(2,1)S(1)}, bf16[64,256]{1,0:T(8,128)(2,1)S(1)}, u32[]{:S(2)}, u32[]{:S(2)}) collective-permute-start(bf16[64,256]{1,0:T(8,128)(2,1)S(1)} %query.2.refs_0_), channel_id=1, source_target_pairs={{0,6},{1,7},{2,4},{3,5},{4,2},{5,3},{6,0},{7,1},{8,14},{9,15},{10,... | collective-permute-start | bytes 98312 | tf_op jit(solution)/shard_map/ppermute | solution.py:435
  24.0 2.3 %collective-permute-start.7 = (bf16[64,256]{1,0:T(8,128)(2,1)S(1)}, bf16[64,256]{1,0:T(8,128)(2,1)S(1)}, u32[]{:S(2)}, u32[]{:S(2)}) collective-permute-start(bf16[64,256]{1,0:T(8,128)(2,1)S(1)} %query.2.refs_0_), channel_id=1, source_target_pairs={{0,2},{1,3},{2,0},{3,1},{4,6},{5,7},{6,4},{7,5},{8,10},{9,11},{10,... | collective-permute-start | bytes 98312 | tf_op jit(solution)/shard_map/ppermute | solution.py:435
  26.3 1.4 %collective-permute-done.9.refs_3_ = bf16[64,256]{1,0:T(8,128)(2,1)S(1)} collective-permute-done((bf16[64,256]{1,0:T(8,128)(2,1)S(1)}, bf16[64,256]{1,0:T(8,128)(2,1)S(1)}, u32[]{:S(2)}, u32[]{:S(2)}) %collective-permute-start.9) | collective-permute-done | bytes 32800 | tf_op jit(solution)/shard_map/ppermute | solution.py:435
  30.0 1.5 %backward_rest.2 = (f32[32,512]{1,0:T(8,128)S(1)}, f32[32,512]{1,0:T(8,128)S(1)}, f32[32,512]{1,0:T(8,128)S(1)}, f32[32,512]{1,0:T(8,128)S(1)}, f32[32,512]{1,0:...) custom-call(s32[16,32]{1,0:T(8,128)S(1)} %get-tuple-element.37.table, ...), custom_call_target="tpu_custom_call" | custom-call | flops 134217728 | bytes 2097152 | tf_op jit(solution)/shard_map/backward_rest/pallas_call | solution.py:602
  31.5 2.2 %collective-permute-start.11 = (f32[32,512]{1,0:T(8,128)S(1)}, f32[32,512]{1,0:T(8,128)S(1)}, u32[]{:S(2)}, u32[]{:S(2)}) collective-permute-start(f32[32,512]{1,0:T(8,128)S(1)} %get-tuple-element.47), channel_id=1, source_target_pairs={{0,24},{8,16},{16,8},{24,0},{1,25},{9,17},{17,9},{25,1},{2,26},{10... | collective-permute-start | bytes 196616 | tf_op jit(solution)/shard_map/ppermute | solution.py:435
  35.1 2.2 %collective-permute-start.17 = (f32[32,512]{1,0:T(8,128)S(1)}, f32[32,512]{1,0:T(8,128)S(1)}, u32[]{:S(2)}, u32[]{:S(2)}) collective-permute-start(f32[32,512]{1,0:T(8,128)S(1)} %get-tuple-element.52), channel_id=1, source_target_pairs={{0,24},{8,16},{16,8},{24,0},{1,25},{9,17},{17,9},{25,1},{2,26},{10... | collective-permute-start | bytes 196616 | tf_op jit(solution)/shard_map/ppermute | solution.py:435
  39.3 1.5 %collective-permute-start.16 = (f32[32,512]{1,0:T(8,128)S(1)}, f32[32,512]{1,0:T(8,128)S(1)}, u32[]{:S(2)}, u32[]{:S(2)}) collective-permute-start(f32[32,512]{1,0:T(8,128)S(1)} %lift.3.refs_0_), channel_id=1, source_target_pairs={{0,24},{8,16},{16,8},{24,0},{1,25},{9,17},{17,9},{25,1},{2,26},{10... | collective-permute-start | bytes 196616 | tf_op jit(solution)/shard_map/ppermute | solution.py:435
  42.9 1.7 %collective-permute-start.22 = (f32[32,512]{1,0:T(8,128)S(1)}, f32[32,512]{1,0:T(8,128)S(1)}, u32[]{:S(2)}, u32[]{:S(2)}) collective-permute-start(f32[32,512]{1,0:T(8,128)S(1)} %lift.4.refs_4_), channel_id=1, source_target_pairs={{0,24},{8,16},{16,8},{24,0},{1,25},{9,17},{17,9},{25,1},{2,26},{10... | collective-permute-start | bytes 196616 | tf_op jit(solution)/shard_map/ppermute | solution.py:435
  46.6 1.5 %collective-permute-done.22.refs_7_ = f32[32,512]{1,0:T(8,128)S(1)} collective-permute-done((f32[32,512]{1,0:T(8,128)S(1)}, f32[32,512]{1,0:T(8,128)S(1)}, u32[]{:S(2)}, u32[]{:S(2)}) %collective-permute-start.22) | collective-permute-done | bytes 65568 | tf_op jit(solution)/shard_map/ppermute | solution.py:435
  49.8 2.4 %forward.3 = (bf16[8,128,256]{2,1,0:T(8,128)(2,1)S(1)}, f32[272,256]{1,0:T(8,128)S(1)}, f32[16,256]{1,0:T(8,128)S(1)}) custom-call(s32[16,32]{1,0:T(8,128)S(1)} %get-tuple-element.37.table, f32[32,512]{1,0:T(8,128)S(1)} %lift.3.refs_0_, f32[32,512]{1,0:T(8,128)S(1)} %collective-permute-done.14.refs_1_, f32[32,512]{1,0:T(8,128)S(1)} %collective-permute-done.15.refs_2_, ...), custom_call_target="tpu_custom_call" | custom-call | flops 134217728 | bytes 2097152 | tf_op jit(solution)/shard_map/forward/pallas_call | solution.py:523
  52.3 1.5 %forward_rest.3.mine_ref = f32[256,256]{1,0:T(8,128)S(1)} custom-call(s32[16,32]{1,0:T(8,128)S(1)} %get-tuple-element.37.table, bf16[8,128,256]{2,1,0:T(8,128)(2,1)S(1)} %get-tuple-element.56.held, bf16[32,256,256]{2,1,0:T(8,128)(2,1)S(1)} %get-tuple-element.38.refs_4_.tile_ref.refs_9_), custom_call_target="tpu_custom_call" | custom-call | flops 134217728 | bytes 2097152 | tf_op jit(solution)/shard_map/forward_rest/pallas_call | solution.py:532
  56.1 2.2 %collective-permute-start.26 = (f32[80,256]{1,0:T(8,128)S(1)}, f32[80,256]{1,0:T(8,128)S(1)}, u32[]{:S(2)}, u32[]{:S(2)}) collective-permute-start(f32[80,256]{1,0:T(8,128)S(1)} %get-tuple-element.62), channel_id=1, source_target_pairs={{0,2},{1,3},{2,0},{3,1},{4,6},{5,7},{6,4},{7,5},{8,10},{9,11},{10,... | collective-permute-start | bytes 245768 | tf_op jit(solution)/shard_map/ppermute | solution.py:435
  58.3 2.7 %collective-permute-done.24.refs_1_ = f32[80,256]{1,0:T(8,128)S(1)} collective-permute-done((f32[80,256]{1,0:T(8,128)S(1)}, f32[80,256]{1,0:T(8,128)S(1)}, u32[]{:S(2)}, u32[]{:S(2)}) %collective-permute-start.24) | collective-permute-done | bytes 81952 | tf_op jit(solution)/shard_map/ppermute | solution.py:435
  61.0 3.2 %collective-permute-done.25.refs_2_ = f32[80,256]{1,0:T(8,128)S(1)} collective-permute-done((f32[80,256]{1,0:T(8,128)S(1)}, f32[80,256]{1,0:T(8,128)S(1)}, u32[]{:S(2)}, u32[]{:S(2)}) %collective-permute-start.25) | collective-permute-done | bytes 81952 | tf_op jit(solution)/shard_map/ppermute | solution.py:435
  64.2 1.8 %query.3.refs_0_ = bf16[64,256]{1,0:T(8,128)(2,1)S(1)} custom-call(f32[80,256]{1,0:T(8,128)S(1)} %get-tuple-element.59.refs_0_, f32[80,256]{1,0:T(8,128)S(1)} %collective-permute-done.24.refs_1_, f32[80,256]{1,0:T(8,128)S(1)} %collective-permute-done.25.refs_2_, f32[80,256]{1,0:T(8,128)S(1)} %collective-permute-done.26.refs_3_, ...), custom_call_target="tpu_custom_call" | custom-call | tf_op jit(solution)/shard_map/query/pallas_call | solution.py:589
  66.0 1.8 %collective-permute-start.29 = (bf16[64,256]{1,0:T(8,128)(2,1)S(1)}, bf16[64,256]{1,0:T(8,128)(2,1)S(1)}, u32[]{:S(2)}, u32[]{:S(2)}) collective-permute-start(bf16[64,256]{1,0:T(8,128)(2,1)S(1)} %query.3.refs_0_), channel_id=1, source_target_pairs={{0,6},{1,7},{2,4},{3,5},{4,2},{5,3},{6,0},{7,1},{8,14},{9,15},{10,... | collective-permute-start | bytes 98312 | tf_op jit(solution)/shard_map/ppermute | solution.py:435
  67.8 2.7 %collective-permute-start.27 = (bf16[64,256]{1,0:T(8,128)(2,1)S(1)}, bf16[64,256]{1,0:T(8,128)(2,1)S(1)}, u32[]{:S(2)}, u32[]{:S(2)}) collective-permute-start(bf16[64,256]{1,0:T(8,128)(2,1)S(1)} %query.3.refs_0_), channel_id=1, source_target_pairs={{0,2},{1,3},{2,0},{3,1},{4,6},{5,7},{6,4},{7,5},{8,10},{9,11},{10,... | collective-permute-start | bytes 98312 | tf_op jit(solution)/shard_map/ppermute | solution.py:435
  74.2 1.5 %backward_rest.3 = (f32[64,512]{1,0:T(8,128)S(1)}, f32[64,512]{1,0:T(8,128)S(1)}, f32[64,512]{1,0:T(8,128)S(1)}, f32[64,512]{1,0:T(8,128)S(1)}) custom-call(s32[16,32]{1,0:T(8,128)S(1)} %get-tuple-element.37.table, bf16[4,64,256]{2,1,0:T(8,128)(2,1)S(1)} %collective-permute-done.30.there_ref, f32[9,64,256]{2,1,0:T(8,128)S(1)} %backward.3.begun_ref, ...), custom_call_target="tpu_custom_call" | custom-call | flops 134217728 | bytes 2097152 | tf_op jit(solution)/shard_map/backward_rest/pallas_call | solution.py:602
  75.7 1.7 %collective-permute-start.31 = (f32[64,512]{1,0:T(8,128)S(1)}, f32[64,512]{1,0:T(8,128)S(1)}, u32[]{:S(2)}, u32[]{:S(2)}) collective-permute-start(f32[64,512]{1,0:T(8,128)S(1)} %get-tuple-element.64), channel_id=1, source_target_pairs={{0,24},{8,16},{16,8},{24,0},{1,25},{9,17},{17,9},{25,1},{2,26},{10... | collective-permute-start | bytes 393224 | tf_op jit(solution)/shard_map/ppermute | solution.py:435
  79.3 3.3 %collective-permute-done.31.refs_1_ = f32[64,512]{1,0:T(8,128)S(1)} collective-permute-done((f32[64,512]{1,0:T(8,128)S(1)}, f32[64,512]{1,0:T(8,128)S(1)}, u32[]{:S(2)}, u32[]{:S(2)}) %collective-permute-start.31) | collective-permute-done | bytes 131104 | tf_op jit(solution)/shard_map/ppermute | solution.py:435
  82.6 2.3 %collective-permute-done.32.refs_2_ = f32[64,512]{1,0:T(8,128)S(1)} collective-permute-done((f32[64,512]{1,0:T(8,128)S(1)}, f32[64,512]{1,0:T(8,128)S(1)}, u32[]{:S(2)}, u32[]{:S(2)}) %collective-permute-start.32) | collective-permute-done | bytes 131104 | tf_op jit(solution)/shard_map/ppermute | solution.py:435
  85.3 1.7 %collective-permute-start.36 = (f32[64,64]{1,0:T(8,128)S(1)}, f32[64,64]{1,0:T(8,128)S(1)}, u32[]{:S(2)}, u32[]{:S(2)}) collective-permute-start(f32[64,64]{1,0:T(8,128)S(1)} %get-tuple-element.67.refs_0_), channel_id=1, source_target_pairs={{0,24},{8,16},{16,8},{24,0},{1,25},{9,17},{17,9},{25,1},{2,26},{10... | collective-permute-start | bytes 49160 | tf_op jit(solution)/shard_map/ppermute | solution.py:435
  88.9 1.5 %collective-permute-done.36.refs_3_ = f32[64,64]{1,0:T(8,128)S(1)} collective-permute-done((f32[64,64]{1,0:T(8,128)S(1)}, f32[64,64]{1,0:T(8,128)S(1)}, u32[]{:S(2)}, u32[]{:S(2)}) %collective-permute-start.36) | collective-permute-done | bytes 16416 | tf_op jit(solution)/shard_map/ppermute | solution.py:435
  93.3 1.8 %collective-permute-start.40 = (f32[64,64]{1,0:T(8,128)S(1)}, f32[64,64]{1,0:T(8,128)S(1)}, u32[]{:S(2)}, u32[]{:S(2)}) collective-permute-start(f32[64,64]{1,0:T(8,128)S(1)} %sum.3.refs_0_), channel_id=1, source_target_pairs={{0,6},{1,7},{2,4},{3,5},{4,2},{5,3},{6,0},{7,1},{8,14},{9,15},{10,... | collective-permute-start | bytes 49160 | tf_op jit(solution)/shard_map/ppermute | solution.py:435
  97.7 1.5 %collective-permute-done.40.refs_3_ = f32[64,64]{1,0:T(8,128)S(1)} collective-permute-done((f32[64,64]{1,0:T(8,128)S(1)}, f32[64,64]{1,0:T(8,128)S(1)}, u32[]{:S(2)}, u32[]{:S(2)}) %collective-permute-start.40) | collective-permute-done | bytes 16416 | tf_op jit(solution)/shard_map/ppermute | solution.py:435
  100.7 2.5 %finish.1 = f32[64,512]{1,0:T(8,128)} custom-call(f32[64,64]{1,0:T(8,128)S(1)} %sum.3.refs_0_, f32[64,64]{1,0:T(8,128)S(1)} %collective-permute-done.38.refs_1_, f32[64,64]{1,0:T(8,128)S(1)} %collective-permute-done.39.refs_2_, f32[64,64]{1,0:T(8,128)S(1)} %collective-permute-done.40.refs_3_, f32[64,512]{1,0:T(8,128)S(1)} %get-tuple-element.68.refs_4_), custom_call_target="tpu_custom_call" | custom-call | tf_op jit(solution)/shard_map/finish/pallas_call | solution.py:628
  (73 shorter events, 33.1 us)
Async XLA Ops:
  1.0 8.9 %collective-permute-start.2 = (bf16[64,512]{1,0:T(8,128)(2,1)S(1)}, bf16[64,512]{1,0:T(8,128)(2,1)S(1)}, u32[]{:S(2)}, u32[]{:S(2)}) collective-permute-start(bf16[64,512]{1,0:T(8,128)(2,1)S(1)} %start.1.after_ref.refs_0_), channel_id=1, source_target_pairs={{0,24},{8,16},{16,8},{24,0},{1,25},{9,17},{17,9},{25,1},{2,26},{10... | collective-permute-start | bytes 196616 | tf_op jit(solution)/shard_map/ppermute | solution.py:435
  4.9 4.9 %collective-permute-start.1 = (bf16[64,512]{1,0:T(8,128)(2,1)S(1)}, bf16[64,512]{1,0:T(8,128)(2,1)S(1)}, u32[]{:S(2)}, u32[]{:S(2)}) collective-permute-start(bf16[64,512]{1,0:T(8,128)(2,1)S(1)} %start.1.after_ref.refs_0_), channel_id=1, source_target_pairs={{0,16},{8,24},{16,0},{24,8},{1,17},{9,25},{17,1},{25,9},{2,18},{10... | collective-permute-start | bytes 196616 | tf_op jit(solution)/shard_map/ppermute | solution.py:435
  5.4 4.4 %collective-permute-start = (bf16[64,512]{1,0:T(8,128)(2,1)S(1)}, bf16[64,512]{1,0:T(8,128)(2,1)S(1)}, u32[]{:S(2)}, u32[]{:S(2)}) collective-permute-start(bf16[64,512]{1,0:T(8,128)(2,1)S(1)} %start.1.after_ref.refs_0_), channel_id=1, source_target_pairs={{0,8},{8,0},{16,24},{24,16},{1,9},{9,1},{17,25},{25,17},{2,10},{10... | collective-permute-start | bytes 196616 | tf_op jit(solution)/shard_map/ppermute | solution.py:435
  13.4 5.8 %collective-permute-start.4 = (bf16[64,256]{1,0:T(8,128)(2,1)S(1)}, bf16[64,256]{1,0:T(8,128)(2,1)S(1)}, u32[]{:S(2)}, u32[]{:S(2)}) collective-permute-start(bf16[64,256]{1,0:T(8,128)(2,1)S(1)} %get-tuple-element.42), channel_id=1, source_target_pairs={{0,6},{1,7},{2,4},{3,5},{4,2},{5,3},{6,0},{7,1},{8,14},{9,15},{10,... | collective-permute-start | bytes 98312 | tf_op jit(solution)/shard_map/ppermute | solution.py:435
  17.0 4.8 %collective-permute-start.5 = (bf16[64,256]{1,0:T(8,128)(2,1)S(1)}, bf16[64,256]{1,0:T(8,128)(2,1)S(1)}, u32[]{:S(2)}, u32[]{:S(2)}) collective-permute-start(bf16[64,256]{1,0:T(8,128)(2,1)S(1)} %get-tuple-element.43), channel_id=1, source_target_pairs={{0,4},{1,5},{2,6},{3,7},{4,0},{5,1},{6,2},{7,3},{8,12},{9,13},{10,... | collective-permute-start | bytes 98312 | tf_op jit(solution)/shard_map/ppermute | solution.py:435
  17.0 4.8 %collective-permute-start.6 = (bf16[64,256]{1,0:T(8,128)(2,1)S(1)}, bf16[64,256]{1,0:T(8,128)(2,1)S(1)}, u32[]{:S(2)}, u32[]{:S(2)}) collective-permute-start(bf16[64,256]{1,0:T(8,128)(2,1)S(1)} %get-tuple-element.44), channel_id=1, source_target_pairs={{0,2},{1,3},{2,0},{3,1},{4,6},{5,7},{6,4},{7,5},{8,10},{9,11},{10,... | collective-permute-start | bytes 98312 | tf_op jit(solution)/shard_map/ppermute | solution.py:435
  21.9 5.9 %collective-permute-start.9 = (bf16[64,256]{1,0:T(8,128)(2,1)S(1)}, bf16[64,256]{1,0:T(8,128)(2,1)S(1)}, u32[]{:S(2)}, u32[]{:S(2)}) collective-permute-start(bf16[64,256]{1,0:T(8,128)(2,1)S(1)} %query.2.refs_0_), channel_id=1, source_target_pairs={{0,6},{1,7},{2,4},{3,5},{4,2},{5,3},{6,0},{7,1},{8,14},{9,15},{10,... | collective-permute-start | bytes 98312 | tf_op jit(solution)/shard_map/ppermute | solution.py:435
  23.6 4.9 %collective-permute-start.8 = (bf16[64,256]{1,0:T(8,128)(2,1)S(1)}, bf16[64,256]{1,0:T(8,128)(2,1)S(1)}, u32[]{:S(2)}, u32[]{:S(2)}) collective-permute-start(bf16[64,256]{1,0:T(8,128)(2,1)S(1)} %query.2.refs_0_), channel_id=1, source_target_pairs={{0,4},{1,5},{2,6},{3,7},{4,0},{5,1},{6,2},{7,3},{8,12},{9,13},{10,... | collective-permute-start | bytes 98312 | tf_op jit(solution)/shard_map/ppermute | solution.py:435
  24.0 4.5 %collective-permute-start.7 = (bf16[64,256]{1,0:T(8,128)(2,1)S(1)}, bf16[64,256]{1,0:T(8,128)(2,1)S(1)}, u32[]{:S(2)}, u32[]{:S(2)}) collective-permute-start(bf16[64,256]{1,0:T(8,128)(2,1)S(1)} %query.2.refs_0_), channel_id=1, source_target_pairs={{0,2},{1,3},{2,0},{3,1},{4,6},{5,7},{6,4},{7,5},{8,10},{9,11},{10,... | collective-permute-start | bytes 98312 | tf_op jit(solution)/shard_map/ppermute | solution.py:435
  31.5 6.8 %collective-permute-start.11 = (f32[32,512]{1,0:T(8,128)S(1)}, f32[32,512]{1,0:T(8,128)S(1)}, u32[]{:S(2)}, u32[]{:S(2)}) collective-permute-start(f32[32,512]{1,0:T(8,128)S(1)} %get-tuple-element.47), channel_id=1, source_target_pairs={{0,24},{8,16},{16,8},{24,0},{1,25},{9,17},{17,9},{25,1},{2,26},{10... | collective-permute-start | bytes 196616 | tf_op jit(solution)/shard_map/ppermute | solution.py:435
  33.7 5.2 %collective-permute-start.12 = (f32[32,512]{1,0:T(8,128)S(1)}, f32[32,512]{1,0:T(8,128)S(1)}, u32[]{:S(2)}, u32[]{:S(2)}) collective-permute-start(f32[32,512]{1,0:T(8,128)S(1)} %get-tuple-element.48), channel_id=1, source_target_pairs={{0,16},{8,24},{16,0},{24,8},{1,17},{9,25},{17,1},{25,9},{2,18},{10... | collective-permute-start | bytes 196616 | tf_op jit(solution)/shard_map/ppermute | solution.py:435
  34.8 4.4 %collective-permute-start.13 = (f32[32,512]{1,0:T(8,128)S(1)}, f32[32,512]{1,0:T(8,128)S(1)}, u32[]{:S(2)}, u32[]{:S(2)}) collective-permute-start(f32[32,512]{1,0:T(8,128)S(1)} %get-tuple-element.49), channel_id=1, source_target_pairs={{0,8},{8,0},{16,24},{24,16},{1,9},{9,1},{17,25},{25,17},{2,10},{10... | collective-permute-start | bytes 196616 | tf_op jit(solution)/shard_map/ppermute | solution.py:435
  35.1 6.9 %collective-permute-start.17 = (f32[32,512]{1,0:T(8,128)S(1)}, f32[32,512]{1,0:T(8,128)S(1)}, u32[]{:S(2)}, u32[]{:S(2)}) collective-permute-start(f32[32,512]{1,0:T(8,128)S(1)} %get-tuple-element.52), channel_id=1, source_target_pairs={{0,24},{8,16},{16,8},{24,0},{1,25},{9,17},{17,9},{25,1},{2,26},{10... | collective-permute-start | bytes 196616 | tf_op jit(solution)/shard_map/ppermute | solution.py:435
  37.2 5.6 %collective-permute-start.18 = (f32[32,512]{1,0:T(8,128)S(1)}, f32[32,512]{1,0:T(8,128)S(1)}, u32[]{:S(2)}, u32[]{:S(2)}) collective-permute-start(f32[32,512]{1,0:T(8,128)S(1)} %get-tuple-element.53), channel_id=1, source_target_pairs={{0,16},{8,24},{16,0},{24,8},{1,17},{9,25},{17,1},{25,9},{2,18},{10... | collective-permute-start | bytes 196616 | tf_op jit(solution)/shard_map/ppermute | solution.py:435
  38.3 4.5 %collective-permute-start.19 = (f32[32,512]{1,0:T(8,128)S(1)}, f32[32,512]{1,0:T(8,128)S(1)}, u32[]{:S(2)}, u32[]{:S(2)}) collective-permute-start(f32[32,512]{1,0:T(8,128)S(1)} %get-tuple-element.54), channel_id=1, source_target_pairs={{0,8},{8,0},{16,24},{24,16},{1,9},{9,1},{17,25},{25,17},{2,10},{10... | collective-permute-start | bytes 196616 | tf_op jit(solution)/shard_map/ppermute | solution.py:435
  39.3 6.2 %collective-permute-start.16 = (f32[32,512]{1,0:T(8,128)S(1)}, f32[32,512]{1,0:T(8,128)S(1)}, u32[]{:S(2)}, u32[]{:S(2)}) collective-permute-start(f32[32,512]{1,0:T(8,128)S(1)} %lift.3.refs_0_), channel_id=1, source_target_pairs={{0,24},{8,16},{16,8},{24,0},{1,25},{9,17},{17,9},{25,1},{2,26},{10... | collective-permute-start | bytes 196616 | tf_op jit(solution)/shard_map/ppermute | solution.py:435
  40.8 5.8 %collective-permute-start.15 = (f32[32,512]{1,0:T(8,128)S(1)}, f32[32,512]{1,0:T(8,128)S(1)}, u32[]{:S(2)}, u32[]{:S(2)}) collective-permute-start(f32[32,512]{1,0:T(8,128)S(1)} %lift.3.refs_0_), channel_id=1, source_target_pairs={{0,16},{8,24},{16,0},{24,8},{1,17},{9,25},{17,1},{25,9},{2,18},{10... | collective-permute-start | bytes 196616 | tf_op jit(solution)/shard_map/ppermute | solution.py:435
  41.9 4.7 %collective-permute-start.14 = (f32[32,512]{1,0:T(8,128)S(1)}, f32[32,512]{1,0:T(8,128)S(1)}, u32[]{:S(2)}, u32[]{:S(2)}) collective-permute-start(f32[32,512]{1,0:T(8,128)S(1)} %lift.3.refs_0_), channel_id=1, source_target_pairs={{0,8},{8,0},{16,24},{24,16},{1,9},{9,1},{17,25},{25,17},{2,10},{10... | collective-permute-start | bytes 196616 | tf_op jit(solution)/shard_map/ppermute | solution.py:435
  42.9 5.2 %collective-permute-start.22 = (f32[32,512]{1,0:T(8,128)S(1)}, f32[32,512]{1,0:T(8,128)S(1)}, u32[]{:S(2)}, u32[]{:S(2)}) collective-permute-start(f32[32,512]{1,0:T(8,128)S(1)} %lift.4.refs_4_), channel_id=1, source_target_pairs={{0,24},{8,16},{16,8},{24,0},{1,25},{9,17},{17,9},{25,1},{2,26},{10... | collective-permute-start | bytes 196616 | tf_op jit(solution)/shard_map/ppermute | solution.py:435
  44.6 4.3 %collective-permute-start.21 = (f32[32,512]{1,0:T(8,128)S(1)}, f32[32,512]{1,0:T(8,128)S(1)}, u32[]{:S(2)}, u32[]{:S(2)}) collective-permute-start(f32[32,512]{1,0:T(8,128)S(1)} %lift.4.refs_4_), channel_id=1, source_target_pairs={{0,16},{8,24},{16,0},{24,8},{1,17},{9,25},{17,1},{25,9},{2,18},{10... | collective-permute-start | bytes 196616 | tf_op jit(solution)/shard_map/ppermute | solution.py:435
  53.8 7.2 %collective-permute-start.24 = (f32[80,256]{1,0:T(8,128)S(1)}, f32[80,256]{1,0:T(8,128)S(1)}, u32[]{:S(2)}, u32[]{:S(2)}) collective-permute-start(f32[80,256]{1,0:T(8,128)S(1)} %get-tuple-element.60), channel_id=1, source_target_pairs={{0,6},{1,7},{2,4},{3,5},{4,2},{5,3},{6,0},{7,1},{8,14},{9,15},{10,... | collective-permute-start | bytes 245768 | tf_op jit(solution)/shard_map/ppermute | solution.py:435
  55.1 9.1 %collective-permute-start.25 = (f32[80,256]{1,0:T(8,128)S(1)}, f32[80,256]{1,0:T(8,128)S(1)}, u32[]{:S(2)}, u32[]{:S(2)}) collective-permute-start(f32[80,256]{1,0:T(8,128)S(1)} %get-tuple-element.61), channel_id=1, source_target_pairs={{0,4},{1,5},{2,6},{3,7},{4,0},{5,1},{6,2},{7,3},{8,12},{9,13},{10,... | collective-permute-start | bytes 245768 | tf_op jit(solution)/shard_map/ppermute | solution.py:435
  56.1 8.1 %collective-permute-start.26 = (f32[80,256]{1,0:T(8,128)S(1)}, f32[80,256]{1,0:T(8,128)S(1)}, u32[]{:S(2)}, u32[]{:S(2)}) collective-permute-start(f32[80,256]{1,0:T(8,128)S(1)} %get-tuple-element.62), channel_id=1, source_target_pairs={{0,2},{1,3},{2,0},{3,1},{4,6},{5,7},{6,4},{7,5},{8,10},{9,11},{10,... | collective-permute-start | bytes 245768 | tf_op jit(solution)/shard_map/ppermute | solution.py:435
  66.0 5.8 %collective-permute-start.29 = (bf16[64,256]{1,0:T(8,128)(2,1)S(1)}, bf16[64,256]{1,0:T(8,128)(2,1)S(1)}, u32[]{:S(2)}, u32[]{:S(2)}) collective-permute-start(bf16[64,256]{1,0:T(8,128)(2,1)S(1)} %query.3.refs_0_), channel_id=1, source_target_pairs={{0,6},{1,7},{2,4},{3,5},{4,2},{5,3},{6,0},{7,1},{8,14},{9,15},{10,... | collective-permute-start | bytes 98312 | tf_op jit(solution)/shard_map/ppermute | solution.py:435
  67.8 4.9 %collective-permute-start.28 = (bf16[64,256]{1,0:T(8,128)(2,1)S(1)}, bf16[64,256]{1,0:T(8,128)(2,1)S(1)}, u32[]{:S(2)}, u32[]{:S(2)}) collective-permute-start(bf16[64,256]{1,0:T(8,128)(2,1)S(1)} %query.3.refs_0_), channel_id=1, source_target_pairs={{0,4},{1,5},{2,6},{3,7},{4,0},{5,1},{6,2},{7,3},{8,12},{9,13},{10,... | collective-permute-start | bytes 98312 | tf_op jit(solution)/shard_map/ppermute | solution.py:435
  67.8 4.9 %collective-permute-start.27 = (bf16[64,256]{1,0:T(8,128)(2,1)S(1)}, bf16[64,256]{1,0:T(8,128)(2,1)S(1)}, u32[]{:S(2)}, u32[]{:S(2)}) collective-permute-start(bf16[64,256]{1,0:T(8,128)(2,1)S(1)} %query.3.refs_0_), channel_id=1, source_target_pairs={{0,2},{1,3},{2,0},{3,1},{4,6},{5,7},{6,4},{7,5},{8,10},{9,11},{10,... | collective-permute-start | bytes 98312 | tf_op jit(solution)/shard_map/ppermute | solution.py:435
  75.7 6.9 %collective-permute-start.31 = (f32[64,512]{1,0:T(8,128)S(1)}, f32[64,512]{1,0:T(8,128)S(1)}, u32[]{:S(2)}, u32[]{:S(2)}) collective-permute-start(f32[64,512]{1,0:T(8,128)S(1)} %get-tuple-element.64), channel_id=1, source_target_pairs={{0,24},{8,16},{16,8},{24,0},{1,25},{9,17},{17,9},{25,1},{2,26},{10... | collective-permute-start | bytes 393224 | tf_op jit(solution)/shard_map/ppermute | solution.py:435
  77.4 7.5 %collective-permute-start.32 = (f32[64,512]{1,0:T(8,128)S(1)}, f32[64,512]{1,0:T(8,128)S(1)}, u32[]{:S(2)}, u32[]{:S(2)}) collective-permute-start(f32[64,512]{1,0:T(8,128)S(1)} %get-tuple-element.65), channel_id=1, source_target_pairs={{0,16},{8,24},{16,0},{24,8},{1,17},{9,25},{17,1},{25,9},{2,18},{10... | collective-permute-start | bytes 393224 | tf_op jit(solution)/shard_map/ppermute | solution.py:435
  78.4 6.6 %collective-permute-start.33 = (f32[64,512]{1,0:T(8,128)S(1)}, f32[64,512]{1,0:T(8,128)S(1)}, u32[]{:S(2)}, u32[]{:S(2)}) collective-permute-start(f32[64,512]{1,0:T(8,128)S(1)} %get-tuple-element.66), channel_id=1, source_target_pairs={{0,8},{8,0},{16,24},{24,16},{1,9},{9,1},{17,25},{25,17},{2,10},{10... | collective-permute-start | bytes 393224 | tf_op jit(solution)/shard_map/ppermute | solution.py:435
  85.3 5.1 %collective-permute-start.36 = (f32[64,64]{1,0:T(8,128)S(1)}, f32[64,64]{1,0:T(8,128)S(1)}, u32[]{:S(2)}, u32[]{:S(2)}) collective-permute-start(f32[64,64]{1,0:T(8,128)S(1)} %get-tuple-element.67.refs_0_), channel_id=1, source_target_pairs={{0,24},{8,16},{16,8},{24,0},{1,25},{9,17},{17,9},{25,1},{2,26},{10... | collective-permute-start | bytes 49160 | tf_op jit(solution)/shard_map/ppermute | solution.py:435
  93.3 5.9 %collective-permute-start.40 = (f32[64,64]{1,0:T(8,128)S(1)}, f32[64,64]{1,0:T(8,128)S(1)}, u32[]{:S(2)}, u32[]{:S(2)}) collective-permute-start(f32[64,64]{1,0:T(8,128)S(1)} %sum.3.refs_0_), channel_id=1, source_target_pairs={{0,6},{1,7},{2,4},{3,5},{4,2},{5,3},{6,0},{7,1},{8,14},{9,15},{10,... | collective-permute-start | bytes 49160 | tf_op jit(solution)/shard_map/ppermute | solution.py:435
  95.1 5.3 %collective-permute-start.39 = (f32[64,64]{1,0:T(8,128)S(1)}, f32[64,64]{1,0:T(8,128)S(1)}, u32[]{:S(2)}, u32[]{:S(2)}) collective-permute-start(f32[64,64]{1,0:T(8,128)S(1)} %sum.3.refs_0_), channel_id=1, source_target_pairs={{0,4},{1,5},{2,6},{3,7},{4,0},{5,1},{6,2},{7,3},{8,12},{9,13},{10,... | collective-permute-start | bytes 49160 | tf_op jit(solution)/shard_map/ppermute | solution.py:435
  (9 other events, 23.6 us)

commit v6 on v5

--- a/solution.py
+++ b/solution.py
@@ -282,14 +282,36 @@
     emit_rows(total, mine_ref, chips, me, side, 0)
 
 
-def next_pair_body(width, mine_ref, got_ref, gram_ref, *outs):
-    count = len(outs)
-    gram = gram_ref[...] + got_ref[count * width :]
+def next_pair_body(width, chips, mine_ref, got_ref, gram_ref, *outs):
+    columns = outs[0].shape[1]
+    gram = pack_gram(unpack_gram(gram_ref[...] + got_ref[chips * width :], width), columns)
     for at, out_ref in enumerate(outs):
-        step = (count - at) % count
-        span = slice(step * width, (step + 1) * width)
-        out_ref[:width] = mine_ref[span] + got_ref[span]
-        out_ref[width:] = gram
+        part, at = divmod(at, chips)
+        step = (chips - at) % chips
+        block = slice(step * width, (step + 1) * width), slice(part * columns, (part + 1) * columns)
+        out_ref[:width] = mine_ref[block] + got_ref[block]
+        if part == 0:
+            out_ref[width:] = gram
+
+
+def factor_query_body(*refs):
+    part_refs, scale_ref, inverse_ref, out_ref = refs[:-3], refs[-3], refs[-2], refs[-1]
+    width, columns = out_ref.shape
+    total = add(part_refs)
+    inverse = inverse_factor(unpack_gram(total[width:], width))
+    inverse_ref[...] = inverse
+    current = lax.dot_general(inverse, total[:width], NN, precision=HIGH, preferred_element_type=jnp.float32)
+    out_ref[...] = (current * scale_ref[:, :columns]).astype(out_ref.dtype)
+
+
+def rest_query_body(*refs):
+    part_refs, inverse_ref, begun_ref, scale_ref, out_ref = refs[:-4], *refs[-4:]
+    columns = begun_ref.shape[1]
+    current = lax.dot_general(
+        inverse_ref[...], add(part_refs), NN, precision=HIGH, preferred_element_type=jnp.float32
+    )
+    out_ref[:, :columns] = begun_ref[...]
+    out_ref[:, columns:] = (current * scale_ref[:, columns:]).astype(out_ref.dtype)
 
 
 def next_query_body(*refs):
@@ -547,12 +569,29 @@
                     **work,
                 )(table, *pieces, pscale, tile_set)
                 got = swap(other, "col", 1)
+            halves = 2 if columns % 256 == 0 else 1
+            span = columns // halves
+            shapes = [f32(width + width * width // span, span)] * chips + [f32(width, span)] * chips
             sums = call(
-                functools.partial(next_pair_body, width),
-                "pair",
-                [WHOLE] * 3,
-                [f32(width + gram_rows, columns)] * chips,
+                functools.partial(next_pair_body, width, chips), "pair", [WHOLE] * 3, shapes[: halves * chips]
             )(mine, got, gram)
+            parts = deal(sums[:chips], "col", 2)
+            if halves == 1:
+                rounded = call(next_query_body, "query", [WHOLE] * (chips + 1), bf16(width, columns))(
+                    *parts, my_qscale
+                )
+            else:
+                more = deal(sums[chips:], "col", 2)
+                inverse, begun = call(
+                    factor_query_body,
+                    "query",
+                    [WHOLE] * (chips + 1),
+                    [f32(width, width), bf16(width, span)],
+                    flops=2 * slots * width * side * side,
+                )(*parts, my_qscale)
+                rounded = call(rest_query_body, "query_rest", [WHOLE] * (chips + 3), bf16(width, columns))(
+                    *more, inverse, begun, my_qscale
+                )
         elif split:
             held, other = call(
                 functools.partial(forward_other_body, n_row),
@@ -585,8 +624,8 @@
             sums = call(
                 pair_body, "pair", [WHOLE] * 2, [f32(width, columns)] + [bf16(width, columns)] * (chips - 1)
             )(mine, got)
-        parts = deal(sums, "col", 2)
-        rounded = call(next_query_body if iteration else query_body, "query", [WHOLE] * (chips + 1), bf16(width, columns))(*parts, my_qscale)
+            parts = deal(sums, "col", 2)
+            rounded = call(query_body, "query", [WHOLE] * (chips + 1), bf16(width, columns))(*parts, my_qscale)
         pieces = spread_to(rounded, "col", 2)
         here = call(join_body, "join", [WHOLE] * chips, bf16(chips, width, columns))(*pieces)
         there = swap(here, "col", 1)

time: 103 us -> 102 us (level)
  waiting for transfers between devices: 31.6 us -> 26.1 us
  starting transfers between devices: 48.8 us -> 52.7 us
    ppermute x41 -> x44, waiting for transfers between devices: 31.6 us -> 26.1 us  [swap(): lax.ppermute(value, axis, [(i, i ^ step) for i in range(lax.axis_size(axi...]
    ppermute x41 -> x44, starting transfers between devices: 48.8 us -> 52.7 us  [swap(): lax.ppermute(value, axis, [(i, i ^ step) for i in range(lax.axis_size(axi...]
    pallas_call x3 -> x4, Pallas kernels: 1.87 us -> 2.11 us  [the longest x1 1.79 us: shards(): call(factor_query_body, 'query', [WHOLE] * (chips + 1), [f32(width, width...]
  transfers between devices with their start and end apart: 41 -> 44, of which waited for: 26 -> 25; matrix products, arithmetic and copies ran while one was open for 0% -> 0% of each run, Pallas kernels for 9% -> 12%
where the time goes in v6:
time: 102 us
  starting transfers between devices  52.7 us (52%)
  waiting for transfers between devices  26.1 us (26%)
  Pallas kernels  22.1 us (22%)
    ppermute x44, starting transfers between devices, swap(): lax.ppermute(value, axis, [(i, i ^ step) for i in range(lax.axis_size(axi...  52.7 us
    ppermute x44, waiting for transfers between devices, swap(): lax.ppermute(value, axis, [(i, i ^ step) for i in range(lax.axis_size(axi...  26.1 us
    pallas_call x1, Pallas kernels, shards(): call(functools.partial(load_body, max(columns // side, 1)), 'load', [SCAL...  3.53 us
    pallas_call x2, Pallas kernels, shards(): call(functools.partial(back_mine_body, chips), 'backward', [SCALARS] + [W...  2.94 us
    pallas_call x1, Pallas kernels, shards(): call(functools.partial(finish_body, root_count), 'finish', [WHOLE] * (chi...  2.52 us
    pallas_call x2, Pallas kernels, shards(): call(back_other_body, 'backward_rest', [SCALARS] + [WHOLE] * 3, [f32(widt...  2.41 us
  transfers between devices with their start and end apart: 44, of which 25 were waited for; matrix products, arithmetic and copies ran while one was open for 0% of the time, Pallas kernels for 12%

profile of v6, /device:TPU:0, one launch (start us, length us, event | category | flops | bytes accessed | tf_op | source)
XLA Modules:
  0.0 102.0 jit_solution(7555404478498494003)
XLA Ops:
  1.0 4.0 %collective-permute-start.2 = (bf16[64,512]{1,0:T(8,128)(2,1)S(1)}, bf16[64,512]{1,0:T(8,128)(2,1)S(1)}, u32[]{:S(2)}, u32[]{:S(2)}) collective-permute-start(bf16[64,512]{1,0:T(8,128)(2,1)S(1)} %start.1.after_ref.refs_0_), channel_id=1, source_target_pairs={{0,24},{8,16},{16,8},{24,0},{1,25},{9,17},{17,9},{25,1},{2,26},{10... | collective-permute-start | bytes 196616 | tf_op jit(solution)/shard_map/ppermute | solution.py:457
  6.3 3.5 %load.1 = (bf16[32,256,256]{2,1,0:T(8,128)(2,1)S(1)}, f32[1,512]{1,0:T(1,128)S(1)}, f32[1,2048]{1,0:T(1,128)S(1)}, f32[1,256]{1,0:T(1,128)S(1)}, s32[16,32]{1,0:T(8,128)S(1)}) custom-call(s32[3]{0:T(128)S(1)} %pad_add_fusion.place, bf16[64,512]{1,0:T(8,128)(2,1)S(1)} %start.1.after_ref.refs_0_, bf16[32,256,256]{2,1,0:T(8,128)(2,1)} %bitcast.8, ...), custom_call_target="tpu_custom_call" | custom-call | bytes 8388608 | tf_op jit(solution)/shard_map/load/pallas_call | solution.py:502
  11.4 1.9 %forward_rest.2.mine_ref = f32[4,64,256]{2,1,0:T(8,128)S(1)} custom-call(s32[16,32]{1,0:T(8,128)S(1)} %get-tuple-element.43.table, bf16[8,64,256]{2,1,0:T(8,128)(2,1)S(1)} %get-tuple-element.45.held, bf16[32,256,256]{2,1,0:T(8,128)(2,1)S(1)} %get-tuple-element.44.refs_4_.tile_ref.refs_9_), custom_call_target="tpu_custom_call" | custom-call | flops 134217728 | bytes 2097152 | tf_op jit(solution)/shard_map/forward_rest/pallas_call | solution.py:605
  13.4 3.7 %collective-permute-start.4 = (bf16[64,256]{1,0:T(8,128)(2,1)S(1)}, bf16[64,256]{1,0:T(8,128)(2,1)S(1)}, u32[]{:S(2)}, u32[]{:S(2)}) collective-permute-start(bf16[64,256]{1,0:T(8,128)(2,1)S(1)} %get-tuple-element.48), channel_id=1, source_target_pairs={{0,6},{1,7},{2,4},{3,5},{4,2},{5,3},{6,0},{7,1},{8,14},{9,15},{10,... | collective-permute-start | bytes 98312 | tf_op jit(solution)/shard_map/ppermute | solution.py:457
  19.1 2.7 %collective-permute-done.5.refs_2_ = bf16[64,256]{1,0:T(8,128)(2,1)S(1)} collective-permute-done((bf16[64,256]{1,0:T(8,128)(2,1)S(1)}, bf16[64,256]{1,0:T(8,128)(2,1)S(1)}, u32[]{:S(2)}, u32[]{:S(2)}) %collective-permute-start.5) | collective-permute-done | bytes 32800 | tf_op jit(solution)/shard_map/ppermute | solution.py:457
  21.9 1.7 %collective-permute-start.9 = (bf16[64,256]{1,0:T(8,128)(2,1)S(1)}, bf16[64,256]{1,0:T(8,128)(2,1)S(1)}, u32[]{:S(2)}, u32[]{:S(2)}) collective-permute-start(bf16[64,256]{1,0:T(8,128)(2,1)S(1)} %query.2.refs_0_), channel_id=1, source_target_pairs={{0,6},{1,7},{2,4},{3,5},{4,2},{5,3},{6,0},{7,1},{8,14},{9,15},{10,... | collective-permute-start | bytes 98312 | tf_op jit(solution)/shard_map/ppermute | solution.py:457
  24.0 2.3 %collective-permute-start.7 = (bf16[64,256]{1,0:T(8,128)(2,1)S(1)}, bf16[64,256]{1,0:T(8,128)(2,1)S(1)}, u32[]{:S(2)}, u32[]{:S(2)}) collective-permute-start(bf16[64,256]{1,0:T(8,128)(2,1)S(1)} %query.2.refs_0_), channel_id=1, source_target_pairs={{0,2},{1,3},{2,0},{3,1},{4,6},{5,7},{6,4},{7,5},{8,10},{9,11},{10,... | collective-permute-start | bytes 98312 | tf_op jit(solution)/shard_map/ppermute | solution.py:457
  26.3 1.4 %collective-permute-done.9.refs_3_ = bf16[64,256]{1,0:T(8,128)(2,1)S(1)} collective-permute-done((bf16[64,256]{1,0:T(8,128)(2,1)S(1)}, bf16[64,256]{1,0:T(8,128)(2,1)S(1)}, u32[]{:S(2)}, u32[]{:S(2)}) %collective-permute-start.9) | collective-permute-done | bytes 32800 | tf_op jit(solution)/shard_map/ppermute | solution.py:457
  28.6 1.5 %backward.2.begun_ref = f32[9,64,256]{2,1,0:T(8,128)S(1)} custom-call(s32[16,32]{1,0:T(8,128)S(1)} %get-tuple-element.43.table, bf16[64,256]{1,0:T(8,128)(2,1)S(1)} %query.2.refs_0_, bf16[64,256]{1,0:T(8,128)(2,1)S(1)} %collective-permute-done.7.refs_1_, bf16[64,256]{1,0:T(8,128)(2,1)S(1)} %collective-permute-done.8.refs_2_, ...), custom_call_target="tpu_custom_call" | custom-call | flops 134217728 | bytes 2097152 | tf_op jit(solution)/shard_map/backward/pallas_call | solution.py:633
  31.3 2.8 %collective-permute-start.11 = (f32[32,512]{1,0:T(8,128)S(1)}, f32[32,512]{1,0:T(8,128)S(1)}, u32[]{:S(2)}, u32[]{:S(2)}) collective-permute-start(f32[32,512]{1,0:T(8,128)S(1)} %get-tuple-element.53), channel_id=1, source_target_pairs={{0,24},{8,16},{16,8},{24,0},{1,25},{9,17},{17,9},{25,1},{2,26},{10... | collective-permute-start | bytes 196616 | tf_op jit(solution)/shard_map/ppermute | solution.py:457
  34.9 2.8 %collective-permute-start.17 = (f32[32,512]{1,0:T(8,128)S(1)}, f32[32,512]{1,0:T(8,128)S(1)}, u32[]{:S(2)}, u32[]{:S(2)}) collective-permute-start(f32[32,512]{1,0:T(8,128)S(1)} %get-tuple-element.58), channel_id=1, source_target_pairs={{0,24},{8,16},{16,8},{24,0},{1,25},{9,17},{17,9},{25,1},{2,26},{10... | collective-permute-start | bytes 196616 | tf_op jit(solution)/shard_map/ppermute | solution.py:457
  39.1 2.2 %collective-permute-start.16 = (f32[32,512]{1,0:T(8,128)S(1)}, f32[32,512]{1,0:T(8,128)S(1)}, u32[]{:S(2)}, u32[]{:S(2)}) collective-permute-start(f32[32,512]{1,0:T(8,128)S(1)} %lift.3.refs_0_), channel_id=1, source_target_pairs={{0,24},{8,16},{16,8},{24,0},{1,25},{9,17},{17,9},{25,1},{2,26},{10... | collective-permute-start | bytes 196616 | tf_op jit(solution)/shard_map/ppermute | solution.py:457
  43.1 1.7 %collective-permute-start.22 = (f32[32,512]{1,0:T(8,128)S(1)}, f32[32,512]{1,0:T(8,128)S(1)}, u32[]{:S(2)}, u32[]{:S(2)}) collective-permute-start(f32[32,512]{1,0:T(8,128)S(1)} %lift.4.refs_4_), channel_id=1, source_target_pairs={{0,24},{8,16},{16,8},{24,0},{1,25},{9,17},{17,9},{25,1},{2,26},{10... | collective-permute-start | bytes 196616 | tf_op jit(solution)/shard_map/ppermute | solution.py:457
  45.1 1.6 %collective-permute-start.20 = (f32[32,512]{1,0:T(8,128)S(1)}, f32[32,512]{1,0:T(8,128)S(1)}, u32[]{:S(2)}, u32[]{:S(2)}) collective-permute-start(f32[32,512]{1,0:T(8,128)S(1)} %lift.4.refs_4_), channel_id=1, source_target_pairs={{0,8},{8,0},{16,24},{24,16},{1,9},{9,1},{17,25},{25,17},{2,10},{10... | collective-permute-start | bytes 196616 | tf_op jit(solution)/shard_map/ppermute | solution.py:457
  46.9 1.4 %collective-permute-done.22.refs_7_ = f32[32,512]{1,0:T(8,128)S(1)} collective-permute-done((f32[32,512]{1,0:T(8,128)S(1)}, f32[32,512]{1,0:T(8,128)S(1)}, u32[]{:S(2)}, u32[]{:S(2)}) %collective-permute-start.22) | collective-permute-done | bytes 65568 | tf_op jit(solution)/shard_map/ppermute | solution.py:457
  49.3 1.9 %forward.3 = (bf16[8,128,256]{2,1,0:T(8,128)(2,1)S(1)}, f32[272,256]{1,0:T(8,128)S(1)}, f32[16,256]{1,0:T(8,128)S(1)}) custom-call(s32[16,32]{1,0:T(8,128)S(1)} %get-tuple-element.43.table, f32[32,512]{1,0:T(8,128)S(1)} %lift.3.refs_0_, f32[32,512]{1,0:T(8,128)S(1)} %collective-permute-done.14.refs_1_, f32[32,512]{1,0:T(8,128)S(1)} %collective-permute-done.15.refs_2_, ...), custom_call_target="tpu_custom_call" | custom-call | flops 134217728 | bytes 2097152 | tf_op jit(solution)/shard_map/forward/pallas_call | solution.py:545
  51.3 2.0 %forward_rest.3.mine_ref = f32[256,256]{1,0:T(8,128)S(1)} custom-call(s32[16,32]{1,0:T(8,128)S(1)} %get-tuple-element.43.table, bf16[8,128,256]{2,1,0:T(8,128)(2,1)S(1)} %get-tuple-element.62.held, bf16[32,256,256]{2,1,0:T(8,128)(2,1)S(1)} %get-tuple-element.44.refs_4_.tile_ref.refs_9_), custom_call_target="tpu_custom_call" | custom-call | flops 134217728 | bytes 2097152 | tf_op jit(solution)/shard_map/forward_rest/pallas_call | solution.py:554
  53.5 1.9 %collective-permute-start.27 = (f32[96,128]{1,0:T(8,128)S(1)}, f32[96,128]{1,0:T(8,128)S(1)}, u32[]{:S(2)}, u32[]{:S(2)}) collective-permute-start(f32[96,128]{1,0:T(8,128)S(1)} %get-tuple-element.70), channel_id=1, source_target_pairs={{0,6},{1,7},{2,4},{3,5},{4,2},{5,3},{6,0},{7,1},{8,14},{9,15},{10,... | collective-permute-start | bytes 147464 | tf_op jit(solution)/shard_map/ppermute | solution.py:457
  56.0 1.9 %collective-permute-start.29 = (f32[96,128]{1,0:T(8,128)S(1)}, f32[96,128]{1,0:T(8,128)S(1)}, u32[]{:S(2)}, u32[]{:S(2)}) collective-permute-start(f32[96,128]{1,0:T(8,128)S(1)} %get-tuple-element.72), channel_id=1, source_target_pairs={{0,2},{1,3},{2,0},{3,1},{4,6},{5,7},{6,4},{7,5},{8,10},{9,11},{10,... | collective-permute-start | bytes 147464 | tf_op jit(solution)/shard_map/ppermute | solution.py:457
  57.9 1.9 %collective-permute-start.24 = (f32[64,128]{1,0:T(8,128)S(1)}, f32[64,128]{1,0:T(8,128)S(1)}, u32[]{:S(2)}, u32[]{:S(2)}) collective-permute-start(f32[64,128]{1,0:T(8,128)S(1)} %get-tuple-element.66), channel_id=1, source_target_pairs={{0,6},{1,7},{2,4},{3,5},{4,2},{5,3},{6,0},{7,1},{8,14},{9,15},{10,... | collective-permute-start | bytes 98312 | tf_op jit(solution)/shard_map/ppermute | solution.py:457
  59.8 2.5 %collective-permute-start.26 = (f32[64,128]{1,0:T(8,128)S(1)}, f32[64,128]{1,0:T(8,128)S(1)}, u32[]{:S(2)}, u32[]{:S(2)}) collective-permute-start(f32[64,128]{1,0:T(8,128)S(1)} %get-tuple-element.68), channel_id=1, source_target_pairs={{0,2},{1,3},{2,0},{3,1},{4,6},{5,7},{6,4},{7,5},{8,10},{9,11},{10,... | collective-permute-start | bytes 98312 | tf_op jit(solution)/shard_map/ppermute | solution.py:457
  62.3 1.8 %query.3 = (f32[64,64]{1,0:T(8,128)S(1)}, bf16[64,128]{1,0:T(8,128)(2,1)S(1)}) custom-call(f32[96,128]{1,0:T(8,128)S(1)} %get-tuple-element.69.refs_0_, f32[96,128]{1,0:T(8,128)S(1)} %collective-permute-done.27.refs_1_, f32[96,128]{1,0:T(8,128)S(1)} %collective-permute-done.28.refs_2_, f32[96,128]{1,0:T(8,128)S(1)} %collective-permute-done.29.refs_3_, ...), custom_call_target="tpu_custom_call" | custom-call | flops 268435456 | tf_op jit(solution)/shard_map/query/pallas_call | solution.py:585
  64.8 2.0 %collective-permute-start.32 = (bf16[64,256]{1,0:T(8,128)(2,1)S(1)}, bf16[64,256]{1,0:T(8,128)(2,1)S(1)}, u32[]{:S(2)}, u32[]{:S(2)}) collective-permute-start(bf16[64,256]{1,0:T(8,128)(2,1)S(1)} %query_rest.1.refs_0_), channel_id=1, source_target_pairs={{0,6},{1,7},{2,4},{3,5},{4,2},{5,3},{6,0},{7,1},{8,14},{9,15},{10,... | collective-permute-start | bytes 98312 | tf_op jit(solution)/shard_map/ppermute | solution.py:457
  72.1 1.5 %backward.3.begun_ref = f32[9,64,256]{2,1,0:T(8,128)S(1)} custom-call(s32[16,32]{1,0:T(8,128)S(1)} %get-tuple-element.43.table, bf16[64,256]{1,0:T(8,128)(2,1)S(1)} %query_rest.1.refs_0_, bf16[64,256]{1,0:T(8,128)(2,1)S(1)} %collective-permute-done.30.refs_1_, bf16[64,256]{1,0:T(8,128)(2,1)S(1)} %collective-permute-done.31.refs_2_, ...), custom_call_target="tpu_custom_call" | custom-call | flops 134217728 | bytes 2097152 | tf_op jit(solution)/shard_map/backward/pallas_call | solution.py:633
  74.8 2.3 %collective-permute-start.34 = (f32[64,512]{1,0:T(8,128)S(1)}, f32[64,512]{1,0:T(8,128)S(1)}, u32[]{:S(2)}, u32[]{:S(2)}) collective-permute-start(f32[64,512]{1,0:T(8,128)S(1)} %get-tuple-element.76), channel_id=1, source_target_pairs={{0,24},{8,16},{16,8},{24,0},{1,25},{9,17},{17,9},{25,1},{2,26},{10... | collective-permute-start | bytes 393224 | tf_op jit(solution)/shard_map/ppermute | solution.py:457
  78.3 3.5 %collective-permute-done.34.refs_1_ = f32[64,512]{1,0:T(8,128)S(1)} collective-permute-done((f32[64,512]{1,0:T(8,128)S(1)}, f32[64,512]{1,0:T(8,128)S(1)}, u32[]{:S(2)}, u32[]{:S(2)}) %collective-permute-start.34) | collective-permute-done | bytes 131104 | tf_op jit(solution)/shard_map/ppermute | solution.py:457
  81.9 2.3 %collective-permute-done.35.refs_2_ = f32[64,512]{1,0:T(8,128)S(1)} collective-permute-done((f32[64,512]{1,0:T(8,128)S(1)}, f32[64,512]{1,0:T(8,128)S(1)}, u32[]{:S(2)}, u32[]{:S(2)}) %collective-permute-start.35) | collective-permute-done | bytes 131104 | tf_op jit(solution)/shard_map/ppermute | solution.py:457
  84.5 1.8 %collective-permute-start.39 = (f32[64,64]{1,0:T(8,128)S(1)}, f32[64,64]{1,0:T(8,128)S(1)}, u32[]{:S(2)}, u32[]{:S(2)}) collective-permute-start(f32[64,64]{1,0:T(8,128)S(1)} %get-tuple-element.79.refs_0_), channel_id=1, source_target_pairs={{0,24},{8,16},{16,8},{24,0},{1,25},{9,17},{17,9},{25,1},{2,26},{10... | collective-permute-start | bytes 49160 | tf_op jit(solution)/shard_map/ppermute | solution.py:457
  92.5 2.0 %collective-permute-start.43 = (f32[64,64]{1,0:T(8,128)S(1)}, f32[64,64]{1,0:T(8,128)S(1)}, u32[]{:S(2)}, u32[]{:S(2)}) collective-permute-start(f32[64,64]{1,0:T(8,128)S(1)} %sum.3.refs_0_), channel_id=1, source_target_pairs={{0,6},{1,7},{2,4},{3,5},{4,2},{5,3},{6,0},{7,1},{8,14},{9,15},{10,... | collective-permute-start | bytes 49160 | tf_op jit(solution)/shard_map/ppermute | solution.py:457
  95.0 1.9 %collective-permute-start.41 = (f32[64,64]{1,0:T(8,128)S(1)}, f32[64,64]{1,0:T(8,128)S(1)}, u32[]{:S(2)}, u32[]{:S(2)}) collective-permute-start(f32[64,64]{1,0:T(8,128)S(1)} %sum.3.refs_0_), channel_id=1, source_target_pairs={{0,2},{1,3},{2,0},{3,1},{4,6},{5,7},{6,4},{7,5},{8,10},{9,11},{10,... | collective-permute-start | bytes 49160 | tf_op jit(solution)/shard_map/ppermute | solution.py:457
  96.9 1.5 %collective-permute-done.43.refs_3_ = f32[64,64]{1,0:T(8,128)S(1)} collective-permute-done((f32[64,64]{1,0:T(8,128)S(1)}, f32[64,64]{1,0:T(8,128)S(1)}, u32[]{:S(2)}, u32[]{:S(2)}) %collective-permute-start.43) | collective-permute-done | bytes 16416 | tf_op jit(solution)/shard_map/ppermute | solution.py:457
  99.4 2.5 %finish.1 = f32[64,512]{1,0:T(8,128)} custom-call(f32[64,64]{1,0:T(8,128)S(1)} %sum.3.refs_0_, f32[64,64]{1,0:T(8,128)S(1)} %collective-permute-done.41.refs_1_, f32[64,64]{1,0:T(8,128)S(1)} %collective-permute-done.42.refs_2_, f32[64,64]{1,0:T(8,128)S(1)} %collective-permute-done.43.refs_3_, f32[64,512]{1,0:T(8,128)S(1)} %get-tuple-element.80.refs_4_), custom_call_target="tpu_custom_call" | custom-call | tf_op jit(solution)/shard_map/finish/pallas_call | solution.py:667
  (80 shorter events, 30.7 us)
Async XLA Ops:
  1.0 8.9 %collective-permute-start.2 = (bf16[64,512]{1,0:T(8,128)(2,1)S(1)}, bf16[64,512]{1,0:T(8,128)(2,1)S(1)}, u32[]{:S(2)}, u32[]{:S(2)}) collective-permute-start(bf16[64,512]{1,0:T(8,128)(2,1)S(1)} %start.1.after_ref.refs_0_), channel_id=1, source_target_pairs={{0,24},{8,16},{16,8},{24,0},{1,25},{9,17},{17,9},{25,1},{2,26},{10... | collective-permute-start | bytes 196616 | tf_op jit(solution)/shard_map/ppermute | solution.py:457
  4.9 4.9 %collective-permute-start.1 = (bf16[64,512]{1,0:T(8,128)(2,1)S(1)}, bf16[64,512]{1,0:T(8,128)(2,1)S(1)}, u32[]{:S(2)}, u32[]{:S(2)}) collective-permute-start(bf16[64,512]{1,0:T(8,128)(2,1)S(1)} %start.1.after_ref.refs_0_), channel_id=1, source_target_pairs={{0,16},{8,24},{16,0},{24,8},{1,17},{9,25},{17,1},{25,9},{2,18},{10... | collective-permute-start | bytes 196616 | tf_op jit(solution)/shard_map/ppermute | solution.py:457
  5.4 4.4 %collective-permute-start = (bf16[64,512]{1,0:T(8,128)(2,1)S(1)}, bf16[64,512]{1,0:T(8,128)(2,1)S(1)}, u32[]{:S(2)}, u32[]{:S(2)}) collective-permute-start(bf16[64,512]{1,0:T(8,128)(2,1)S(1)} %start.1.after_ref.refs_0_), channel_id=1, source_target_pairs={{0,8},{8,0},{16,24},{24,16},{1,9},{9,1},{17,25},{25,17},{2,10},{10... | collective-permute-start | bytes 196616 | tf_op jit(solution)/shard_map/ppermute | solution.py:457
  13.4 5.8 %collective-permute-start.4 = (bf16[64,256]{1,0:T(8,128)(2,1)S(1)}, bf16[64,256]{1,0:T(8,128)(2,1)S(1)}, u32[]{:S(2)}, u32[]{:S(2)}) collective-permute-start(bf16[64,256]{1,0:T(8,128)(2,1)S(1)} %get-tuple-element.48), channel_id=1, source_target_pairs={{0,6},{1,7},{2,4},{3,5},{4,2},{5,3},{6,0},{7,1},{8,14},{9,15},{10,... | collective-permute-start | bytes 98312 | tf_op jit(solution)/shard_map/ppermute | solution.py:457
  17.0 4.8 %collective-permute-start.5 = (bf16[64,256]{1,0:T(8,128)(2,1)S(1)}, bf16[64,256]{1,0:T(8,128)(2,1)S(1)}, u32[]{:S(2)}, u32[]{:S(2)}) collective-permute-start(bf16[64,256]{1,0:T(8,128)(2,1)S(1)} %get-tuple-element.49), channel_id=1, source_target_pairs={{0,4},{1,5},{2,6},{3,7},{4,0},{5,1},{6,2},{7,3},{8,12},{9,13},{10,... | collective-permute-start | bytes 98312 | tf_op jit(solution)/shard_map/ppermute | solution.py:457
  17.0 4.8 %collective-permute-start.6 = (bf16[64,256]{1,0:T(8,128)(2,1)S(1)}, bf16[64,256]{1,0:T(8,128)(2,1)S(1)}, u32[]{:S(2)}, u32[]{:S(2)}) collective-permute-start(bf16[64,256]{1,0:T(8,128)(2,1)S(1)} %get-tuple-element.50), channel_id=1, source_target_pairs={{0,2},{1,3},{2,0},{3,1},{4,6},{5,7},{6,4},{7,5},{8,10},{9,11},{10,... | collective-permute-start | bytes 98312 | tf_op jit(solution)/shard_map/ppermute | solution.py:457
  21.9 5.9 %collective-permute-start.9 = (bf16[64,256]{1,0:T(8,128)(2,1)S(1)}, bf16[64,256]{1,0:T(8,128)(2,1)S(1)}, u32[]{:S(2)}, u32[]{:S(2)}) collective-permute-start(bf16[64,256]{1,0:T(8,128)(2,1)S(1)} %query.2.refs_0_), channel_id=1, source_target_pairs={{0,6},{1,7},{2,4},{3,5},{4,2},{5,3},{6,0},{7,1},{8,14},{9,15},{10,... | collective-permute-start | bytes 98312 | tf_op jit(solution)/shard_map/ppermute | solution.py:457
  23.6 4.9 %collective-permute-start.8 = (bf16[64,256]{1,0:T(8,128)(2,1)S(1)}, bf16[64,256]{1,0:T(8,128)(2,1)S(1)}, u32[]{:S(2)}, u32[]{:S(2)}) collective-permute-start(bf16[64,256]{1,0:T(8,128)(2,1)S(1)} %query.2.refs_0_), channel_id=1, source_target_pairs={{0,4},{1,5},{2,6},{3,7},{4,0},{5,1},{6,2},{7,3},{8,12},{9,13},{10,... | collective-permute-start | bytes 98312 | tf_op jit(solution)/shard_map/ppermute | solution.py:457
  24.0 4.5 %collective-permute-start.7 = (bf16[64,256]{1,0:T(8,128)(2,1)S(1)}, bf16[64,256]{1,0:T(8,128)(2,1)S(1)}, u32[]{:S(2)}, u32[]{:S(2)}) collective-permute-start(bf16[64,256]{1,0:T(8,128)(2,1)S(1)} %query.2.refs_0_), channel_id=1, source_target_pairs={{0,2},{1,3},{2,0},{3,1},{4,6},{5,7},{6,4},{7,5},{8,10},{9,11},{10,... | collective-permute-start | bytes 98312 | tf_op jit(solution)/shard_map/ppermute | solution.py:457
  31.3 6.3 %collective-permute-start.11 = (f32[32,512]{1,0:T(8,128)S(1)}, f32[32,512]{1,0:T(8,128)S(1)}, u32[]{:S(2)}, u32[]{:S(2)}) collective-permute-start(f32[32,512]{1,0:T(8,128)S(1)} %get-tuple-element.53), channel_id=1, source_target_pairs={{0,24},{8,16},{16,8},{24,0},{1,25},{9,17},{17,9},{25,1},{2,26},{10... | collective-permute-start | bytes 196616 | tf_op jit(solution)/shard_map/ppermute | solution.py:457
  34.2 4.9 %collective-permute-start.13 = (f32[32,512]{1,0:T(8,128)S(1)}, f32[32,512]{1,0:T(8,128)S(1)}, u32[]{:S(2)}, u32[]{:S(2)}) collective-permute-start(f32[32,512]{1,0:T(8,128)S(1)} %get-tuple-element.55), channel_id=1, source_target_pairs={{0,8},{8,0},{16,24},{24,16},{1,9},{9,1},{17,25},{25,17},{2,10},{10... | collective-permute-start | bytes 196616 | tf_op jit(solution)/shard_map/ppermute | solution.py:457
  34.9 6.5 %collective-permute-start.17 = (f32[32,512]{1,0:T(8,128)S(1)}, f32[32,512]{1,0:T(8,128)S(1)}, u32[]{:S(2)}, u32[]{:S(2)}) collective-permute-start(f32[32,512]{1,0:T(8,128)S(1)} %get-tuple-element.58), channel_id=1, source_target_pairs={{0,24},{8,16},{16,8},{24,0},{1,25},{9,17},{17,9},{25,1},{2,26},{10... | collective-permute-start | bytes 196616 | tf_op jit(solution)/shard_map/ppermute | solution.py:457
  37.7 5.4 %collective-permute-start.18 = (f32[32,512]{1,0:T(8,128)S(1)}, f32[32,512]{1,0:T(8,128)S(1)}, u32[]{:S(2)}, u32[]{:S(2)}) collective-permute-start(f32[32,512]{1,0:T(8,128)S(1)} %get-tuple-element.59), channel_id=1, source_target_pairs={{0,16},{8,24},{16,0},{24,8},{1,17},{9,25},{17,1},{25,9},{2,18},{10... | collective-permute-start | bytes 196616 | tf_op jit(solution)/shard_map/ppermute | solution.py:457
  37.7 5.4 %collective-permute-start.19 = (f32[32,512]{1,0:T(8,128)S(1)}, f32[32,512]{1,0:T(8,128)S(1)}, u32[]{:S(2)}, u32[]{:S(2)}) collective-permute-start(f32[32,512]{1,0:T(8,128)S(1)} %get-tuple-element.60), channel_id=1, source_target_pairs={{0,8},{8,0},{16,24},{24,16},{1,9},{9,1},{17,25},{25,17},{2,10},{10... | collective-permute-start | bytes 196616 | tf_op jit(solution)/shard_map/ppermute | solution.py:457
  39.1 6.0 %collective-permute-start.16 = (f32[32,512]{1,0:T(8,128)S(1)}, f32[32,512]{1,0:T(8,128)S(1)}, u32[]{:S(2)}, u32[]{:S(2)}) collective-permute-start(f32[32,512]{1,0:T(8,128)S(1)} %lift.3.refs_0_), channel_id=1, source_target_pairs={{0,24},{8,16},{16,8},{24,0},{1,25},{9,17},{17,9},{25,1},{2,26},{10... | collective-permute-start | bytes 196616 | tf_op jit(solution)/shard_map/ppermute | solution.py:457
  41.3 5.7 %collective-permute-start.15 = (f32[32,512]{1,0:T(8,128)S(1)}, f32[32,512]{1,0:T(8,128)S(1)}, u32[]{:S(2)}, u32[]{:S(2)}) collective-permute-start(f32[32,512]{1,0:T(8,128)S(1)} %lift.3.refs_0_), channel_id=1, source_target_pairs={{0,16},{8,24},{16,0},{24,8},{1,17},{9,25},{17,1},{25,9},{2,18},{10... | collective-permute-start | bytes 196616 | tf_op jit(solution)/shard_map/ppermute | solution.py:457
  41.4 5.5 %collective-permute-start.14 = (f32[32,512]{1,0:T(8,128)S(1)}, f32[32,512]{1,0:T(8,128)S(1)}, u32[]{:S(2)}, u32[]{:S(2)}) collective-permute-start(f32[32,512]{1,0:T(8,128)S(1)} %lift.3.refs_0_), channel_id=1, source_target_pairs={{0,8},{8,0},{16,24},{24,16},{1,9},{9,1},{17,25},{25,17},{2,10},{10... | collective-permute-start | bytes 196616 | tf_op jit(solution)/shard_map/ppermute | solution.py:457
  43.1 5.2 %collective-permute-start.22 = (f32[32,512]{1,0:T(8,128)S(1)}, f32[32,512]{1,0:T(8,128)S(1)}, u32[]{:S(2)}, u32[]{:S(2)}) collective-permute-start(f32[32,512]{1,0:T(8,128)S(1)} %lift.4.refs_4_), channel_id=1, source_target_pairs={{0,24},{8,16},{16,8},{24,0},{1,25},{9,17},{17,9},{25,1},{2,26},{10... | collective-permute-start | bytes 196616 | tf_op jit(solution)/shard_map/ppermute | solution.py:457
  53.5 6.3 %collective-permute-start.27 = (f32[96,128]{1,0:T(8,128)S(1)}, f32[96,128]{1,0:T(8,128)S(1)}, u32[]{:S(2)}, u32[]{:S(2)}) collective-permute-start(f32[96,128]{1,0:T(8,128)S(1)} %get-tuple-element.70), channel_id=1, source_target_pairs={{0,6},{1,7},{2,4},{3,5},{4,2},{5,3},{6,0},{7,1},{8,14},{9,15},{10,... | collective-permute-start | bytes 147464 | tf_op jit(solution)/shard_map/ppermute | solution.py:457
  55.4 6.9 %collective-permute-start.28 = (f32[96,128]{1,0:T(8,128)S(1)}, f32[96,128]{1,0:T(8,128)S(1)}, u32[]{:S(2)}, u32[]{:S(2)}) collective-permute-start(f32[96,128]{1,0:T(8,128)S(1)} %get-tuple-element.71), channel_id=1, source_target_pairs={{0,4},{1,5},{2,6},{3,7},{4,0},{5,1},{6,2},{7,3},{8,12},{9,13},{10,... | collective-permute-start | bytes 147464 | tf_op jit(solution)/shard_map/ppermute | solution.py:457
  56.0 6.3 %collective-permute-start.29 = (f32[96,128]{1,0:T(8,128)S(1)}, f32[96,128]{1,0:T(8,128)S(1)}, u32[]{:S(2)}, u32[]{:S(2)}) collective-permute-start(f32[96,128]{1,0:T(8,128)S(1)} %get-tuple-element.72), channel_id=1, source_target_pairs={{0,2},{1,3},{2,0},{3,1},{4,6},{5,7},{6,4},{7,5},{8,10},{9,11},{10,... | collective-permute-start | bytes 147464 | tf_op jit(solution)/shard_map/ppermute | solution.py:457
  57.9 6.2 %collective-permute-start.24 = (f32[64,128]{1,0:T(8,128)S(1)}, f32[64,128]{1,0:T(8,128)S(1)}, u32[]{:S(2)}, u32[]{:S(2)}) collective-permute-start(f32[64,128]{1,0:T(8,128)S(1)} %get-tuple-element.66), channel_id=1, source_target_pairs={{0,6},{1,7},{2,4},{3,5},{4,2},{5,3},{6,0},{7,1},{8,14},{9,15},{10,... | collective-permute-start | bytes 98312 | tf_op jit(solution)/shard_map/ppermute | solution.py:457
  59.8 4.8 %collective-permute-start.25 = (f32[64,128]{1,0:T(8,128)S(1)}, f32[64,128]{1,0:T(8,128)S(1)}, u32[]{:S(2)}, u32[]{:S(2)}) collective-permute-start(f32[64,128]{1,0:T(8,128)S(1)} %get-tuple-element.67), channel_id=1, source_target_pairs={{0,4},{1,5},{2,6},{3,7},{4,0},{5,1},{6,2},{7,3},{8,12},{9,13},{10,... | collective-permute-start | bytes 98312 | tf_op jit(solution)/shard_map/ppermute | solution.py:457
  59.8 4.8 %collective-permute-start.26 = (f32[64,128]{1,0:T(8,128)S(1)}, f32[64,128]{1,0:T(8,128)S(1)}, u32[]{:S(2)}, u32[]{:S(2)}) collective-permute-start(f32[64,128]{1,0:T(8,128)S(1)} %get-tuple-element.68), channel_id=1, source_target_pairs={{0,2},{1,3},{2,0},{3,1},{4,6},{5,7},{6,4},{7,5},{8,10},{9,11},{10,... | collective-permute-start | bytes 98312 | tf_op jit(solution)/shard_map/ppermute | solution.py:457
  64.8 5.9 %collective-permute-start.32 = (bf16[64,256]{1,0:T(8,128)(2,1)S(1)}, bf16[64,256]{1,0:T(8,128)(2,1)S(1)}, u32[]{:S(2)}, u32[]{:S(2)}) collective-permute-start(bf16[64,256]{1,0:T(8,128)(2,1)S(1)} %query_rest.1.refs_0_), channel_id=1, source_target_pairs={{0,6},{1,7},{2,4},{3,5},{4,2},{5,3},{6,0},{7,1},{8,14},{9,15},{10,... | collective-permute-start | bytes 98312 | tf_op jit(solution)/shard_map/ppermute | solution.py:457
  66.8 5.2 %collective-permute-start.31 = (bf16[64,256]{1,0:T(8,128)(2,1)S(1)}, bf16[64,256]{1,0:T(8,128)(2,1)S(1)}, u32[]{:S(2)}, u32[]{:S(2)}) collective-permute-start(bf16[64,256]{1,0:T(8,128)(2,1)S(1)} %query_rest.1.refs_0_), channel_id=1, source_target_pairs={{0,4},{1,5},{2,6},{3,7},{4,0},{5,1},{6,2},{7,3},{8,12},{9,13},{10,... | collective-permute-start | bytes 98312 | tf_op jit(solution)/shard_map/ppermute | solution.py:457
  74.8 7.1 %collective-permute-start.34 = (f32[64,512]{1,0:T(8,128)S(1)}, f32[64,512]{1,0:T(8,128)S(1)}, u32[]{:S(2)}, u32[]{:S(2)}) collective-permute-start(f32[64,512]{1,0:T(8,128)S(1)} %get-tuple-element.76), channel_id=1, source_target_pairs={{0,24},{8,16},{16,8},{24,0},{1,25},{9,17},{17,9},{25,1},{2,26},{10... | collective-permute-start | bytes 393224 | tf_op jit(solution)/shard_map/ppermute | solution.py:457
  77.1 7.1 %collective-permute-start.35 = (f32[64,512]{1,0:T(8,128)S(1)}, f32[64,512]{1,0:T(8,128)S(1)}, u32[]{:S(2)}, u32[]{:S(2)}) collective-permute-start(f32[64,512]{1,0:T(8,128)S(1)} %get-tuple-element.77), channel_id=1, source_target_pairs={{0,16},{8,24},{16,0},{24,8},{1,17},{9,25},{17,1},{25,9},{2,18},{10... | collective-permute-start | bytes 393224 | tf_op jit(solution)/shard_map/ppermute | solution.py:457
  77.3 6.9 %collective-permute-start.36 = (f32[64,512]{1,0:T(8,128)S(1)}, f32[64,512]{1,0:T(8,128)S(1)}, u32[]{:S(2)}, u32[]{:S(2)}) collective-permute-start(f32[64,512]{1,0:T(8,128)S(1)} %get-tuple-element.78), channel_id=1, source_target_pairs={{0,8},{8,0},{16,24},{24,16},{1,9},{9,1},{17,25},{25,17},{2,10},{10... | collective-permute-start | bytes 393224 | tf_op jit(solution)/shard_map/ppermute | solution.py:457
  84.5 5.0 %collective-permute-start.39 = (f32[64,64]{1,0:T(8,128)S(1)}, f32[64,64]{1,0:T(8,128)S(1)}, u32[]{:S(2)}, u32[]{:S(2)}) collective-permute-start(f32[64,64]{1,0:T(8,128)S(1)} %get-tuple-element.79.refs_0_), channel_id=1, source_target_pairs={{0,24},{8,16},{16,8},{24,0},{1,25},{9,17},{17,9},{25,1},{2,26},{10... | collective-permute-start | bytes 49160 | tf_op jit(solution)/shard_map/ppermute | solution.py:457
  92.5 5.8 %collective-permute-start.43 = (f32[64,64]{1,0:T(8,128)S(1)}, f32[64,64]{1,0:T(8,128)S(1)}, u32[]{:S(2)}, u32[]{:S(2)}) collective-permute-start(f32[64,64]{1,0:T(8,128)S(1)} %sum.3.refs_0_), channel_id=1, source_target_pairs={{0,6},{1,7},{2,4},{3,5},{4,2},{5,3},{6,0},{7,1},{8,14},{9,15},{10,... | collective-permute-start | bytes 49160 | tf_op jit(solution)/shard_map/ppermute | solution.py:457
  94.6 4.9 %collective-permute-start.42 = (f32[64,64]{1,0:T(8,128)S(1)}, f32[64,64]{1,0:T(8,128)S(1)}, u32[]{:S(2)}, u32[]{:S(2)}) collective-permute-start(f32[64,64]{1,0:T(8,128)S(1)} %sum.3.refs_0_), channel_id=1, source_target_pairs={{0,4},{1,5},{2,6},{3,7},{4,0},{5,1},{6,2},{7,3},{8,12},{9,13},{10,... | collective-permute-start | bytes 49160 | tf_op jit(solution)/shard_map/ppermute | solution.py:457
  (12 other events, 37.6 us)

commit v7 on v6

--- a/solution.py
+++ b/solution.py
@@ -42,8 +42,8 @@
     return jnp.concatenate(done, axis=0)[:, width:]
 
 
-SLOT, QUERY_GIVE, PRODUCT_TAKE, QUERY_TAKE, PRODUCT_GIVE = range(5)
-FIELDS, LISTS, ALL = 5, 3, 2
+SLOT, QUERY, PRODUCT = range(3)
+FIELDS, LISTS, ALL = 3, 3, 2
 SINGLES = FIELDS * LISTS
 ROW_AT, COL_AT = 3, 4
 WHOLE = pl.BlockSpec(memory_space=pltpu.VMEM)
@@ -115,6 +115,10 @@
         get(total, me ^ ((count - at) % count), out_ref, side, part * out_ref.shape[0])
 
 
+def spare(held):
+    held[held.shape[0] - 1] = jnp.zeros(held.shape[1:], held.dtype)
+
+
 def collect(held, piece_refs, me, side):
     sets = held.shape[1] // piece_refs[0].shape[0]
     count = len(piece_refs) // sets
@@ -153,8 +157,8 @@
     lax.fori_loop(0, jnp.minimum((rest + GROUP - 1) // GROUP, slots // 2 // GROUP), step, 0)
 
 
-forward = functools.partial(products, take=PRODUCT_TAKE, give=QUERY_GIVE, dims=NT)
-backward = functools.partial(products, take=QUERY_TAKE, give=PRODUCT_GIVE, dims=NN)
+forward = functools.partial(products, take=PRODUCT, give=QUERY, dims=NT)
+backward = functools.partial(products, take=QUERY, give=PRODUCT, dims=NN)
 
 
 def emit_half(total, out_ref, me, side, flip):
@@ -171,6 +175,7 @@
     pieces, (tile_ref, mine_ref, other_ref, held, total) = refs[:n_in], refs[n_in:]
     side = tile_ref.shape[1]
     collect(held, pieces, table[SINGLES, ROW_AT], side)
+    spare(held)
     total[...] = jnp.zeros_like(total)
     forward(ALL, table=table, held=held, tile_ref=tile_ref, total=total)
     emit_half(total, mine_ref, table[SINGLES, COL_AT], side, 0)
@@ -181,6 +186,7 @@
     pieces, (tile_ref, held, other_ref, total) = refs[:n_in], refs[n_in:]
     side, me = tile_ref.shape[1], table[SINGLES, COL_AT]
     collect(held, pieces, table[SINGLES, ROW_AT], side)
+    spare(held)
     total[...] = jnp.zeros_like(total)
     forward(1 - me % 2, table=table, held=held, tile_ref=tile_ref, total=total)
     emit_half(total, other_ref, me, side, 1)
@@ -198,6 +204,7 @@
     side = tile_ref.shape[1]
     for flip, ref in enumerate((here_ref, there_ref)):
         collect_half(held, [ref.at[step] for step in range(ref.shape[0])], table[SINGLES, COL_AT], side, flip)
+    spare(held)
     total[...] = jnp.zeros_like(total)
     backward(ALL, table=table, held=held, tile_ref=tile_ref, total=total)
     emit(total, out_refs, table[SINGLES, ROW_AT], side)
@@ -207,6 +214,7 @@
     pieces, (tile_ref, total, held) = refs[:n_in], refs[n_in:]
     me = table[SINGLES, COL_AT]
     collect_half(held, pieces, me, tile_ref.shape[1], 0)
+    spare(held)
     total[...] = jnp.zeros_like(total)
     backward(me % 2, table=table, held=held, tile_ref=tile_ref, total=total)
 
@@ -215,6 +223,7 @@
     out_refs, (held, total) = refs[:-2], refs[-2:]
     side, me = tile_ref.shape[1], table[SINGLES, COL_AT]
     collect_half(held, [there_ref.at[step] for step in range(there_ref.shape[0])], me, side, 1)
+    spare(held)
     total[...] = begun_ref[...]
     backward(1 - me % 2, table=table, held=held, tile_ref=tile_ref, total=total)
     emit(total, out_refs, table[SINGLES, ROW_AT], side)
@@ -233,6 +242,7 @@
 def split_panel(pieces, scale_ref, spread, held, me):
     width, side = spread.shape[1:]
     collect(spread, pieces, me, side)
+    spare(held)
     for tile in range(spread.shape[0]):
         value = spread[tile] * scale_ref[:, tile * side : (tile + 1) * side]
         high = value.astype(jnp.bfloat16)
@@ -345,32 +355,30 @@
     out_ref[...] = (held[...] * scale).astype(out_ref.dtype)
 
 
-def write_table(table, ids, place, per, query_tiles, product_tiles):
-    slots = ids.shape[1]
-    for which in range(LISTS):
+def clear_table(table, lists, query_tiles, product_tiles):
+    for which in lists:
         table[SINGLES, which] = 0
-        for at in range(slots):
+        for at in range(table.shape[1]):
             table[which * FIELDS + SLOT, at] = 0
-            table[which * FIELDS + QUERY_GIVE, at] = query_tiles
-            table[which * FIELDS + PRODUCT_TAKE, at] = 0
-            table[which * FIELDS + QUERY_TAKE, at] = 0
-            table[which * FIELDS + PRODUCT_GIVE, at] = product_tiles
+            table[which * FIELDS + QUERY, at] = query_tiles
+            table[which * FIELDS + PRODUCT, at] = product_tiles
+
+
+def fill_table(table, ids, place, per):
     table[SINGLES, ROW_AT] = place[0]
     table[SINGLES, COL_AT] = place[1]
 
     def step(slot, carry):
         query, product = ids[0, slot], ids[1, slot]
-        for which in (query // per % 2, ALL):
-            at = table[SINGLES, which]
-            table[which * FIELDS + SLOT, at] = slot
-            table[which * FIELDS + QUERY_GIVE, at] = query
-            table[which * FIELDS + PRODUCT_TAKE, at] = product
-            table[which * FIELDS + QUERY_TAKE, at] = query
-            table[which * FIELDS + PRODUCT_GIVE, at] = product
-            table[SINGLES, which] = at + 1
+        which = query // per % 2 if per else ALL
+        at = table[SINGLES, which]
+        table[which * FIELDS + SLOT, at] = slot
+        table[which * FIELDS + QUERY, at] = query
+        table[which * FIELDS + PRODUCT, at] = product
+        table[SINGLES, which] = at + 1
         return carry
 
-    lax.fori_loop(0, jnp.minimum(place[2], slots), step, 0)
+    lax.fori_loop(0, jnp.minimum(place[2], ids.shape[1]), step, 0)
 
 
 def load_body(per, place, after_ref, tile_ref, id_ref, product_ref, query_ref, *refs):
@@ -386,9 +394,11 @@
         loads.append(pltpu.make_async_copy(tile_ref.at[span], keep.at[span], sems.at[3 + step]))
     for load in loads:
         load.start()
+    side = tile_ref.shape[1]
+    lists = (0, 1) if per else (ALL,)
+    clear_table(table, lists, query_ref.shape[1] // side, product_ref.shape[1] // side)
     loads[0].wait()
-    side = tile_ref.shape[1]
-    write_table(table, ids, place, per, query_ref.shape[1] // side, product_ref.shape[1] // side)
+    fill_table(table, ids, place, per)
     loads[1].wait()
     product_out[...] = 1.0 / jnp.sqrt(degrees[...].astype(jnp.float32))
     share = my_product_ref.shape[1]
@@ -500,7 +510,7 @@
     pieces = spread_to(scaled, "row")
     split = columns % side == 0
     tile_set, my_pscale, pscale, my_qscale, table = call(
-        functools.partial(load_body, max(columns // side, 1)),
+        functools.partial(load_body, columns // side if split else 0),
         "load",
         [SCALARS, WHOLE] + [AWAY] * 4,
         [
@@ -533,7 +543,7 @@
     half_work = dict(flops=slots * width * side * side, moved=slots * side * side)
     query_scratch = pltpu.VMEM((query_tiles + 1, width, side), jnp.float32)
     product_scratch = pltpu.VMEM((product_tiles + 1, width, side), jnp.float32)
-    query_held = pltpu.VMEM((query_tiles, width, side), jnp.bfloat16)
+    query_held = pltpu.VMEM((query_tiles + 1, width, side), jnp.bfloat16)
     for iteration in range(ITERS):
         sets = SETS if iteration < ITERS - 1 else 1
         if iteration > 0:
@@ -546,7 +556,7 @@
                     functools.partial(next_other_body, len(pieces), chips),
                     "forward",
                     [SCALARS] + arrays,
-                    [bf16(product_tiles, 2 * width, side), message, f32(gram_rows, columns)],
+                    [bf16(product_tiles + 1, 2 * width, side), message, f32(gram_rows, columns)],
                     [spread, query_scratch],
                     **half_work,
                 )(table, *pieces, pscale, tile_set)
@@ -565,7 +575,7 @@
                     "forward",
                     [SCALARS] + arrays,
                     [f32(chips * width, columns), message, f32(gram_rows, columns)],
-                    [spread, pltpu.VMEM((product_tiles, 2 * width, side), jnp.bfloat16), query_scratch],
+                    [spread, pltpu.VMEM((product_tiles + 1, 2 * width, side), jnp.bfloat16), query_scratch],
                     **work,
                 )(table, *pieces, pscale, tile_set)
                 got = swap(other, "col", 1)
@@ -597,7 +607,7 @@
                 functools.partial(forward_other_body, n_row),
                 "forward",
                 [SCALARS] + [WHOLE] * (n_row + 1),
-                [bf16(product_tiles, width, side), half],
+                [bf16(product_tiles + 1, width, side), half],
                 [query_scratch],
                 **half_work,
             )(table, *pieces, tile_set)
@@ -616,7 +626,7 @@
                 "forward",
                 [SCALARS] + [WHOLE] * (n_row + 1),
                 [half] * 2,
-                [pltpu.VMEM((product_tiles, width, side), jnp.bfloat16), query_scratch],
+                [pltpu.VMEM((product_tiles + 1, width, side), jnp.bfloat16), query_scratch],
                 **work,
             )(table, *pieces, tile_set)
             got = swap(other, "col", 1)

time: 102 us -> 102 us (level)
  transfers between devices with their start and end apart: 44 -> 44, of which waited for: 25 -> 26; matrix products, arithmetic and copies ran while one was open for 0% -> 0% of each run, Pallas kernels for 12% -> 10%
where the time goes in v7:
time: 102 us
  starting transfers between devices  52.5 us (51%)
  waiting for transfers between devices  26.8 us (26%)
  Pallas kernels  22.1 us (22%)
    ppermute x44, starting transfers between devices, swap(): lax.ppermute(value, axis, [(i, i ^ step) for i in range(lax.axis_size(axi...  52.5 us
    ppermute x44, waiting for transfers between devices, swap(): lax.ppermute(value, axis, [(i, i ^ step) for i in range(lax.axis_size(axi...  26.8 us
    pallas_call x1, Pallas kernels, shards(): call(functools.partial(load_body, columns // side if split else 0), 'load...  3.53 us
    pallas_call x2, Pallas kernels, shards(): call(back_other_body, 'backward_rest', [SCALARS] + [WHOLE] * 3, [f32(widt...  3.02 us
    pallas_call x1, Pallas kernels, shards(): call(functools.partial(finish_body, root_count), 'finish', [WHOLE] * (chi...  2.52 us
    pallas_call x1, Pallas kernels, shards(): call(functools.partial(next_other_body, len(pieces), chips), 'forward', [...  2.41 us
    pallas_call x2, Pallas kernels, shards(): call(functools.partial(back_mine_body, chips), 'backward', [SCALARS] + [W...  2.33 us
  transfers between devices with their start and end apart: 44, of which 26 were waited for; matrix products, arithmetic and copies ran while one was open for 0% of the time, Pallas kernels for 10%

profile of v7, /device:TPU:0, one launch (start us, length us, event | category | flops | bytes accessed | tf_op | source)
XLA Modules:
  0.0 102.3 jit_solution(15703009191659388090)
XLA Ops:
  1.0 4.0 %collective-permute-start.2 = (bf16[64,512]{1,0:T(8,128)(2,1)S(1)}, bf16[64,512]{1,0:T(8,128)(2,1)S(1)}, u32[]{:S(2)}, u32[]{:S(2)}) collective-permute-start(bf16[64,512]{1,0:T(8,128)(2,1)S(1)} %start.1.after_ref.refs_0_), channel_id=1, source_target_pairs={{0,24},{8,16},{16,8},{24,0},{1,25},{9,17},{17,9},{25,1},{2,26},{10... | collective-permute-start | bytes 196616 | tf_op jit(solution)/shard_map/ppermute | solution.py:467
  6.3 3.5 %load.1 = (bf16[32,256,256]{2,1,0:T(8,128)(2,1)S(1)}, f32[1,512]{1,0:T(1,128)S(1)}, f32[1,2048]{1,0:T(1,128)S(1)}, f32[1,256]{1,0:T(1,128)S(1)}, s32[10,32]{1,0:T(8,128)S(1)}) custom-call(s32[3]{0:T(128)S(1)} %pad_add_fusion.place, bf16[64,512]{1,0:T(8,128)(2,1)S(1)} %start.1.after_ref.refs_0_, bf16[32,256,256]{2,1,0:T(8,128)(2,1)} %bitcast.8, ...), custom_call_target="tpu_custom_call" | custom-call | bytes 8388608 | tf_op jit(solution)/shard_map/load/pallas_call | solution.py:512
  9.9 1.9 %forward.2 = (bf16[9,64,256]{2,1,0:T(8,128)(2,1)S(1)}, f32[4,64,256]{2,1,0:T(8,128)S(1)}) custom-call(s32[10,32]{1,0:T(8,128)S(1)} %get-tuple-element.43.table, bf16[64,512]{1,0:T(8,128)(2,1)S(1)} %start.1.after_ref.refs_0_, bf16[64,512]{1,0:T(8,128)(2,1)S(1)} %collective-permute-done.refs_1_, bf16[64,512]{1,0:T(8,128)(2,1)S(1)} %collective-permute-done.1.refs_2_, ...), custom_call_target="tpu_custom_call" | custom-call | flops 134217728 | bytes 2097152 | tf_op jit(solution)/shard_map/forward/pallas_call | solution.py:606
  11.8 1.5 %forward_rest.2.mine_ref = f32[4,64,256]{2,1,0:T(8,128)S(1)} custom-call(s32[10,32]{1,0:T(8,128)S(1)} %get-tuple-element.43.table, bf16[9,64,256]{2,1,0:T(8,128)(2,1)S(1)} %get-tuple-element.45.held, bf16[32,256,256]{2,1,0:T(8,128)(2,1)S(1)} %get-tuple-element.44.refs_4_.tile_ref.refs_9_), custom_call_target="tpu_custom_call" | custom-call | flops 134217728 | bytes 2097152 | tf_op jit(solution)/shard_map/forward_rest/pallas_call | solution.py:615
  13.4 3.6 %collective-permute-start.4 = (bf16[64,256]{1,0:T(8,128)(2,1)S(1)}, bf16[64,256]{1,0:T(8,128)(2,1)S(1)}, u32[]{:S(2)}, u32[]{:S(2)}) collective-permute-start(bf16[64,256]{1,0:T(8,128)(2,1)S(1)} %get-tuple-element.48), channel_id=1, source_target_pairs={{0,6},{1,7},{2,4},{3,5},{4,2},{5,3},{6,0},{7,1},{8,14},{9,15},{10,... | collective-permute-start | bytes 98312 | tf_op jit(solution)/shard_map/ppermute | solution.py:467
  19.2 2.6 %collective-permute-done.5.refs_2_ = bf16[64,256]{1,0:T(8,128)(2,1)S(1)} collective-permute-done((bf16[64,256]{1,0:T(8,128)(2,1)S(1)}, bf16[64,256]{1,0:T(8,128)(2,1)S(1)}, u32[]{:S(2)}, u32[]{:S(2)}) %collective-permute-start.5) | collective-permute-done | bytes 32800 | tf_op jit(solution)/shard_map/ppermute | solution.py:467
  21.9 1.7 %collective-permute-start.9 = (bf16[64,256]{1,0:T(8,128)(2,1)S(1)}, bf16[64,256]{1,0:T(8,128)(2,1)S(1)}, u32[]{:S(2)}, u32[]{:S(2)}) collective-permute-start(bf16[64,256]{1,0:T(8,128)(2,1)S(1)} %query.2.refs_0_), channel_id=1, source_target_pairs={{0,6},{1,7},{2,4},{3,5},{4,2},{5,3},{6,0},{7,1},{8,14},{9,15},{10,... | collective-permute-start | bytes 98312 | tf_op jit(solution)/shard_map/ppermute | solution.py:467
  24.0 2.3 %collective-permute-start.7 = (bf16[64,256]{1,0:T(8,128)(2,1)S(1)}, bf16[64,256]{1,0:T(8,128)(2,1)S(1)}, u32[]{:S(2)}, u32[]{:S(2)}) collective-permute-start(bf16[64,256]{1,0:T(8,128)(2,1)S(1)} %query.2.refs_0_), channel_id=1, source_target_pairs={{0,2},{1,3},{2,0},{3,1},{4,6},{5,7},{6,4},{7,5},{8,10},{9,11},{10,... | collective-permute-start | bytes 98312 | tf_op jit(solution)/shard_map/ppermute | solution.py:467
  30.0 1.5 %backward_rest.2 = (f32[32,512]{1,0:T(8,128)S(1)}, f32[32,512]{1,0:T(8,128)S(1)}, f32[32,512]{1,0:T(8,128)S(1)}, f32[32,512]{1,0:T(8,128)S(1)}, f32[32,512]{1,0:...) custom-call(s32[10,32]{1,0:T(8,128)S(1)} %get-tuple-element.43.table, ...), custom_call_target="tpu_custom_call" | custom-call | flops 134217728 | bytes 2097152 | tf_op jit(solution)/shard_map/backward_rest/pallas_call | solution.py:651
  31.5 2.2 %collective-permute-start.11 = (f32[32,512]{1,0:T(8,128)S(1)}, f32[32,512]{1,0:T(8,128)S(1)}, u32[]{:S(2)}, u32[]{:S(2)}) collective-permute-start(f32[32,512]{1,0:T(8,128)S(1)} %get-tuple-element.53), channel_id=1, source_target_pairs={{0,24},{8,16},{16,8},{24,0},{1,25},{9,17},{17,9},{25,1},{2,26},{10... | collective-permute-start | bytes 196616 | tf_op jit(solution)/shard_map/ppermute | solution.py:467
  35.1 2.1 %collective-permute-start.17 = (f32[32,512]{1,0:T(8,128)S(1)}, f32[32,512]{1,0:T(8,128)S(1)}, u32[]{:S(2)}, u32[]{:S(2)}) collective-permute-start(f32[32,512]{1,0:T(8,128)S(1)} %get-tuple-element.58), channel_id=1, source_target_pairs={{0,24},{8,16},{16,8},{24,0},{1,25},{9,17},{17,9},{25,1},{2,26},{10... | collective-permute-start | bytes 196616 | tf_op jit(solution)/shard_map/ppermute | solution.py:467
  39.2 1.6 %collective-permute-start.16 = (f32[32,512]{1,0:T(8,128)S(1)}, f32[32,512]{1,0:T(8,128)S(1)}, u32[]{:S(2)}, u32[]{:S(2)}) collective-permute-start(f32[32,512]{1,0:T(8,128)S(1)} %lift.3.refs_0_), channel_id=1, source_target_pairs={{0,24},{8,16},{16,8},{24,0},{1,25},{9,17},{17,9},{25,1},{2,26},{10... | collective-permute-start | bytes 196616 | tf_op jit(solution)/shard_map/ppermute | solution.py:467
  42.8 1.7 %collective-permute-start.22 = (f32[32,512]{1,0:T(8,128)S(1)}, f32[32,512]{1,0:T(8,128)S(1)}, u32[]{:S(2)}, u32[]{:S(2)}) collective-permute-start(f32[32,512]{1,0:T(8,128)S(1)} %lift.4.refs_4_), channel_id=1, source_target_pairs={{0,24},{8,16},{16,8},{24,0},{1,25},{9,17},{17,9},{25,1},{2,26},{10... | collective-permute-start | bytes 196616 | tf_op jit(solution)/shard_map/ppermute | solution.py:467
  46.5 1.5 %collective-permute-done.22.refs_7_ = f32[32,512]{1,0:T(8,128)S(1)} collective-permute-done((f32[32,512]{1,0:T(8,128)S(1)}, f32[32,512]{1,0:T(8,128)S(1)}, u32[]{:S(2)}, u32[]{:S(2)}) %collective-permute-start.22) | collective-permute-done | bytes 65568 | tf_op jit(solution)/shard_map/ppermute | solution.py:467
  49.3 2.4 %forward.3 = (bf16[9,128,256]{2,1,0:T(8,128)(2,1)S(1)}, f32[272,256]{1,0:T(8,128)S(1)}, f32[16,256]{1,0:T(8,128)S(1)}) custom-call(s32[10,32]{1,0:T(8,128)S(1)} %get-tuple-element.43.table, f32[32,512]{1,0:T(8,128)S(1)} %lift.3.refs_0_, f32[32,512]{1,0:T(8,128)S(1)} %collective-permute-done.14.refs_1_, f32[32,512]{1,0:T(8,128)S(1)} %collective-permute-done.15.refs_2_, ...), custom_call_target="tpu_custom_call" | custom-call | flops 134217728 | bytes 2097152 | tf_op jit(solution)/shard_map/forward/pallas_call | solution.py:555
  51.8 1.5 %forward_rest.3.mine_ref = f32[256,256]{1,0:T(8,128)S(1)} custom-call(s32[10,32]{1,0:T(8,128)S(1)} %get-tuple-element.43.table, bf16[9,128,256]{2,1,0:T(8,128)(2,1)S(1)} %get-tuple-element.62.held, bf16[32,256,256]{2,1,0:T(8,128)(2,1)S(1)} %get-tuple-element.44.refs_4_.tile_ref.refs_9_), custom_call_target="tpu_custom_call" | custom-call | flops 134217728 | bytes 2097152 | tf_op jit(solution)/shard_map/forward_rest/pallas_call | solution.py:564
  53.4 1.8 %collective-permute-start.27 = (f32[96,128]{1,0:T(8,128)S(1)}, f32[96,128]{1,0:T(8,128)S(1)}, u32[]{:S(2)}, u32[]{:S(2)}) collective-permute-start(f32[96,128]{1,0:T(8,128)S(1)} %get-tuple-element.70), channel_id=1, source_target_pairs={{0,6},{1,7},{2,4},{3,5},{4,2},{5,3},{6,0},{7,1},{8,14},{9,15},{10,... | collective-permute-start | bytes 147464 | tf_op jit(solution)/shard_map/ppermute | solution.py:467
  56.1 1.8 %collective-permute-start.29 = (f32[96,128]{1,0:T(8,128)S(1)}, f32[96,128]{1,0:T(8,128)S(1)}, u32[]{:S(2)}, u32[]{:S(2)}) collective-permute-start(f32[96,128]{1,0:T(8,128)S(1)} %get-tuple-element.72), channel_id=1, source_target_pairs={{0,2},{1,3},{2,0},{3,1},{4,6},{5,7},{6,4},{7,5},{8,10},{9,11},{10,... | collective-permute-start | bytes 147464 | tf_op jit(solution)/shard_map/ppermute | solution.py:467
  57.8 1.7 %collective-permute-start.24 = (f32[64,128]{1,0:T(8,128)S(1)}, f32[64,128]{1,0:T(8,128)S(1)}, u32[]{:S(2)}, u32[]{:S(2)}) collective-permute-start(f32[64,128]{1,0:T(8,128)S(1)} %get-tuple-element.66), channel_id=1, source_target_pairs={{0,6},{1,7},{2,4},{3,5},{4,2},{5,3},{6,0},{7,1},{8,14},{9,15},{10,... | collective-permute-start | bytes 98312 | tf_op jit(solution)/shard_map/ppermute | solution.py:467
  59.9 2.4 %collective-permute-start.26 = (f32[64,128]{1,0:T(8,128)S(1)}, f32[64,128]{1,0:T(8,128)S(1)}, u32[]{:S(2)}, u32[]{:S(2)}) collective-permute-start(f32[64,128]{1,0:T(8,128)S(1)} %get-tuple-element.68), channel_id=1, source_target_pairs={{0,2},{1,3},{2,0},{3,1},{4,6},{5,7},{6,4},{7,5},{8,10},{9,11},{10,... | collective-permute-start | bytes 98312 | tf_op jit(solution)/shard_map/ppermute | solution.py:467
  62.2 1.8 %query.3 = (f32[64,64]{1,0:T(8,128)S(1)}, bf16[64,128]{1,0:T(8,128)(2,1)S(1)}) custom-call(f32[96,128]{1,0:T(8,128)S(1)} %get-tuple-element.69.refs_0_, f32[96,128]{1,0:T(8,128)S(1)} %collective-permute-done.27.refs_1_, f32[96,128]{1,0:T(8,128)S(1)} %collective-permute-done.28.refs_2_, f32[96,128]{1,0:T(8,128)S(1)} %collective-permute-done.29.refs_3_, ...), custom_call_target="tpu_custom_call" | custom-call | flops 268435456 | tf_op jit(solution)/shard_map/query/pallas_call | solution.py:595
  64.7 2.0 %collective-permute-start.32 = (bf16[64,256]{1,0:T(8,128)(2,1)S(1)}, bf16[64,256]{1,0:T(8,128)(2,1)S(1)}, u32[]{:S(2)}, u32[]{:S(2)}) collective-permute-start(bf16[64,256]{1,0:T(8,128)(2,1)S(1)} %query_rest.1.refs_0_), channel_id=1, source_target_pairs={{0,6},{1,7},{2,4},{3,5},{4,2},{5,3},{6,0},{7,1},{8,14},{9,15},{10,... | collective-permute-start | bytes 98312 | tf_op jit(solution)/shard_map/ppermute | solution.py:467
  70.5 1.5 %collective-permute-done.31.refs_2_ = bf16[64,256]{1,0:T(8,128)(2,1)S(1)} collective-permute-done((bf16[64,256]{1,0:T(8,128)(2,1)S(1)}, bf16[64,256]{1,0:T(8,128)(2,1)S(1)}, u32[]{:S(2)}, u32[]{:S(2)}) %collective-permute-start.31) | collective-permute-done | bytes 32800 | tf_op jit(solution)/shard_map/ppermute | solution.py:467
  73.5 1.5 %backward_rest.3 = (f32[64,512]{1,0:T(8,128)S(1)}, f32[64,512]{1,0:T(8,128)S(1)}, f32[64,512]{1,0:T(8,128)S(1)}, f32[64,512]{1,0:T(8,128)S(1)}) custom-call(s32[10,32]{1,0:T(8,128)S(1)} %get-tuple-element.43.table, bf16[4,64,256]{2,1,0:T(8,128)(2,1)S(1)} %collective-permute-done.33.there_ref, f32[9,64,256]{2,1,0:T(8,128)S(1)} %backward.3.begun_ref, ...), custom_call_target="tpu_custom_call" | custom-call | flops 134217728 | bytes 2097152 | tf_op jit(solution)/shard_map/backward_rest/pallas_call | solution.py:651
  75.0 1.6 %collective-permute-start.34 = (f32[64,512]{1,0:T(8,128)S(1)}, f32[64,512]{1,0:T(8,128)S(1)}, u32[]{:S(2)}, u32[]{:S(2)}) collective-permute-start(f32[64,512]{1,0:T(8,128)S(1)} %get-tuple-element.76), channel_id=1, source_target_pairs={{0,24},{8,16},{16,8},{24,0},{1,25},{9,17},{17,9},{25,1},{2,26},{10... | collective-permute-start | bytes 393224 | tf_op jit(solution)/shard_map/ppermute | solution.py:467
  78.6 3.8 %collective-permute-done.34.refs_1_ = f32[64,512]{1,0:T(8,128)S(1)} collective-permute-done((f32[64,512]{1,0:T(8,128)S(1)}, f32[64,512]{1,0:T(8,128)S(1)}, u32[]{:S(2)}, u32[]{:S(2)}) %collective-permute-start.34) | collective-permute-done | bytes 131104 | tf_op jit(solution)/shard_map/ppermute | solution.py:467
  82.4 1.9 %collective-permute-done.35.refs_2_ = f32[64,512]{1,0:T(8,128)S(1)} collective-permute-done((f32[64,512]{1,0:T(8,128)S(1)}, f32[64,512]{1,0:T(8,128)S(1)}, u32[]{:S(2)}, u32[]{:S(2)}) %collective-permute-start.35) | collective-permute-done | bytes 131104 | tf_op jit(solution)/shard_map/ppermute | solution.py:467
  84.5 1.8 %collective-permute-start.39 = (f32[64,64]{1,0:T(8,128)S(1)}, f32[64,64]{1,0:T(8,128)S(1)}, u32[]{:S(2)}, u32[]{:S(2)}) collective-permute-start(f32[64,64]{1,0:T(8,128)S(1)} %get-tuple-element.79.refs_0_), channel_id=1, source_target_pairs={{0,24},{8,16},{16,8},{24,0},{1,25},{9,17},{17,9},{25,1},{2,26},{10... | collective-permute-start | bytes 49160 | tf_op jit(solution)/shard_map/ppermute | solution.py:467
  92.3 2.1 %collective-permute-start.43 = (f32[64,64]{1,0:T(8,128)S(1)}, f32[64,64]{1,0:T(8,128)S(1)}, u32[]{:S(2)}, u32[]{:S(2)}) collective-permute-start(f32[64,64]{1,0:T(8,128)S(1)} %sum.3.refs_0_), channel_id=1, source_target_pairs={{0,6},{1,7},{2,4},{3,5},{4,2},{5,3},{6,0},{7,1},{8,14},{9,15},{10,... | collective-permute-start | bytes 49160 | tf_op jit(solution)/shard_map/ppermute | solution.py:467
  94.3 1.4 %collective-permute-start.42 = (f32[64,64]{1,0:T(8,128)S(1)}, f32[64,64]{1,0:T(8,128)S(1)}, u32[]{:S(2)}, u32[]{:S(2)}) collective-permute-start(f32[64,64]{1,0:T(8,128)S(1)} %sum.3.refs_0_), channel_id=1, source_target_pairs={{0,4},{1,5},{2,6},{3,7},{4,0},{5,1},{6,2},{7,3},{8,12},{9,13},{10,... | collective-permute-start | bytes 49160 | tf_op jit(solution)/shard_map/ppermute | solution.py:467
  96.7 1.6 %collective-permute-done.43.refs_3_ = f32[64,64]{1,0:T(8,128)S(1)} collective-permute-done((f32[64,64]{1,0:T(8,128)S(1)}, f32[64,64]{1,0:T(8,128)S(1)}, u32[]{:S(2)}, u32[]{:S(2)}) %collective-permute-start.43) | collective-permute-done | bytes 16416 | tf_op jit(solution)/shard_map/ppermute | solution.py:467
  99.8 2.5 %finish.1 = f32[64,512]{1,0:T(8,128)} custom-call(f32[64,64]{1,0:T(8,128)S(1)} %sum.3.refs_0_, f32[64,64]{1,0:T(8,128)S(1)} %collective-permute-done.41.refs_1_, f32[64,64]{1,0:T(8,128)S(1)} %collective-permute-done.42.refs_2_, f32[64,64]{1,0:T(8,128)S(1)} %collective-permute-done.43.refs_3_, f32[64,512]{1,0:T(8,128)S(1)} %get-tuple-element.80.refs_4_), custom_call_target="tpu_custom_call" | custom-call | tf_op jit(solution)/shard_map/finish/pallas_call | solution.py:677
  (80 shorter events, 34.5 us)
Async XLA Ops:
  1.0 8.9 %collective-permute-start.2 = (bf16[64,512]{1,0:T(8,128)(2,1)S(1)}, bf16[64,512]{1,0:T(8,128)(2,1)S(1)}, u32[]{:S(2)}, u32[]{:S(2)}) collective-permute-start(bf16[64,512]{1,0:T(8,128)(2,1)S(1)} %start.1.after_ref.refs_0_), channel_id=1, source_target_pairs={{0,24},{8,16},{16,8},{24,0},{1,25},{9,17},{17,9},{25,1},{2,26},{10... | collective-permute-start | bytes 196616 | tf_op jit(solution)/shard_map/ppermute | solution.py:467
  4.9 4.9 %collective-permute-start.1 = (bf16[64,512]{1,0:T(8,128)(2,1)S(1)}, bf16[64,512]{1,0:T(8,128)(2,1)S(1)}, u32[]{:S(2)}, u32[]{:S(2)}) collective-permute-start(bf16[64,512]{1,0:T(8,128)(2,1)S(1)} %start.1.after_ref.refs_0_), channel_id=1, source_target_pairs={{0,16},{8,24},{16,0},{24,8},{1,17},{9,25},{17,1},{25,9},{2,18},{10... | collective-permute-start | bytes 196616 | tf_op jit(solution)/shard_map/ppermute | solution.py:467
  13.4 5.8 %collective-permute-start.4 = (bf16[64,256]{1,0:T(8,128)(2,1)S(1)}, bf16[64,256]{1,0:T(8,128)(2,1)S(1)}, u32[]{:S(2)}, u32[]{:S(2)}) collective-permute-start(bf16[64,256]{1,0:T(8,128)(2,1)S(1)} %get-tuple-element.48), channel_id=1, source_target_pairs={{0,6},{1,7},{2,4},{3,5},{4,2},{5,3},{6,0},{7,1},{8,14},{9,15},{10,... | collective-permute-start | bytes 98312 | tf_op jit(solution)/shard_map/ppermute | solution.py:467
  17.0 4.8 %collective-permute-start.5 = (bf16[64,256]{1,0:T(8,128)(2,1)S(1)}, bf16[64,256]{1,0:T(8,128)(2,1)S(1)}, u32[]{:S(2)}, u32[]{:S(2)}) collective-permute-start(bf16[64,256]{1,0:T(8,128)(2,1)S(1)} %get-tuple-element.49), channel_id=1, source_target_pairs={{0,4},{1,5},{2,6},{3,7},{4,0},{5,1},{6,2},{7,3},{8,12},{9,13},{10,... | collective-permute-start | bytes 98312 | tf_op jit(solution)/shard_map/ppermute | solution.py:467
  17.0 4.8 %collective-permute-start.6 = (bf16[64,256]{1,0:T(8,128)(2,1)S(1)}, bf16[64,256]{1,0:T(8,128)(2,1)S(1)}, u32[]{:S(2)}, u32[]{:S(2)}) collective-permute-start(bf16[64,256]{1,0:T(8,128)(2,1)S(1)} %get-tuple-element.50), channel_id=1, source_target_pairs={{0,2},{1,3},{2,0},{3,1},{4,6},{5,7},{6,4},{7,5},{8,10},{9,11},{10,... | collective-permute-start | bytes 98312 | tf_op jit(solution)/shard_map/ppermute | solution.py:467
  21.9 5.9 %collective-permute-start.9 = (bf16[64,256]{1,0:T(8,128)(2,1)S(1)}, bf16[64,256]{1,0:T(8,128)(2,1)S(1)}, u32[]{:S(2)}, u32[]{:S(2)}) collective-permute-start(bf16[64,256]{1,0:T(8,128)(2,1)S(1)} %query.2.refs_0_), channel_id=1, source_target_pairs={{0,6},{1,7},{2,4},{3,5},{4,2},{5,3},{6,0},{7,1},{8,14},{9,15},{10,... | collective-permute-start | bytes 98312 | tf_op jit(solution)/shard_map/ppermute | solution.py:467
  23.6 4.9 %collective-permute-start.8 = (bf16[64,256]{1,0:T(8,128)(2,1)S(1)}, bf16[64,256]{1,0:T(8,128)(2,1)S(1)}, u32[]{:S(2)}, u32[]{:S(2)}) collective-permute-start(bf16[64,256]{1,0:T(8,128)(2,1)S(1)} %query.2.refs_0_), channel_id=1, source_target_pairs={{0,4},{1,5},{2,6},{3,7},{4,0},{5,1},{6,2},{7,3},{8,12},{9,13},{10,... | collective-permute-start | bytes 98312 | tf_op jit(solution)/shard_map/ppermute | solution.py:467
  24.0 4.5 %collective-permute-start.7 = (bf16[64,256]{1,0:T(8,128)(2,1)S(1)}, bf16[64,256]{1,0:T(8,128)(2,1)S(1)}, u32[]{:S(2)}, u32[]{:S(2)}) collective-permute-start(bf16[64,256]{1,0:T(8,128)(2,1)S(1)} %query.2.refs_0_), channel_id=1, source_target_pairs={{0,2},{1,3},{2,0},{3,1},{4,6},{5,7},{6,4},{7,5},{8,10},{9,11},{10,... | collective-permute-start | bytes 98312 | tf_op jit(solution)/shard_map/ppermute | solution.py:467
  31.5 6.2 %collective-permute-start.11 = (f32[32,512]{1,0:T(8,128)S(1)}, f32[32,512]{1,0:T(8,128)S(1)}, u32[]{:S(2)}, u32[]{:S(2)}) collective-permute-start(f32[32,512]{1,0:T(8,128)S(1)} %get-tuple-element.53), channel_id=1, source_target_pairs={{0,24},{8,16},{16,8},{24,0},{1,25},{9,17},{17,9},{25,1},{2,26},{10... | collective-permute-start | bytes 196616 | tf_op jit(solution)/shard_map/ppermute | solution.py:467
  33.7 4.9 %collective-permute-start.12 = (f32[32,512]{1,0:T(8,128)S(1)}, f32[32,512]{1,0:T(8,128)S(1)}, u32[]{:S(2)}, u32[]{:S(2)}) collective-permute-start(f32[32,512]{1,0:T(8,128)S(1)} %get-tuple-element.54), channel_id=1, source_target_pairs={{0,16},{8,24},{16,0},{24,8},{1,17},{9,25},{17,1},{25,9},{2,18},{10... | collective-permute-start | bytes 196616 | tf_op jit(solution)/shard_map/ppermute | solution.py:467
  34.2 4.9 %collective-permute-start.13 = (f32[32,512]{1,0:T(8,128)S(1)}, f32[32,512]{1,0:T(8,128)S(1)}, u32[]{:S(2)}, u32[]{:S(2)}) collective-permute-start(f32[32,512]{1,0:T(8,128)S(1)} %get-tuple-element.55), channel_id=1, source_target_pairs={{0,8},{8,0},{16,24},{24,16},{1,9},{9,1},{17,25},{25,17},{2,10},{10... | collective-permute-start | bytes 196616 | tf_op jit(solution)/shard_map/ppermute | solution.py:467
  35.1 6.2 %collective-permute-start.17 = (f32[32,512]{1,0:T(8,128)S(1)}, f32[32,512]{1,0:T(8,128)S(1)}, u32[]{:S(2)}, u32[]{:S(2)}) collective-permute-start(f32[32,512]{1,0:T(8,128)S(1)} %get-tuple-element.58), channel_id=1, source_target_pairs={{0,24},{8,16},{16,8},{24,0},{1,25},{9,17},{17,9},{25,1},{2,26},{10... | collective-permute-start | bytes 196616 | tf_op jit(solution)/shard_map/ppermute | solution.py:467
  37.2 5.5 %collective-permute-start.18 = (f32[32,512]{1,0:T(8,128)S(1)}, f32[32,512]{1,0:T(8,128)S(1)}, u32[]{:S(2)}, u32[]{:S(2)}) collective-permute-start(f32[32,512]{1,0:T(8,128)S(1)} %get-tuple-element.59), channel_id=1, source_target_pairs={{0,16},{8,24},{16,0},{24,8},{1,17},{9,25},{17,1},{25,9},{2,18},{10... | collective-permute-start | bytes 196616 | tf_op jit(solution)/shard_map/ppermute | solution.py:467
  37.7 5.0 %collective-permute-start.19 = (f32[32,512]{1,0:T(8,128)S(1)}, f32[32,512]{1,0:T(8,128)S(1)}, u32[]{:S(2)}, u32[]{:S(2)}) collective-permute-start(f32[32,512]{1,0:T(8,128)S(1)} %get-tuple-element.60), channel_id=1, source_target_pairs={{0,8},{8,0},{16,24},{24,16},{1,9},{9,1},{17,25},{25,17},{2,10},{10... | collective-permute-start | bytes 196616 | tf_op jit(solution)/shard_map/ppermute | solution.py:467
  39.2 5.8 %collective-permute-start.16 = (f32[32,512]{1,0:T(8,128)S(1)}, f32[32,512]{1,0:T(8,128)S(1)}, u32[]{:S(2)}, u32[]{:S(2)}) collective-permute-start(f32[32,512]{1,0:T(8,128)S(1)} %lift.3.refs_0_), channel_id=1, source_target_pairs={{0,24},{8,16},{16,8},{24,0},{1,25},{9,17},{17,9},{25,1},{2,26},{10... | collective-permute-start | bytes 196616 | tf_op jit(solution)/shard_map/ppermute | solution.py:467
  40.8 5.7 %collective-permute-start.15 = (f32[32,512]{1,0:T(8,128)S(1)}, f32[32,512]{1,0:T(8,128)S(1)}, u32[]{:S(2)}, u32[]{:S(2)}) collective-permute-start(f32[32,512]{1,0:T(8,128)S(1)} %lift.3.refs_0_), channel_id=1, source_target_pairs={{0,16},{8,24},{16,0},{24,8},{1,17},{9,25},{17,1},{25,9},{2,18},{10... | collective-permute-start | bytes 196616 | tf_op jit(solution)/shard_map/ppermute | solution.py:467
  41.3 5.2 %collective-permute-start.14 = (f32[32,512]{1,0:T(8,128)S(1)}, f32[32,512]{1,0:T(8,128)S(1)}, u32[]{:S(2)}, u32[]{:S(2)}) collective-permute-start(f32[32,512]{1,0:T(8,128)S(1)} %lift.3.refs_0_), channel_id=1, source_target_pairs={{0,8},{8,0},{16,24},{24,16},{1,9},{9,1},{17,25},{25,17},{2,10},{10... | collective-permute-start | bytes 196616 | tf_op jit(solution)/shard_map/ppermute | solution.py:467
  42.8 5.2 %collective-permute-start.22 = (f32[32,512]{1,0:T(8,128)S(1)}, f32[32,512]{1,0:T(8,128)S(1)}, u32[]{:S(2)}, u32[]{:S(2)}) collective-permute-start(f32[32,512]{1,0:T(8,128)S(1)} %lift.4.refs_4_), channel_id=1, source_target_pairs={{0,24},{8,16},{16,8},{24,0},{1,25},{9,17},{17,9},{25,1},{2,26},{10... | collective-permute-start | bytes 196616 | tf_op jit(solution)/shard_map/ppermute | solution.py:467
  53.4 6.4 %collective-permute-start.27 = (f32[96,128]{1,0:T(8,128)S(1)}, f32[96,128]{1,0:T(8,128)S(1)}, u32[]{:S(2)}, u32[]{:S(2)}) collective-permute-start(f32[96,128]{1,0:T(8,128)S(1)} %get-tuple-element.70), channel_id=1, source_target_pairs={{0,6},{1,7},{2,4},{3,5},{4,2},{5,3},{6,0},{7,1},{8,14},{9,15},{10,... | collective-permute-start | bytes 147464 | tf_op jit(solution)/shard_map/ppermute | solution.py:467
  55.2 7.0 %collective-permute-start.28 = (f32[96,128]{1,0:T(8,128)S(1)}, f32[96,128]{1,0:T(8,128)S(1)}, u32[]{:S(2)}, u32[]{:S(2)}) collective-permute-start(f32[96,128]{1,0:T(8,128)S(1)} %get-tuple-element.71), channel_id=1, source_target_pairs={{0,4},{1,5},{2,6},{3,7},{4,0},{5,1},{6,2},{7,3},{8,12},{9,13},{10,... | collective-permute-start | bytes 147464 | tf_op jit(solution)/shard_map/ppermute | solution.py:467
  56.1 6.2 %collective-permute-start.29 = (f32[96,128]{1,0:T(8,128)S(1)}, f32[96,128]{1,0:T(8,128)S(1)}, u32[]{:S(2)}, u32[]{:S(2)}) collective-permute-start(f32[96,128]{1,0:T(8,128)S(1)} %get-tuple-element.72), channel_id=1, source_target_pairs={{0,2},{1,3},{2,0},{3,1},{4,6},{5,7},{6,4},{7,5},{8,10},{9,11},{10,... | collective-permute-start | bytes 147464 | tf_op jit(solution)/shard_map/ppermute | solution.py:467
  57.8 6.2 %collective-permute-start.24 = (f32[64,128]{1,0:T(8,128)S(1)}, f32[64,128]{1,0:T(8,128)S(1)}, u32[]{:S(2)}, u32[]{:S(2)}) collective-permute-start(f32[64,128]{1,0:T(8,128)S(1)} %get-tuple-element.66), channel_id=1, source_target_pairs={{0,6},{1,7},{2,4},{3,5},{4,2},{5,3},{6,0},{7,1},{8,14},{9,15},{10,... | collective-permute-start | bytes 98312 | tf_op jit(solution)/shard_map/ppermute | solution.py:467
  59.6 4.9 %collective-permute-start.25 = (f32[64,128]{1,0:T(8,128)S(1)}, f32[64,128]{1,0:T(8,128)S(1)}, u32[]{:S(2)}, u32[]{:S(2)}) collective-permute-start(f32[64,128]{1,0:T(8,128)S(1)} %get-tuple-element.67), channel_id=1, source_target_pairs={{0,4},{1,5},{2,6},{3,7},{4,0},{5,1},{6,2},{7,3},{8,12},{9,13},{10,... | collective-permute-start | bytes 98312 | tf_op jit(solution)/shard_map/ppermute | solution.py:467
  59.9 4.6 %collective-permute-start.26 = (f32[64,128]{1,0:T(8,128)S(1)}, f32[64,128]{1,0:T(8,128)S(1)}, u32[]{:S(2)}, u32[]{:S(2)}) collective-permute-start(f32[64,128]{1,0:T(8,128)S(1)} %get-tuple-element.68), channel_id=1, source_target_pairs={{0,2},{1,3},{2,0},{3,1},{4,6},{5,7},{6,4},{7,5},{8,10},{9,11},{10,... | collective-permute-start | bytes 98312 | tf_op jit(solution)/shard_map/ppermute | solution.py:467
  64.7 5.8 %collective-permute-start.32 = (bf16[64,256]{1,0:T(8,128)(2,1)S(1)}, bf16[64,256]{1,0:T(8,128)(2,1)S(1)}, u32[]{:S(2)}, u32[]{:S(2)}) collective-permute-start(bf16[64,256]{1,0:T(8,128)(2,1)S(1)} %query_rest.1.refs_0_), channel_id=1, source_target_pairs={{0,6},{1,7},{2,4},{3,5},{4,2},{5,3},{6,0},{7,1},{8,14},{9,15},{10,... | collective-permute-start | bytes 98312 | tf_op jit(solution)/shard_map/ppermute | solution.py:467
  66.7 5.2 %collective-permute-start.31 = (bf16[64,256]{1,0:T(8,128)(2,1)S(1)}, bf16[64,256]{1,0:T(8,128)(2,1)S(1)}, u32[]{:S(2)}, u32[]{:S(2)}) collective-permute-start(bf16[64,256]{1,0:T(8,128)(2,1)S(1)} %query_rest.1.refs_0_), channel_id=1, source_target_pairs={{0,4},{1,5},{2,6},{3,7},{4,0},{5,1},{6,2},{7,3},{8,12},{9,13},{10,... | collective-permute-start | bytes 98312 | tf_op jit(solution)/shard_map/ppermute | solution.py:467
  75.0 7.3 %collective-permute-start.34 = (f32[64,512]{1,0:T(8,128)S(1)}, f32[64,512]{1,0:T(8,128)S(1)}, u32[]{:S(2)}, u32[]{:S(2)}) collective-permute-start(f32[64,512]{1,0:T(8,128)S(1)} %get-tuple-element.76), channel_id=1, source_target_pairs={{0,24},{8,16},{16,8},{24,0},{1,25},{9,17},{17,9},{25,1},{2,26},{10... | collective-permute-start | bytes 393224 | tf_op jit(solution)/shard_map/ppermute | solution.py:467
  76.7 7.6 %collective-permute-start.35 = (f32[64,512]{1,0:T(8,128)S(1)}, f32[64,512]{1,0:T(8,128)S(1)}, u32[]{:S(2)}, u32[]{:S(2)}) collective-permute-start(f32[64,512]{1,0:T(8,128)S(1)} %get-tuple-element.77), channel_id=1, source_target_pairs={{0,16},{8,24},{16,0},{24,8},{1,17},{9,25},{17,1},{25,9},{2,18},{10... | collective-permute-start | bytes 393224 | tf_op jit(solution)/shard_map/ppermute | solution.py:467
  77.2 7.0 %collective-permute-start.36 = (f32[64,512]{1,0:T(8,128)S(1)}, f32[64,512]{1,0:T(8,128)S(1)}, u32[]{:S(2)}, u32[]{:S(2)}) collective-permute-start(f32[64,512]{1,0:T(8,128)S(1)} %get-tuple-element.78), channel_id=1, source_target_pairs={{0,8},{8,0},{16,24},{24,16},{1,9},{9,1},{17,25},{25,17},{2,10},{10... | collective-permute-start | bytes 393224 | tf_op jit(solution)/shard_map/ppermute | solution.py:467
  84.5 4.9 %collective-permute-start.39 = (f32[64,64]{1,0:T(8,128)S(1)}, f32[64,64]{1,0:T(8,128)S(1)}, u32[]{:S(2)}, u32[]{:S(2)}) collective-permute-start(f32[64,64]{1,0:T(8,128)S(1)} %get-tuple-element.79.refs_0_), channel_id=1, source_target_pairs={{0,24},{8,16},{16,8},{24,0},{1,25},{9,17},{17,9},{25,1},{2,26},{10... | collective-permute-start | bytes 49160 | tf_op jit(solution)/shard_map/ppermute | solution.py:467
  92.3 6.0 %collective-permute-start.43 = (f32[64,64]{1,0:T(8,128)S(1)}, f32[64,64]{1,0:T(8,128)S(1)}, u32[]{:S(2)}, u32[]{:S(2)}) collective-permute-start(f32[64,64]{1,0:T(8,128)S(1)} %sum.3.refs_0_), channel_id=1, source_target_pairs={{0,6},{1,7},{2,4},{3,5},{4,2},{5,3},{6,0},{7,1},{8,14},{9,15},{10,... | collective-permute-start | bytes 49160 | tf_op jit(solution)/shard_map/ppermute | solution.py:467
  94.3 5.1 %collective-permute-start.42 = (f32[64,64]{1,0:T(8,128)S(1)}, f32[64,64]{1,0:T(8,128)S(1)}, u32[]{:S(2)}, u32[]{:S(2)}) collective-permute-start(f32[64,64]{1,0:T(8,128)S(1)} %sum.3.refs_0_), channel_id=1, source_target_pairs={{0,4},{1,5},{2,6},{3,7},{4,0},{5,1},{6,2},{7,3},{8,12},{9,13},{10,... | collective-permute-start | bytes 49160 | tf_op jit(solution)/shard_map/ppermute | solution.py:467
  (12 other events, 36.4 us)

commit v8 on v7

--- a/solution.py
+++ b/solution.py
@@ -453,11 +453,11 @@
     refs[-1][...] = add(refs[:-1])
 
 
-def finish_body(after, *refs):
-    grams, lifted_ref, out_ref = refs[:-2], refs[-2], refs[-1]
+def finish_body(after, table, total_ref, got_ref, lifted_ref, out_ref):
+    gram = jnp.where(table[SINGLES, COL_AT] % 2 == 1, total_ref[...], got_ref[...])
     out_ref[...] = (
         lax.dot_general(
-            inverse_factor(add(grams)), lifted_ref[...], NN, precision=HIGH, preferred_element_type=jnp.float32
+            inverse_factor(gram), lifted_ref[...], NN, precision=HIGH, preferred_element_type=jnp.float32
         )
         * after
     )
@@ -480,8 +480,22 @@
     return call(sum_body, "sum", [WHOLE] * len(values), f32(*values[0].shape))(*values)
 
 
-def terms_over_col(gram):
-    return spread_to(add_up(gram, swap(gram, "col", 1)), "col", 2)
+def core_one_terms(value, axis):
+    n_row, n_col = lax.axis_size("row"), lax.axis_size("col")
+    terms = [value]
+    reach = [(step, 0) for step in range(1, n_row)] if axis == "row" else [(0, step) for step in range(2, n_col, 2)]
+    for row_step, col_step in reach:
+        pairs = [
+            (row * n_col + col, (row ^ row_step) * n_col + (col ^ col_step))
+            for row in range(n_row)
+            for col in range(1, n_col, 2)
+        ]
+        terms.append(lax.ppermute(value, ("row", "col"), pairs))
+    return terms
+
+
+def hand_over(value):
+    return lax.ppermute(value, "col", [(col, col - 1) for col in range(1, lax.axis_size("col"), 2)])
 
 
 def shards(tiles, tile_ids, tile_count, query_degree, product_degree, panel):
@@ -674,9 +688,12 @@
     lifted, gram = call(
         lift_body, "lift", [WHOLE] * (n_row + 1), [f32(width, share), f32(width, width)]
     )(*parts[0], my_pscale)
+    total = add_up(gram, swap(gram, "col", 1))
+    for axis in ("row", "col"):
+        total = add_up(*core_one_terms(total, axis))
     return call(
-        functools.partial(finish_body, root_count), "finish", [WHOLE] * (chips + 1), f32(width, share)
-    )(*terms_over_col(add_up(*spread_to(gram, "row"))), lifted)
+        functools.partial(finish_body, root_count), "finish", [SCALARS] + [WHOLE] * 3, f32(width, share)
+    )(table, total, hand_over(total), lifted)
 
 
 def solution(mesh):

time: 102 us -> 113 us (1.11)
  waiting for transfers between devices: 26.8 us -> 39.8 us
  starting transfers between devices: 52.5 us -> 50.6 us
    ppermute x0 -> x7, waiting for transfers between devices: none -> 18.2 us  [the longest x1 18.2 us: hand_over(): lax.ppermute(value, 'col', [(col, col - 1) for col in range(1, lax.axis_s...]
    ppermute x44 -> x38, starting transfers between devices: 52.5 us -> 45.3 us  [swap(): lax.ppermute(value, axis, [(i, i ^ step) for i in range(lax.axis_size(axi...]
    ppermute x0 -> x7, starting transfers between devices: none -> 5.26 us  [the longest x6 3.97 us: core_one_terms(): terms.append(lax.ppermute(value, ('row', 'col'), pairs))]
    ppermute x44 -> x38, waiting for transfers between devices: 26.8 us -> 21.6 us  [swap(): lax.ppermute(value, axis, [(i, i ^ step) for i in range(lax.axis_size(axi...]
  transfers between devices with their start and end apart: 44 -> 45, of which waited for: 26 -> 21; matrix products, arithmetic and copies ran while one was open for 0% -> 0% of each run, Pallas kernels for 10% -> 9%
where the time goes in v8:
time: 113 us
  starting transfers between devices  50.6 us (45%)
  waiting for transfers between devices  39.8 us (35%)
  Pallas kernels  21.3 us (19%)
    ppermute x38, starting transfers between devices, swap(): lax.ppermute(value, axis, [(i, i ^ step) for i in range(lax.axis_size(axi...  45.3 us
    ppermute x38, waiting for transfers between devices, swap(): lax.ppermute(value, axis, [(i, i ^ step) for i in range(lax.axis_size(axi...  21.6 us
    ppermute x1, waiting for transfers between devices, hand_over(): lax.ppermute(value, 'col', [(col, col - 1) for col in range(1, lax.axis_s...  18.2 us
    ppermute x6, starting transfers between devices, core_one_terms(): terms.append(lax.ppermute(value, ('row', 'col'), pairs))  3.97 us
    pallas_call x1, Pallas kernels, shards(): call(functools.partial(load_body, columns // side if split else 0), 'load...  3.53 us
    pallas_call x1, Pallas kernels, shards(): call(functools.partial(finish_body, root_count), 'finish', [SCALARS] + [W...  3.18 us
    pallas_call x2, Pallas kernels, shards(): call(back_other_body, 'backward_rest', [SCALARS] + [WHOLE] * 3, [f32(widt...  2.4 us
    pallas_call x2, Pallas kernels, shards(): call(functools.partial(back_mine_body, chips), 'backward', [SCALARS] + [W...  2.33 us
  transfers between devices with their start and end apart: 45, of which 21 were waited for; matrix products, arithmetic and copies ran while one was open for 0% of the time, Pallas kernels for 9%

profile of v8, /device:TPU:0, one launch (start us, length us, event | category | flops | bytes accessed | tf_op | source)
XLA Modules:
  0.0 112.7 jit_solution(9595854072084971486)
XLA Ops:
  1.0 4.0 %collective-permute-start.2 = (bf16[64,512]{1,0:T(8,128)(2,1)S(1)}, bf16[64,512]{1,0:T(8,128)(2,1)S(1)}, u32[]{:S(2)}, u32[]{:S(2)}) collective-permute-start(bf16[64,512]{1,0:T(8,128)(2,1)S(1)} %start.1.after_ref.refs_0_), channel_id=1, source_target_pairs={{0,24},{8,16},{16,8},{24,0},{1,25},{9,17},{17,9},{25,1},{2,26},{10... | collective-permute-start | bytes 196616 | tf_op jit(solution)/shard_map/ppermute | solution.py:467
  6.3 3.5 %load.1 = (bf16[32,256,256]{2,1,0:T(8,128)(2,1)S(1)}, f32[1,512]{1,0:T(1,128)S(1)}, f32[1,2048]{1,0:T(1,128)S(1)}, f32[1,256]{1,0:T(1,128)S(1)}, s32[10,32]{1,0:T(8,128)S(1)}) custom-call(s32[3]{0:T(128)S(1)} %pad_add_fusion.place, bf16[64,512]{1,0:T(8,128)(2,1)S(1)} %start.1.after_ref.refs_0_, bf16[32,256,256]{2,1,0:T(8,128)(2,1)} %bitcast.8, ...), custom_call_target="tpu_custom_call" | custom-call | bytes 8388608 | tf_op jit(solution)/shard_map/load/pallas_call | solution.py:526
  9.9 1.4 %forward.2 = (bf16[9,64,256]{2,1,0:T(8,128)(2,1)S(1)}, f32[4,64,256]{2,1,0:T(8,128)S(1)}) custom-call(s32[10,32]{1,0:T(8,128)S(1)} %get-tuple-element.43.table, bf16[64,512]{1,0:T(8,128)(2,1)S(1)} %start.1.after_ref.refs_0_, bf16[64,512]{1,0:T(8,128)(2,1)S(1)} %collective-permute-done.refs_1_, bf16[64,512]{1,0:T(8,128)(2,1)S(1)} %collective-permute-done.1.refs_2_, ...), custom_call_target="tpu_custom_call" | custom-call | flops 134217728 | bytes 2097152 | tf_op jit(solution)/shard_map/forward/pallas_call | solution.py:620
  11.4 1.5 %forward_rest.2.mine_ref = f32[4,64,256]{2,1,0:T(8,128)S(1)} custom-call(s32[10,32]{1,0:T(8,128)S(1)} %get-tuple-element.43.table, bf16[9,64,256]{2,1,0:T(8,128)(2,1)S(1)} %get-tuple-element.45.held, bf16[32,256,256]{2,1,0:T(8,128)(2,1)S(1)} %get-tuple-element.44.refs_4_.tile_ref.refs_9_), custom_call_target="tpu_custom_call" | custom-call | flops 134217728 | bytes 2097152 | tf_op jit(solution)/shard_map/forward_rest/pallas_call | solution.py:629
  13.0 4.1 %collective-permute-start.4 = (bf16[64,256]{1,0:T(8,128)(2,1)S(1)}, bf16[64,256]{1,0:T(8,128)(2,1)S(1)}, u32[]{:S(2)}, u32[]{:S(2)}) collective-permute-start(bf16[64,256]{1,0:T(8,128)(2,1)S(1)} %get-tuple-element.48), channel_id=1, source_target_pairs={{0,6},{1,7},{2,4},{3,5},{4,2},{5,3},{6,0},{7,1},{8,14},{9,15},{10,... | collective-permute-start | bytes 98312 | tf_op jit(solution)/shard_map/ppermute | solution.py:467
  17.7 1.4 %collective-permute-done.4.refs_1_ = bf16[64,256]{1,0:T(8,128)(2,1)S(1)} collective-permute-done((bf16[64,256]{1,0:T(8,128)(2,1)S(1)}, bf16[64,256]{1,0:T(8,128)(2,1)S(1)}, u32[]{:S(2)}, u32[]{:S(2)}) %collective-permute-start.4) | collective-permute-done | bytes 32800 | tf_op jit(solution)/shard_map/ppermute | solution.py:467
  19.0 2.8 %collective-permute-done.5.refs_2_ = bf16[64,256]{1,0:T(8,128)(2,1)S(1)} collective-permute-done((bf16[64,256]{1,0:T(8,128)(2,1)S(1)}, bf16[64,256]{1,0:T(8,128)(2,1)S(1)}, u32[]{:S(2)}, u32[]{:S(2)}) %collective-permute-start.5) | collective-permute-done | bytes 32800 | tf_op jit(solution)/shard_map/ppermute | solution.py:467
  21.9 1.6 %collective-permute-start.9 = (bf16[64,256]{1,0:T(8,128)(2,1)S(1)}, bf16[64,256]{1,0:T(8,128)(2,1)S(1)}, u32[]{:S(2)}, u32[]{:S(2)}) collective-permute-start(bf16[64,256]{1,0:T(8,128)(2,1)S(1)} %query.2.refs_0_), channel_id=1, source_target_pairs={{0,6},{1,7},{2,4},{3,5},{4,2},{5,3},{6,0},{7,1},{8,14},{9,15},{10,... | collective-permute-start | bytes 98312 | tf_op jit(solution)/shard_map/ppermute | solution.py:467
  24.0 2.3 %collective-permute-start.7 = (bf16[64,256]{1,0:T(8,128)(2,1)S(1)}, bf16[64,256]{1,0:T(8,128)(2,1)S(1)}, u32[]{:S(2)}, u32[]{:S(2)}) collective-permute-start(bf16[64,256]{1,0:T(8,128)(2,1)S(1)} %query.2.refs_0_), channel_id=1, source_target_pairs={{0,2},{1,3},{2,0},{3,1},{4,6},{5,7},{6,4},{7,5},{8,10},{9,11},{10,... | collective-permute-start | bytes 98312 | tf_op jit(solution)/shard_map/ppermute | solution.py:467
  26.3 1.5 %collective-permute-done.9.refs_3_ = bf16[64,256]{1,0:T(8,128)(2,1)S(1)} collective-permute-done((bf16[64,256]{1,0:T(8,128)(2,1)S(1)}, bf16[64,256]{1,0:T(8,128)(2,1)S(1)}, u32[]{:S(2)}, u32[]{:S(2)}) %collective-permute-start.9) | collective-permute-done | bytes 32800 | tf_op jit(solution)/shard_map/ppermute | solution.py:467
  31.2 2.5 %collective-permute-start.11 = (f32[32,512]{1,0:T(8,128)S(1)}, f32[32,512]{1,0:T(8,128)S(1)}, u32[]{:S(2)}, u32[]{:S(2)}) collective-permute-start(f32[32,512]{1,0:T(8,128)S(1)} %get-tuple-element.53), channel_id=1, source_target_pairs={{0,24},{8,16},{16,8},{24,0},{1,25},{9,17},{17,9},{25,1},{2,26},{10... | collective-permute-start | bytes 196616 | tf_op jit(solution)/shard_map/ppermute | solution.py:467
  34.7 2.4 %collective-permute-start.17 = (f32[32,512]{1,0:T(8,128)S(1)}, f32[32,512]{1,0:T(8,128)S(1)}, u32[]{:S(2)}, u32[]{:S(2)}) collective-permute-start(f32[32,512]{1,0:T(8,128)S(1)} %get-tuple-element.58), channel_id=1, source_target_pairs={{0,24},{8,16},{16,8},{24,0},{1,25},{9,17},{17,9},{25,1},{2,26},{10... | collective-permute-start | bytes 196616 | tf_op jit(solution)/shard_map/ppermute | solution.py:467
  41.7 1.4 %collective-permute-start.14 = (f32[32,512]{1,0:T(8,128)S(1)}, f32[32,512]{1,0:T(8,128)S(1)}, u32[]{:S(2)}, u32[]{:S(2)}) collective-permute-start(f32[32,512]{1,0:T(8,128)S(1)} %lift.3.refs_0_), channel_id=1, source_target_pairs={{0,8},{8,0},{16,24},{24,16},{1,9},{9,1},{17,25},{25,17},{2,10},{10... | collective-permute-start | bytes 196616 | tf_op jit(solution)/shard_map/ppermute | solution.py:467
  45.3 1.4 %collective-permute-start.20 = (f32[32,512]{1,0:T(8,128)S(1)}, f32[32,512]{1,0:T(8,128)S(1)}, u32[]{:S(2)}, u32[]{:S(2)}) collective-permute-start(f32[32,512]{1,0:T(8,128)S(1)} %lift.4.refs_4_), channel_id=1, source_target_pairs={{0,8},{8,0},{16,24},{24,16},{1,9},{9,1},{17,25},{25,17},{2,10},{10... | collective-permute-start | bytes 196616 | tf_op jit(solution)/shard_map/ppermute | solution.py:467
  46.8 1.6 %collective-permute-done.22.refs_7_ = f32[32,512]{1,0:T(8,128)S(1)} collective-permute-done((f32[32,512]{1,0:T(8,128)S(1)}, f32[32,512]{1,0:T(8,128)S(1)}, u32[]{:S(2)}, u32[]{:S(2)}) %collective-permute-start.22) | collective-permute-done | bytes 65568 | tf_op jit(solution)/shard_map/ppermute | solution.py:467
  49.5 1.9 %forward.3 = (bf16[9,128,256]{2,1,0:T(8,128)(2,1)S(1)}, f32[272,256]{1,0:T(8,128)S(1)}, f32[16,256]{1,0:T(8,128)S(1)}) custom-call(s32[10,32]{1,0:T(8,128)S(1)} %get-tuple-element.43.table, f32[32,512]{1,0:T(8,128)S(1)} %lift.3.refs_0_, f32[32,512]{1,0:T(8,128)S(1)} %collective-permute-done.14.refs_1_, f32[32,512]{1,0:T(8,128)S(1)} %collective-permute-done.15.refs_2_, ...), custom_call_target="tpu_custom_call" | custom-call | flops 134217728 | bytes 2097152 | tf_op jit(solution)/shard_map/forward/pallas_call | solution.py:569
  51.6 1.5 %forward_rest.3.mine_ref = f32[256,256]{1,0:T(8,128)S(1)} custom-call(s32[10,32]{1,0:T(8,128)S(1)} %get-tuple-element.43.table, bf16[9,128,256]{2,1,0:T(8,128)(2,1)S(1)} %get-tuple-element.62.held, bf16[32,256,256]{2,1,0:T(8,128)(2,1)S(1)} %get-tuple-element.44.refs_4_.tile_ref.refs_9_), custom_call_target="tpu_custom_call" | custom-call | flops 134217728 | bytes 2097152 | tf_op jit(solution)/shard_map/forward_rest/pallas_call | solution.py:578
  53.2 2.5 %collective-permute-start.27 = (f32[96,128]{1,0:T(8,128)S(1)}, f32[96,128]{1,0:T(8,128)S(1)}, u32[]{:S(2)}, u32[]{:S(2)}) collective-permute-start(f32[96,128]{1,0:T(8,128)S(1)} %get-tuple-element.70), channel_id=1, source_target_pairs={{0,6},{1,7},{2,4},{3,5},{4,2},{5,3},{6,0},{7,1},{8,14},{9,15},{10,... | collective-permute-start | bytes 147464 | tf_op jit(solution)/shard_map/ppermute | solution.py:467
  56.4 1.2 %collective-permute-start.29 = (f32[96,128]{1,0:T(8,128)S(1)}, f32[96,128]{1,0:T(8,128)S(1)}, u32[]{:S(2)}, u32[]{:S(2)}) collective-permute-start(f32[96,128]{1,0:T(8,128)S(1)} %get-tuple-element.72), channel_id=1, source_target_pairs={{0,2},{1,3},{2,0},{3,1},{4,6},{5,7},{6,4},{7,5},{8,10},{9,11},{10,... | collective-permute-start | bytes 147464 | tf_op jit(solution)/shard_map/ppermute | solution.py:467
  57.6 2.5 %collective-permute-start.24 = (f32[64,128]{1,0:T(8,128)S(1)}, f32[64,128]{1,0:T(8,128)S(1)}, u32[]{:S(2)}, u32[]{:S(2)}) collective-permute-start(f32[64,128]{1,0:T(8,128)S(1)} %get-tuple-element.66), channel_id=1, source_target_pairs={{0,6},{1,7},{2,4},{3,5},{4,2},{5,3},{6,0},{7,1},{8,14},{9,15},{10,... | collective-permute-start | bytes 98312 | tf_op jit(solution)/shard_map/ppermute | solution.py:467
  60.2 1.9 %collective-permute-start.26 = (f32[64,128]{1,0:T(8,128)S(1)}, f32[64,128]{1,0:T(8,128)S(1)}, u32[]{:S(2)}, u32[]{:S(2)}) collective-permute-start(f32[64,128]{1,0:T(8,128)S(1)} %get-tuple-element.68), channel_id=1, source_target_pairs={{0,2},{1,3},{2,0},{3,1},{4,6},{5,7},{6,4},{7,5},{8,10},{9,11},{10,... | collective-permute-start | bytes 98312 | tf_op jit(solution)/shard_map/ppermute | solution.py:467
  62.3 1.8 %query.3 = (f32[64,64]{1,0:T(8,128)S(1)}, bf16[64,128]{1,0:T(8,128)(2,1)S(1)}) custom-call(f32[96,128]{1,0:T(8,128)S(1)} %get-tuple-element.69.refs_0_, f32[96,128]{1,0:T(8,128)S(1)} %collective-permute-done.27.refs_1_, f32[96,128]{1,0:T(8,128)S(1)} %collective-permute-done.28.refs_2_, f32[96,128]{1,0:T(8,128)S(1)} %collective-permute-done.29.refs_3_, ...), custom_call_target="tpu_custom_call" | custom-call | flops 268435456 | tf_op jit(solution)/shard_map/query/pallas_call | solution.py:609
  65.2 1.9 %collective-permute-start.32 = (bf16[64,256]{1,0:T(8,128)(2,1)S(1)}, bf16[64,256]{1,0:T(8,128)(2,1)S(1)}, u32[]{:S(2)}, u32[]{:S(2)}) collective-permute-start(bf16[64,256]{1,0:T(8,128)(2,1)S(1)} %query_rest.1.refs_0_), channel_id=1, source_target_pairs={{0,6},{1,7},{2,4},{3,5},{4,2},{5,3},{6,0},{7,1},{8,14},{9,15},{10,... | collective-permute-start | bytes 98312 | tf_op jit(solution)/shard_map/ppermute | solution.py:467
  67.6 2.0 %collective-permute-start.30 = (bf16[64,256]{1,0:T(8,128)(2,1)S(1)}, bf16[64,256]{1,0:T(8,128)(2,1)S(1)}, u32[]{:S(2)}, u32[]{:S(2)}) collective-permute-start(bf16[64,256]{1,0:T(8,128)(2,1)S(1)} %query_rest.1.refs_0_), channel_id=1, source_target_pairs={{0,2},{1,3},{2,0},{3,1},{4,6},{5,7},{6,4},{7,5},{8,10},{9,11},{10,... | collective-permute-start | bytes 98312 | tf_op jit(solution)/shard_map/ppermute | solution.py:467
  69.6 1.5 %collective-permute-done.32.refs_3_ = bf16[64,256]{1,0:T(8,128)(2,1)S(1)} collective-permute-done((bf16[64,256]{1,0:T(8,128)(2,1)S(1)}, bf16[64,256]{1,0:T(8,128)(2,1)S(1)}, u32[]{:S(2)}, u32[]{:S(2)}) %collective-permute-start.32) | collective-permute-done | bytes 32800 | tf_op jit(solution)/shard_map/ppermute | solution.py:467
  74.8 1.4 %collective-permute-start.34 = (f32[64,512]{1,0:T(8,128)S(1)}, f32[64,512]{1,0:T(8,128)S(1)}, u32[]{:S(2)}, u32[]{:S(2)}) collective-permute-start(f32[64,512]{1,0:T(8,128)S(1)} %get-tuple-element.76), channel_id=1, source_target_pairs={{0,24},{8,16},{16,8},{24,0},{1,25},{9,17},{17,9},{25,1},{2,26},{10... | collective-permute-start | bytes 393224 | tf_op jit(solution)/shard_map/ppermute | solution.py:467
  76.3 1.5 %collective-permute-start.35 = (f32[64,512]{1,0:T(8,128)S(1)}, f32[64,512]{1,0:T(8,128)S(1)}, u32[]{:S(2)}, u32[]{:S(2)}) collective-permute-start(f32[64,512]{1,0:T(8,128)S(1)} %get-tuple-element.77), channel_id=1, source_target_pairs={{0,16},{8,24},{16,0},{24,8},{1,17},{9,25},{17,1},{25,9},{2,18},{10... | collective-permute-start | bytes 393224 | tf_op jit(solution)/shard_map/ppermute | solution.py:467
  78.4 3.8 %collective-permute-done.34.refs_1_ = f32[64,512]{1,0:T(8,128)S(1)} collective-permute-done((f32[64,512]{1,0:T(8,128)S(1)}, f32[64,512]{1,0:T(8,128)S(1)}, u32[]{:S(2)}, u32[]{:S(2)}) %collective-permute-start.34) | collective-permute-done | bytes 131104 | tf_op jit(solution)/shard_map/ppermute | solution.py:467
  82.1 2.2 %collective-permute-done.35.refs_2_ = f32[64,512]{1,0:T(8,128)S(1)} collective-permute-done((f32[64,512]{1,0:T(8,128)S(1)}, f32[64,512]{1,0:T(8,128)S(1)}, u32[]{:S(2)}, u32[]{:S(2)}) %collective-permute-start.35) | collective-permute-done | bytes 131104 | tf_op jit(solution)/shard_map/ppermute | solution.py:467
  90.0 1.3 %collective-permute-start.44 = (f32[64,64]{1,0:T(8,128)S(1)}, f32[64,64]{1,0:T(8,128)S(1)}, u32[]{:S(2)}, u32[]{:S(2)}) collective-permute-start(f32[64,64]{1,0:T(8,128)S(1)} %sum.5.total_ref), channel_id=1, source_target_pairs={{1,0},{3,2},{5,4},{7,6},{9,8},{11,10},{13,12},{15,14},{17,16},{19,... | collective-permute-start | bytes 49160 | tf_op jit(solution)/shard_map/ppermute | solution.py:498
  91.3 18.2 %collective-permute-done.44.got_ref = f32[64,64]{1,0:T(8,128)S(1)} collective-permute-done((f32[64,64]{1,0:T(8,128)S(1)}, f32[64,64]{1,0:T(8,128)S(1)}, u32[]{:S(2)}, u32[]{:S(2)}) %collective-permute-start.44) | collective-permute-done | bytes 16416 | tf_op jit(solution)/shard_map/ppermute | solution.py:498
  109.5 3.2 %finish.1 = f32[64,512]{1,0:T(8,128)} custom-call(s32[10,32]{1,0:T(8,128)S(1)} %get-tuple-element.43.table, f32[64,64]{1,0:T(8,128)S(1)} %sum.5.total_ref, f32[64,64]{1,0:T(8,128)S(1)} %collective-permute-done.44.got_ref, f32[64,512]{1,0:T(8,128)S(1)} %get-tuple-element.80.lifted_ref), custom_call_target="tpu_custom_call" | custom-call | tf_op jit(solution)/shard_map/finish/pallas_call | solution.py:694
  (83 shorter events, 28.2 us)
Async XLA Ops:
  1.0 8.9 %collective-permute-start.2 = (bf16[64,512]{1,0:T(8,128)(2,1)S(1)}, bf16[64,512]{1,0:T(8,128)(2,1)S(1)}, u32[]{:S(2)}, u32[]{:S(2)}) collective-permute-start(bf16[64,512]{1,0:T(8,128)(2,1)S(1)} %start.1.after_ref.refs_0_), channel_id=1, source_target_pairs={{0,24},{8,16},{16,8},{24,0},{1,25},{9,17},{17,9},{25,1},{2,26},{10... | collective-permute-start | bytes 196616 | tf_op jit(solution)/shard_map/ppermute | solution.py:467
  4.9 4.9 %collective-permute-start.1 = (bf16[64,512]{1,0:T(8,128)(2,1)S(1)}, bf16[64,512]{1,0:T(8,128)(2,1)S(1)}, u32[]{:S(2)}, u32[]{:S(2)}) collective-permute-start(bf16[64,512]{1,0:T(8,128)(2,1)S(1)} %start.1.after_ref.refs_0_), channel_id=1, source_target_pairs={{0,16},{8,24},{16,0},{24,8},{1,17},{9,25},{17,1},{25,9},{2,18},{10... | collective-permute-start | bytes 196616 | tf_op jit(solution)/shard_map/ppermute | solution.py:467
  13.0 6.1 %collective-permute-start.4 = (bf16[64,256]{1,0:T(8,128)(2,1)S(1)}, bf16[64,256]{1,0:T(8,128)(2,1)S(1)}, u32[]{:S(2)}, u32[]{:S(2)}) collective-permute-start(bf16[64,256]{1,0:T(8,128)(2,1)S(1)} %get-tuple-element.48), channel_id=1, source_target_pairs={{0,6},{1,7},{2,4},{3,5},{4,2},{5,3},{6,0},{7,1},{8,14},{9,15},{10,... | collective-permute-start | bytes 98312 | tf_op jit(solution)/shard_map/ppermute | solution.py:467
  17.0 4.8 %collective-permute-start.5 = (bf16[64,256]{1,0:T(8,128)(2,1)S(1)}, bf16[64,256]{1,0:T(8,128)(2,1)S(1)}, u32[]{:S(2)}, u32[]{:S(2)}) collective-permute-start(bf16[64,256]{1,0:T(8,128)(2,1)S(1)} %get-tuple-element.49), channel_id=1, source_target_pairs={{0,4},{1,5},{2,6},{3,7},{4,0},{5,1},{6,2},{7,3},{8,12},{9,13},{10,... | collective-permute-start | bytes 98312 | tf_op jit(solution)/shard_map/ppermute | solution.py:467
  17.0 4.8 %collective-permute-start.6 = (bf16[64,256]{1,0:T(8,128)(2,1)S(1)}, bf16[64,256]{1,0:T(8,128)(2,1)S(1)}, u32[]{:S(2)}, u32[]{:S(2)}) collective-permute-start(bf16[64,256]{1,0:T(8,128)(2,1)S(1)} %get-tuple-element.50), channel_id=1, source_target_pairs={{0,2},{1,3},{2,0},{3,1},{4,6},{5,7},{6,4},{7,5},{8,10},{9,11},{10,... | collective-permute-start | bytes 98312 | tf_op jit(solution)/shard_map/ppermute | solution.py:467
  21.9 5.9 %collective-permute-start.9 = (bf16[64,256]{1,0:T(8,128)(2,1)S(1)}, bf16[64,256]{1,0:T(8,128)(2,1)S(1)}, u32[]{:S(2)}, u32[]{:S(2)}) collective-permute-start(bf16[64,256]{1,0:T(8,128)(2,1)S(1)} %query.2.refs_0_), channel_id=1, source_target_pairs={{0,6},{1,7},{2,4},{3,5},{4,2},{5,3},{6,0},{7,1},{8,14},{9,15},{10,... | collective-permute-start | bytes 98312 | tf_op jit(solution)/shard_map/ppermute | solution.py:467
  23.4 4.9 %collective-permute-start.8 = (bf16[64,256]{1,0:T(8,128)(2,1)S(1)}, bf16[64,256]{1,0:T(8,128)(2,1)S(1)}, u32[]{:S(2)}, u32[]{:S(2)}) collective-permute-start(bf16[64,256]{1,0:T(8,128)(2,1)S(1)} %query.2.refs_0_), channel_id=1, source_target_pairs={{0,4},{1,5},{2,6},{3,7},{4,0},{5,1},{6,2},{7,3},{8,12},{9,13},{10,... | collective-permute-start | bytes 98312 | tf_op jit(solution)/shard_map/ppermute | solution.py:467
  24.0 4.5 %collective-permute-start.7 = (bf16[64,256]{1,0:T(8,128)(2,1)S(1)}, bf16[64,256]{1,0:T(8,128)(2,1)S(1)}, u32[]{:S(2)}, u32[]{:S(2)}) collective-permute-start(bf16[64,256]{1,0:T(8,128)(2,1)S(1)} %query.2.refs_0_), channel_id=1, source_target_pairs={{0,2},{1,3},{2,0},{3,1},{4,6},{5,7},{6,4},{7,5},{8,10},{9,11},{10,... | collective-permute-start | bytes 98312 | tf_op jit(solution)/shard_map/ppermute | solution.py:467
  31.2 6.9 %collective-permute-start.11 = (f32[32,512]{1,0:T(8,128)S(1)}, f32[32,512]{1,0:T(8,128)S(1)}, u32[]{:S(2)}, u32[]{:S(2)}) collective-permute-start(f32[32,512]{1,0:T(8,128)S(1)} %get-tuple-element.53), channel_id=1, source_target_pairs={{0,24},{8,16},{16,8},{24,0},{1,25},{9,17},{17,9},{25,1},{2,26},{10... | collective-permute-start | bytes 196616 | tf_op jit(solution)/shard_map/ppermute | solution.py:467
  33.7 4.8 %collective-permute-start.12 = (f32[32,512]{1,0:T(8,128)S(1)}, f32[32,512]{1,0:T(8,128)S(1)}, u32[]{:S(2)}, u32[]{:S(2)}) collective-permute-start(f32[32,512]{1,0:T(8,128)S(1)} %get-tuple-element.54), channel_id=1, source_target_pairs={{0,16},{8,24},{16,0},{24,8},{1,17},{9,25},{17,1},{25,9},{2,18},{10... | collective-permute-start | bytes 196616 | tf_op jit(solution)/shard_map/ppermute | solution.py:467
  34.6 4.9 %collective-permute-start.13 = (f32[32,512]{1,0:T(8,128)S(1)}, f32[32,512]{1,0:T(8,128)S(1)}, u32[]{:S(2)}, u32[]{:S(2)}) collective-permute-start(f32[32,512]{1,0:T(8,128)S(1)} %get-tuple-element.55), channel_id=1, source_target_pairs={{0,8},{8,0},{16,24},{24,16},{1,9},{9,1},{17,25},{25,17},{2,10},{10... | collective-permute-start | bytes 196616 | tf_op jit(solution)/shard_map/ppermute | solution.py:467
  34.7 6.9 %collective-permute-start.17 = (f32[32,512]{1,0:T(8,128)S(1)}, f32[32,512]{1,0:T(8,128)S(1)}, u32[]{:S(2)}, u32[]{:S(2)}) collective-permute-start(f32[32,512]{1,0:T(8,128)S(1)} %get-tuple-element.58), channel_id=1, source_target_pairs={{0,24},{8,16},{16,8},{24,0},{1,25},{9,17},{17,9},{25,1},{2,26},{10... | collective-permute-start | bytes 196616 | tf_op jit(solution)/shard_map/ppermute | solution.py:467
  37.2 5.9 %collective-permute-start.18 = (f32[32,512]{1,0:T(8,128)S(1)}, f32[32,512]{1,0:T(8,128)S(1)}, u32[]{:S(2)}, u32[]{:S(2)}) collective-permute-start(f32[32,512]{1,0:T(8,128)S(1)} %get-tuple-element.59), channel_id=1, source_target_pairs={{0,16},{8,24},{16,0},{24,8},{1,17},{9,25},{17,1},{25,9},{2,18},{10... | collective-permute-start | bytes 196616 | tf_op jit(solution)/shard_map/ppermute | solution.py:467
  38.1 5.0 %collective-permute-start.19 = (f32[32,512]{1,0:T(8,128)S(1)}, f32[32,512]{1,0:T(8,128)S(1)}, u32[]{:S(2)}, u32[]{:S(2)}) collective-permute-start(f32[32,512]{1,0:T(8,128)S(1)} %get-tuple-element.60), channel_id=1, source_target_pairs={{0,8},{8,0},{16,24},{24,16},{1,9},{9,1},{17,25},{25,17},{2,10},{10... | collective-permute-start | bytes 196616 | tf_op jit(solution)/shard_map/ppermute | solution.py:467
  39.5 5.7 %collective-permute-start.16 = (f32[32,512]{1,0:T(8,128)S(1)}, f32[32,512]{1,0:T(8,128)S(1)}, u32[]{:S(2)}, u32[]{:S(2)}) collective-permute-start(f32[32,512]{1,0:T(8,128)S(1)} %lift.3.refs_0_), channel_id=1, source_target_pairs={{0,24},{8,16},{16,8},{24,0},{1,25},{9,17},{17,9},{25,1},{2,26},{10... | collective-permute-start | bytes 196616 | tf_op jit(solution)/shard_map/ppermute | solution.py:467
  40.8 6.0 %collective-permute-start.15 = (f32[32,512]{1,0:T(8,128)S(1)}, f32[32,512]{1,0:T(8,128)S(1)}, u32[]{:S(2)}, u32[]{:S(2)}) collective-permute-start(f32[32,512]{1,0:T(8,128)S(1)} %lift.3.refs_0_), channel_id=1, source_target_pairs={{0,16},{8,24},{16,0},{24,8},{1,17},{9,25},{17,1},{25,9},{2,18},{10... | collective-permute-start | bytes 196616 | tf_op jit(solution)/shard_map/ppermute | solution.py:467
  41.7 5.1 %collective-permute-start.14 = (f32[32,512]{1,0:T(8,128)S(1)}, f32[32,512]{1,0:T(8,128)S(1)}, u32[]{:S(2)}, u32[]{:S(2)}) collective-permute-start(f32[32,512]{1,0:T(8,128)S(1)} %lift.3.refs_0_), channel_id=1, source_target_pairs={{0,8},{8,0},{16,24},{24,16},{1,9},{9,1},{17,25},{25,17},{2,10},{10... | collective-permute-start | bytes 196616 | tf_op jit(solution)/shard_map/ppermute | solution.py:467
  43.1 5.3 %collective-permute-start.22 = (f32[32,512]{1,0:T(8,128)S(1)}, f32[32,512]{1,0:T(8,128)S(1)}, u32[]{:S(2)}, u32[]{:S(2)}) collective-permute-start(f32[32,512]{1,0:T(8,128)S(1)} %lift.4.refs_4_), channel_id=1, source_target_pairs={{0,24},{8,16},{16,8},{24,0},{1,25},{9,17},{17,9},{25,1},{2,26},{10... | collective-permute-start | bytes 196616 | tf_op jit(solution)/shard_map/ppermute | solution.py:467
  44.4 4.7 %collective-permute-start.21 = (f32[32,512]{1,0:T(8,128)S(1)}, f32[32,512]{1,0:T(8,128)S(1)}, u32[]{:S(2)}, u32[]{:S(2)}) collective-permute-start(f32[32,512]{1,0:T(8,128)S(1)} %lift.4.refs_4_), channel_id=1, source_target_pairs={{0,16},{8,24},{16,0},{24,8},{1,17},{9,25},{17,1},{25,9},{2,18},{10... | collective-permute-start | bytes 196616 | tf_op jit(solution)/shard_map/ppermute | solution.py:467
  53.2 6.9 %collective-permute-start.27 = (f32[96,128]{1,0:T(8,128)S(1)}, f32[96,128]{1,0:T(8,128)S(1)}, u32[]{:S(2)}, u32[]{:S(2)}) collective-permute-start(f32[96,128]{1,0:T(8,128)S(1)} %get-tuple-element.70), channel_id=1, source_target_pairs={{0,6},{1,7},{2,4},{3,5},{4,2},{5,3},{6,0},{7,1},{8,14},{9,15},{10,... | collective-permute-start | bytes 147464 | tf_op jit(solution)/shard_map/ppermute | solution.py:467
  55.8 6.5 %collective-permute-start.28 = (f32[96,128]{1,0:T(8,128)S(1)}, f32[96,128]{1,0:T(8,128)S(1)}, u32[]{:S(2)}, u32[]{:S(2)}) collective-permute-start(f32[96,128]{1,0:T(8,128)S(1)} %get-tuple-element.71), channel_id=1, source_target_pairs={{0,4},{1,5},{2,6},{3,7},{4,0},{5,1},{6,2},{7,3},{8,12},{9,13},{10,... | collective-permute-start | bytes 147464 | tf_op jit(solution)/shard_map/ppermute | solution.py:467
  56.4 5.9 %collective-permute-start.29 = (f32[96,128]{1,0:T(8,128)S(1)}, f32[96,128]{1,0:T(8,128)S(1)}, u32[]{:S(2)}, u32[]{:S(2)}) collective-permute-start(f32[96,128]{1,0:T(8,128)S(1)} %get-tuple-element.72), channel_id=1, source_target_pairs={{0,2},{1,3},{2,0},{3,1},{4,6},{5,7},{6,4},{7,5},{8,10},{9,11},{10,... | collective-permute-start | bytes 147464 | tf_op jit(solution)/shard_map/ppermute | solution.py:467
  57.6 6.4 %collective-permute-start.24 = (f32[64,128]{1,0:T(8,128)S(1)}, f32[64,128]{1,0:T(8,128)S(1)}, u32[]{:S(2)}, u32[]{:S(2)}) collective-permute-start(f32[64,128]{1,0:T(8,128)S(1)} %get-tuple-element.66), channel_id=1, source_target_pairs={{0,6},{1,7},{2,4},{3,5},{4,2},{5,3},{6,0},{7,1},{8,14},{9,15},{10,... | collective-permute-start | bytes 98312 | tf_op jit(solution)/shard_map/ppermute | solution.py:467
  60.2 4.8 %collective-permute-start.25 = (f32[64,128]{1,0:T(8,128)S(1)}, f32[64,128]{1,0:T(8,128)S(1)}, u32[]{:S(2)}, u32[]{:S(2)}) collective-permute-start(f32[64,128]{1,0:T(8,128)S(1)} %get-tuple-element.67), channel_id=1, source_target_pairs={{0,4},{1,5},{2,6},{3,7},{4,0},{5,1},{6,2},{7,3},{8,12},{9,13},{10,... | collective-permute-start | bytes 98312 | tf_op jit(solution)/shard_map/ppermute | solution.py:467
  60.2 4.8 %collective-permute-start.26 = (f32[64,128]{1,0:T(8,128)S(1)}, f32[64,128]{1,0:T(8,128)S(1)}, u32[]{:S(2)}, u32[]{:S(2)}) collective-permute-start(f32[64,128]{1,0:T(8,128)S(1)} %get-tuple-element.68), channel_id=1, source_target_pairs={{0,2},{1,3},{2,0},{3,1},{4,6},{5,7},{6,4},{7,5},{8,10},{9,11},{10,... | collective-permute-start | bytes 98312 | tf_op jit(solution)/shard_map/ppermute | solution.py:467
  65.2 5.9 %collective-permute-start.32 = (bf16[64,256]{1,0:T(8,128)(2,1)S(1)}, bf16[64,256]{1,0:T(8,128)(2,1)S(1)}, u32[]{:S(2)}, u32[]{:S(2)}) collective-permute-start(bf16[64,256]{1,0:T(8,128)(2,1)S(1)} %query_rest.1.refs_0_), channel_id=1, source_target_pairs={{0,6},{1,7},{2,4},{3,5},{4,2},{5,3},{6,0},{7,1},{8,14},{9,15},{10,... | collective-permute-start | bytes 98312 | tf_op jit(solution)/shard_map/ppermute | solution.py:467
  67.0 5.2 %collective-permute-start.31 = (bf16[64,256]{1,0:T(8,128)(2,1)S(1)}, bf16[64,256]{1,0:T(8,128)(2,1)S(1)}, u32[]{:S(2)}, u32[]{:S(2)}) collective-permute-start(bf16[64,256]{1,0:T(8,128)(2,1)S(1)} %query_rest.1.refs_0_), channel_id=1, source_target_pairs={{0,4},{1,5},{2,6},{3,7},{4,0},{5,1},{6,2},{7,3},{8,12},{9,13},{10,... | collective-permute-start | bytes 98312 | tf_op jit(solution)/shard_map/ppermute | solution.py:467
  67.6 4.5 %collective-permute-start.30 = (bf16[64,256]{1,0:T(8,128)(2,1)S(1)}, bf16[64,256]{1,0:T(8,128)(2,1)S(1)}, u32[]{:S(2)}, u32[]{:S(2)}) collective-permute-start(bf16[64,256]{1,0:T(8,128)(2,1)S(1)} %query_rest.1.refs_0_), channel_id=1, source_target_pairs={{0,2},{1,3},{2,0},{3,1},{4,6},{5,7},{6,4},{7,5},{8,10},{9,11},{10,... | collective-permute-start | bytes 98312 | tf_op jit(solution)/shard_map/ppermute | solution.py:467
  74.8 7.3 %collective-permute-start.34 = (f32[64,512]{1,0:T(8,128)S(1)}, f32[64,512]{1,0:T(8,128)S(1)}, u32[]{:S(2)}, u32[]{:S(2)}) collective-permute-start(f32[64,512]{1,0:T(8,128)S(1)} %get-tuple-element.76), channel_id=1, source_target_pairs={{0,24},{8,16},{16,8},{24,0},{1,25},{9,17},{17,9},{25,1},{2,26},{10... | collective-permute-start | bytes 393224 | tf_op jit(solution)/shard_map/ppermute | solution.py:467
  76.3 8.1 %collective-permute-start.35 = (f32[64,512]{1,0:T(8,128)S(1)}, f32[64,512]{1,0:T(8,128)S(1)}, u32[]{:S(2)}, u32[]{:S(2)}) collective-permute-start(f32[64,512]{1,0:T(8,128)S(1)} %get-tuple-element.77), channel_id=1, source_target_pairs={{0,16},{8,24},{16,0},{24,8},{1,17},{9,25},{17,1},{25,9},{2,18},{10... | collective-permute-start | bytes 393224 | tf_op jit(solution)/shard_map/ppermute | solution.py:467
  77.8 6.6 %collective-permute-start.36 = (f32[64,512]{1,0:T(8,128)S(1)}, f32[64,512]{1,0:T(8,128)S(1)}, u32[]{:S(2)}, u32[]{:S(2)}) collective-permute-start(f32[64,512]{1,0:T(8,128)S(1)} %get-tuple-element.78), channel_id=1, source_target_pairs={{0,8},{8,0},{16,24},{24,16},{1,9},{9,1},{17,25},{25,17},{2,10},{10... | collective-permute-start | bytes 393224 | tf_op jit(solution)/shard_map/ppermute | solution.py:467
  90.0 19.5 %collective-permute-start.44 = (f32[64,64]{1,0:T(8,128)S(1)}, f32[64,64]{1,0:T(8,128)S(1)}, u32[]{:S(2)}, u32[]{:S(2)}) collective-permute-start(f32[64,64]{1,0:T(8,128)S(1)} %sum.5.total_ref), channel_id=1, source_target_pairs={{1,0},{3,2},{5,4},{7,6},{9,8},{11,10},{13,12},{15,14},{17,16},{19,... | collective-permute-start | bytes 49160 | tf_op jit(solution)/shard_map/ppermute | solution.py:498
  (13 other events, 24.1 us)

commit v9 on v8

--- a/solution.py
+++ b/solution.py
@@ -486,16 +486,12 @@
     reach = [(step, 0) for step in range(1, n_row)] if axis == "row" else [(0, step) for step in range(2, n_col, 2)]
     for row_step, col_step in reach:
         pairs = [
-            (row * n_col + col, (row ^ row_step) * n_col + (col ^ col_step))
+            (row * n_col + col, ((row ^ row_step) * n_col + (col ^ col_step)) if col % 2 else row * n_col + col)
             for row in range(n_row)
-            for col in range(1, n_col, 2)
+            for col in range(n_col)
         ]
         terms.append(lax.ppermute(value, ("row", "col"), pairs))
     return terms
-
-
-def hand_over(value):
-    return lax.ppermute(value, "col", [(col, col - 1) for col in range(1, lax.axis_size("col"), 2)])
 
 
 def shards(tiles, tile_ids, tile_count, query_degree, product_degree, panel):
@@ -693,7 +689,7 @@
         total = add_up(*core_one_terms(total, axis))
     return call(
         functools.partial(finish_body, root_count), "finish", [SCALARS] + [WHOLE] * 3, f32(width, share)
-    )(table, total, hand_over(total), lifted)
+    )(table, total, swap(total, "col", 1), lifted)
 
 
 def solution(mesh):

time: 113 us -> 112 us (level)
  waiting for transfers between devices: 39.8 us -> 22.5 us
  starting transfers between devices: 50.6 us -> 66.4 us
    ppermute x1 -> x0, waiting for transfers between devices: 18.2 us -> none  [hand_over(): lax.ppermute(value, 'col', [(col, col - 1) for col in range(1, lax.axis_s...]
    ppermute x38 -> x39, starting transfers between devices: 45.3 us -> 62.4 us  [swap(): lax.ppermute(value, axis, [(i, i ^ step) for i in range(lax.axis_size(axi...]
    ppermute x1 -> x0, starting transfers between devices: 1.29 us -> none  [hand_over(): lax.ppermute(value, 'col', [(col, col - 1) for col in range(1, lax.axis_s...]
    ppermute x38 -> x39, waiting for transfers between devices: 21.6 us -> 22.5 us  [swap(): lax.ppermute(value, axis, [(i, i ^ step) for i in range(lax.axis_size(axi...]
  transfers between devices with their start and end apart: 45 -> 45, of which waited for: 21 -> 19; matrix products, arithmetic and copies ran while one was open for 0% -> 0% of each run, Pallas kernels for 9% -> 10%
where the time goes in v9:
time: 112 us; the launch traced here: 111 us
  starting transfers between devices  66.4 us (59%)
  waiting for transfers between devices  22.5 us (20%)
  Pallas kernels  21.3 us (19%)
    ppermute x39, starting transfers between devices, swap(): lax.ppermute(value, axis, [(i, i ^ step) for i in range(lax.axis_size(axi...  62.4 us
    ppermute x39, waiting for transfers between devices, swap(): lax.ppermute(value, axis, [(i, i ^ step) for i in range(lax.axis_size(axi...  22.5 us
    ppermute x6, starting transfers between devices, core_one_terms(): terms.append(lax.ppermute(value, ('row', 'col'), pairs))  3.97 us
    pallas_call x1, Pallas kernels, shards(): call(functools.partial(load_body, columns // side if split else 0), 'load...  3.53 us
    pallas_call x1, Pallas kernels, shards(): call(functools.partial(finish_body, root_count), 'finish', [SCALARS] + [W...  3.19 us
    pallas_call x2, Pallas kernels, shards(): call(back_other_body, 'backward_rest', [SCALARS] + [WHOLE] * 3, [f32(widt...  2.4 us
    pallas_call x2, Pallas kernels, shards(): call(functools.partial(back_mine_body, chips), 'backward', [SCALARS] + [W...  2.33 us
  transfers between devices with their start and end apart: 45, of which 19 were waited for; matrix products, arithmetic and copies ran while one was open for 0% of the time, Pallas kernels for 10%

profile of v9, /device:TPU:0, one launch (start us, length us, event | category | flops | bytes accessed | tf_op | source)
XLA Modules:
  0.0 111.2 jit_solution(18194591615206863415)
XLA Ops:
  1.0 4.0 %collective-permute-start.2 = (bf16[64,512]{1,0:T(8,128)(2,1)S(1)}, bf16[64,512]{1,0:T(8,128)(2,1)S(1)}, u32[]{:S(2)}, u32[]{:S(2)}) collective-permute-start(bf16[64,512]{1,0:T(8,128)(2,1)S(1)} %start.1.after_ref.refs_0_), channel_id=1, source_target_pairs={{0,24},{8,16},{16,8},{24,0},{1,25},{9,17},{17,9},{25,1},{2,26},{10... | collective-permute-start | bytes 196616 | tf_op jit(solution)/shard_map/ppermute | solution.py:467
  6.3 3.5 %load.1 = (bf16[32,256,256]{2,1,0:T(8,128)(2,1)S(1)}, f32[1,512]{1,0:T(1,128)S(1)}, f32[1,2048]{1,0:T(1,128)S(1)}, f32[1,256]{1,0:T(1,128)S(1)}, s32[10,32]{1,0:T(8,128)S(1)}) custom-call(s32[3]{0:T(128)S(1)} %pad_add_fusion.place, bf16[64,512]{1,0:T(8,128)(2,1)S(1)} %start.1.after_ref.refs_0_, bf16[32,256,256]{2,1,0:T(8,128)(2,1)} %bitcast.8, ...), custom_call_target="tpu_custom_call" | custom-call | bytes 8388608 | tf_op jit(solution)/shard_map/load/pallas_call | solution.py:522
  9.9 1.4 %forward.2 = (bf16[9,64,256]{2,1,0:T(8,128)(2,1)S(1)}, f32[4,64,256]{2,1,0:T(8,128)S(1)}) custom-call(s32[10,32]{1,0:T(8,128)S(1)} %get-tuple-element.43.table, bf16[64,512]{1,0:T(8,128)(2,1)S(1)} %start.1.after_ref.refs_0_, bf16[64,512]{1,0:T(8,128)(2,1)S(1)} %collective-permute-done.refs_1_, bf16[64,512]{1,0:T(8,128)(2,1)S(1)} %collective-permute-done.1.refs_2_, ...), custom_call_target="tpu_custom_call" | custom-call | flops 134217728 | bytes 2097152 | tf_op jit(solution)/shard_map/forward/pallas_call | solution.py:616
  11.4 1.5 %forward_rest.2.mine_ref = f32[4,64,256]{2,1,0:T(8,128)S(1)} custom-call(s32[10,32]{1,0:T(8,128)S(1)} %get-tuple-element.43.table, bf16[9,64,256]{2,1,0:T(8,128)(2,1)S(1)} %get-tuple-element.45.held, bf16[32,256,256]{2,1,0:T(8,128)(2,1)S(1)} %get-tuple-element.44.refs_4_.tile_ref.refs_9_), custom_call_target="tpu_custom_call" | custom-call | flops 134217728 | bytes 2097152 | tf_op jit(solution)/shard_map/forward_rest/pallas_call | solution.py:625
  13.0 4.1 %collective-permute-start.4 = (bf16[64,256]{1,0:T(8,128)(2,1)S(1)}, bf16[64,256]{1,0:T(8,128)(2,1)S(1)}, u32[]{:S(2)}, u32[]{:S(2)}) collective-permute-start(bf16[64,256]{1,0:T(8,128)(2,1)S(1)} %get-tuple-element.48), channel_id=1, source_target_pairs={{0,6},{1,7},{2,4},{3,5},{4,2},{5,3},{6,0},{7,1},{8,14},{9,15},{10,... | collective-permute-start | bytes 98312 | tf_op jit(solution)/shard_map/ppermute | solution.py:467
  17.7 1.4 %collective-permute-done.4.refs_1_ = bf16[64,256]{1,0:T(8,128)(2,1)S(1)} collective-permute-done((bf16[64,256]{1,0:T(8,128)(2,1)S(1)}, bf16[64,256]{1,0:T(8,128)(2,1)S(1)}, u32[]{:S(2)}, u32[]{:S(2)}) %collective-permute-start.4) | collective-permute-done | bytes 32800 | tf_op jit(solution)/shard_map/ppermute | solution.py:467
  19.1 2.8 %collective-permute-done.5.refs_2_ = bf16[64,256]{1,0:T(8,128)(2,1)S(1)} collective-permute-done((bf16[64,256]{1,0:T(8,128)(2,1)S(1)}, bf16[64,256]{1,0:T(8,128)(2,1)S(1)}, u32[]{:S(2)}, u32[]{:S(2)}) %collective-permute-start.5) | collective-permute-done | bytes 32800 | tf_op jit(solution)/shard_map/ppermute | solution.py:467
  21.9 1.9 %collective-permute-start.9 = (bf16[64,256]{1,0:T(8,128)(2,1)S(1)}, bf16[64,256]{1,0:T(8,128)(2,1)S(1)}, u32[]{:S(2)}, u32[]{:S(2)}) collective-permute-start(bf16[64,256]{1,0:T(8,128)(2,1)S(1)} %query.2.refs_0_), channel_id=1, source_target_pairs={{0,6},{1,7},{2,4},{3,5},{4,2},{5,3},{6,0},{7,1},{8,14},{9,15},{10,... | collective-permute-start | bytes 98312 | tf_op jit(solution)/shard_map/ppermute | solution.py:467
  24.2 2.1 %collective-permute-start.7 = (bf16[64,256]{1,0:T(8,128)(2,1)S(1)}, bf16[64,256]{1,0:T(8,128)(2,1)S(1)}, u32[]{:S(2)}, u32[]{:S(2)}) collective-permute-start(bf16[64,256]{1,0:T(8,128)(2,1)S(1)} %query.2.refs_0_), channel_id=1, source_target_pairs={{0,2},{1,3},{2,0},{3,1},{4,6},{5,7},{6,4},{7,5},{8,10},{9,11},{10,... | collective-permute-start | bytes 98312 | tf_op jit(solution)/shard_map/ppermute | solution.py:467
  26.3 1.4 %collective-permute-done.9.refs_3_ = bf16[64,256]{1,0:T(8,128)(2,1)S(1)} collective-permute-done((bf16[64,256]{1,0:T(8,128)(2,1)S(1)}, bf16[64,256]{1,0:T(8,128)(2,1)S(1)}, u32[]{:S(2)}, u32[]{:S(2)}) %collective-permute-start.9) | collective-permute-done | bytes 32800 | tf_op jit(solution)/shard_map/ppermute | solution.py:467
  31.5 2.2 %collective-permute-start.11 = (f32[32,512]{1,0:T(8,128)S(1)}, f32[32,512]{1,0:T(8,128)S(1)}, u32[]{:S(2)}, u32[]{:S(2)}) collective-permute-start(f32[32,512]{1,0:T(8,128)S(1)} %get-tuple-element.53), channel_id=1, source_target_pairs={{0,24},{8,16},{16,8},{24,0},{1,25},{9,17},{17,9},{25,1},{2,26},{10... | collective-permute-start | bytes 196616 | tf_op jit(solution)/shard_map/ppermute | solution.py:467
  35.0 2.2 %collective-permute-start.17 = (f32[32,512]{1,0:T(8,128)S(1)}, f32[32,512]{1,0:T(8,128)S(1)}, u32[]{:S(2)}, u32[]{:S(2)}) collective-permute-start(f32[32,512]{1,0:T(8,128)S(1)} %get-tuple-element.58), channel_id=1, source_target_pairs={{0,24},{8,16},{16,8},{24,0},{1,25},{9,17},{17,9},{25,1},{2,26},{10... | collective-permute-start | bytes 196616 | tf_op jit(solution)/shard_map/ppermute | solution.py:467
  39.2 1.6 %collective-permute-start.16 = (f32[32,512]{1,0:T(8,128)S(1)}, f32[32,512]{1,0:T(8,128)S(1)}, u32[]{:S(2)}, u32[]{:S(2)}) collective-permute-start(f32[32,512]{1,0:T(8,128)S(1)} %lift.3.refs_0_), channel_id=1, source_target_pairs={{0,24},{8,16},{16,8},{24,0},{1,25},{9,17},{17,9},{25,1},{2,26},{10... | collective-permute-start | bytes 196616 | tf_op jit(solution)/shard_map/ppermute | solution.py:467
  41.3 1.4 %collective-permute-start.14 = (f32[32,512]{1,0:T(8,128)S(1)}, f32[32,512]{1,0:T(8,128)S(1)}, u32[]{:S(2)}, u32[]{:S(2)}) collective-permute-start(f32[32,512]{1,0:T(8,128)S(1)} %lift.3.refs_0_), channel_id=1, source_target_pairs={{0,8},{8,0},{16,24},{24,16},{1,9},{9,1},{17,25},{25,17},{2,10},{10... | collective-permute-start | bytes 196616 | tf_op jit(solution)/shard_map/ppermute | solution.py:467
  42.8 1.7 %collective-permute-start.22 = (f32[32,512]{1,0:T(8,128)S(1)}, f32[32,512]{1,0:T(8,128)S(1)}, u32[]{:S(2)}, u32[]{:S(2)}) collective-permute-start(f32[32,512]{1,0:T(8,128)S(1)} %lift.4.refs_4_), channel_id=1, source_target_pairs={{0,24},{8,16},{16,8},{24,0},{1,25},{9,17},{17,9},{25,1},{2,26},{10... | collective-permute-start | bytes 196616 | tf_op jit(solution)/shard_map/ppermute | solution.py:467
  45.0 1.3 %collective-permute-start.20 = (f32[32,512]{1,0:T(8,128)S(1)}, f32[32,512]{1,0:T(8,128)S(1)}, u32[]{:S(2)}, u32[]{:S(2)}) collective-permute-start(f32[32,512]{1,0:T(8,128)S(1)} %lift.4.refs_4_), channel_id=1, source_target_pairs={{0,8},{8,0},{16,24},{24,16},{1,9},{9,1},{17,25},{25,17},{2,10},{10... | collective-permute-start | bytes 196616 | tf_op jit(solution)/shard_map/ppermute | solution.py:467
  46.5 1.5 %collective-permute-done.22.refs_7_ = f32[32,512]{1,0:T(8,128)S(1)} collective-permute-done((f32[32,512]{1,0:T(8,128)S(1)}, f32[32,512]{1,0:T(8,128)S(1)}, u32[]{:S(2)}, u32[]{:S(2)}) %collective-permute-start.22) | collective-permute-done | bytes 65568 | tf_op jit(solution)/shard_map/ppermute | solution.py:467
  49.3 1.9 %forward.3 = (bf16[9,128,256]{2,1,0:T(8,128)(2,1)S(1)}, f32[272,256]{1,0:T(8,128)S(1)}, f32[16,256]{1,0:T(8,128)S(1)}) custom-call(s32[10,32]{1,0:T(8,128)S(1)} %get-tuple-element.43.table, f32[32,512]{1,0:T(8,128)S(1)} %lift.3.refs_0_, f32[32,512]{1,0:T(8,128)S(1)} %collective-permute-done.14.refs_1_, f32[32,512]{1,0:T(8,128)S(1)} %collective-permute-done.15.refs_2_, ...), custom_call_target="tpu_custom_call" | custom-call | flops 134217728 | bytes 2097152 | tf_op jit(solution)/shard_map/forward/pallas_call | solution.py:565
  51.3 1.5 %forward_rest.3.mine_ref = f32[256,256]{1,0:T(8,128)S(1)} custom-call(s32[10,32]{1,0:T(8,128)S(1)} %get-tuple-element.43.table, bf16[9,128,256]{2,1,0:T(8,128)(2,1)S(1)} %get-tuple-element.62.held, bf16[32,256,256]{2,1,0:T(8,128)(2,1)S(1)} %get-tuple-element.44.refs_4_.tile_ref.refs_9_), custom_call_target="tpu_custom_call" | custom-call | flops 134217728 | bytes 2097152 | tf_op jit(solution)/shard_map/forward_rest/pallas_call | solution.py:574
  53.0 2.6 %collective-permute-start.27 = (f32[96,128]{1,0:T(8,128)S(1)}, f32[96,128]{1,0:T(8,128)S(1)}, u32[]{:S(2)}, u32[]{:S(2)}) collective-permute-start(f32[96,128]{1,0:T(8,128)S(1)} %get-tuple-element.70), channel_id=1, source_target_pairs={{0,6},{1,7},{2,4},{3,5},{4,2},{5,3},{6,0},{7,1},{8,14},{9,15},{10,... | collective-permute-start | bytes 147464 | tf_op jit(solution)/shard_map/ppermute | solution.py:467
  56.0 1.4 %collective-permute-start.29 = (f32[96,128]{1,0:T(8,128)S(1)}, f32[96,128]{1,0:T(8,128)S(1)}, u32[]{:S(2)}, u32[]{:S(2)}) collective-permute-start(f32[96,128]{1,0:T(8,128)S(1)} %get-tuple-element.72), channel_id=1, source_target_pairs={{0,2},{1,3},{2,0},{3,1},{4,6},{5,7},{6,4},{7,5},{8,10},{9,11},{10,... | collective-permute-start | bytes 147464 | tf_op jit(solution)/shard_map/ppermute | solution.py:467
  57.4 2.5 %collective-permute-start.24 = (f32[64,128]{1,0:T(8,128)S(1)}, f32[64,128]{1,0:T(8,128)S(1)}, u32[]{:S(2)}, u32[]{:S(2)}) collective-permute-start(f32[64,128]{1,0:T(8,128)S(1)} %get-tuple-element.66), channel_id=1, source_target_pairs={{0,6},{1,7},{2,4},{3,5},{4,2},{5,3},{6,0},{7,1},{8,14},{9,15},{10,... | collective-permute-start | bytes 98312 | tf_op jit(solution)/shard_map/ppermute | solution.py:467
  59.9 1.8 %collective-permute-start.26 = (f32[64,128]{1,0:T(8,128)S(1)}, f32[64,128]{1,0:T(8,128)S(1)}, u32[]{:S(2)}, u32[]{:S(2)}) collective-permute-start(f32[64,128]{1,0:T(8,128)S(1)} %get-tuple-element.68), channel_id=1, source_target_pairs={{0,2},{1,3},{2,0},{3,1},{4,6},{5,7},{6,4},{7,5},{8,10},{9,11},{10,... | collective-permute-start | bytes 98312 | tf_op jit(solution)/shard_map/ppermute | solution.py:467
  61.8 1.8 %query.3 = (f32[64,64]{1,0:T(8,128)S(1)}, bf16[64,128]{1,0:T(8,128)(2,1)S(1)}) custom-call(f32[96,128]{1,0:T(8,128)S(1)} %get-tuple-element.69.refs_0_, f32[96,128]{1,0:T(8,128)S(1)} %collective-permute-done.27.refs_1_, f32[96,128]{1,0:T(8,128)S(1)} %collective-permute-done.28.refs_2_, f32[96,128]{1,0:T(8,128)S(1)} %collective-permute-done.29.refs_3_, ...), custom_call_target="tpu_custom_call" | custom-call | flops 268435456 | tf_op jit(solution)/shard_map/query/pallas_call | solution.py:605
  64.9 1.9 %collective-permute-start.32 = (bf16[64,256]{1,0:T(8,128)(2,1)S(1)}, bf16[64,256]{1,0:T(8,128)(2,1)S(1)}, u32[]{:S(2)}, u32[]{:S(2)}) collective-permute-start(bf16[64,256]{1,0:T(8,128)(2,1)S(1)} %query_rest.1.refs_0_), channel_id=1, source_target_pairs={{0,6},{1,7},{2,4},{3,5},{4,2},{5,3},{6,0},{7,1},{8,14},{9,15},{10,... | collective-permute-start | bytes 98312 | tf_op jit(solution)/shard_map/ppermute | solution.py:467
  67.4 2.0 %collective-permute-start.30 = (bf16[64,256]{1,0:T(8,128)(2,1)S(1)}, bf16[64,256]{1,0:T(8,128)(2,1)S(1)}, u32[]{:S(2)}, u32[]{:S(2)}) collective-permute-start(bf16[64,256]{1,0:T(8,128)(2,1)S(1)} %query_rest.1.refs_0_), channel_id=1, source_target_pairs={{0,2},{1,3},{2,0},{3,1},{4,6},{5,7},{6,4},{7,5},{8,10},{9,11},{10,... | collective-permute-start | bytes 98312 | tf_op jit(solution)/shard_map/ppermute | solution.py:467
  69.4 1.7 %collective-permute-done.32.refs_3_ = bf16[64,256]{1,0:T(8,128)(2,1)S(1)} collective-permute-done((bf16[64,256]{1,0:T(8,128)(2,1)S(1)}, bf16[64,256]{1,0:T(8,128)(2,1)S(1)}, u32[]{:S(2)}, u32[]{:S(2)}) %collective-permute-start.32) | collective-permute-done | bytes 32800 | tf_op jit(solution)/shard_map/ppermute | solution.py:467
  74.6 1.7 %collective-permute-start.34 = (f32[64,512]{1,0:T(8,128)S(1)}, f32[64,512]{1,0:T(8,128)S(1)}, u32[]{:S(2)}, u32[]{:S(2)}) collective-permute-start(f32[64,512]{1,0:T(8,128)S(1)} %get-tuple-element.76), channel_id=1, source_target_pairs={{0,24},{8,16},{16,8},{24,0},{1,25},{9,17},{17,9},{25,1},{2,26},{10... | collective-permute-start | bytes 393224 | tf_op jit(solution)/shard_map/ppermute | solution.py:467
  78.1 3.8 %collective-permute-done.34.refs_1_ = f32[64,512]{1,0:T(8,128)S(1)} collective-permute-done((f32[64,512]{1,0:T(8,128)S(1)}, f32[64,512]{1,0:T(8,128)S(1)}, u32[]{:S(2)}, u32[]{:S(2)}) %collective-permute-start.34) | collective-permute-done | bytes 131104 | tf_op jit(solution)/shard_map/ppermute | solution.py:467
  81.9 2.2 %collective-permute-done.35.refs_2_ = f32[64,512]{1,0:T(8,128)S(1)} collective-permute-done((f32[64,512]{1,0:T(8,128)S(1)}, f32[64,512]{1,0:T(8,128)S(1)}, u32[]{:S(2)}, u32[]{:S(2)}) %collective-permute-start.35) | collective-permute-done | bytes 131104 | tf_op jit(solution)/shard_map/ppermute | solution.py:467
  89.8 17.4 %collective-permute-start.44 = (f32[64,64]{1,0:T(8,128)S(1)}, f32[64,64]{1,0:T(8,128)S(1)}, u32[]{:S(2)}, u32[]{:S(2)}) collective-permute-start(f32[64,64]{1,0:T(8,128)S(1)} %sum.5.total_ref), channel_id=1, source_target_pairs={{0,1},{1,0},{2,3},{3,2},{4,5},{5,4},{6,7},{7,6},{8,9},{9,8},{10,11... | collective-permute-start | bytes 49160 | tf_op jit(solution)/shard_map/ppermute | solution.py:467
  108.0 3.2 %finish.1 = f32[64,512]{1,0:T(8,128)} custom-call(s32[10,32]{1,0:T(8,128)S(1)} %get-tuple-element.43.table, f32[64,64]{1,0:T(8,128)S(1)} %sum.5.total_ref, f32[64,64]{1,0:T(8,128)S(1)} %collective-permute-done.44.got_ref, f32[64,512]{1,0:T(8,128)S(1)} %get-tuple-element.80.lifted_ref), custom_call_target="tpu_custom_call" | custom-call | tf_op jit(solution)/shard_map/finish/pallas_call | solution.py:690
  (83 shorter events, 26.8 us)
Async XLA Ops:
  1.0 8.9 %collective-permute-start.2 = (bf16[64,512]{1,0:T(8,128)(2,1)S(1)}, bf16[64,512]{1,0:T(8,128)(2,1)S(1)}, u32[]{:S(2)}, u32[]{:S(2)}) collective-permute-start(bf16[64,512]{1,0:T(8,128)(2,1)S(1)} %start.1.after_ref.refs_0_), channel_id=1, source_target_pairs={{0,24},{8,16},{16,8},{24,0},{1,25},{9,17},{17,9},{25,1},{2,26},{10... | collective-permute-start | bytes 196616 | tf_op jit(solution)/shard_map/ppermute | solution.py:467
  4.9 4.9 %collective-permute-start.1 = (bf16[64,512]{1,0:T(8,128)(2,1)S(1)}, bf16[64,512]{1,0:T(8,128)(2,1)S(1)}, u32[]{:S(2)}, u32[]{:S(2)}) collective-permute-start(bf16[64,512]{1,0:T(8,128)(2,1)S(1)} %start.1.after_ref.refs_0_), channel_id=1, source_target_pairs={{0,16},{8,24},{16,0},{24,8},{1,17},{9,25},{17,1},{25,9},{2,18},{10... | collective-permute-start | bytes 196616 | tf_op jit(solution)/shard_map/ppermute | solution.py:467
  5.4 4.4 %collective-permute-start = (bf16[64,512]{1,0:T(8,128)(2,1)S(1)}, bf16[64,512]{1,0:T(8,128)(2,1)S(1)}, u32[]{:S(2)}, u32[]{:S(2)}) collective-permute-start(bf16[64,512]{1,0:T(8,128)(2,1)S(1)} %start.1.after_ref.refs_0_), channel_id=1, source_target_pairs={{0,8},{8,0},{16,24},{24,16},{1,9},{9,1},{17,25},{25,17},{2,10},{10... | collective-permute-start | bytes 196616 | tf_op jit(solution)/shard_map/ppermute | solution.py:467
  13.0 6.1 %collective-permute-start.4 = (bf16[64,256]{1,0:T(8,128)(2,1)S(1)}, bf16[64,256]{1,0:T(8,128)(2,1)S(1)}, u32[]{:S(2)}, u32[]{:S(2)}) collective-permute-start(bf16[64,256]{1,0:T(8,128)(2,1)S(1)} %get-tuple-element.48), channel_id=1, source_target_pairs={{0,6},{1,7},{2,4},{3,5},{4,2},{5,3},{6,0},{7,1},{8,14},{9,15},{10,... | collective-permute-start | bytes 98312 | tf_op jit(solution)/shard_map/ppermute | solution.py:467
  17.0 4.8 %collective-permute-start.5 = (bf16[64,256]{1,0:T(8,128)(2,1)S(1)}, bf16[64,256]{1,0:T(8,128)(2,1)S(1)}, u32[]{:S(2)}, u32[]{:S(2)}) collective-permute-start(bf16[64,256]{1,0:T(8,128)(2,1)S(1)} %get-tuple-element.49), channel_id=1, source_target_pairs={{0,4},{1,5},{2,6},{3,7},{4,0},{5,1},{6,2},{7,3},{8,12},{9,13},{10,... | collective-permute-start | bytes 98312 | tf_op jit(solution)/shard_map/ppermute | solution.py:467
  17.0 4.8 %collective-permute-start.6 = (bf16[64,256]{1,0:T(8,128)(2,1)S(1)}, bf16[64,256]{1,0:T(8,128)(2,1)S(1)}, u32[]{:S(2)}, u32[]{:S(2)}) collective-permute-start(bf16[64,256]{1,0:T(8,128)(2,1)S(1)} %get-tuple-element.50), channel_id=1, source_target_pairs={{0,2},{1,3},{2,0},{3,1},{4,6},{5,7},{6,4},{7,5},{8,10},{9,11},{10,... | collective-permute-start | bytes 98312 | tf_op jit(solution)/shard_map/ppermute | solution.py:467
  21.9 5.9 %collective-permute-start.9 = (bf16[64,256]{1,0:T(8,128)(2,1)S(1)}, bf16[64,256]{1,0:T(8,128)(2,1)S(1)}, u32[]{:S(2)}, u32[]{:S(2)}) collective-permute-start(bf16[64,256]{1,0:T(8,128)(2,1)S(1)} %query.2.refs_0_), channel_id=1, source_target_pairs={{0,6},{1,7},{2,4},{3,5},{4,2},{5,3},{6,0},{7,1},{8,14},{9,15},{10,... | collective-permute-start | bytes 98312 | tf_op jit(solution)/shard_map/ppermute | solution.py:467
  23.8 5.0 %collective-permute-start.8 = (bf16[64,256]{1,0:T(8,128)(2,1)S(1)}, bf16[64,256]{1,0:T(8,128)(2,1)S(1)}, u32[]{:S(2)}, u32[]{:S(2)}) collective-permute-start(bf16[64,256]{1,0:T(8,128)(2,1)S(1)} %query.2.refs_0_), channel_id=1, source_target_pairs={{0,4},{1,5},{2,6},{3,7},{4,0},{5,1},{6,2},{7,3},{8,12},{9,13},{10,... | collective-permute-start | bytes 98312 | tf_op jit(solution)/shard_map/ppermute | solution.py:467
  24.2 4.7 %collective-permute-start.7 = (bf16[64,256]{1,0:T(8,128)(2,1)S(1)}, bf16[64,256]{1,0:T(8,128)(2,1)S(1)}, u32[]{:S(2)}, u32[]{:S(2)}) collective-permute-start(bf16[64,256]{1,0:T(8,128)(2,1)S(1)} %query.2.refs_0_), channel_id=1, source_target_pairs={{0,2},{1,3},{2,0},{3,1},{4,6},{5,7},{6,4},{7,5},{8,10},{9,11},{10,... | collective-permute-start | bytes 98312 | tf_op jit(solution)/shard_map/ppermute | solution.py:467
  31.5 6.2 %collective-permute-start.11 = (f32[32,512]{1,0:T(8,128)S(1)}, f32[32,512]{1,0:T(8,128)S(1)}, u32[]{:S(2)}, u32[]{:S(2)}) collective-permute-start(f32[32,512]{1,0:T(8,128)S(1)} %get-tuple-element.53), channel_id=1, source_target_pairs={{0,24},{8,16},{16,8},{24,0},{1,25},{9,17},{17,9},{25,1},{2,26},{10... | collective-permute-start | bytes 196616 | tf_op jit(solution)/shard_map/ppermute | solution.py:467
  33.7 4.8 %collective-permute-start.12 = (f32[32,512]{1,0:T(8,128)S(1)}, f32[32,512]{1,0:T(8,128)S(1)}, u32[]{:S(2)}, u32[]{:S(2)}) collective-permute-start(f32[32,512]{1,0:T(8,128)S(1)} %get-tuple-element.54), channel_id=1, source_target_pairs={{0,16},{8,24},{16,0},{24,8},{1,17},{9,25},{17,1},{25,9},{2,18},{10... | collective-permute-start | bytes 196616 | tf_op jit(solution)/shard_map/ppermute | solution.py:467
  34.2 4.9 %collective-permute-start.13 = (f32[32,512]{1,0:T(8,128)S(1)}, f32[32,512]{1,0:T(8,128)S(1)}, u32[]{:S(2)}, u32[]{:S(2)}) collective-permute-start(f32[32,512]{1,0:T(8,128)S(1)} %get-tuple-element.55), channel_id=1, source_target_pairs={{0,8},{8,0},{16,24},{24,16},{1,9},{9,1},{17,25},{25,17},{2,10},{10... | collective-permute-start | bytes 196616 | tf_op jit(solution)/shard_map/ppermute | solution.py:467
  35.0 6.3 %collective-permute-start.17 = (f32[32,512]{1,0:T(8,128)S(1)}, f32[32,512]{1,0:T(8,128)S(1)}, u32[]{:S(2)}, u32[]{:S(2)}) collective-permute-start(f32[32,512]{1,0:T(8,128)S(1)} %get-tuple-element.58), channel_id=1, source_target_pairs={{0,24},{8,16},{16,8},{24,0},{1,25},{9,17},{17,9},{25,1},{2,26},{10... | collective-permute-start | bytes 196616 | tf_op jit(solution)/shard_map/ppermute | solution.py:467
  37.2 5.5 %collective-permute-start.18 = (f32[32,512]{1,0:T(8,128)S(1)}, f32[32,512]{1,0:T(8,128)S(1)}, u32[]{:S(2)}, u32[]{:S(2)}) collective-permute-start(f32[32,512]{1,0:T(8,128)S(1)} %get-tuple-element.59), channel_id=1, source_target_pairs={{0,16},{8,24},{16,0},{24,8},{1,17},{9,25},{17,1},{25,9},{2,18},{10... | collective-permute-start | bytes 196616 | tf_op jit(solution)/shard_map/ppermute | solution.py:467
  37.7 5.0 %collective-permute-start.19 = (f32[32,512]{1,0:T(8,128)S(1)}, f32[32,512]{1,0:T(8,128)S(1)}, u32[]{:S(2)}, u32[]{:S(2)}) collective-permute-start(f32[32,512]{1,0:T(8,128)S(1)} %get-tuple-element.60), channel_id=1, source_target_pairs={{0,8},{8,0},{16,24},{24,16},{1,9},{9,1},{17,25},{25,17},{2,10},{10... | collective-permute-start | bytes 196616 | tf_op jit(solution)/shard_map/ppermute | solution.py:467
  39.2 5.8 %collective-permute-start.16 = (f32[32,512]{1,0:T(8,128)S(1)}, f32[32,512]{1,0:T(8,128)S(1)}, u32[]{:S(2)}, u32[]{:S(2)}) collective-permute-start(f32[32,512]{1,0:T(8,128)S(1)} %lift.3.refs_0_), channel_id=1, source_target_pairs={{0,24},{8,16},{16,8},{24,0},{1,25},{9,17},{17,9},{25,1},{2,26},{10... | collective-permute-start | bytes 196616 | tf_op jit(solution)/shard_map/ppermute | solution.py:467
  40.8 5.7 %collective-permute-start.15 = (f32[32,512]{1,0:T(8,128)S(1)}, f32[32,512]{1,0:T(8,128)S(1)}, u32[]{:S(2)}, u32[]{:S(2)}) collective-permute-start(f32[32,512]{1,0:T(8,128)S(1)} %lift.3.refs_0_), channel_id=1, source_target_pairs={{0,16},{8,24},{16,0},{24,8},{1,17},{9,25},{17,1},{25,9},{2,18},{10... | collective-permute-start | bytes 196616 | tf_op jit(solution)/shard_map/ppermute | solution.py:467
  41.3 5.2 %collective-permute-start.14 = (f32[32,512]{1,0:T(8,128)S(1)}, f32[32,512]{1,0:T(8,128)S(1)}, u32[]{:S(2)}, u32[]{:S(2)}) collective-permute-start(f32[32,512]{1,0:T(8,128)S(1)} %lift.3.refs_0_), channel_id=1, source_target_pairs={{0,8},{8,0},{16,24},{24,16},{1,9},{9,1},{17,25},{25,17},{2,10},{10... | collective-permute-start | bytes 196616 | tf_op jit(solution)/shard_map/ppermute | solution.py:467
  42.8 5.2 %collective-permute-start.22 = (f32[32,512]{1,0:T(8,128)S(1)}, f32[32,512]{1,0:T(8,128)S(1)}, u32[]{:S(2)}, u32[]{:S(2)}) collective-permute-start(f32[32,512]{1,0:T(8,128)S(1)} %lift.4.refs_4_), channel_id=1, source_target_pairs={{0,24},{8,16},{16,8},{24,0},{1,25},{9,17},{17,9},{25,1},{2,26},{10... | collective-permute-start | bytes 196616 | tf_op jit(solution)/shard_map/ppermute | solution.py:467
  53.0 7.0 %collective-permute-start.27 = (f32[96,128]{1,0:T(8,128)S(1)}, f32[96,128]{1,0:T(8,128)S(1)}, u32[]{:S(2)}, u32[]{:S(2)}) collective-permute-start(f32[96,128]{1,0:T(8,128)S(1)} %get-tuple-element.70), channel_id=1, source_target_pairs={{0,6},{1,7},{2,4},{3,5},{4,2},{5,3},{6,0},{7,1},{8,14},{9,15},{10,... | collective-permute-start | bytes 147464 | tf_op jit(solution)/shard_map/ppermute | solution.py:467
  55.5 6.2 %collective-permute-start.28 = (f32[96,128]{1,0:T(8,128)S(1)}, f32[96,128]{1,0:T(8,128)S(1)}, u32[]{:S(2)}, u32[]{:S(2)}) collective-permute-start(f32[96,128]{1,0:T(8,128)S(1)} %get-tuple-element.71), channel_id=1, source_target_pairs={{0,4},{1,5},{2,6},{3,7},{4,0},{5,1},{6,2},{7,3},{8,12},{9,13},{10,... | collective-permute-start | bytes 147464 | tf_op jit(solution)/shard_map/ppermute | solution.py:467
  56.0 5.8 %collective-permute-start.29 = (f32[96,128]{1,0:T(8,128)S(1)}, f32[96,128]{1,0:T(8,128)S(1)}, u32[]{:S(2)}, u32[]{:S(2)}) collective-permute-start(f32[96,128]{1,0:T(8,128)S(1)} %get-tuple-element.72), channel_id=1, source_target_pairs={{0,2},{1,3},{2,0},{3,1},{4,6},{5,7},{6,4},{7,5},{8,10},{9,11},{10,... | collective-permute-start | bytes 147464 | tf_op jit(solution)/shard_map/ppermute | solution.py:467
  57.4 6.2 %collective-permute-start.24 = (f32[64,128]{1,0:T(8,128)S(1)}, f32[64,128]{1,0:T(8,128)S(1)}, u32[]{:S(2)}, u32[]{:S(2)}) collective-permute-start(f32[64,128]{1,0:T(8,128)S(1)} %get-tuple-element.66), channel_id=1, source_target_pairs={{0,6},{1,7},{2,4},{3,5},{4,2},{5,3},{6,0},{7,1},{8,14},{9,15},{10,... | collective-permute-start | bytes 98312 | tf_op jit(solution)/shard_map/ppermute | solution.py:467
  59.9 4.8 %collective-permute-start.25 = (f32[64,128]{1,0:T(8,128)S(1)}, f32[64,128]{1,0:T(8,128)S(1)}, u32[]{:S(2)}, u32[]{:S(2)}) collective-permute-start(f32[64,128]{1,0:T(8,128)S(1)} %get-tuple-element.67), channel_id=1, source_target_pairs={{0,4},{1,5},{2,6},{3,7},{4,0},{5,1},{6,2},{7,3},{8,12},{9,13},{10,... | collective-permute-start | bytes 98312 | tf_op jit(solution)/shard_map/ppermute | solution.py:467
  59.9 4.8 %collective-permute-start.26 = (f32[64,128]{1,0:T(8,128)S(1)}, f32[64,128]{1,0:T(8,128)S(1)}, u32[]{:S(2)}, u32[]{:S(2)}) collective-permute-start(f32[64,128]{1,0:T(8,128)S(1)} %get-tuple-element.68), channel_id=1, source_target_pairs={{0,2},{1,3},{2,0},{3,1},{4,6},{5,7},{6,4},{7,5},{8,10},{9,11},{10,... | collective-permute-start | bytes 98312 | tf_op jit(solution)/shard_map/ppermute | solution.py:467
  64.9 6.1 %collective-permute-start.32 = (bf16[64,256]{1,0:T(8,128)(2,1)S(1)}, bf16[64,256]{1,0:T(8,128)(2,1)S(1)}, u32[]{:S(2)}, u32[]{:S(2)}) collective-permute-start(bf16[64,256]{1,0:T(8,128)(2,1)S(1)} %query_rest.1.refs_0_), channel_id=1, source_target_pairs={{0,6},{1,7},{2,4},{3,5},{4,2},{5,3},{6,0},{7,1},{8,14},{9,15},{10,... | collective-permute-start | bytes 98312 | tf_op jit(solution)/shard_map/ppermute | solution.py:467
  66.8 5.2 %collective-permute-start.31 = (bf16[64,256]{1,0:T(8,128)(2,1)S(1)}, bf16[64,256]{1,0:T(8,128)(2,1)S(1)}, u32[]{:S(2)}, u32[]{:S(2)}) collective-permute-start(bf16[64,256]{1,0:T(8,128)(2,1)S(1)} %query_rest.1.refs_0_), channel_id=1, source_target_pairs={{0,4},{1,5},{2,6},{3,7},{4,0},{5,1},{6,2},{7,3},{8,12},{9,13},{10,... | collective-permute-start | bytes 98312 | tf_op jit(solution)/shard_map/ppermute | solution.py:467
  67.4 4.5 %collective-permute-start.30 = (bf16[64,256]{1,0:T(8,128)(2,1)S(1)}, bf16[64,256]{1,0:T(8,128)(2,1)S(1)}, u32[]{:S(2)}, u32[]{:S(2)}) collective-permute-start(bf16[64,256]{1,0:T(8,128)(2,1)S(1)} %query_rest.1.refs_0_), channel_id=1, source_target_pairs={{0,2},{1,3},{2,0},{3,1},{4,6},{5,7},{6,4},{7,5},{8,10},{9,11},{10,... | collective-permute-start | bytes 98312 | tf_op jit(solution)/shard_map/ppermute | solution.py:467
  74.6 7.3 %collective-permute-start.34 = (f32[64,512]{1,0:T(8,128)S(1)}, f32[64,512]{1,0:T(8,128)S(1)}, u32[]{:S(2)}, u32[]{:S(2)}) collective-permute-start(f32[64,512]{1,0:T(8,128)S(1)} %get-tuple-element.76), channel_id=1, source_target_pairs={{0,24},{8,16},{16,8},{24,0},{1,25},{9,17},{17,9},{25,1},{2,26},{10... | collective-permute-start | bytes 393224 | tf_op jit(solution)/shard_map/ppermute | solution.py:467
  76.3 7.8 %collective-permute-start.35 = (f32[64,512]{1,0:T(8,128)S(1)}, f32[64,512]{1,0:T(8,128)S(1)}, u32[]{:S(2)}, u32[]{:S(2)}) collective-permute-start(f32[64,512]{1,0:T(8,128)S(1)} %get-tuple-element.77), channel_id=1, source_target_pairs={{0,16},{8,24},{16,0},{24,8},{1,17},{9,25},{17,1},{25,9},{2,18},{10... | collective-permute-start | bytes 393224 | tf_op jit(solution)/shard_map/ppermute | solution.py:467
  77.2 6.9 %collective-permute-start.36 = (f32[64,512]{1,0:T(8,128)S(1)}, f32[64,512]{1,0:T(8,128)S(1)}, u32[]{:S(2)}, u32[]{:S(2)}) collective-permute-start(f32[64,512]{1,0:T(8,128)S(1)} %get-tuple-element.78), channel_id=1, source_target_pairs={{0,8},{8,0},{16,24},{24,16},{1,9},{9,1},{17,25},{25,17},{2,10},{10... | collective-permute-start | bytes 393224 | tf_op jit(solution)/shard_map/ppermute | solution.py:467
  89.8 18.2 %collective-permute-start.44 = (f32[64,64]{1,0:T(8,128)S(1)}, f32[64,64]{1,0:T(8,128)S(1)}, u32[]{:S(2)}, u32[]{:S(2)}) collective-permute-start(f32[64,64]{1,0:T(8,128)S(1)} %sum.5.total_ref), channel_id=1, source_target_pairs={{0,1},{1,0},{2,3},{3,2},{4,5},{5,4},{6,7},{7,6},{8,9},{9,8},{10,11... | collective-permute-start | bytes 49160 | tf_op jit(solution)/shard_map/ppermute | solution.py:467
  (13 other events, 24.0 us)

commit v10 on v7

--- a/solution.py
+++ b/solution.py
@@ -480,8 +480,18 @@
     return call(sum_body, "sum", [WHOLE] * len(values), f32(*values[0].shape))(*values)
 
 
-def terms_over_col(gram):
-    return spread_to(add_up(gram, swap(gram, "col", 1)), "col", 2)
+def crossed_terms(value, axis):
+    n_row, n_col = lax.axis_size("row"), lax.axis_size("col")
+    terms = [value]
+    reach = [(step, 1) for step in range(1, n_row)] if axis == "row" else [(0, step + 1) for step in range(2, n_col, 2)]
+    for row_step, col_step in reach:
+        pairs = [
+            (row * n_col + col, (row ^ row_step) * n_col + (col ^ col_step))
+            for row in range(n_row)
+            for col in range(n_col)
+        ]
+        terms.append(lax.ppermute(value, ("row", "col"), pairs))
+    return terms
 
 
 def shards(tiles, tile_ids, tile_count, query_degree, product_degree, panel):
@@ -674,9 +684,10 @@
     lifted, gram = call(
         lift_body, "lift", [WHOLE] * (n_row + 1), [f32(width, share), f32(width, width)]
     )(*parts[0], my_pscale)
+    total = add_up(*crossed_terms(gram, "row"))
     return call(
         functools.partial(finish_body, root_count), "finish", [WHOLE] * (chips + 1), f32(width, share)
-    )(*terms_over_col(add_up(*spread_to(gram, "row"))), lifted)
+    )(*crossed_terms(add_up(total, swap(total, "col", 1)), "col"), lifted)
 
 
 def solution(mesh):

time: 102 us -> 102 us (level)
  starting transfers between devices: 52.5 us -> 51.4 us
    ppermute x44 -> x38, starting transfers between devices: 52.5 us -> 44.6 us  [swap(): lax.ppermute(value, axis, [(i, i ^ step) for i in range(lax.axis_size(axi...]
    ppermute x0 -> x6, starting transfers between devices: none -> 6.77 us  [crossed_terms(): terms.append(lax.ppermute(value, ('row', 'col'), pairs))]
    ppermute x0 -> x6, waiting for transfers between devices: none -> 6.12 us  [crossed_terms(): terms.append(lax.ppermute(value, ('row', 'col'), pairs))]
    ppermute x44 -> x38, waiting for transfers between devices: 26.8 us -> 20.7 us  [swap(): lax.ppermute(value, axis, [(i, i ^ step) for i in range(lax.axis_size(axi...]
  transfers between devices with their start and end apart: 44 -> 44, of which waited for: 26 -> 27; matrix products, arithmetic and copies ran while one was open for 0% -> 0% of each run, Pallas kernels for 10% -> 11%
where the time goes in v10:
time: 102 us; the launch traced here: 101 us
  starting transfers between devices  51.4 us (50%)
  waiting for transfers between devices  26.8 us (26%)
  Pallas kernels  22.1 us (22%)
    ppermute x38, starting transfers between devices, swap(): lax.ppermute(value, axis, [(i, i ^ step) for i in range(lax.axis_size(axi...  44.6 us
    ppermute x38, waiting for transfers between devices, swap(): lax.ppermute(value, axis, [(i, i ^ step) for i in range(lax.axis_size(axi...  20.7 us
    ppermute x6, starting transfers between devices, crossed_terms(): terms.append(lax.ppermute(value, ('row', 'col'), pairs))  6.77 us
    ppermute x6, waiting for transfers between devices, crossed_terms(): terms.append(lax.ppermute(value, ('row', 'col'), pairs))  6.12 us
    pallas_call x1, Pallas kernels, shards(): call(functools.partial(load_body, columns // side if split else 0), 'load...  3.53 us
    pallas_call x2, Pallas kernels, shards(): call(back_other_body, 'backward_rest', [SCALARS] + [WHOLE] * 3, [f32(widt...  3.01 us
    pallas_call x1, Pallas kernels, shards(): call(functools.partial(finish_body, root_count), 'finish', [WHOLE] * (chi...  2.52 us
    pallas_call x1, Pallas kernels, shards(): call(functools.partial(next_other_body, len(pieces), chips), 'forward', [...  2.41 us
  transfers between devices with their start and end apart: 44, of which 27 were waited for; matrix products, arithmetic and copies ran while one was open for 0% of the time, Pallas kernels for 11%

profile of v10, /device:TPU:0, one launch (start us, length us, event | category | flops | bytes accessed | tf_op | source)
XLA Modules:
  0.0 101.3 jit_solution(17558199424081446590)
XLA Ops:
  1.0 4.0 %collective-permute-start.2 = (bf16[64,512]{1,0:T(8,128)(2,1)S(1)}, bf16[64,512]{1,0:T(8,128)(2,1)S(1)}, u32[]{:S(2)}, u32[]{:S(2)}) collective-permute-start(bf16[64,512]{1,0:T(8,128)(2,1)S(1)} %start.1.after_ref.refs_0_), channel_id=1, source_target_pairs={{0,24},{8,16},{16,8},{24,0},{1,25},{9,17},{17,9},{25,1},{2,26},{10... | collective-permute-start | bytes 196616 | tf_op jit(solution)/shard_map/ppermute | solution.py:467
  6.3 3.5 %load.1 = (bf16[32,256,256]{2,1,0:T(8,128)(2,1)S(1)}, f32[1,512]{1,0:T(1,128)S(1)}, f32[1,2048]{1,0:T(1,128)S(1)}, f32[1,256]{1,0:T(1,128)S(1)}, s32[10,32]{1,0:T(8,128)S(1)}) custom-call(s32[3]{0:T(128)S(1)} %pad_add_fusion.place, bf16[64,512]{1,0:T(8,128)(2,1)S(1)} %start.1.after_ref.refs_0_, bf16[32,256,256]{2,1,0:T(8,128)(2,1)} %bitcast.8, ...), custom_call_target="tpu_custom_call" | custom-call | bytes 8388608 | tf_op jit(solution)/shard_map/load/pallas_call | solution.py:522
  9.9 1.9 %forward.2 = (bf16[9,64,256]{2,1,0:T(8,128)(2,1)S(1)}, f32[4,64,256]{2,1,0:T(8,128)S(1)}) custom-call(s32[10,32]{1,0:T(8,128)S(1)} %get-tuple-element.43.table, bf16[64,512]{1,0:T(8,128)(2,1)S(1)} %start.1.after_ref.refs_0_, bf16[64,512]{1,0:T(8,128)(2,1)S(1)} %collective-permute-done.refs_1_, bf16[64,512]{1,0:T(8,128)(2,1)S(1)} %collective-permute-done.1.refs_2_, ...), custom_call_target="tpu_custom_call" | custom-call | flops 134217728 | bytes 2097152 | tf_op jit(solution)/shard_map/forward/pallas_call | solution.py:616
  11.8 1.5 %forward_rest.2.mine_ref = f32[4,64,256]{2,1,0:T(8,128)S(1)} custom-call(s32[10,32]{1,0:T(8,128)S(1)} %get-tuple-element.43.table, bf16[9,64,256]{2,1,0:T(8,128)(2,1)S(1)} %get-tuple-element.45.held, bf16[32,256,256]{2,1,0:T(8,128)(2,1)S(1)} %get-tuple-element.44.refs_4_.tile_ref.refs_9_), custom_call_target="tpu_custom_call" | custom-call | flops 134217728 | bytes 2097152 | tf_op jit(solution)/shard_map/forward_rest/pallas_call | solution.py:625
  13.4 3.6 %collective-permute-start.4 = (bf16[64,256]{1,0:T(8,128)(2,1)S(1)}, bf16[64,256]{1,0:T(8,128)(2,1)S(1)}, u32[]{:S(2)}, u32[]{:S(2)}) collective-permute-start(bf16[64,256]{1,0:T(8,128)(2,1)S(1)} %get-tuple-element.48), channel_id=1, source_target_pairs={{0,6},{1,7},{2,4},{3,5},{4,2},{5,3},{6,0},{7,1},{8,14},{9,15},{10,... | collective-permute-start | bytes 98312 | tf_op jit(solution)/shard_map/ppermute | solution.py:467
  19.2 2.6 %collective-permute-done.5.refs_2_ = bf16[64,256]{1,0:T(8,128)(2,1)S(1)} collective-permute-done((bf16[64,256]{1,0:T(8,128)(2,1)S(1)}, bf16[64,256]{1,0:T(8,128)(2,1)S(1)}, u32[]{:S(2)}, u32[]{:S(2)}) %collective-permute-start.5) | collective-permute-done | bytes 32800 | tf_op jit(solution)/shard_map/ppermute | solution.py:467
  21.9 1.7 %collective-permute-start.9 = (bf16[64,256]{1,0:T(8,128)(2,1)S(1)}, bf16[64,256]{1,0:T(8,128)(2,1)S(1)}, u32[]{:S(2)}, u32[]{:S(2)}) collective-permute-start(bf16[64,256]{1,0:T(8,128)(2,1)S(1)} %query.2.refs_0_), channel_id=1, source_target_pairs={{0,6},{1,7},{2,4},{3,5},{4,2},{5,3},{6,0},{7,1},{8,14},{9,15},{10,... | collective-permute-start | bytes 98312 | tf_op jit(solution)/shard_map/ppermute | solution.py:467
  24.0 2.3 %collective-permute-start.7 = (bf16[64,256]{1,0:T(8,128)(2,1)S(1)}, bf16[64,256]{1,0:T(8,128)(2,1)S(1)}, u32[]{:S(2)}, u32[]{:S(2)}) collective-permute-start(bf16[64,256]{1,0:T(8,128)(2,1)S(1)} %query.2.refs_0_), channel_id=1, source_target_pairs={{0,2},{1,3},{2,0},{3,1},{4,6},{5,7},{6,4},{7,5},{8,10},{9,11},{10,... | collective-permute-start | bytes 98312 | tf_op jit(solution)/shard_map/ppermute | solution.py:467
  30.0 1.5 %backward_rest.2 = (f32[32,512]{1,0:T(8,128)S(1)}, f32[32,512]{1,0:T(8,128)S(1)}, f32[32,512]{1,0:T(8,128)S(1)}, f32[32,512]{1,0:T(8,128)S(1)}, f32[32,512]{1,0:...) custom-call(s32[10,32]{1,0:T(8,128)S(1)} %get-tuple-element.43.table, ...), custom_call_target="tpu_custom_call" | custom-call | flops 134217728 | bytes 2097152 | tf_op jit(solution)/shard_map/backward_rest/pallas_call | solution.py:661
  31.5 2.7 %collective-permute-start.11 = (f32[32,512]{1,0:T(8,128)S(1)}, f32[32,512]{1,0:T(8,128)S(1)}, u32[]{:S(2)}, u32[]{:S(2)}) collective-permute-start(f32[32,512]{1,0:T(8,128)S(1)} %get-tuple-element.53), channel_id=1, source_target_pairs={{0,24},{8,16},{16,8},{24,0},{1,25},{9,17},{17,9},{25,1},{2,26},{10... | collective-permute-start | bytes 196616 | tf_op jit(solution)/shard_map/ppermute | solution.py:467
  35.1 2.6 %collective-permute-start.17 = (f32[32,512]{1,0:T(8,128)S(1)}, f32[32,512]{1,0:T(8,128)S(1)}, u32[]{:S(2)}, u32[]{:S(2)}) collective-permute-start(f32[32,512]{1,0:T(8,128)S(1)} %get-tuple-element.58), channel_id=1, source_target_pairs={{0,24},{8,16},{16,8},{24,0},{1,25},{9,17},{17,9},{25,1},{2,26},{10... | collective-permute-start | bytes 196616 | tf_op jit(solution)/shard_map/ppermute | solution.py:467
  39.1 2.1 %collective-permute-start.16 = (f32[32,512]{1,0:T(8,128)S(1)}, f32[32,512]{1,0:T(8,128)S(1)}, u32[]{:S(2)}, u32[]{:S(2)}) collective-permute-start(f32[32,512]{1,0:T(8,128)S(1)} %lift.3.refs_0_), channel_id=1, source_target_pairs={{0,24},{8,16},{16,8},{24,0},{1,25},{9,17},{17,9},{25,1},{2,26},{10... | collective-permute-start | bytes 196616 | tf_op jit(solution)/shard_map/ppermute | solution.py:467
  43.1 1.7 %collective-permute-start.22 = (f32[32,512]{1,0:T(8,128)S(1)}, f32[32,512]{1,0:T(8,128)S(1)}, u32[]{:S(2)}, u32[]{:S(2)}) collective-permute-start(f32[32,512]{1,0:T(8,128)S(1)} %lift.4.refs_4_), channel_id=1, source_target_pairs={{0,24},{8,16},{16,8},{24,0},{1,25},{9,17},{17,9},{25,1},{2,26},{10... | collective-permute-start | bytes 196616 | tf_op jit(solution)/shard_map/ppermute | solution.py:467
  45.1 1.6 %collective-permute-start.20 = (f32[32,512]{1,0:T(8,128)S(1)}, f32[32,512]{1,0:T(8,128)S(1)}, u32[]{:S(2)}, u32[]{:S(2)}) collective-permute-start(f32[32,512]{1,0:T(8,128)S(1)} %lift.4.refs_4_), channel_id=1, source_target_pairs={{0,8},{8,0},{16,24},{24,16},{1,9},{9,1},{17,25},{25,17},{2,10},{10... | collective-permute-start | bytes 196616 | tf_op jit(solution)/shard_map/ppermute | solution.py:467
  46.9 1.4 %collective-permute-done.22.refs_7_ = f32[32,512]{1,0:T(8,128)S(1)} collective-permute-done((f32[32,512]{1,0:T(8,128)S(1)}, f32[32,512]{1,0:T(8,128)S(1)}, u32[]{:S(2)}, u32[]{:S(2)}) %collective-permute-start.22) | collective-permute-done | bytes 65568 | tf_op jit(solution)/shard_map/ppermute | solution.py:467
  49.3 2.4 %forward.3 = (bf16[9,128,256]{2,1,0:T(8,128)(2,1)S(1)}, f32[272,256]{1,0:T(8,128)S(1)}, f32[16,256]{1,0:T(8,128)S(1)}) custom-call(s32[10,32]{1,0:T(8,128)S(1)} %get-tuple-element.43.table, f32[32,512]{1,0:T(8,128)S(1)} %lift.3.refs_0_, f32[32,512]{1,0:T(8,128)S(1)} %collective-permute-done.14.refs_1_, f32[32,512]{1,0:T(8,128)S(1)} %collective-permute-done.15.refs_2_, ...), custom_call_target="tpu_custom_call" | custom-call | flops 134217728 | bytes 2097152 | tf_op jit(solution)/shard_map/forward/pallas_call | solution.py:565
  51.8 1.5 %forward_rest.3.mine_ref = f32[256,256]{1,0:T(8,128)S(1)} custom-call(s32[10,32]{1,0:T(8,128)S(1)} %get-tuple-element.43.table, bf16[9,128,256]{2,1,0:T(8,128)(2,1)S(1)} %get-tuple-element.62.held, bf16[32,256,256]{2,1,0:T(8,128)(2,1)S(1)} %get-tuple-element.44.refs_4_.tile_ref.refs_9_), custom_call_target="tpu_custom_call" | custom-call | flops 134217728 | bytes 2097152 | tf_op jit(solution)/shard_map/forward_rest/pallas_call | solution.py:574
  53.5 1.7 %collective-permute-start.27 = (f32[96,128]{1,0:T(8,128)S(1)}, f32[96,128]{1,0:T(8,128)S(1)}, u32[]{:S(2)}, u32[]{:S(2)}) collective-permute-start(f32[96,128]{1,0:T(8,128)S(1)} %get-tuple-element.70), channel_id=1, source_target_pairs={{0,6},{1,7},{2,4},{3,5},{4,2},{5,3},{6,0},{7,1},{8,14},{9,15},{10,... | collective-permute-start | bytes 147464 | tf_op jit(solution)/shard_map/ppermute | solution.py:467
  56.3 1.6 %collective-permute-start.29 = (f32[96,128]{1,0:T(8,128)S(1)}, f32[96,128]{1,0:T(8,128)S(1)}, u32[]{:S(2)}, u32[]{:S(2)}) collective-permute-start(f32[96,128]{1,0:T(8,128)S(1)} %get-tuple-element.72), channel_id=1, source_target_pairs={{0,2},{1,3},{2,0},{3,1},{4,6},{5,7},{6,4},{7,5},{8,10},{9,11},{10,... | collective-permute-start | bytes 147464 | tf_op jit(solution)/shard_map/ppermute | solution.py:467
  57.9 1.7 %collective-permute-start.24 = (f32[64,128]{1,0:T(8,128)S(1)}, f32[64,128]{1,0:T(8,128)S(1)}, u32[]{:S(2)}, u32[]{:S(2)}) collective-permute-start(f32[64,128]{1,0:T(8,128)S(1)} %get-tuple-element.66), channel_id=1, source_target_pairs={{0,6},{1,7},{2,4},{3,5},{4,2},{5,3},{6,0},{7,1},{8,14},{9,15},{10,... | collective-permute-start | bytes 98312 | tf_op jit(solution)/shard_map/ppermute | solution.py:467
  60.0 2.3 %collective-permute-start.26 = (f32[64,128]{1,0:T(8,128)S(1)}, f32[64,128]{1,0:T(8,128)S(1)}, u32[]{:S(2)}, u32[]{:S(2)}) collective-permute-start(f32[64,128]{1,0:T(8,128)S(1)} %get-tuple-element.68), channel_id=1, source_target_pairs={{0,2},{1,3},{2,0},{3,1},{4,6},{5,7},{6,4},{7,5},{8,10},{9,11},{10,... | collective-permute-start | bytes 98312 | tf_op jit(solution)/shard_map/ppermute | solution.py:467
  62.3 1.8 %query.3 = (f32[64,64]{1,0:T(8,128)S(1)}, bf16[64,128]{1,0:T(8,128)(2,1)S(1)}) custom-call(f32[96,128]{1,0:T(8,128)S(1)} %get-tuple-element.69.refs_0_, f32[96,128]{1,0:T(8,128)S(1)} %collective-permute-done.27.refs_1_, f32[96,128]{1,0:T(8,128)S(1)} %collective-permute-done.28.refs_2_, f32[96,128]{1,0:T(8,128)S(1)} %collective-permute-done.29.refs_3_, ...), custom_call_target="tpu_custom_call" | custom-call | flops 268435456 | tf_op jit(solution)/shard_map/query/pallas_call | solution.py:605
  64.8 2.0 %collective-permute-start.32 = (bf16[64,256]{1,0:T(8,128)(2,1)S(1)}, bf16[64,256]{1,0:T(8,128)(2,1)S(1)}, u32[]{:S(2)}, u32[]{:S(2)}) collective-permute-start(bf16[64,256]{1,0:T(8,128)(2,1)S(1)} %query_rest.1.refs_0_), channel_id=1, source_target_pairs={{0,6},{1,7},{2,4},{3,5},{4,2},{5,3},{6,0},{7,1},{8,14},{9,15},{10,... | collective-permute-start | bytes 98312 | tf_op jit(solution)/shard_map/ppermute | solution.py:467
  69.2 1.6 %collective-permute-done.32.refs_3_ = bf16[64,256]{1,0:T(8,128)(2,1)S(1)} collective-permute-done((bf16[64,256]{1,0:T(8,128)(2,1)S(1)}, bf16[64,256]{1,0:T(8,128)(2,1)S(1)}, u32[]{:S(2)}, u32[]{:S(2)}) %collective-permute-start.32) | collective-permute-done | bytes 32800 | tf_op jit(solution)/shard_map/ppermute | solution.py:467
  73.6 1.5 %backward_rest.3 = (f32[64,512]{1,0:T(8,128)S(1)}, f32[64,512]{1,0:T(8,128)S(1)}, f32[64,512]{1,0:T(8,128)S(1)}, f32[64,512]{1,0:T(8,128)S(1)}) custom-call(s32[10,32]{1,0:T(8,128)S(1)} %get-tuple-element.43.table, bf16[4,64,256]{2,1,0:T(8,128)(2,1)S(1)} %collective-permute-done.33.there_ref, f32[9,64,256]{2,1,0:T(8,128)S(1)} %backward.3.begun_ref, ...), custom_call_target="tpu_custom_call" | custom-call | flops 134217728 | bytes 2097152 | tf_op jit(solution)/shard_map/backward_rest/pallas_call | solution.py:661
  75.1 1.9 %collective-permute-start.34 = (f32[64,512]{1,0:T(8,128)S(1)}, f32[64,512]{1,0:T(8,128)S(1)}, u32[]{:S(2)}, u32[]{:S(2)}) collective-permute-start(f32[64,512]{1,0:T(8,128)S(1)} %get-tuple-element.76), channel_id=1, source_target_pairs={{0,24},{8,16},{16,8},{24,0},{1,25},{9,17},{17,9},{25,1},{2,26},{10... | collective-permute-start | bytes 393224 | tf_op jit(solution)/shard_map/ppermute | solution.py:467
  78.7 3.7 %collective-permute-done.34.refs_1_ = f32[64,512]{1,0:T(8,128)S(1)} collective-permute-done((f32[64,512]{1,0:T(8,128)S(1)}, f32[64,512]{1,0:T(8,128)S(1)}, u32[]{:S(2)}, u32[]{:S(2)}) %collective-permute-start.34) | collective-permute-done | bytes 131104 | tf_op jit(solution)/shard_map/ppermute | solution.py:467
  82.3 2.0 %collective-permute-done.35.refs_2_ = f32[64,512]{1,0:T(8,128)S(1)} collective-permute-done((f32[64,512]{1,0:T(8,128)S(1)}, f32[64,512]{1,0:T(8,128)S(1)}, u32[]{:S(2)}, u32[]{:S(2)}) %collective-permute-start.35) | collective-permute-done | bytes 131104 | tf_op jit(solution)/shard_map/ppermute | solution.py:467
  87.5 1.6 %collective-permute-done.39.refs_3_ = f32[64,64]{1,0:T(8,128)S(1)} collective-permute-done((f32[64,64]{1,0:T(8,128)S(1)}, f32[64,64]{1,0:T(8,128)S(1)}, u32[]{:S(2)}, u32[]{:S(2)}) %collective-permute-start.39) | collective-permute-done | bytes 16416 | tf_op jit(solution)/shard_map/ppermute | solution.py:493
  91.9 1.5 %collective-permute-start.43 = (f32[64,64]{1,0:T(8,128)S(1)}, f32[64,64]{1,0:T(8,128)S(1)}, u32[]{:S(2)}, u32[]{:S(2)}) collective-permute-start(f32[64,64]{1,0:T(8,128)S(1)} %sum.3.refs_0_), channel_id=1, source_target_pairs={{0,7},{1,6},{2,5},{3,4},{4,3},{5,2},{6,1},{7,0},{8,15},{9,14},{10,... | collective-permute-start | bytes 49160 | tf_op jit(solution)/shard_map/ppermute | solution.py:493
  97.0 1.8 %collective-permute-done.42.refs_2_ = f32[64,64]{1,0:T(8,128)S(1)} collective-permute-done((f32[64,64]{1,0:T(8,128)S(1)}, f32[64,64]{1,0:T(8,128)S(1)}, u32[]{:S(2)}, u32[]{:S(2)}) %collective-permute-start.42) | collective-permute-done | bytes 16416 | tf_op jit(solution)/shard_map/ppermute | solution.py:493
  98.8 2.5 %finish.1 = f32[64,512]{1,0:T(8,128)} custom-call(f32[64,64]{1,0:T(8,128)S(1)} %sum.3.refs_0_, f32[64,64]{1,0:T(8,128)S(1)} %collective-permute-done.41.refs_1_, f32[64,64]{1,0:T(8,128)S(1)} %collective-permute-done.42.refs_2_, f32[64,64]{1,0:T(8,128)S(1)} %collective-permute-done.43.refs_3_, f32[64,512]{1,0:T(8,128)S(1)} %get-tuple-element.80.refs_4_), custom_call_target="tpu_custom_call" | custom-call | tf_op jit(solution)/shard_map/finish/pallas_call | solution.py:688
  (80 shorter events, 32.5 us)
Async XLA Ops:
  1.0 8.9 %collective-permute-start.2 = (bf16[64,512]{1,0:T(8,128)(2,1)S(1)}, bf16[64,512]{1,0:T(8,128)(2,1)S(1)}, u32[]{:S(2)}, u32[]{:S(2)}) collective-permute-start(bf16[64,512]{1,0:T(8,128)(2,1)S(1)} %start.1.after_ref.refs_0_), channel_id=1, source_target_pairs={{0,24},{8,16},{16,8},{24,0},{1,25},{9,17},{17,9},{25,1},{2,26},{10... | collective-permute-start | bytes 196616 | tf_op jit(solution)/shard_map/ppermute | solution.py:467
  4.9 4.9 %collective-permute-start.1 = (bf16[64,512]{1,0:T(8,128)(2,1)S(1)}, bf16[64,512]{1,0:T(8,128)(2,1)S(1)}, u32[]{:S(2)}, u32[]{:S(2)}) collective-permute-start(bf16[64,512]{1,0:T(8,128)(2,1)S(1)} %start.1.after_ref.refs_0_), channel_id=1, source_target_pairs={{0,16},{8,24},{16,0},{24,8},{1,17},{9,25},{17,1},{25,9},{2,18},{10... | collective-permute-start | bytes 196616 | tf_op jit(solution)/shard_map/ppermute | solution.py:467
  13.4 5.8 %collective-permute-start.4 = (bf16[64,256]{1,0:T(8,128)(2,1)S(1)}, bf16[64,256]{1,0:T(8,128)(2,1)S(1)}, u32[]{:S(2)}, u32[]{:S(2)}) collective-permute-start(bf16[64,256]{1,0:T(8,128)(2,1)S(1)} %get-tuple-element.48), channel_id=1, source_target_pairs={{0,6},{1,7},{2,4},{3,5},{4,2},{5,3},{6,0},{7,1},{8,14},{9,15},{10,... | collective-permute-start | bytes 98312 | tf_op jit(solution)/shard_map/ppermute | solution.py:467
  17.0 4.8 %collective-permute-start.5 = (bf16[64,256]{1,0:T(8,128)(2,1)S(1)}, bf16[64,256]{1,0:T(8,128)(2,1)S(1)}, u32[]{:S(2)}, u32[]{:S(2)}) collective-permute-start(bf16[64,256]{1,0:T(8,128)(2,1)S(1)} %get-tuple-element.49), channel_id=1, source_target_pairs={{0,4},{1,5},{2,6},{3,7},{4,0},{5,1},{6,2},{7,3},{8,12},{9,13},{10,... | collective-permute-start | bytes 98312 | tf_op jit(solution)/shard_map/ppermute | solution.py:467
  17.0 4.8 %collective-permute-start.6 = (bf16[64,256]{1,0:T(8,128)(2,1)S(1)}, bf16[64,256]{1,0:T(8,128)(2,1)S(1)}, u32[]{:S(2)}, u32[]{:S(2)}) collective-permute-start(bf16[64,256]{1,0:T(8,128)(2,1)S(1)} %get-tuple-element.50), channel_id=1, source_target_pairs={{0,2},{1,3},{2,0},{3,1},{4,6},{5,7},{6,4},{7,5},{8,10},{9,11},{10,... | collective-permute-start | bytes 98312 | tf_op jit(solution)/shard_map/ppermute | solution.py:467
  21.9 5.9 %collective-permute-start.9 = (bf16[64,256]{1,0:T(8,128)(2,1)S(1)}, bf16[64,256]{1,0:T(8,128)(2,1)S(1)}, u32[]{:S(2)}, u32[]{:S(2)}) collective-permute-start(bf16[64,256]{1,0:T(8,128)(2,1)S(1)} %query.2.refs_0_), channel_id=1, source_target_pairs={{0,6},{1,7},{2,4},{3,5},{4,2},{5,3},{6,0},{7,1},{8,14},{9,15},{10,... | collective-permute-start | bytes 98312 | tf_op jit(solution)/shard_map/ppermute | solution.py:467
  23.6 4.9 %collective-permute-start.8 = (bf16[64,256]{1,0:T(8,128)(2,1)S(1)}, bf16[64,256]{1,0:T(8,128)(2,1)S(1)}, u32[]{:S(2)}, u32[]{:S(2)}) collective-permute-start(bf16[64,256]{1,0:T(8,128)(2,1)S(1)} %query.2.refs_0_), channel_id=1, source_target_pairs={{0,4},{1,5},{2,6},{3,7},{4,0},{5,1},{6,2},{7,3},{8,12},{9,13},{10,... | collective-permute-start | bytes 98312 | tf_op jit(solution)/shard_map/ppermute | solution.py:467
  24.0 4.5 %collective-permute-start.7 = (bf16[64,256]{1,0:T(8,128)(2,1)S(1)}, bf16[64,256]{1,0:T(8,128)(2,1)S(1)}, u32[]{:S(2)}, u32[]{:S(2)}) collective-permute-start(bf16[64,256]{1,0:T(8,128)(2,1)S(1)} %query.2.refs_0_), channel_id=1, source_target_pairs={{0,2},{1,3},{2,0},{3,1},{4,6},{5,7},{6,4},{7,5},{8,10},{9,11},{10,... | collective-permute-start | bytes 98312 | tf_op jit(solution)/shard_map/ppermute | solution.py:467
  31.5 6.2 %collective-permute-start.11 = (f32[32,512]{1,0:T(8,128)S(1)}, f32[32,512]{1,0:T(8,128)S(1)}, u32[]{:S(2)}, u32[]{:S(2)}) collective-permute-start(f32[32,512]{1,0:T(8,128)S(1)} %get-tuple-element.53), channel_id=1, source_target_pairs={{0,24},{8,16},{16,8},{24,0},{1,25},{9,17},{17,9},{25,1},{2,26},{10... | collective-permute-start | bytes 196616 | tf_op jit(solution)/shard_map/ppermute | solution.py:467
  34.2 4.9 %collective-permute-start.13 = (f32[32,512]{1,0:T(8,128)S(1)}, f32[32,512]{1,0:T(8,128)S(1)}, u32[]{:S(2)}, u32[]{:S(2)}) collective-permute-start(f32[32,512]{1,0:T(8,128)S(1)} %get-tuple-element.55), channel_id=1, source_target_pairs={{0,8},{8,0},{16,24},{24,16},{1,9},{9,1},{17,25},{25,17},{2,10},{10... | collective-permute-start | bytes 196616 | tf_op jit(solution)/shard_map/ppermute | solution.py:467
  35.1 6.4 %collective-permute-start.17 = (f32[32,512]{1,0:T(8,128)S(1)}, f32[32,512]{1,0:T(8,128)S(1)}, u32[]{:S(2)}, u32[]{:S(2)}) collective-permute-start(f32[32,512]{1,0:T(8,128)S(1)} %get-tuple-element.58), channel_id=1, source_target_pairs={{0,24},{8,16},{16,8},{24,0},{1,25},{9,17},{17,9},{25,1},{2,26},{10... | collective-permute-start | bytes 196616 | tf_op jit(solution)/shard_map/ppermute | solution.py:467
  37.7 5.4 %collective-permute-start.18 = (f32[32,512]{1,0:T(8,128)S(1)}, f32[32,512]{1,0:T(8,128)S(1)}, u32[]{:S(2)}, u32[]{:S(2)}) collective-permute-start(f32[32,512]{1,0:T(8,128)S(1)} %get-tuple-element.59), channel_id=1, source_target_pairs={{0,16},{8,24},{16,0},{24,8},{1,17},{9,25},{17,1},{25,9},{2,18},{10... | collective-permute-start | bytes 196616 | tf_op jit(solution)/shard_map/ppermute | solution.py:467
  37.7 5.4 %collective-permute-start.19 = (f32[32,512]{1,0:T(8,128)S(1)}, f32[32,512]{1,0:T(8,128)S(1)}, u32[]{:S(2)}, u32[]{:S(2)}) collective-permute-start(f32[32,512]{1,0:T(8,128)S(1)} %get-tuple-element.60), channel_id=1, source_target_pairs={{0,8},{8,0},{16,24},{24,16},{1,9},{9,1},{17,25},{25,17},{2,10},{10... | collective-permute-start | bytes 196616 | tf_op jit(solution)/shard_map/ppermute | solution.py:467
  39.1 6.0 %collective-permute-start.16 = (f32[32,512]{1,0:T(8,128)S(1)}, f32[32,512]{1,0:T(8,128)S(1)}, u32[]{:S(2)}, u32[]{:S(2)}) collective-permute-start(f32[32,512]{1,0:T(8,128)S(1)} %lift.3.refs_0_), channel_id=1, source_target_pairs={{0,24},{8,16},{16,8},{24,0},{1,25},{9,17},{17,9},{25,1},{2,26},{10... | collective-permute-start | bytes 196616 | tf_op jit(solution)/shard_map/ppermute | solution.py:467
  41.3 5.6 %collective-permute-start.15 = (f32[32,512]{1,0:T(8,128)S(1)}, f32[32,512]{1,0:T(8,128)S(1)}, u32[]{:S(2)}, u32[]{:S(2)}) collective-permute-start(f32[32,512]{1,0:T(8,128)S(1)} %lift.3.refs_0_), channel_id=1, source_target_pairs={{0,16},{8,24},{16,0},{24,8},{1,17},{9,25},{17,1},{25,9},{2,18},{10... | collective-permute-start | bytes 196616 | tf_op jit(solution)/shard_map/ppermute | solution.py:467
  41.4 5.5 %collective-permute-start.14 = (f32[32,512]{1,0:T(8,128)S(1)}, f32[32,512]{1,0:T(8,128)S(1)}, u32[]{:S(2)}, u32[]{:S(2)}) collective-permute-start(f32[32,512]{1,0:T(8,128)S(1)} %lift.3.refs_0_), channel_id=1, source_target_pairs={{0,8},{8,0},{16,24},{24,16},{1,9},{9,1},{17,25},{25,17},{2,10},{10... | collective-permute-start | bytes 196616 | tf_op jit(solution)/shard_map/ppermute | solution.py:467
  43.1 5.2 %collective-permute-start.22 = (f32[32,512]{1,0:T(8,128)S(1)}, f32[32,512]{1,0:T(8,128)S(1)}, u32[]{:S(2)}, u32[]{:S(2)}) collective-permute-start(f32[32,512]{1,0:T(8,128)S(1)} %lift.4.refs_4_), channel_id=1, source_target_pairs={{0,24},{8,16},{16,8},{24,0},{1,25},{9,17},{17,9},{25,1},{2,26},{10... | collective-permute-start | bytes 196616 | tf_op jit(solution)/shard_map/ppermute | solution.py:467
  53.5 6.5 %collective-permute-start.27 = (f32[96,128]{1,0:T(8,128)S(1)}, f32[96,128]{1,0:T(8,128)S(1)}, u32[]{:S(2)}, u32[]{:S(2)}) collective-permute-start(f32[96,128]{1,0:T(8,128)S(1)} %get-tuple-element.70), channel_id=1, source_target_pairs={{0,6},{1,7},{2,4},{3,5},{4,2},{5,3},{6,0},{7,1},{8,14},{9,15},{10,... | collective-permute-start | bytes 147464 | tf_op jit(solution)/shard_map/ppermute | solution.py:467
  55.2 7.1 %collective-permute-start.28 = (f32[96,128]{1,0:T(8,128)S(1)}, f32[96,128]{1,0:T(8,128)S(1)}, u32[]{:S(2)}, u32[]{:S(2)}) collective-permute-start(f32[96,128]{1,0:T(8,128)S(1)} %get-tuple-element.71), channel_id=1, source_target_pairs={{0,4},{1,5},{2,6},{3,7},{4,0},{5,1},{6,2},{7,3},{8,12},{9,13},{10,... | collective-permute-start | bytes 147464 | tf_op jit(solution)/shard_map/ppermute | solution.py:467
  56.3 6.0 %collective-permute-start.29 = (f32[96,128]{1,0:T(8,128)S(1)}, f32[96,128]{1,0:T(8,128)S(1)}, u32[]{:S(2)}, u32[]{:S(2)}) collective-permute-start(f32[96,128]{1,0:T(8,128)S(1)} %get-tuple-element.72), channel_id=1, source_target_pairs={{0,2},{1,3},{2,0},{3,1},{4,6},{5,7},{6,4},{7,5},{8,10},{9,11},{10,... | collective-permute-start | bytes 147464 | tf_op jit(solution)/shard_map/ppermute | solution.py:467
  57.9 6.2 %collective-permute-start.24 = (f32[64,128]{1,0:T(8,128)S(1)}, f32[64,128]{1,0:T(8,128)S(1)}, u32[]{:S(2)}, u32[]{:S(2)}) collective-permute-start(f32[64,128]{1,0:T(8,128)S(1)} %get-tuple-element.66), channel_id=1, source_target_pairs={{0,6},{1,7},{2,4},{3,5},{4,2},{5,3},{6,0},{7,1},{8,14},{9,15},{10,... | collective-permute-start | bytes 98312 | tf_op jit(solution)/shard_map/ppermute | solution.py:467
  59.6 5.0 %collective-permute-start.25 = (f32[64,128]{1,0:T(8,128)S(1)}, f32[64,128]{1,0:T(8,128)S(1)}, u32[]{:S(2)}, u32[]{:S(2)}) collective-permute-start(f32[64,128]{1,0:T(8,128)S(1)} %get-tuple-element.67), channel_id=1, source_target_pairs={{0,4},{1,5},{2,6},{3,7},{4,0},{5,1},{6,2},{7,3},{8,12},{9,13},{10,... | collective-permute-start | bytes 98312 | tf_op jit(solution)/shard_map/ppermute | solution.py:467
  60.0 4.6 %collective-permute-start.26 = (f32[64,128]{1,0:T(8,128)S(1)}, f32[64,128]{1,0:T(8,128)S(1)}, u32[]{:S(2)}, u32[]{:S(2)}) collective-permute-start(f32[64,128]{1,0:T(8,128)S(1)} %get-tuple-element.68), channel_id=1, source_target_pairs={{0,2},{1,3},{2,0},{3,1},{4,6},{5,7},{6,4},{7,5},{8,10},{9,11},{10,... | collective-permute-start | bytes 98312 | tf_op jit(solution)/shard_map/ppermute | solution.py:467
  64.8 6.0 %collective-permute-start.32 = (bf16[64,256]{1,0:T(8,128)(2,1)S(1)}, bf16[64,256]{1,0:T(8,128)(2,1)S(1)}, u32[]{:S(2)}, u32[]{:S(2)}) collective-permute-start(bf16[64,256]{1,0:T(8,128)(2,1)S(1)} %query_rest.1.refs_0_), channel_id=1, source_target_pairs={{0,6},{1,7},{2,4},{3,5},{4,2},{5,3},{6,0},{7,1},{8,14},{9,15},{10,... | collective-permute-start | bytes 98312 | tf_op jit(solution)/shard_map/ppermute | solution.py:467
  66.8 5.2 %collective-permute-start.31 = (bf16[64,256]{1,0:T(8,128)(2,1)S(1)}, bf16[64,256]{1,0:T(8,128)(2,1)S(1)}, u32[]{:S(2)}, u32[]{:S(2)}) collective-permute-start(bf16[64,256]{1,0:T(8,128)(2,1)S(1)} %query_rest.1.refs_0_), channel_id=1, source_target_pairs={{0,4},{1,5},{2,6},{3,7},{4,0},{5,1},{6,2},{7,3},{8,12},{9,13},{10,... | collective-permute-start | bytes 98312 | tf_op jit(solution)/shard_map/ppermute | solution.py:467
  75.1 7.2 %collective-permute-start.34 = (f32[64,512]{1,0:T(8,128)S(1)}, f32[64,512]{1,0:T(8,128)S(1)}, u32[]{:S(2)}, u32[]{:S(2)}) collective-permute-start(f32[64,512]{1,0:T(8,128)S(1)} %get-tuple-element.76), channel_id=1, source_target_pairs={{0,24},{8,16},{16,8},{24,0},{1,25},{9,17},{17,9},{25,1},{2,26},{10... | collective-permute-start | bytes 393224 | tf_op jit(solution)/shard_map/ppermute | solution.py:467
  77.0 7.3 %collective-permute-start.35 = (f32[64,512]{1,0:T(8,128)S(1)}, f32[64,512]{1,0:T(8,128)S(1)}, u32[]{:S(2)}, u32[]{:S(2)}) collective-permute-start(f32[64,512]{1,0:T(8,128)S(1)} %get-tuple-element.77), channel_id=1, source_target_pairs={{0,16},{8,24},{16,0},{24,8},{1,17},{9,25},{17,1},{25,9},{2,18},{10... | collective-permute-start | bytes 393224 | tf_op jit(solution)/shard_map/ppermute | solution.py:467
  77.3 7.0 %collective-permute-start.36 = (f32[64,512]{1,0:T(8,128)S(1)}, f32[64,512]{1,0:T(8,128)S(1)}, u32[]{:S(2)}, u32[]{:S(2)}) collective-permute-start(f32[64,512]{1,0:T(8,128)S(1)} %get-tuple-element.78), channel_id=1, source_target_pairs={{0,8},{8,0},{16,24},{24,16},{1,9},{9,1},{17,25},{25,17},{2,10},{10... | collective-permute-start | bytes 393224 | tf_op jit(solution)/shard_map/ppermute | solution.py:467
  84.6 4.5 %collective-permute-start.39 = (f32[64,64]{1,0:T(8,128)S(1)}, f32[64,64]{1,0:T(8,128)S(1)}, u32[]{:S(2)}, u32[]{:S(2)}) collective-permute-start(f32[64,64]{1,0:T(8,128)S(1)} %get-tuple-element.79.refs_0_), channel_id=1, source_target_pairs={{0,25},{1,24},{2,27},{3,26},{4,29},{5,28},{6,31},{7,30},{8,17},{9,... | collective-permute-start | bytes 49160 | tf_op jit(solution)/shard_map/ppermute | solution.py:493
  91.9 5.1 %collective-permute-start.43 = (f32[64,64]{1,0:T(8,128)S(1)}, f32[64,64]{1,0:T(8,128)S(1)}, u32[]{:S(2)}, u32[]{:S(2)}) collective-permute-start(f32[64,64]{1,0:T(8,128)S(1)} %sum.3.refs_0_), channel_id=1, source_target_pairs={{0,7},{1,6},{2,5},{3,4},{4,3},{5,2},{6,1},{7,0},{8,15},{9,14},{10,... | collective-permute-start | bytes 49160 | tf_op jit(solution)/shard_map/ppermute | solution.py:493
  93.4 5.4 %collective-permute-start.42 = (f32[64,64]{1,0:T(8,128)S(1)}, f32[64,64]{1,0:T(8,128)S(1)}, u32[]{:S(2)}, u32[]{:S(2)}) collective-permute-start(f32[64,64]{1,0:T(8,128)S(1)} %sum.3.refs_0_), channel_id=1, source_target_pairs={{0,5},{1,4},{2,7},{3,6},{4,1},{5,0},{6,3},{7,2},{8,13},{9,12},{10,... | collective-permute-start | bytes 49160 | tf_op jit(solution)/shard_map/ppermute | solution.py:493
  94.4 4.4 %collective-permute-start.41 = (f32[64,64]{1,0:T(8,128)S(1)}, f32[64,64]{1,0:T(8,128)S(1)}, u32[]{:S(2)}, u32[]{:S(2)}) collective-permute-start(f32[64,64]{1,0:T(8,128)S(1)} %sum.3.refs_0_), channel_id=1, source_target_pairs={{0,3},{1,2},{2,1},{3,0},{4,7},{5,6},{6,5},{7,4},{8,11},{9,10},{10,... | collective-permute-start | bytes 49160 | tf_op jit(solution)/shard_map/ppermute | solution.py:493
  (12 other events, 36.3 us)
